TPU v7x, 32 devices: a whole 2x2x4 slice. The times are simulated.
32 devices in a mesh: batch: 8 (over z, y), tensor: 4 (over x, core).
Axes of the slice: x: 2, y: 2, z: 4, core: 2. Of those that a mesh axis runs over, the one named last changes fastest.
Arguments:
- features: bfloat16 [8, 24, 24, 1024], P('batch', None, None, 'tensor'), may hold values from -6 to 6
- labels: int32 [8, 24, 24], P('batch'), may hold values from 0 to 149
- valid: int32 [8, 24, 24], P('batch'), may hold values 0 or 1
- sizes: int32 [8, 2], P('batch'), may hold values from 12 to 24, as said below
- params: float32 [4, 7897088], P('tensor', 'batch'), as said below
- first_moment: float32 [4, 7897088], P('tensor', 'batch'), may hold values from -5e-05 to 5e-05
- squared_mean: float32 [4, 7897088], P('tensor', 'batch'), may hold values from 8e-11 to 3.2e-10
- average: float32 [4, 7897088], P('tensor', 'batch')
Outputs:
- new_params: float32 [4, 7897088], P('tensor', 'batch')
- new_first: float32 [4, 7897088], P('tensor', 'batch')
- new_second: float32 [4, 7897088], P('tensor', 'batch')
- new_average: float32 [4, 7897088], P('tensor', 'batch')
- param_copy: bfloat16 [4, 7897088], P('tensor', 'batch')
- grad_norm: float32 [], replicated
- loss_sum: float32 [], replicated
- loss_weight: float32 [], replicated
- unite_shift_grad: float32 [512], P('tensor')
Inputs may be any that keep to these rules, and one draw needn't show every extreme that they name: `sizes`: every image spans at least half the map in each direction, and some image fills the whole map. `params`: gammas lie near one and are positive.
All inputs are finite; a program needn't handle non-finite values. No bound on the sum of `valid` on one device may be relied on, other than what follows from the above.
Results may differ from a plain program's by a relative error of at most 0.028.
Values may be sent and summed in bfloat16 or wider, within the bound.
A program may use at most 256 MiB of HBM per device.

v0:
```python
import jax
import jax.numpy as jnp
from jax import lax
from jax.sharding import PartitionSpec as P

C_IN = 1024
MID = 512
C_OUT = 2048
PPM = 512
AUXW = 256
NCLS = 150
MAP = 24
STEP = 3


BIN_COUNTS = (1, 2, 3, 6)
BIN_STARTS = (0, 1, 5, 14)


def segment_shapes(splits):
    return [
        (C_IN, MID // splits),
        (C_IN, C_OUT // splits),
        (9, MID, MID // splits),
        (MID, C_OUT // splits),
        (4, C_OUT // splits, PPM),
        (9, C_OUT + 4 * PPM, PPM // splits),
        (PPM // splits, NCLS),
        (9, C_IN, AUXW // splits),
        (AUXW // splits, NCLS),
        (2, (2 * MID + 2 * C_OUT + 5 * PPM + AUXW) // splits),
    ]


def unflatten(rows, splits):
    split_parts = []
    start = 0
    for shape in segment_shapes(splits):
        count = 1
        for extent in shape:
            count = count * extent
        count = count // rows.shape[0]
        split_parts.append(rows[:, start : start + count].reshape(shape))
        start = start + count
    return split_parts


def gain_pieces(gains, splits):
    widths = [MID, C_OUT, MID, C_OUT, PPM, PPM, PPM, PPM, PPM, AUXW]
    split_parts = []
    start = 0
    for width in widths:
        step_width = width // splits
        split_parts.append(gains[:, start : start + step_width])
        start = start + step_width
    return split_parts


def shifted(field, down, right):
    image_height, width = (field.shape[1], field.shape[2])
    rows_pad, cols_pad = (abs(down), abs(right))
    padded = jnp.pad(field, ((0, 0), (rows_pad, rows_pad), (cols_pad, cols_pad), (0, 0)))
    return padded[
        :,
        rows_pad + down : rows_pad + down + image_height,
        cols_pad + right : cols_pad + right + width,
        :,
    ]


def conv_forward(field, kernel, spacing):
    total = jnp.zeros(field.shape[:-1] + (kernel.shape[2],), jnp.float32)
    for tap in range(9):
        moved = shifted(field, (tap // 3 - 1) * spacing, (tap % 3 - 1) * spacing)
        total = total + jnp.dot(moved, kernel[tap], preferred_element_type=jnp.float32)
    return total


def conv_input_back(grad, kernel, spacing):
    total = jnp.zeros(grad.shape[:-1] + (kernel.shape[1],), jnp.float32)
    for tap in range(9):
        product = jnp.dot(grad, kernel[tap].T, preferred_element_type=jnp.float32)
        total = total + shifted(product, -(tap // 3 - 1) * spacing, -(tap % 3 - 1) * spacing)
    return total


def conv_kernel_back(field, grad, spacing):
    return jnp.stack(
        [
            jnp.einsum(
                "ihwc,ihwd->cd",
                shifted(field, (tap // 3 - 1) * spacing, (tap % 3 - 1) * spacing),
                grad,
                preferred_element_type=jnp.float32,
            )
            for tap in range(9)
        ]
    )


def silu_slope(value):
    gate = jax.nn.sigmoid(value)
    return gate * (1.0 + value * (1.0 - gate))


def channel_sums(values):
    return values.reshape(-1, values.shape[-1]).sum(0)


def masked_norm_apply(items, extra):
    sends = []
    for value, mask, norm in items:
        sends = sends + [
            channel_sums(value * mask),
            channel_sums(value * value * mask),
            jnp.sum(mask) * jnp.ones((1,), jnp.float32),
        ]
    totals = lax.psum(tuple(sends + extra), "batch")
    results = []
    for index, (value, mask, norm) in enumerate(items):
        count = totals[3 * index + 2]
        mean = totals[3 * index] / count
        spread = totals[3 * index + 1] / count - mean * mean
        scaling = lax.rsqrt(spread + 1e-05)
        normed = (value - mean) * scaling
        results.append((norm[0] * normed + norm[1], normed, scaling, count, mask, norm[0]))
    return (results, totals[3 * len(items) :])


def norm_backward(items):
    sends = []
    for grad, kept in items:
        sends = sends + [channel_sums(grad), channel_sums(grad * kept[1])]
    totals = lax.psum(tuple(sends), "batch")
    results = []
    for index, (grad, kept) in enumerate(items):
        outcome, normed, scaling, count, mask, gamma = kept
        first_sum, second_sum = (totals[2 * index], totals[2 * index + 1])
        inner = grad - mask * (first_sum + normed * second_sum) / count
        results.append(gamma * scaling * inner)
    return (results, sends, totals)


def bin_tables(extent, bins, length):
    which = jnp.arange(bins, dtype=jnp.int32)[None, :, None]
    place = jnp.arange(length, dtype=jnp.int32)[None, None, :]
    edge = extent[:, None, None]
    lower = which * edge // bins
    upper = ((which + 1) * edge + bins - 1) // bins
    member = ((place >= lower) & (place < upper)).astype(jnp.float32)
    target = jnp.minimum(place * bins // edge, bins - 1)
    chosen = (target == which).astype(jnp.float32)
    return (member, chosen)


def spread_bins(merged, branch, tables, images):
    joined = [merged]
    for group, bins in enumerate(BIN_COUNTS):
        rows_in, cols_in, rows_pick, cols_pick, cell_count = tables[group]
        piece = branch[:, BIN_STARTS[group] : BIN_STARTS[group] + bins * bins].reshape(
            images, bins, bins, -1
        )
        joined.append(
            jnp.einsum(
                "ikh,ilw,iklc->ihwc",
                rows_pick.astype(jnp.bfloat16),
                cols_pick.astype(jnp.bfloat16),
                piece,
                preferred_element_type=jnp.float32,
            ).astype(jnp.bfloat16)
        )
    return jnp.concatenate(joined, axis=-1)


def pick_bins(d_joined, width, tables, images):
    branch_width = (d_joined.shape[-1] - width) // 4
    d_up = []
    for group, bins in enumerate(BIN_COUNTS):
        rows_in, cols_in, rows_pick, cols_pick, cell_count = tables[group]
        piece = d_joined[..., width + group * branch_width : width + (group + 1) * branch_width]
        d_up.append(
            jnp.einsum("ikh,ilw,ihwc->iklc", rows_pick, cols_pick, piece).reshape(
                images, bins * bins, -1
            )
        )
    return (d_joined[..., :width], jnp.concatenate(d_up, axis=1))


def gather_channels(field):
    return lax.all_gather(field, "tensor", axis=3, tiled=True)


def scatter_channels(field):
    return lax.psum_scatter(
        field.astype(jnp.bfloat16), "tensor", scatter_dimension=3, tiled=True
    ).astype(jnp.float32)


def local(features, labels, valid, sizes, params, first_moment, squared_mean, average):
    splits = lax.axis_size("tensor")
    owners = lax.axis_size("batch")
    images = features.shape[0]
    gathered = lax.all_gather(params.astype(jnp.bfloat16), "batch", axis=0, tiled=True)
    (
        w_reduce,
        w_short,
        w_middle,
        w_expand,
        w_branch,
        w_unite,
        w_classes,
        w_aux,
        w_aux_classes,
        gains,
    ) = unflatten(gathered, splits)
    norms = [(piece[0], piece[1]) for piece in gain_pieces(gains.astype(jnp.float32), splits)]
    rows_at = jnp.arange(MAP, dtype=jnp.int32)
    inside = (rows_at[None, :, None] < sizes[:, 0][:, None, None]) & (
        rows_at[None, None, :] < sizes[:, 1][:, None, None]
    )
    inside = inside.astype(jnp.float32)[..., None]
    counted = inside * valid.astype(jnp.float32)[..., None]
    labels_hot = (labels[..., None] == jnp.arange(NCLS, dtype=jnp.int32)).astype(jnp.float32)
    class_local = channel_sums(labels_hot * counted)
    whole = lax.all_gather(features, "tensor", axis=3, tiled=True)
    pre_reduce = jnp.dot(whole, w_reduce, preferred_element_type=jnp.float32)
    pre_short = jnp.dot(whole, w_short, preferred_element_type=jnp.float32)
    pre_aux = conv_forward(whole, w_aux, 1)
    leading_part, label_tally = masked_norm_apply(
        [
            (pre_reduce, inside, norms[0]),
            (pre_short, inside, norms[1]),
            (pre_aux, inside, norms[9]),
        ],
        [class_local],
    )
    class_pixel_counts = label_tally[0]
    hidden_one = jax.nn.silu(leading_part[0][0]).astype(jnp.bfloat16)
    aux_act = jax.nn.silu(leading_part[2][0]).astype(jnp.bfloat16)
    hidden_full = gather_channels(hidden_one)
    pre_middle = conv_forward(hidden_full, w_middle, 4)
    second, unused = masked_norm_apply([(pre_middle, inside, norms[2])], [])
    hidden_two = jax.nn.silu(second[0][0]).astype(jnp.bfloat16)
    hidden_two_full = gather_channels(hidden_two)
    pre_expand = jnp.dot(hidden_two_full, w_expand, preferred_element_type=jnp.float32)
    third, unused = masked_norm_apply([(pre_expand, inside, norms[3])], [])
    summed = third[0][0] + leading_part[1][0]
    merged = jax.nn.silu(summed).astype(jnp.bfloat16)
    tables = []
    pooled_list = []
    partial_list = []
    for group, bins in enumerate(BIN_COUNTS):
        rows_in, rows_pick = bin_tables(sizes[:, 0], bins, MAP)
        cols_in, cols_pick = bin_tables(sizes[:, 1], bins, MAP)
        cell_count = (
            jnp.sum(rows_in, axis=2)[:, :, None, None] * jnp.sum(cols_in, axis=2)[:, None, :, None]
        )
        tables.append((rows_in, cols_in, rows_pick, cols_pick, cell_count))
        pooled = (
            jnp.einsum(
                "ikh,ilw,ihwc->iklc",
                rows_in.astype(jnp.bfloat16),
                cols_in.astype(jnp.bfloat16),
                merged,
                preferred_element_type=jnp.float32,
            )
            / cell_count
        )
        pooled = pooled.astype(jnp.bfloat16).reshape(images, bins * bins, -1)
        pooled_list.append(pooled)
        partial_list.append(
            jnp.einsum("ipc,cd->ipd", pooled, w_branch[group], preferred_element_type=jnp.float32)
        )
    branch_pre = lax.psum_scatter(
        jnp.concatenate(partial_list, axis=1).astype(jnp.bfloat16),
        "tensor",
        scatter_dimension=2,
        tiled=True,
    ).astype(jnp.float32)
    branch_items = []
    for group, bins in enumerate(BIN_COUNTS):
        piece = branch_pre[:, BIN_STARTS[group] : BIN_STARTS[group] + bins * bins]
        branch_items.append(
            (piece, jnp.ones(piece.shape[:-1] + (1,), jnp.float32), norms[4 + group])
        )
    fourth, unused = masked_norm_apply(branch_items, [])
    branch_act = jnp.concatenate([jax.nn.silu(kept[0]) for kept in fourth], axis=1).astype(
        jnp.bfloat16
    )
    merged_full, branch_full = (
        lax.all_gather(merged, "tensor", axis=3, tiled=True),
        lax.all_gather(branch_act, "tensor", axis=2, tiled=True),
    )
    joined = spread_bins(merged_full, branch_full, tables, images)
    pre_unite = conv_forward(joined, w_unite, 1)
    fifth, unused = masked_norm_apply([(pre_unite, inside, norms[8])], [])
    united = jax.nn.silu(fifth[0][0]).astype(jnp.bfloat16)
    logit_main, logit_aux = (
        lax.psum_scatter(
            jnp.dot(united, w_classes, preferred_element_type=jnp.float32).astype(jnp.bfloat16),
            "tensor",
            scatter_dimension=1,
            tiled=True,
        ).astype(jnp.float32),
        lax.psum_scatter(
            jnp.dot(aux_act, w_aux_classes, preferred_element_type=jnp.float32).astype(
                jnp.bfloat16
            ),
            "tensor",
            scatter_dimension=1,
            tiled=True,
        ).astype(jnp.float32),
    )
    total_valid = jnp.sum(class_pixel_counts)
    class_weight = total_valid / (NCLS * class_pixel_counts + total_valid)
    loss_weight = jnp.sum(class_pixel_counts * class_weight)
    cell_weight = jnp.sum(labels_hot * class_weight, axis=-1, keepdims=True) * counted
    band_rows = labels.shape[1] // splits
    band_start = lax.axis_index("tensor") * band_rows
    hot_band = lax.dynamic_slice_in_dim(labels_hot, band_start, band_rows, 1)
    weight_band = lax.dynamic_slice_in_dim(cell_weight, band_start, band_rows, 1)
    log_main = jax.nn.log_softmax(logit_main, axis=-1)
    log_aux = jax.nn.log_softmax(logit_aux, axis=-1)
    loss_cells = -jnp.sum(hot_band * (log_main + 0.4 * log_aux), axis=-1, keepdims=True)
    loss_local = jnp.sum(weight_band * loss_cells)
    band_main = (weight_band * (jnp.exp(log_main) - hot_band) / loss_weight).astype(jnp.bfloat16)
    band_aux = (0.4 * weight_band * (jnp.exp(log_aux) - hot_band) / loss_weight).astype(
        jnp.bfloat16
    )
    grad_main, grad_aux = (
        lax.all_gather(band_main, "tensor", axis=1, tiled=True),
        lax.all_gather(band_aux, "tensor", axis=1, tiled=True),
    )
    reduced = {}

    def settle(index, value):
        reduced[index] = value

    settle(6, jnp.einsum("ihwc,ihwk->ck", united, grad_main, preferred_element_type=jnp.float32))
    settle(8, jnp.einsum("ihwc,ihwk->ck", aux_act, grad_aux, preferred_element_type=jnp.float32))
    d_united = jnp.dot(grad_main, w_classes.T, preferred_element_type=jnp.float32) * silu_slope(
        fifth[0][0]
    )
    d_aux = jnp.dot(grad_aux, w_aux_classes.T, preferred_element_type=jnp.float32) * silu_slope(
        leading_part[2][0]
    )
    back_one, sums_one, totals_one = norm_backward([(d_united, fifth[0]), (d_aux, leading_part[2])])
    unite_shift_grad = totals_one[0]
    d_unite_pre = back_one[0].astype(jnp.bfloat16)
    d_aux_pre = back_one[1].astype(jnp.bfloat16)
    settle(5, conv_kernel_back(joined, d_unite_pre, 1))
    d_merged, d_branch = pick_bins(conv_input_back(d_unite_pre, w_unite, 1), C_OUT, tables, images)
    d_merged, d_branch = (
        lax.psum_scatter(
            d_merged.astype(jnp.bfloat16), "tensor", scatter_dimension=3, tiled=True
        ).astype(jnp.float32),
        lax.psum_scatter(
            d_branch.astype(jnp.bfloat16), "tensor", scatter_dimension=2, tiled=True
        ).astype(jnp.float32),
    )
    settle(7, conv_kernel_back(whole, d_aux_pre, 1))
    branch_back = []
    for group, bins in enumerate(BIN_COUNTS):
        piece = d_branch[:, BIN_STARTS[group] : BIN_STARTS[group] + bins * bins]
        branch_back.append((piece * silu_slope(fourth[group][0]), fourth[group]))
    back_two, sums_two, unused = norm_backward(branch_back)
    d_branch_pre = jnp.concatenate(back_two, axis=1).astype(jnp.bfloat16)
    d_branch_full = lax.all_gather(d_branch_pre, "tensor", axis=2, tiled=True)
    branch_grads = []
    for group, bins in enumerate(BIN_COUNTS):
        rows_in, cols_in, rows_pick, cols_pick, cell_count = tables[group]
        piece = d_branch_full[:, BIN_STARTS[group] : BIN_STARTS[group] + bins * bins]
        branch_grads.append(
            jnp.einsum("ipc,ipd->cd", pooled_list[group], piece, preferred_element_type=jnp.float32)
        )
        d_pooled = jnp.dot(piece, w_branch[group].T, preferred_element_type=jnp.float32).reshape(
            images, bins, bins, -1
        )
        d_merged = d_merged + jnp.einsum(
            "ikh,ilw,iklc->ihwc", rows_in, cols_in, d_pooled / cell_count
        )
    settle(4, jnp.stack(branch_grads))
    d_summed = d_merged * silu_slope(summed)
    back_three, sums_three, unused = norm_backward(
        [(d_summed, third[0]), (d_summed, leading_part[1])]
    )
    d_expand_pre = back_three[0].astype(jnp.bfloat16)
    d_short_pre = back_three[1].astype(jnp.bfloat16)
    settle(
        3,
        jnp.einsum(
            "ihwc,ihwd->cd", hidden_two_full, d_expand_pre, preferred_element_type=jnp.float32
        ),
    )
    settle(1, jnp.einsum("ihwc,ihwd->cd", whole, d_short_pre, preferred_element_type=jnp.float32))
    d_two = scatter_channels(jnp.dot(d_expand_pre, w_expand.T, preferred_element_type=jnp.float32))
    back_four, sums_four, unused = norm_backward([(d_two * silu_slope(second[0][0]), second[0])])
    d_middle_pre = back_four[0].astype(jnp.bfloat16)
    settle(2, conv_kernel_back(hidden_full, d_middle_pre, 4))
    d_one = scatter_channels(conv_input_back(d_middle_pre, w_middle, 4))
    back_five, sums_five, unused = norm_backward(
        [(d_one * silu_slope(leading_part[0][0]), leading_part[0])]
    )
    settle(
        0,
        jnp.einsum(
            "ihwc,ihwd->cd",
            whole,
            back_five[0].astype(jnp.bfloat16),
            preferred_element_type=jnp.float32,
        ),
    )
    beta_grads = (
        [sums_five[0], sums_three[2], sums_four[0], sums_three[0]]
        + [sums_two[2 * g] for g in range(4)]
        + [sums_one[0], sums_one[2]]
    )
    gamma_grads = (
        [sums_five[1], sums_three[3], sums_four[1], sums_three[1]]
        + [sums_two[2 * g + 1] for g in range(4)]
        + [sums_one[1], sums_one[3]]
    )
    settle(9, jnp.stack([jnp.concatenate(gamma_grads), jnp.concatenate(beta_grads)]))
    ordered = [reduced[index] for index in range(10)]
    grad_share = lax.psum_scatter(
        jnp.concatenate([part.reshape(owners, -1) for part in ordered], axis=1),
        "batch",
        scatter_dimension=0,
        tiled=True,
    )
    square_all, loss_sum = lax.psum(
        (jnp.sum(grad_share * grad_share), loss_local), ("batch", "tensor")
    )
    grad_norm = jnp.sqrt(square_all)
    clipped = grad_share * jnp.minimum(1.0, 0.05 / (grad_norm + 1e-06))
    new_first = 0.5 * first_moment + 0.5 * clipped
    new_second = 0.5 * squared_mean + 0.5 * clipped * clipped
    keep = 1.0 - 0.5**STEP
    new_params = params - 0.01 * (
        new_first / keep / (jnp.sqrt(new_second / keep) + 1e-08) + 0.01 * params
    )
    new_average = 0.999 * average + 0.001 * new_params
    return (
        new_params,
        new_first,
        new_second,
        new_average,
        new_params.astype(jnp.bfloat16),
        grad_norm,
        loss_sum,
        loss_weight,
        unite_shift_grad,
    )


def solution(mesh):
    return jax.shard_map(
        local,
        mesh=mesh,
        in_specs=(
            P("batch", None, None, "tensor"),
            P("batch", None, None),
            P("batch", None, None),
            P("batch", None),
            P("tensor", "batch"),
            P("tensor", "batch"),
            P("tensor", "batch"),
            P("tensor", "batch"),
        ),
        out_specs=(
            P("tensor", "batch"),
            P("tensor", "batch"),
            P("tensor", "batch"),
            P("tensor", "batch"),
            P("tensor", "batch"),
            P(),
            P(),
            P(),
            P("tensor"),
        ),
        check_vma=False,
    )
```

profile of v0, /device:TPU:0, one launch (start us, length us, event | category | flops | bytes accessed | tf_op | source)
XLA Modules:
  0.0 2348.6 jit_solution(17972075741411014744)
XLA Ops:
  7.2 7.5 convert_bitcast_fusion
  43.7 574.8 %all-gather.12.cloned.1.call-done = bf16[8,1,987136]{2,1,0:T(2,128)(2,1)} async-done(((bf16[1,1,987136]{2,1,0:T(2,128)(2,1)}), bf16[8,1,987136]{2,1,0:T(2,128)(2,1)}) %all-gather.12.cloned.1.call-update) | async-done | bytes 15794192 | tf_op jit(solution)/shard_map/all_gather | solution.py:203
  618.5 14.6 copy.233
  633.3 3.0 fusion.511
  643.5 20.7 all-reduce.36
  666.0 7.8 all-gather
  682.4 17.2 all-reduce.35
  701.9 7.1 all-gather.1
  712.3 19.4 all-reduce.34
  762.2 9.2 slice.629
  772.3 11.7 reshape.3149
  797.8 20.4 all-reduce.33
  822.1 14.0 all_gather.32
  840.2 3.6 fusion.24
  843.9 3.8 fusion.34
  860.2 19.1 all-reduce.32
  884.4 14.1 reduce-scatter.16.cloned.1.call-done
  902.3 5.9 all_gather.33
  908.5 21.4 all-reduce.31
  930.6 6.5 convolution_bitcast_fusion
  937.1 6.4 convolution_bitcast_fusion.1
  943.5 5.1 convolution_bitcast_fusion.2
  948.6 5.1 convolution_bitcast_fusion.3
  953.7 5.0 convolution_bitcast_fusion.4
  958.8 5.0 convolution_bitcast_fusion.5
  963.7 5.0 convolution_bitcast_fusion.6
  968.7 4.9 convolution_bitcast_fusion.7
  973.6 26.8 %fusion.7 = bf16[1,24,24,4096]{3,2,1,0:T(8,128)(2,1)} fusion(f32[1,24,24,4096]{3,2,1,0:T(8,128)} %convolution_bitcast_fusion.6, f32[1,24,24,4096]{3,2,1,0:T(8,128)} %convolution_bitcast_fusion.1, f32[1,24,24,4096]{3,2,1,0:T(8,128)} %convolution_bitcast_fusion.4, f32[1,24,24,4096]{3,2,1,0:T(8,128)} %convolution_bitcast_fusion.3, ...), kind=kOutput, calls=%fused_computation.16 | convolution fusion | flops 625213440 | bytes 81412096 | tf_op jit(solution)/shard_map/dot_general | solution.py:82
  1001.9 3.4 slice.1045
  1005.3 5.2 fusion.16
  1014.2 5.4 fusion.15
  1019.6 5.4 fusion.14
  1024.9 2.9 fusion.13
  1027.9 3.0 fusion.12
  1030.9 2.9 fusion.11
  1033.8 2.9 fusion.10
  1036.8 3.0 fusion.9
  1041.3 5.6 fusion.8
  1047.1 16.1 reshape.3181
  1064.6 17.9 all-reduce.30
  1085.1 5.2 all_gather.34
  1097.8 3.5 fusion.88
  1101.4 18.5 all-reduce.29
  1123.0 3.6 copy.164
  1133.2 5.1 reshape.3180
  1140.1 8.6 reduce-scatter.26.cloned.1.call-done
  1151.1 21.4 all-reduce.28
  1195.5 3.4 copy.166
  1198.9 4.8 reshape.3331
  1206.2 3.5 reshape.3175
  1214.3 5.9 all_gather.35
  1222.8 6.1 reduce-scatter.28.cloned.1.call-done
  1238.0 21.9 all-reduce.27
  1260.1 4.3 convolution_bitcast_fusion.17
  1276.1 3.5 copy.151
  1279.6 3.7 reshape.3194
  1284.2 3.1 constant_dynamic-update-slice_fusion.6
  1293.0 13.7 constant_dynamic-update-slice_fusion.2
  1308.4 7.3 dynamic-update-slice.7
  1320.5 918.3 %all-reduce.39.cloned.1.call-done = f32[8,987136]{1,0:T(8,128)} async-done(((f32[8,987136]{1,0:T(8,128)}), f32[8,987136]{1,0:T(8,128)}) %all-reduce.39.cloned.1.call-update) | async-done | bytes 31588368
  2238.9 15.6 multiply_reduce_fusion
  2254.5 39.8 %all-reduce.26 = (f32[]{:T(128)}, f32[]{:T(128)}) all-reduce(f32[]{:T(128)} %multiply_reduce_fusion, f32[]{:T(128)} %fusion.340), channel_id=1, replica_groups=mesh['batch'=8,'tensor'=4] {'batch','tensor'}, use_global_device_ids=true, to_apply=%region_104.107 | all-reduce | flops 2 | bytes 16 | tf_op jit(solution)/shard_map/psum | solution.py:431
  2295.1 37.4 %fusion.503 = (bf16[1,987136]{1,0:T(2,128)(2,1)}, f32[1,987136]{1,0:T(1,128)S(1)}, f32[1,987136]{1,0:T(1,128)}, f32[1,987136]{1,0:T(1,128)}) fusion(f32[1,987136]{1,0:T(1,128)} %param.15, f32[]{:T(128)S(6)} %min.35, f32[8,987136]{1,0:T(8,128)} %all-reduce.39.cloned.1.call-done, u32[]{:T(128)} %bitcast.360, f32[1,987136]{1,0:T(1,128)} %param.16, ...), kind=kLoop, calls=%fused_computation.857 | loop fusion | flops 15794176 | bytes 29614088 | tf_op jit(solution)/shard_map/convert_element_type | solution.py:448
  2332.5 8.0 multiply_add_fusion.1
  (813 shorter events, 221.0 us)
Async XLA Ops:
  7.2 611.4 %all-gather.12.cloned.1.call-start = ((), (), s32[]{:S(2)}) async-start(), calls=%async_computation.12 | async-start | bytes 35536896 | tf_op jit(solution)/shard_map/all_gather | solution.py:203
  14.8 626.9 %all-gather.8.cloned.1.call-start = ((), (), s32[]{:S(2)}) async-start(), calls=%async_computation.7 | async-start | bytes 1474560 | tf_op jit(solution)/shard_map/all_gather | solution.py:225
  15.5 781.3 %reduce-scatter.22.cloned.1.call-start = ((), (), s32[]{:S(2)}) async-start(), calls=%async_computation.13 | async-start | bytes 163840
  29.7 603.4 %copy-start.214 = (s32[2]{0:T(128)}, s32[2]{0:T(128)S(1)}, u32[]{:S(2)}) copy-start(s32[2]{0:T(128)S(1)} %get-tuple-element.205) | copy-start | bytes 28
  29.7 603.4 %copy-start.216 = (s32[2]{0:T(128)}, s32[2]{0:T(128)S(1)}, u32[]{:S(2)}) copy-start(s32[2]{0:T(128)S(1)} %get-tuple-element.206) | copy-start | bytes 28
  30.4 602.8 %copy-start.224 = (s32[3]{0:T(128)}, s32[3]{0:T(128)S(1)}, u32[]{:S(2)}) copy-start(s32[3]{0:T(128)S(1)} %get-tuple-element.203) | copy-start | bytes 40
  30.4 602.8 %copy-start.226 = (s32[3]{0:T(128)}, s32[3]{0:T(128)S(1)}, u32[]{:S(2)}) copy-start(s32[3]{0:T(128)S(1)} %get-tuple-element.204) | copy-start | bytes 40
  32.4 600.8 %copy-start.185 = (s32[6]{0:T(128)}, s32[6]{0:T(128)S(1)}, u32[]{:S(2)}) copy-start(s32[6]{0:T(128)S(1)} %get-tuple-element.193) | copy-start | bytes 76
  32.4 600.8 %copy-start.188 = (s32[6]{0:T(128)}, s32[6]{0:T(128)S(1)}, u32[]{:S(2)}) copy-start(s32[6]{0:T(128)S(1)} %get-tuple-element.194) | copy-start | bytes 76
  33.1 600.1 %copy-start.218 = (s32[2]{0:T(128)}, s32[2]{0:T(128)S(1)}, u32[]{:S(2)}) copy-start(s32[2]{0:T(128)S(1)} %get-tuple-element.197) | copy-start | bytes 28
  33.1 600.1 %copy-start.221 = (s32[2]{0:T(128)}, s32[2]{0:T(128)S(1)}, u32[]{:S(2)}) copy-start(s32[2]{0:T(128)S(1)} %get-tuple-element.198) | copy-start | bytes 28
  33.8 599.5 %copy-start.191 = (s32[3]{0:T(128)}, s32[3]{0:T(128)S(1)}, u32[]{:S(2)}) copy-start(s32[3]{0:T(128)S(1)} %get-tuple-element.195) | copy-start | bytes 40
  33.8 599.5 %copy-start.194 = (s32[3]{0:T(128)}, s32[3]{0:T(128)S(1)}, u32[]{:S(2)}) copy-start(s32[3]{0:T(128)S(1)} %get-tuple-element.196) | copy-start | bytes 40
  641.1 59.7 %copy-start.84 = (f32[128]{0:T(128)}, f32[128]{0:T(128)S(1)}, u32[]{:S(2)}) copy-start(f32[128]{0:T(128)S(1)} %get-tuple-element.163) | copy-start | bytes 1540
  641.1 59.7 %copy-start.86 = (f32[128]{0:T(128)}, f32[128]{0:T(128)S(1)}, u32[]{:S(2)}) copy-start(f32[128]{0:T(128)S(1)} %get-tuple-element.165) | copy-start | bytes 1540
  641.7 92.2 %copy-start.70 = (f32[1,512]{1,0:T(1,128)}, f32[1,512]{1,0:T(1,128)S(1)}, u32[]{:S(2)}) copy-start(f32[1,512]{1,0:T(1,128)S(1)} %get-tuple-element.173) | copy-start | bytes 6148
  641.7 92.3 %copy-start.72 = (f32[1,512]{1,0:T(1,128)}, f32[1,512]{1,0:T(1,128)S(1)}, u32[]{:S(2)}) copy-start(f32[1,512]{1,0:T(1,128)S(1)} %get-tuple-element.175) | copy-start | bytes 6148
  680.1 28.9 %copy-start.6 = (bf16[1,24,24,1024]{3,2,1,0:T(8,128)(2,1)S(1)}, bf16[1,24,24,1024]{3,2,1,0:T(8,128)(2,1)}, u32[]{:S(2)}) copy-start(bf16[1,24,24,1024]{3,2,1,0:T(8,128)(2,1)} %all-gather.8.cloned.1.call-done) | copy-start | bytes 3538948
  712.3 28.8 %copy-start.21 = (f32[24,24,512]{2,1,0:T(8,128)}, f32[24,24,512]{2,1,0:T(8,128)S(1)}, u32[]{:S(2)}) copy-start(f32[24,24,512]{2,1,0:T(8,128)S(1)} %get-tuple-element.187) | copy-start | bytes 3538948
  756.0 81.0 %all-gather.10.cloned.1.call-start = ((), (), s32[]{:S(2)}) async-start(), calls=%async_computation.11 | async-start | bytes 2949120 | tf_op jit(solution)/shard_map/all_gather | solution.py:291
  788.3 110.2 %reduce-scatter.16.cloned.1.call-start = ((), (), s32[]{:S(2)}) async-start(), calls=%async_computation.8 | async-start | bytes 368640 | tf_op jit(solution)/shard_map/reduce_scatter | solution.py:299
  794.5 27.6 %copy-start.126 = (f32[128]{0:T(128)S(1)}, f32[128]{0:T(128)}, u32[]{:S(2)}) copy-start(f32[128]{0:T(128)} %get-tuple-element.157) | copy-start | bytes 1540
  794.5 41.7 %copy-start.203 = (s32[24]{0:T(128)S(1)}, s32[24]{0:T(128)}, u32[]{:S(2)}) copy-start(s32[24]{0:T(128)} %get-tuple-element.210) | copy-start | bytes 292
  794.5 41.9 %copy-start.150 = (s32[24]{0:T(128)S(1)}, s32[24]{0:T(128)}, u32[]{:S(2)}) copy-start(s32[24]{0:T(128)} %get-tuple-element.209) | copy-start | bytes 292
  794.5 42.1 %copy-start.141 = (s32[24]{0:T(128)S(1)}, s32[24]{0:T(128)}, u32[]{:S(2)}) copy-start(s32[24]{0:T(128)} %get-tuple-element.215) | copy-start | bytes 292
  797.7 41.2 %copy-start.42 = (f32[1,50,128]{2,1,0:T(8,128)}, f32[1,50,128]{2,1,0:T(8,128)S(1)}, u32[]{:S(2)}) copy-start(f32[1,50,128]{2,1,0:T(8,128)S(1)} %convert_element_type.674) | copy-start | bytes 76804
  880.9 182.3 %reduce-scatter.24.cloned.1.call-start = ((), (), s32[]{:S(2)}) async-start(), calls=%async_computation.14 | async-start | bytes 163840
  884.4 52.7 %copy-start.67 = (f32[1,6,24,1]{2,1,3,0:T(8,128)}, f32[1,6,24,1]{2,1,3,0:T(8,128)S(1)}, u32[]{:S(2)}) copy-start(f32[1,6,24,1]{2,1,3,0:T(8,128)S(1)} %get-tuple-element.110) | copy-start | bytes 1732
  899.5 37.6 %copy-start.61 = (f32[6,24]{1,0:T(8,128)}, f32[6,24]{1,0:T(8,128)S(1)}, u32[]{:S(2)}) copy-start(f32[6,24]{1,0:T(8,128)S(1)} %convert_reduce_fusion.1) | copy-start | bytes 1732
  900.6 36.5 %copy-start.65 = (f32[6,24]{1,0:T(8,128)}, f32[6,24]{1,0:T(8,128)S(1)}, u32[]{:S(2)}) copy-start(f32[6,24]{1,0:T(8,128)S(1)} %log.9) | copy-start | bytes 1732
  908.5 28.6 %copy-start.228 = (f32[128]{0:T(128)}, f32[128]{0:T(128)S(1)}, u32[]{:S(2)}) copy-start(f32[128]{0:T(128)S(1)} %get-tuple-element.33) | copy-start | bytes 1540
  908.5 28.7 %copy-start.229 = (f32[128]{0:T(128)}, f32[128]{0:T(128)S(1)}, u32[]{:S(2)}) copy-start(f32[128]{0:T(128)S(1)} %get-tuple-element.32) | copy-start | bytes 1540
  1014.1 83.6 %reduce-scatter.18.cloned.1.call-start = ((), (), s32[]{:S(2)}) async-start(), calls=%async_computation.9 | async-start | bytes 2949120 | tf_op jit(solution)/shard_map/reduce_scatter | solution.py:354
  1040.8 108.0 %reduce-scatter.26.cloned.1.call-start = ((), (), s32[]{:S(2)}) async-start(), calls=%async_computation.15 | async-start | bytes 819200
  1047.0 35.5 %copy-start.173 = (f32[128]{0:T(128)S(1)}, f32[128]{0:T(128)}, u32[]{:S(2)}) copy-start(f32[128]{0:T(128)} %get-tuple-element.139) | copy-start | bytes 1540
  1047.0 36.1 %copy-start.172 = (f32[128]{0:T(128)S(1)}, f32[128]{0:T(128)}, u32[]{:S(2)}) copy-start(f32[128]{0:T(128)} %get-tuple-element.116) | copy-start | bytes 1540
  1047.0 36.7 %copy-start.171 = (f32[128]{0:T(128)S(1)}, f32[128]{0:T(128)}, u32[]{:S(2)}) copy-start(f32[128]{0:T(128)} %get-tuple-element.170) | copy-start | bytes 1540
  1047.0 37.4 %copy-start.161 = (f32[128]{0:T(128)S(1)}, f32[128]{0:T(128)}, u32[]{:S(2)}) copy-start(f32[128]{0:T(128)} %get-tuple-element.167) | copy-start | bytes 1540
  1047.0 43.5 %copy-start.64 = (bf16[4,512]{1,0:T(4,128)(2,1)S(1)}, bf16[4,512]{1,0:T(4,128)(2,1)}, u32[]{:S(2)}) copy-start(bf16[4,512]{1,0:T(4,128)(2,1)} %copy-done.63) | copy-start | bytes 12292
  1047.0 44.8 %copy-start.49 = (bf16[512,512,1]{1,0,2:T(8,128)(2,1)S(1)}, bf16[512,512,1]{1,0,2:T(8,128)(2,1)}, u32[]{:S(2)}) copy-start(bf16[512,512,1]{1,0,2:T(8,128)(2,1)} %reshape.3269) | copy-start | bytes 1572868
  1047.1 44.8 %copy-start.164 = (f32[3,3]{1,0:T(4,128)S(1)}, f32[3,3]{1,0:T(4,128)}, u32[]{:S(2)}) copy-start(f32[3,3]{1,0:T(4,128)} %broadcast_multiply_fusion.3) | copy-start | bytes 112
  1063.2 29.0 %copy-start.225 = (s32[3]{0:T(128)S(1)}, s32[3]{0:T(128)}, u32[]{:S(2)}) copy-start(s32[3]{0:T(128)} %copy-done.224) | copy-start | bytes 40
  1063.2 29.0 %copy-start.227 = (s32[3]{0:T(128)S(1)}, s32[3]{0:T(128)}, u32[]{:S(2)}) copy-start(s32[3]{0:T(128)} %copy-done.226) | copy-start | bytes 40
  1063.2 31.6 %copy-start.48 = (bf16[512,512,1]{1,0,2:T(8,128)(2,1)S(1)}, bf16[512,512,1]{1,0,2:T(8,128)(2,1)}, u32[]{:S(2)}) copy-start(bf16[512,512,1]{1,0,2:T(8,128)(2,1)} %reshape.3272) | copy-start | bytes 1572868
  1063.2 31.6 %copy-start.143 = (f32[6,6]{1,0:T(8,128)S(1)}, f32[6,6]{1,0:T(8,128)}, u32[]{:S(2)}) copy-start(f32[6,6]{1,0:T(8,128)} %broadcast_multiply_fusion.2) | copy-start | bytes 436
  1063.2 31.9 %copy-start.146 = (s32[6]{0:T(128)S(1)}, s32[6]{0:T(128)}, u32[]{:S(2)}) copy-start(s32[6]{0:T(128)} %copy-done.145) | copy-start | bytes 76
  1063.2 31.9 %copy-start.148 = (s32[6]{0:T(128)S(1)}, s32[6]{0:T(128)}, u32[]{:S(2)}) copy-start(s32[6]{0:T(128)} %copy-done.147) | copy-start | bytes 76
  1064.3 27.8 %copy-start.168 = (f32[1,1,128]{2,1,0:T(1,128)}, f32[1,1,128]{2,1,0:T(1,128)S(1)}, u32[]{:S(2)}) copy-start(f32[1,1,128]{2,1,0:T(1,128)S(1)} %get-tuple-element.125) | copy-start | bytes 1540
  1064.4 27.7 %copy-start.167 = (f32[128]{0:T(128)}, f32[128]{0:T(128)S(1)}, u32[]{:S(2)}) copy-start(f32[128]{0:T(128)S(1)} %get-tuple-element.46) | copy-start | bytes 1540
  1064.4 28.0 %copy-start.193 = (s32[3]{0:T(128)S(1)}, s32[3]{0:T(128)}, u32[]{:S(2)}) copy-start(s32[3]{0:T(128)} %copy-done.191) | copy-start | bytes 40
  1064.4 31.0 %copy-start.187 = (s32[6]{0:T(128)S(1)}, s32[6]{0:T(128)}, u32[]{:S(2)}) copy-start(s32[6]{0:T(128)} %copy-done.185) | copy-start | bytes 76
  1064.4 31.0 %copy-start.190 = (s32[6]{0:T(128)S(1)}, s32[6]{0:T(128)}, u32[]{:S(2)}) copy-start(s32[6]{0:T(128)} %copy-done.188) | copy-start | bytes 76
  1129.6 80.1 %reduce-scatter.20.cloned.1.call-start = ((), (), s32[]{:S(2)}) async-start(), calls=%async_computation.10 | async-start | bytes 368640 | tf_op jit(solution)/shard_map/reduce_scatter | solution.py:305
  1139.0 33.5 %copy-start.149 = (f32[128]{0:T(128)S(1)}, f32[128]{0:T(128)}, u32[]{:S(2)}) copy-start(f32[128]{0:T(128)} %get-tuple-element.111) | copy-start | bytes 1540
  1139.0 34.3 %copy-start.10 = (bf16[9,512,128]{2,1,0:T(8,128)(2,1)S(1)}, bf16[9,512,128]{2,1,0:T(8,128)(2,1)}, u32[]{:S(2)}) copy-start(bf16[9,512,128]{2,1,0:T(8,128)(2,1)} %copy-done.9) | copy-start | bytes 3538948
  1186.5 42.3 %reduce-scatter.28.cloned.1.call-start = ((), (), s32[]{:S(2)}) async-start(), calls=%async_computation.16 | async-start | bytes 819200
  1204.8 1034.0 %all-reduce.39.cloned.1.call-start = ((), (), s32[]{:S(2)}) async-start(), calls=%async_computation.17 | async-start | bytes 63176704
  1221.2 38.8 %copy-start.7 = (bf16[1,24,24,1024]{3,2,1,0:T(8,128)(2,1)S(1)}, bf16[1,24,24,1024]{3,2,1,0:T(8,128)(2,1)}, u32[]{:S(2)}) copy-start(bf16[1,24,24,1024]{3,2,1,0:T(8,128)(2,1)} %all-gather.8.cloned.1.call-done) | copy-start | bytes 3538948
  1221.2 38.8 %copy-start.37 = (f32[1,24,24,512]{3,2,1,0:T(8,128)S(1)}, f32[1,24,24,512]{3,2,1,0:T(8,128)}, u32[]{:S(2)}) copy-start(f32[1,24,24,512]{3,2,1,0:T(8,128)} %copy-done.36) | copy-start | bytes 3538948
  1221.2 38.8 %copy-start.109 = (f32[512]{0:T(512)S(1)}, f32[512]{0:T(512)}, u32[]{:S(2)}) copy-start(f32[512]{0:T(512)} %copy-done.107) | copy-start | bytes 6148
  1221.2 38.8 %copy-start.112 = (f32[512]{0:T(512)S(1)}, f32[512]{0:T(512)}, u32[]{:S(2)}) copy-start(f32[512]{0:T(512)} %copy-done.110) | copy-start | bytes 6148
  1222.7 37.3 %copy-start.162 = (f32[512]{0:T(512)S(1)}, f32[512]{0:T(512)}, u32[]{:S(2)}) copy-start(f32[512]{0:T(512)} %get-tuple-element.104) | copy-start | bytes 6148
  1222.8 37.3 %copy-start.182 = (f32[512]{0:T(512)S(1)}, f32[512]{0:T(512)}, u32[]{:S(2)}) copy-start(f32[512]{0:T(512)} %copy-done.181) | copy-start | bytes 6148
  2295.1 37.4 %copy-start.27 = (f32[1,987136]{1,0:T(1,128)S(1)}, f32[1,987136]{1,0:T(1,128)}, u32[]{:S(2)}) copy-start(f32[1,987136]{1,0:T(1,128)} %param.18) | copy-start | bytes 11845636
  (186 other events, 1788.0 us)
Sparse Core Ops, SparseCore 0:
  14.9 603.5 all-gather.11
  620.1 17.5 all-gather.7
  756.1 16.6 reduce-scatter.21
  788.4 21.1 all-gather.9
  881.0 17.4 reduce-scatter.15
  1014.2 15.9 reduce-scatter.23
  1040.9 29.3 reduce-scatter.17
  1129.7 19.0 reduce-scatter.25
  1186.6 16.5 reduce-scatter.19
  1206.4 22.4 reduce-scatter.27
  1318.9 919.9 all-reduce.38
where the time goes:
time: 2360 us; the launch traced here: 2350 us
  waiting for transfers between devices  1520 us (64%)
  blocking collectives  284 us (12%)
  matrix products  207 us (9%)
  local copies, waits for them, and re-layouts  183 us (8%)
  other arithmetic  128 us (5%)
    unnamed x16, waiting for transfers between devices  934 us
    all_gather x1, waiting for transfers between devices, local(): lax.all_gather(params.astype(jnp.bfloat16), 'batch', axis=0, tiled=True)  575 us
    psum x5, blocking collectives, norm_backward(): totals = lax.psum(tuple(sends), 'batch')  101 us
    psum x5, blocking collectives, masked_norm_apply(): totals = lax.psum(tuple(sends + extra), 'batch')  96.8 us
    unnamed x525, local copies, waits for them, and re-layouts  85.6 us
    dot_general x18, matrix products, conv_input_back(): product = jnp.dot(grad, kernel[tap].T, preferred_element_type=jnp.float32)  81.5 us
    dot_general x27, matrix products, conv_kernel_back(): jnp.einsum('ihwc,ihwd->cd', shifted(field, (tap // 3 - 1) * spacing, (tap...  50 us
  transfers between devices with their start and end apart: 11, of which 5 were waited for; matrix products, arithmetic and copies ran while one was open for 8% of the time, Pallas kernels for 0%

commit v1 on v0

--- a/solution.py
+++ b/solution.py
@@ -1,6 +1,10 @@
+import functools
+
 import jax
 import jax.numpy as jnp
 from jax import lax
+from jax.experimental import pallas as pl
+from jax.experimental.pallas import tpu as pltpu
 from jax.sharding import PartitionSpec as P
 
 C_IN = 1024
@@ -453,9 +457,565 @@
     )
 
 
+MESH = pl.DeviceIdType.MESH
+ANY = pl.BlockSpec(memory_space=pl.ANY)
+
+
+def gather_kernel(owners, count, order, *refs):
+    pieces, fulls = refs[:count], refs[count : 2 * count]
+    near_send, far_send, pass_send, recv, keep = refs[2 * count :]
+    me = lax.axis_index("batch")
+    half = owners // 2
+    partner = me + 1 - 2 * lax.rem(me, 2)
+
+    def peer_of(base, step):
+        return lax.rem(base + 2 * step, owners)
+
+    barrier = pltpu.get_barrier_semaphore()
+    pl.semaphore_signal(barrier, inc=1, device_id={"batch": partner}, device_id_type=MESH)
+    for step in range(1, half):
+        pl.semaphore_signal(
+            barrier, inc=1, device_id={"batch": peer_of(me, step)}, device_id_type=MESH
+        )
+    pl.semaphore_wait(barrier, half)
+
+    def near(seg):
+        return pltpu.make_async_remote_copy(
+            src_ref=pieces[seg],
+            dst_ref=fulls[seg].at[me],
+            send_sem=near_send.at[seg],
+            recv_sem=recv.at[seg, me],
+            device_id={"batch": partner},
+            device_id_type=MESH,
+        )
+
+    def far(seg, step):
+        return pltpu.make_async_remote_copy(
+            src_ref=pieces[seg],
+            dst_ref=fulls[seg].at[me],
+            send_sem=far_send.at[seg, step],
+            recv_sem=recv.at[seg, me],
+            device_id={"batch": peer_of(me, step)},
+            device_id_type=MESH,
+        )
+
+    def passed(seg, step, base):
+        source = peer_of(base, step)
+        return pltpu.make_async_remote_copy(
+            src_ref=fulls[seg].at[source],
+            dst_ref=fulls[seg].at[source],
+            send_sem=pass_send.at[seg, step],
+            recv_sem=recv.at[seg, source],
+            device_id={"batch": partner},
+            device_id_type=MESH,
+        )
+
+    for seg in order:
+        pltpu.make_async_copy(pieces[seg], fulls[seg].at[me], keep.at[seg]).start()
+        for step in range(1, half):
+            far(seg, step).start()
+        near(seg).start()
+    for seg in order:
+        for step in range(1, half):
+            passed(seg, step, me).wait_recv()
+            passed(seg, step, me).start()
+    for seg in order:
+        for step in range(half):
+            passed(seg, step, partner).wait_recv()
+    for seg in order:
+        pltpu.make_async_copy(pieces[seg], fulls[seg].at[me], keep.at[seg]).wait()
+        near(seg).wait_send()
+        for step in range(1, half):
+            far(seg, step).wait_send()
+            passed(seg, step, me).wait_send()
+
+
+def gather_weights(pieces, owners, order):
+    count = len(pieces)
+    half = owners // 2
+    return pl.pallas_call(
+        functools.partial(gather_kernel, owners, count, order),
+        out_shape=[jax.ShapeDtypeStruct((owners,) + p.shape, p.dtype) for p in pieces],
+        in_specs=[ANY] * count,
+        out_specs=[ANY] * count,
+        scratch_shapes=[
+            pltpu.SemaphoreType.DMA((count,)),
+            pltpu.SemaphoreType.DMA((count, half)),
+            pltpu.SemaphoreType.DMA((count, half)),
+            pltpu.SemaphoreType.DMA((count, owners)),
+            pltpu.SemaphoreType.DMA((count,)),
+        ],
+        compiler_params=pltpu.CompilerParams(collective_id=0, has_side_effects=True),
+        name="gather_weights",
+    )(*pieces)
+
+
+def scatter_kernel(owners, count, order, *refs):
+    half = owners // 2
+    parts, outs = refs[:count], refs[count : 2 * count]
+    first, second = refs[2 * count : 3 * count], refs[3 * count : 4 * count]
+    near_send, near_recv, far_send, far_recv = refs[4 * count :]
+    me = lax.axis_index("batch")
+    side = lax.rem(me, 2)
+    partner = me + 1 - 2 * side
+
+    def peer_of(base, step):
+        return lax.rem(base + 2 * step, owners)
+
+    barrier = pltpu.get_barrier_semaphore()
+    pl.semaphore_signal(barrier, inc=1, device_id={"batch": partner}, device_id_type=MESH)
+    for step in range(1, half):
+        pl.semaphore_signal(
+            barrier, inc=1, device_id={"batch": peer_of(me, step)}, device_id_type=MESH
+        )
+    pl.semaphore_wait(barrier, half)
+
+    def near(seg, step):
+        return pltpu.make_async_remote_copy(
+            src_ref=parts[seg].at[peer_of(partner, step)],
+            dst_ref=first[seg].at[step],
+            send_sem=near_send.at[seg, step],
+            recv_sem=near_recv.at[seg, step],
+            device_id={"batch": partner},
+            device_id_type=MESH,
+        )
+
+    def far(seg, step):
+        return pltpu.make_async_remote_copy(
+            src_ref=first[seg].at[step],
+            dst_ref=second[seg].at[step],
+            send_sem=far_send.at[seg, step],
+            recv_sem=far_recv.at[seg, step],
+            device_id={"batch": peer_of(me, step)},
+            device_id_type=MESH,
+        )
+
+    def rows_of(seg):
+        return min(64, parts[seg].shape[1])
+
+    steps = list(range(1, half)) + [0]
+    for seg in order:
+        for step in steps:
+            near(seg, step).start()
+    for seg in order:
+        rows = rows_of(seg)
+        for step in steps:
+            near(seg, step).wait_recv()
+            mine = peer_of(me, step)
+
+            def add(k, carry, seg=seg, step=step, mine=mine, rows=rows):
+                at = pl.ds(pl.multiple_of(k * rows, rows), rows)
+                total = parts[seg][mine, at, :].astype(jnp.float32) + first[seg][
+                    step, at, :
+                ].astype(jnp.float32)
+                if step == 0:
+                    outs[seg][at, :] = total
+                else:
+                    first[seg][step, at, :] = total.astype(jnp.bfloat16)
+                return carry
+
+            lax.fori_loop(0, parts[seg].shape[1] // rows, add, 0)
+            if step:
+                far(seg, step).start()
+    for seg in order:
+        rows = rows_of(seg)
+        for step in range(1, half):
+            far(seg, step).wait_recv()
+
+        def add_far(k, carry, seg=seg, rows=rows):
+            at = pl.ds(pl.multiple_of(k * rows, rows), rows)
+            total = outs[seg][at, :]
+            for step in range(1, half):
+                total = total + second[seg][step, at, :].astype(jnp.float32)
+            outs[seg][at, :] = total
+            return carry
+
+        lax.fori_loop(0, parts[seg].shape[1] // rows, add_far, 0)
+    for seg in order:
+        for step in steps:
+            near(seg, step).wait_send()
+            if step:
+                far(seg, step).wait_send()
+
+
+def scatter_grads(parts, order):
+    count = len(parts)
+    owners = parts[0].shape[0]
+    half = owners // 2
+    buffers = [pltpu.VMEM((half,) + p.shape[1:], jnp.bfloat16) for p in parts]
+    vmem = pl.BlockSpec(memory_space=pltpu.VMEM)
+    return pl.pallas_call(
+        functools.partial(scatter_kernel, owners, count, order),
+        out_shape=[jax.ShapeDtypeStruct(p.shape[1:], jnp.float32) for p in parts],
+        in_specs=[vmem] * count,
+        out_specs=[vmem] * count,
+        scratch_shapes=buffers
+        + buffers
+        + [pltpu.SemaphoreType.DMA((count, half)) for _ in range(4)],
+        compiler_params=pltpu.CompilerParams(
+            collective_id=1, has_side_effects=True, vmem_limit_bytes=60 * 1024 * 1024
+        ),
+        name="scatter_grads",
+    )(*parts)
+
+
+def update_kernel(scale, grad, param, first, second, average, o_param, o_first, o_second, o_average):
+    clipped = grad[...] * scale[0]
+    new_first = 0.5 * first[...] + 0.5 * clipped
+    new_second = 0.5 * second[...] + 0.5 * clipped * clipped
+    keep = 1.0 - 0.5**STEP
+    old = param[...]
+    new = old - 0.01 * (new_first / keep / (jnp.sqrt(new_second / keep) + 1e-08) + 0.01 * old)
+    o_param[...] = new
+    o_first[...] = new_first
+    o_second[...] = new_second
+    o_average[...] = 0.999 * average[...] + 0.001 * new
+
+
+def update(scale, grad, param, first, second, average):
+    rows = grad.shape[0]
+    block = pl.BlockSpec((512, 128), lambda i: (i, 0))
+    return pl.pallas_call(
+        update_kernel,
+        grid=(pl.cdiv(rows, 512),),
+        out_shape=[jax.ShapeDtypeStruct((rows, 128), jnp.float32)] * 4,
+        in_specs=[pl.BlockSpec(memory_space=pltpu.SMEM)] + [block] * 5,
+        out_specs=[block] * 4,
+        name="update",
+    )(scale.reshape(1), grad, param, first, second, average)
+
+
+PIECES = (0, 1, 2, 3, 4, 5, 7)
+SMALL = (6, 8, 9)
+
+
+def piece_shapes(splits, owners):
+    shapes = []
+    for shape in segment_shapes(splits):
+        count = 1
+        for extent in shape:
+            count = count * extent
+        lanes = shape[-1] if shape[-1] % 128 == 0 else 128
+        shapes.append((count // owners // lanes, lanes, count // owners))
+    return shapes
+
+
+def fits(splits, owners):
+    shapes = piece_shapes(splits, owners)
+    return owners % 2 == 0 and all(
+        rows * lanes == count and (rows % 64 == 0 or rows in (16, 32))
+        for rows, lanes, count in [shapes[k] for k in PIECES]
+    ) and sum(shapes[k][2] for k in SMALL) % 2048 == 0
+
+
+def local_fast(features, labels, valid, sizes, params, first_moment, squared_mean, average):
+    splits = lax.axis_size("tensor")
+    owners = lax.axis_size("batch")
+    images = features.shape[0]
+    shapes = piece_shapes(splits, owners)
+    low = params.reshape(-1, 128).astype(jnp.bfloat16)
+    starts = [0]
+    for rows, lanes, count in shapes:
+        starts.append(starts[-1] + count)
+    tail = starts[6] // 128
+    flat_tail = low[tail:].reshape(-1)
+    pieces = []
+    for k in range(6):
+        pieces.append(low[starts[k] // 128 : starts[k + 1] // 128].reshape(shapes[k][:2]))
+    cut = [
+        flat_tail[starts[k] - starts[6] : starts[k + 1] - starts[6]] for k in range(6, 10)
+    ]
+    pieces.append(cut[1].reshape(shapes[7][:2]))
+    pieces.append(jnp.concatenate([cut[0], cut[2], cut[3]]).reshape(-1, 128))
+    full = gather_weights(pieces, owners, (0, 1, 6, 7, 2, 3, 4, 5))
+    whole_shapes = segment_shapes(splits)
+    small = full[7].reshape(owners, -1)
+    ends = [shapes[6][2], shapes[6][2] + shapes[8][2]]
+    parts_of = [
+        full[0],
+        full[1],
+        full[2],
+        full[3],
+        full[4],
+        full[5],
+        small[:, : ends[0]],
+        full[6],
+        small[:, ends[0] : ends[1]],
+        small[:, ends[1] :],
+    ]
+    unpacked = [part.reshape(shape) for part, shape in zip(parts_of, whole_shapes)]
+    (
+        w_reduce,
+        w_short,
+        w_middle,
+        w_expand,
+        w_branch,
+        w_unite,
+        w_classes,
+        w_aux,
+        w_aux_classes,
+        gains,
+    ) = unpacked
+    norms = [(piece[0], piece[1]) for piece in gain_pieces(gains.astype(jnp.float32), splits)]
+    rows_at = jnp.arange(MAP, dtype=jnp.int32)
+    inside = (rows_at[None, :, None] < sizes[:, 0][:, None, None]) & (
+        rows_at[None, None, :] < sizes[:, 1][:, None, None]
+    )
+    inside = inside.astype(jnp.float32)[..., None]
+    counted = inside * valid.astype(jnp.float32)[..., None]
+    labels_hot = (labels[..., None] == jnp.arange(NCLS, dtype=jnp.int32)).astype(jnp.float32)
+    class_local = channel_sums(labels_hot * counted)
+    whole = lax.all_gather(features, "tensor", axis=3, tiled=True)
+    pre_reduce = jnp.dot(whole, w_reduce, preferred_element_type=jnp.float32)
+    pre_short = jnp.dot(whole, w_short, preferred_element_type=jnp.float32)
+    pre_aux = conv_forward(whole, w_aux, 1)
+    leading_part, label_tally = masked_norm_apply(
+        [
+            (pre_reduce, inside, norms[0]),
+            (pre_short, inside, norms[1]),
+            (pre_aux, inside, norms[9]),
+        ],
+        [class_local],
+    )
+    class_pixel_counts = label_tally[0]
+    hidden_one = jax.nn.silu(leading_part[0][0]).astype(jnp.bfloat16)
+    aux_act = jax.nn.silu(leading_part[2][0]).astype(jnp.bfloat16)
+    hidden_full = gather_channels(hidden_one)
+    pre_middle = conv_forward(hidden_full, w_middle, 4)
+    second, unused = masked_norm_apply([(pre_middle, inside, norms[2])], [])
+    hidden_two = jax.nn.silu(second[0][0]).astype(jnp.bfloat16)
+    hidden_two_full = gather_channels(hidden_two)
+    pre_expand = jnp.dot(hidden_two_full, w_expand, preferred_element_type=jnp.float32)
+    third, unused = masked_norm_apply([(pre_expand, inside, norms[3])], [])
+    summed = third[0][0] + leading_part[1][0]
+    merged = jax.nn.silu(summed).astype(jnp.bfloat16)
+    tables = []
+    pooled_list = []
+    partial_list = []
+    for group, bins in enumerate(BIN_COUNTS):
+        rows_in, rows_pick = bin_tables(sizes[:, 0], bins, MAP)
+        cols_in, cols_pick = bin_tables(sizes[:, 1], bins, MAP)
+        cell_count = (
+            jnp.sum(rows_in, axis=2)[:, :, None, None] * jnp.sum(cols_in, axis=2)[:, None, :, None]
+        )
+        tables.append((rows_in, cols_in, rows_pick, cols_pick, cell_count))
+        pooled = (
+            jnp.einsum(
+                "ikh,ilw,ihwc->iklc",
+                rows_in.astype(jnp.bfloat16),
+                cols_in.astype(jnp.bfloat16),
+                merged,
+                preferred_element_type=jnp.float32,
+            )
+            / cell_count
+        )
+        pooled = pooled.astype(jnp.bfloat16).reshape(images, bins * bins, -1)
+        pooled_list.append(pooled)
+        partial_list.append(
+            jnp.einsum("ipc,cd->ipd", pooled, w_branch[group], preferred_element_type=jnp.float32)
+        )
+    branch_pre = lax.psum_scatter(
+        jnp.concatenate(partial_list, axis=1).astype(jnp.bfloat16),
+        "tensor",
+        scatter_dimension=2,
+        tiled=True,
+    ).astype(jnp.float32)
+    branch_items = []
+    for group, bins in enumerate(BIN_COUNTS):
+        piece = branch_pre[:, BIN_STARTS[group] : BIN_STARTS[group] + bins * bins]
+        branch_items.append(
+            (piece, jnp.ones(piece.shape[:-1] + (1,), jnp.float32), norms[4 + group])
+        )
+    fourth, unused = masked_norm_apply(branch_items, [])
+    branch_act = jnp.concatenate([jax.nn.silu(kept[0]) for kept in fourth], axis=1).astype(
+        jnp.bfloat16
+    )
+    merged_full, branch_full = (
+        lax.all_gather(merged, "tensor", axis=3, tiled=True),
+        lax.all_gather(branch_act, "tensor", axis=2, tiled=True),
+    )
+    joined = spread_bins(merged_full, branch_full, tables, images)
+    pre_unite = conv_forward(joined, w_unite, 1)
+    fifth, unused = masked_norm_apply([(pre_unite, inside, norms[8])], [])
+    united = jax.nn.silu(fifth[0][0]).astype(jnp.bfloat16)
+    logit_main, logit_aux = (
+        lax.psum_scatter(
+            jnp.dot(united, w_classes, preferred_element_type=jnp.float32).astype(jnp.bfloat16),
+            "tensor",
+            scatter_dimension=1,
+            tiled=True,
+        ).astype(jnp.float32),
+        lax.psum_scatter(
+            jnp.dot(aux_act, w_aux_classes, preferred_element_type=jnp.float32).astype(
+                jnp.bfloat16
+            ),
+            "tensor",
+            scatter_dimension=1,
+            tiled=True,
+        ).astype(jnp.float32),
+    )
+    total_valid = jnp.sum(class_pixel_counts)
+    class_weight = total_valid / (NCLS * class_pixel_counts + total_valid)
+    loss_weight = jnp.sum(class_pixel_counts * class_weight)
+    cell_weight = jnp.sum(labels_hot * class_weight, axis=-1, keepdims=True) * counted
+    band_rows = labels.shape[1] // splits
+    band_start = lax.axis_index("tensor") * band_rows
+    hot_band = lax.dynamic_slice_in_dim(labels_hot, band_start, band_rows, 1)
+    weight_band = lax.dynamic_slice_in_dim(cell_weight, band_start, band_rows, 1)
+    log_main = jax.nn.log_softmax(logit_main, axis=-1)
+    log_aux = jax.nn.log_softmax(logit_aux, axis=-1)
+    loss_cells = -jnp.sum(hot_band * (log_main + 0.4 * log_aux), axis=-1, keepdims=True)
+    loss_local = jnp.sum(weight_band * loss_cells)
+    band_main = (weight_band * (jnp.exp(log_main) - hot_band) / loss_weight).astype(jnp.bfloat16)
+    band_aux = (0.4 * weight_band * (jnp.exp(log_aux) - hot_band) / loss_weight).astype(
+        jnp.bfloat16
+    )
+    grad_main, grad_aux = (
+        lax.all_gather(band_main, "tensor", axis=1, tiled=True),
+        lax.all_gather(band_aux, "tensor", axis=1, tiled=True),
+    )
+    reduced = {}
+
+    def settle(index, value):
+        reduced[index] = value
+
+    settle(6, jnp.einsum("ihwc,ihwk->ck", united, grad_main, preferred_element_type=jnp.float32))
+    settle(8, jnp.einsum("ihwc,ihwk->ck", aux_act, grad_aux, preferred_element_type=jnp.float32))
+    d_united = jnp.dot(grad_main, w_classes.T, preferred_element_type=jnp.float32) * silu_slope(
+        fifth[0][0]
+    )
+    d_aux = jnp.dot(grad_aux, w_aux_classes.T, preferred_element_type=jnp.float32) * silu_slope(
+        leading_part[2][0]
+    )
+    back_one, sums_one, totals_one = norm_backward([(d_united, fifth[0]), (d_aux, leading_part[2])])
+    unite_shift_grad = totals_one[0]
+    d_unite_pre = back_one[0].astype(jnp.bfloat16)
+    d_aux_pre = back_one[1].astype(jnp.bfloat16)
+    settle(5, conv_kernel_back(joined, d_unite_pre, 1))
+    d_merged, d_branch = pick_bins(conv_input_back(d_unite_pre, w_unite, 1), C_OUT, tables, images)
+    d_merged, d_branch = (
+        lax.psum_scatter(
+            d_merged.astype(jnp.bfloat16), "tensor", scatter_dimension=3, tiled=True
+        ).astype(jnp.float32),
+        lax.psum_scatter(
+            d_branch.astype(jnp.bfloat16), "tensor", scatter_dimension=2, tiled=True
+        ).astype(jnp.float32),
+    )
+    settle(7, conv_kernel_back(whole, d_aux_pre, 1))
+    branch_back = []
+    for group, bins in enumerate(BIN_COUNTS):
+        piece = d_branch[:, BIN_STARTS[group] : BIN_STARTS[group] + bins * bins]
+        branch_back.append((piece * silu_slope(fourth[group][0]), fourth[group]))
+    back_two, sums_two, unused = norm_backward(branch_back)
+    d_branch_pre = jnp.concatenate(back_two, axis=1).astype(jnp.bfloat16)
+    d_branch_full = lax.all_gather(d_branch_pre, "tensor", axis=2, tiled=True)
+    branch_grads = []
+    for group, bins in enumerate(BIN_COUNTS):
+        rows_in, cols_in, rows_pick, cols_pick, cell_count = tables[group]
+        piece = d_branch_full[:, BIN_STARTS[group] : BIN_STARTS[group] + bins * bins]
+        branch_grads.append(
+            jnp.einsum("ipc,ipd->cd", pooled_list[group], piece, preferred_element_type=jnp.float32)
+        )
+        d_pooled = jnp.dot(piece, w_branch[group].T, preferred_element_type=jnp.float32).reshape(
+            images, bins, bins, -1
+        )
+        d_merged = d_merged + jnp.einsum(
+            "ikh,ilw,iklc->ihwc", rows_in, cols_in, d_pooled / cell_count
+        )
+    settle(4, jnp.stack(branch_grads))
+    d_summed = d_merged * silu_slope(summed)
+    back_three, sums_three, unused = norm_backward(
+        [(d_summed, third[0]), (d_summed, leading_part[1])]
+    )
+    d_expand_pre = back_three[0].astype(jnp.bfloat16)
+    d_short_pre = back_three[1].astype(jnp.bfloat16)
+    settle(
+        3,
+        jnp.einsum(
+            "ihwc,ihwd->cd", hidden_two_full, d_expand_pre, preferred_element_type=jnp.float32
+        ),
+    )
+    settle(1, jnp.einsum("ihwc,ihwd->cd", whole, d_short_pre, preferred_element_type=jnp.float32))
+    d_two = scatter_channels(jnp.dot(d_expand_pre, w_expand.T, preferred_element_type=jnp.float32))
+    back_four, sums_four, unused = norm_backward([(d_two * silu_slope(second[0][0]), second[0])])
+    d_middle_pre = back_four[0].astype(jnp.bfloat16)
+    settle(2, conv_kernel_back(hidden_full, d_middle_pre, 4))
+    d_one = scatter_channels(conv_input_back(d_middle_pre, w_middle, 4))
+    back_five, sums_five, unused = norm_backward(
+        [(d_one * silu_slope(leading_part[0][0]), leading_part[0])]
+    )
+    settle(
+        0,
+        jnp.einsum(
+            "ihwc,ihwd->cd",
+            whole,
+            back_five[0].astype(jnp.bfloat16),
+            preferred_element_type=jnp.float32,
+        ),
+    )
+    beta_grads = (
+        [sums_five[0], sums_three[2], sums_four[0], sums_three[0]]
+        + [sums_two[2 * g] for g in range(4)]
+        + [sums_one[0], sums_one[2]]
+    )
+    gamma_grads = (
+        [sums_five[1], sums_three[3], sums_four[1], sums_three[1]]
+        + [sums_two[2 * g + 1] for g in range(4)]
+        + [sums_one[1], sums_one[3]]
+    )
+    settle(9, jnp.stack([jnp.concatenate(gamma_grads), jnp.concatenate(beta_grads)]))
+    rounded = [reduced[index].astype(jnp.bfloat16) for index in range(10)]
+    sends = [
+        rounded[k].reshape((owners,) + shapes[k][:2]) for k in PIECES
+    ]
+    sends.append(
+        jnp.concatenate([rounded[k].reshape(owners, -1) for k in SMALL], axis=1).reshape(
+            owners, -1, 128
+        )
+    )
+    own = scatter_grads(sends, (5, 4, 6, 7, 3, 1, 2, 0))
+    own_small = own[7].reshape(-1)
+    grad_share = jnp.concatenate(
+        [own[k].reshape(-1, 128) for k in range(6)]
+        + [
+            jnp.concatenate(
+                [own_small[: ends[0]], own[6].reshape(-1), own_small[ends[0] :]]
+            ).reshape(-1, 128)
+        ]
+    )
+    square_all, loss_sum = lax.psum(
+        (jnp.sum(grad_share * grad_share), loss_local), ("batch", "tensor")
+    )
+    grad_norm = jnp.sqrt(square_all)
+    scale = jnp.minimum(1.0, 0.05 / (grad_norm + 1e-06))
+    new_params, new_first, new_second, new_average = [
+        item.reshape(params.shape)
+        for item in update(
+            scale,
+            grad_share,
+            params.reshape(-1, 128),
+            first_moment.reshape(-1, 128),
+            squared_mean.reshape(-1, 128),
+            average.reshape(-1, 128),
+        )
+    ]
+    return (
+        new_params,
+        new_first,
+        new_second,
+        new_average,
+        new_params.astype(jnp.bfloat16),
+        grad_norm,
+        loss_sum,
+        loss_weight,
+        unite_shift_grad,
+    )
+
+
 def solution(mesh):
+    chosen = local_fast if fits(mesh.shape["tensor"], mesh.shape["batch"]) else local
     return jax.shard_map(
-        local,
+        chosen,
         mesh=mesh,
         in_specs=(
             P("batch", None, None, "tensor"),

time: 2360 us -> 1190 us (0.50)
  waiting for transfers between devices: 1520 us -> 50.9 us
  Pallas kernels: 0 us -> 429 us
  local copies, waits for them, and re-layouts: 183 us -> 77.4 us
  other arithmetic: 128 us -> 85.4 us
  blocking collectives: 284 us -> 317 us
    unnamed x16 -> x13, waiting for transfers between devices: 934 us -> 36.2 us
    all_gather x3 -> x2, waiting for transfers between devices: 575 us -> 0.02 us  [the longest x1 0.02 us: local_fast(): lax.all_gather(merged, 'tensor', axis=3, tiled=True)]
    pallas_call x0 -> x3, Pallas kernels: none -> 429 us  [the longest x1 212 us: gather_weights(): pl.pallas_call(functools.partial(gather_kernel, owners, count, order), ou...]
    unnamed x525 -> x479, local copies, waits for them, and re-layouts: 85.6 us -> 42 us
    reshape x18 -> x13, local copies, waits for them, and re-layouts: 53.2 us -> 11.8 us  [the longest x3 5.72 us: local_fast(): part.reshape(shape)]
    psum x5, blocking collectives: 96.8 us -> 137 us  [masked_norm_apply(): totals = lax.psum(tuple(sends + extra), 'batch')]
    convert_element_type x12 -> x13, other arithmetic: 45.3 us -> 17.8 us  [the longest x1 7.53 us: local_fast(): new_params.astype(jnp.bfloat16)]
  transfers between devices with their start and end apart: 11 -> 9, of which waited for: 5 -> 4; matrix products, arithmetic and copies ran while one was open for 8% -> 12% of each run, Pallas kernels for 0% -> 18%
where the time goes in v1:
time: 1190 us; the launch traced here: 1180 us
  Pallas kernels  429 us (36%)
  blocking collectives  317 us (27%)
  matrix products  198 us (17%)
  other arithmetic  85.4 us (7%)
  local copies, waits for them, and re-layouts  77.4 us (7%)
  waiting for transfers between devices  50.9 us (4%)
  between operations  22 us (2%)
    pallas_call x1, Pallas kernels, gather_weights(): pl.pallas_call(functools.partial(gather_kernel, owners, count, order), ou...  212 us
    pallas_call x1, Pallas kernels, scatter_grads(): pl.pallas_call(functools.partial(scatter_kernel, owners, count, order), o...  198 us
    psum x5, blocking collectives, masked_norm_apply(): totals = lax.psum(tuple(sends + extra), 'batch')  137 us
    psum x5, blocking collectives, norm_backward(): totals = lax.psum(tuple(sends), 'batch')  102 us
    dot_general x18, matrix products, conv_input_back(): product = jnp.dot(grad, kernel[tap].T, preferred_element_type=jnp.float32)  83.1 us
    dot_general x27, matrix products, conv_kernel_back(): jnp.einsum('ihwc,ihwd->cd', shifted(field, (tap // 3 - 1) * spacing, (tap...  50.5 us
    unnamed x479, local copies, waits for them, and re-layouts  42 us
    psum x1, blocking collectives, local_fast(): lax.psum((jnp.sum(grad_share * grad_share), loss_local), ('batch', 'tenso...  41.3 us
  transfers between devices with their start and end apart: 9, of which 4 were waited for; matrix products, arithmetic and copies ran while one was open for 12% of the time, Pallas kernels for 18%

profile of v1, /device:TPU:0, one launch (start us, length us, event | category | flops | bytes accessed | tf_op | source)
XLA Modules:
  0.0 1180.2 jit_solution(4600580809551813433)
XLA Ops:
  8.0 2.3 convert_element_type.684
  26.0 2.0 minimum_bitcast_fusion.1
  32.9 211.7 %gather_weights.1 = (bf16[8,128,128]{2,1,0:T(8,128)(2,1)}, bf16[8,128,512]{2,1,0:T(8,128)(2,1)}, bf16[8,576,128]{2,1,0:T(8,128)(2,1)}, bf16[8,64,512]{2,1,0:T(8,...) custom-call(bf16[128,128]{1,0:T(8,128)(2,1)} %slice.607.refs_0_, ...), custom_call_target="tpu_custom_call" | custom-call | tf_op jit(solution)/shard_map/gather_weights/pallas_call | solution.py:536
  251.0 4.2 reshape.3270
  258.2 1.9 fusion.522
  266.2 1.9 multiply_reduce_fusion.14
  268.2 58.7 %all-reduce.35 = (f32[128]{0:T(128)S(1)}, f32[]{:T(128)}, f32[128]{0:T(128)S(1)}) all-reduce(f32[128]{0:T(128)S(1)} %get-tuple-element.69, f32[]{:T(128)} %convert_reduce_fusion.2, f32[128]{0:T(128)S(1)} %get-tuple-element.68), channel_id=1, replica_groups=mesh['batch'=8,'tensor'=4] {'batch'}, use_global_device_ids=true, to_apply=%region_5.6 | all-reduce | flops 257 | bytes 2056 | tf_op jit(solution)/shard_map/psum | solution.py:122
  328.2 7.5 all-gather
  338.9 19.1 %all-reduce.34 = (f32[128]{0:T(128)S(1)}, f32[128]{0:T(128)S(1)}) all-reduce(f32[128]{0:T(128)S(1)} %get-tuple-element.67, f32[128]{0:T(128)S(1)} %get-tuple-element.66), channel_id=1, replica_groups=mesh['batch'=8,'tensor'=4] {'batch'}, use_global_device_ids=true, to_apply=%region_9.10 | all-reduce | flops 256 | bytes 2048 | tf_op jit(solution)/shard_map/psum | solution.py:122
  359.4 6.7 all-gather.1
  369.9 17.6 %all-reduce.33 = (f32[512]{0:T(512)S(1)}, f32[512]{0:T(512)S(1)}, f32[512]{0:T(512)S(1)}, f32[512]{0:T(512)S(1)}) all-reduce(f32[512]{0:T(512)S(1)} %get-tuple-element.54, f32[512]{0:T(512)S(1)} %get-tuple-element.53, f32[512]{0:T(512)S(1)} %get-tuple-element.52, ...), channel_id=1, replica_groups=mesh['batch'=8,'tensor'=4] {'batch'}, use_global_device_ids=true, to_apply=%region_17.18 | all-reduce | flops 2048 | bytes 16384 | tf_op jit(solution)/shard_map/psum | solution.py:122
  410.7 10.9 reduce-scatter.22.cloned.1.call-done
  422.6 24.5 %all-reduce.32 = (f32[128]{0:T(128)S(1)}, f32[]{:T(128)}, f32[128]{0:T(128)S(1)}, f32[128]{0:T(128)S(1)}, f32[]{:T(128)}, /*index=5*/f32[128]{0:T(128)S(1)}, f32...) all-reduce(f32[128]{0:T(128)S(1)} %get-tuple-element.79, ...), channel_id=1, replica_groups=mesh['batch'=8,'tensor'=4] {'batch'}, use_global_device_ids=true, to_apply=%region_41.43 | all-reduce | flops 1028 | bytes 8224 | tf_op jit(solution)/shard_map/psum | solution.py:122
  447.1 3.1 fusion.579
  451.0 1.9 multiply_convert_fusion.15
  454.4 5.6 all_gather.28
  462.8 1.9 bitcast_dynamic-update-slice_fusion
  466.2 3.7 fusion.30
  469.9 3.5 fusion.75
  482.0 2.1 fusion.193
  486.0 17.1 %all-reduce.31 = (f32[150]{0:T(256)S(1)}, f32[128]{0:T(128)S(1)}, f32[128]{0:T(128)S(1)}) all-reduce(f32[150]{0:T(256)S(1)} %copy-done.129, f32[128]{0:T(128)S(1)} %get-tuple-element.65, f32[128]{0:T(128)S(1)} %get-tuple-element.64), channel_id=1, replica_groups=mesh['batch'=8,'tensor'=4] {'batch'}, use_global_device_ids=true, to_apply=%region_50.52 | all-reduce | flops 406 | bytes 3248 | tf_op jit(solution)/shard_map/psum | solution.py:122
  509.0 14.7 %reduce-scatter.16.cloned.1.call-done = bf16[1,6,24,150]{3,2,1,0:T(8,128)(2,1)} async-done(((bf16[1,24,24,150]{3,2,1,0:T(8,128)(2,1)}), bf16[1,6,24,150]{3,2,1,0:T(8,128)(2,1)}) %reduce-scatter.16.cloned.1.call-update) | async-done | bytes 43216 | tf_op jit(solution)/shard_map/reduce_scatter | solution.py:842
  528.0 5.9 all_gather.29
  534.2 21.4 %all-reduce.30 = (f32[128]{0:T(128)S(1)}, f32[128]{0:T(128)S(1)}) all-reduce(f32[128]{0:T(128)S(1)} %get-tuple-element.73, f32[128]{0:T(128)S(1)} %get-tuple-element.72), channel_id=1, replica_groups=mesh['batch'=8,'tensor'=4] {'batch'}, use_global_device_ids=true, to_apply=%region_60.63 | all-reduce | flops 256 | bytes 2048 | tf_op jit(solution)/shard_map/psum | solution.py:138
  556.4 6.4 convolution_bitcast_fusion
  562.8 6.4 convolution_bitcast_fusion.2
  569.2 5.0 convolution_bitcast_fusion.3
  574.2 5.1 convolution_bitcast_fusion.5
  579.3 5.0 convolution_bitcast_fusion.7
  584.3 5.1 convolution_bitcast_fusion.4
  589.3 5.0 convolution_bitcast_fusion.1
  594.4 5.0 convolution_bitcast_fusion.6
  599.4 3.0 fusion.61
  602.4 26.6 %fusion.7 = bf16[1,24,24,4096]{3,2,1,0:T(8,128)(2,1)} fusion(f32[1,24,24,4096]{3,2,1,0:T(8,128)} %convolution_bitcast_fusion.6, f32[1,24,24,4096]{3,2,1,0:T(8,128)} %convolution_bitcast_fusion.1, f32[1,24,24,4096]{3,2,1,0:T(8,128)} %convolution_bitcast_fusion.4, f32[1,24,24,4096]{3,2,1,0:T(8,128)} %convolution_bitcast_fusion.3, ...), kind=kOutput, calls=%fused_computation.15 | convolution fusion | flops 625213440 | bytes 81412096 | tf_op jit(solution)/shard_map/dot_general | solution.py:86
  634.3 5.1 fusion.57
  639.4 4.9 fusion.53
  644.3 2.6 fusion.51
  646.9 2.6 fusion.47
  649.5 2.6 fusion.43
  652.2 2.6 fusion.41
  654.8 2.6 fusion.37
  661.6 5.3 fusion.33
  668.7 17.1 %all-reduce.29 = (f32[128]{0:T(128)S(1)}, f32[128]{0:T(128)S(1)}, f32[128]{0:T(128)S(1)}, f32[128]{0:T(128)S(1)}, f32[128]{0:T(128)S(1)}, /*index=5*/f32[128]{0:...) all-reduce(f32[128]{0:T(128)S(1)} %get-tuple-element.81, ...), channel_id=1, replica_groups=mesh['batch'=8,'tensor'=4] {'batch'}, use_global_device_ids=true, to_apply=%region_76.79 | all-reduce | flops 1024 | bytes 8192 | tf_op jit(solution)/shard_map/psum | solution.py:138
  689.6 5.4 all_gather.30
  704.1 3.8 fusion.113
  707.9 19.2 %all-reduce.28 = (f32[512]{0:T(512)S(1)}, f32[512]{0:T(512)S(1)}) all-reduce(f32[512]{0:T(512)} %get-tuple-element.56, f32[512]{0:T(512)} %get-tuple-element.57), channel_id=1, replica_groups=mesh['batch'=8,'tensor'=4] {'batch'}, use_global_device_ids=true, to_apply=%region_80.83 | all-reduce | flops 1024 | bytes 8192 | tf_op jit(solution)/shard_map/psum | solution.py:138
  731.1 3.6 copy.174
  734.7 2.8 reshape.3423
  742.3 13.9 %reduce-scatter.26.cloned.1.call-done = bf16[128,576]{1,0:T(8,128)(2,1)} async-done(((bf16[512,576]{1,0:T(8,128)(2,1)}), bf16[128,576]{1,0:T(8,128)(2,1)}) %reduce-scatter.26.cloned.1.call-update) | async-done | bytes 147472
  758.5 21.6 %all-reduce.27 = (f32[128]{0:T(128)S(1)}, f32[128]{0:T(128)S(1)}, f32[64]{0:T(128)S(1)}, f32[64]{0:T(128)S(1)}) all-reduce(f32[128]{0:T(128)S(1)} %get-tuple-element.61, f32[128]{0:T(128)S(1)} %get-tuple-element.60, f32[64]{0:T(128)S(1)} %copy-done.184, f32[64]{0:T(128)S(1)} %copy-done.183), channel_id=1, replica_groups=mesh['batch'=8,'tensor'=4] {'batch'}, use_global_device_ids=true, to_apply=%region_85.88 | all-reduce | flops 384 | bytes 3072 | tf_op jit(solution)/shard_map/psum | solution.py:138
  801.2 2.7 fusion.90
  804.9 3.4 copy.176
  808.3 4.8 reshape.3425
  819.6 5.9 all_gather.31
  827.2 10.5 reduce-scatter.28.cloned.1.call-done
  840.0 22.2 %all-reduce.26 = (f32[128]{0:T(128)}, f32[128]{0:T(128)}, f32[512]{0:T(512)}, f32[64]{0:T(128)S(1)}, f32[64]{0:T(128)S(1)}) all-reduce(f32[128]{0:T(128)S(1)} %get-tuple-element.59, f32[128]{0:T(128)S(1)} %get-tuple-element.58, f32[512]{0:T(512)S(1)} %copy-done.92, ...), channel_id=1, replica_groups=mesh['batch'=8,'tensor'=4] {'batch'}, use_global_device_ids=true, to_apply=%region_90.93 | all-reduce | flops 896 | bytes 7168 | tf_op jit(solution)/shard_map/psum | solution.py:138
  877.9 2.8 copy.162
  880.7 2.2 convert_element_type.786.refs_6_
  882.9 3.4 fusion.80
  889.9 198.1 %scatter_grads.1 = (f32[128,128]{1,0:T(8,128)}, f32[128,512]{1,0:T(8,128)}, f32[576,128]{1,0:T(8,128)}, f32[64,512]{1,0:T(8,128)}, f32[256,512]{1,0:T(8,128)}, /...) custom-call(bf16[8,128,128]{2,1,0:T(8,128)(2,1)} %bitcast.1507, bf16[8,128,512]{2,1,0:T(8,128)(2,1)} %bitcast.1475, ...), custom_call_target="tpu_custom_call" | custom-call | tf_op jit(solution)/shard_map/scatter_grads/pallas_call | solution.py:647
  1099.9 3.7 multiply_reduce_fusion
  1103.7 41.3 %all-reduce.25 = (f32[]{:T(128)}, f32[]{:T(128)}) all-reduce(f32[]{:T(128)} %multiply_reduce_fusion, f32[]{:T(128)} %fusion.435), channel_id=1, replica_groups=mesh['batch'=8,'tensor'=4] {'batch','tensor'}, use_global_device_ids=true, to_apply=%region_103.106 | all-reduce | flops 2 | bytes 16 | tf_op jit(solution)/shard_map/psum | solution.py:986
  1145.7 18.8 %update.1 = (f32[7712,128]{1,0:T(8,128)}, f32[7712,128]{1,0:T(8,128)}, f32[7712,128]{1,0:T(8,128)}, f32[7712,128]{1,0:T(8,128)}) custom-call(f32[1]{0:T(128)} %bitcast.357.scale, f32[7712,128]{1,0:T(8,128)} %bitcast_dynamic-update-slice_fusion.1.grad, f32[7712,128]{1,0:T(8,128)} %bitcast.1442, f32[7712,128]{1,0:T(8,128)} %bitcast.1476, ...), custom_call_target="tpu_custom_call" | custom-call | tf_op jit(solution)/shard_map/update/pallas_call | solution.py:678
  1164.6 7.5 convert_element_type.790
  (783 shorter events, 192.2 us)
Async XLA Ops:
  7.2 259.1 %all-gather.6.cloned.1.call-start = ((), (), s32[]{:S(2)}) async-start(), calls=%async_computation.7 | async-start | bytes 1474560 | tf_op jit(solution)/shard_map/all_gather | solution.py:768
  7.9 413.7 %reduce-scatter.22.cloned.1.call-start = ((), (), s32[]{:S(2)}) async-start(), calls=%async_computation.12 | async-start | bytes 163840
  16.9 230.4 %copy-start.197 = (s32[2]{0:T(128)}, s32[2]{0:T(128)S(1)}, u32[]{:S(2)}) copy-start(s32[2]{0:T(128)S(1)} %get-tuple-element.242) | copy-start | bytes 28
  16.9 375.5 %copy-start.195 = (s32[2]{0:T(128)}, s32[2]{0:T(128)S(1)}, u32[]{:S(2)}) copy-start(s32[2]{0:T(128)S(1)} %get-tuple-element.241) | copy-start | bytes 28
  17.6 229.6 %copy-start.191 = (s32[2]{0:T(128)}, s32[2]{0:T(128)S(1)}, u32[]{:S(2)}) copy-start(s32[2]{0:T(128)S(1)} %get-tuple-element.233) | copy-start | bytes 28
  17.6 229.6 %copy-start.193 = (s32[2]{0:T(128)}, s32[2]{0:T(128)S(1)}, u32[]{:S(2)}) copy-start(s32[2]{0:T(128)S(1)} %get-tuple-element.234) | copy-start | bytes 28
  18.3 230.1 %copy-start.200 = (s32[3]{0:T(128)}, s32[3]{0:T(128)S(1)}, u32[]{:S(2)}) copy-start(s32[3]{0:T(128)S(1)} %get-tuple-element.239) | copy-start | bytes 40
  18.3 230.1 %copy-start.203 = (s32[3]{0:T(128)}, s32[3]{0:T(128)S(1)}, u32[]{:S(2)}) copy-start(s32[3]{0:T(128)S(1)} %get-tuple-element.240) | copy-start | bytes 40
  19.0 229.2 %copy-start.162 = (s32[3]{0:T(128)}, s32[3]{0:T(128)S(1)}, u32[]{:S(2)}) copy-start(s32[3]{0:T(128)S(1)} %get-tuple-element.231) | copy-start | bytes 40
  19.0 229.2 %copy-start.165 = (s32[3]{0:T(128)}, s32[3]{0:T(128)S(1)}, u32[]{:S(2)}) copy-start(s32[3]{0:T(128)S(1)} %get-tuple-element.232) | copy-start | bytes 40
  19.6 373.5 %copy-start.130 = (s32[6]{0:T(128)}, s32[6]{0:T(128)S(1)}, u32[]{:S(2)}) copy-start(s32[6]{0:T(128)S(1)} %get-tuple-element.237) | copy-start | bytes 76
  19.7 373.5 %copy-start.132 = (s32[6]{0:T(128)}, s32[6]{0:T(128)S(1)}, u32[]{:S(2)}) copy-start(s32[6]{0:T(128)S(1)} %get-tuple-element.238) | copy-start | bytes 76
  20.3 228.9 %copy-start.156 = (s32[6]{0:T(128)}, s32[6]{0:T(128)S(1)}, u32[]{:S(2)}) copy-start(s32[6]{0:T(128)S(1)} %get-tuple-element.229) | copy-start | bytes 76
  20.3 228.9 %copy-start.159 = (s32[6]{0:T(128)}, s32[6]{0:T(128)S(1)}, u32[]{:S(2)}) copy-start(s32[6]{0:T(128)S(1)} %get-tuple-element.230) | copy-start | bytes 76
  31.6 214.2 %copy-start.73 = (s32[1,24,24]{2,1,0:T(8,128)S(1)}, s32[1,24,24]{2,1,0:T(8,128)}, u32[]{:S(2)}) copy-start(s32[1,24,24]{2,1,0:T(8,128)} %param.13) | copy-start | bytes 6916
  245.7 112.3 %copy-start.53 = (f32[2,1984]{1,0:T(2,128)}, f32[2,1984]{1,0:T(2,128)S(1)}, u32[]{:S(2)}) copy-start(f32[2,1984]{1,0:T(2,128)S(1)} %reshape.3300) | copy-start | bytes 47620
  262.2 133.5 %copy-start.127 = (f32[6,6]{1,0:T(8,128)}, f32[6,6]{1,0:T(8,128)S(1)}, u32[]{:S(2)}) copy-start(f32[6,6]{1,0:T(8,128)S(1)} %broadcast_multiply_fusion.2) | copy-start | bytes 436
  262.8 65.3 %copy-start.104 = (f32[128]{0:T(128)}, f32[128]{0:T(128)S(1)}, u32[]{:S(2)}) copy-start(f32[128]{0:T(128)S(1)} %get-tuple-element.197) | copy-start | bytes 1540
  262.8 65.3 %copy-start.107 = (f32[128]{0:T(128)}, f32[128]{0:T(128)S(1)}, u32[]{:S(2)}) copy-start(f32[128]{0:T(128)S(1)} %get-tuple-element.199) | copy-start | bytes 1540
  262.8 96.5 %copy-start.74 = (f32[128]{0:T(128)}, f32[128]{0:T(128)S(1)}, u32[]{:S(2)}) copy-start(f32[128]{0:T(128)S(1)} %get-tuple-element.196) | copy-start | bytes 1540
  262.8 96.5 %copy-start.76 = (f32[128]{0:T(128)}, f32[128]{0:T(128)S(1)}, u32[]{:S(2)}) copy-start(f32[128]{0:T(128)S(1)} %get-tuple-element.198) | copy-start | bytes 1540
  262.8 127.1 %copy-start.65 = (f32[1,512]{1,0:T(1,128)}, f32[1,512]{1,0:T(1,128)S(1)}, u32[]{:S(2)}) copy-start(f32[1,512]{1,0:T(1,128)S(1)} %get-tuple-element.206) | copy-start | bytes 6148
  262.8 127.1 %copy-start.67 = (f32[1,512]{1,0:T(1,128)}, f32[1,512]{1,0:T(1,128)S(1)}, u32[]{:S(2)}) copy-start(f32[1,512]{1,0:T(1,128)S(1)} %get-tuple-element.208) | copy-start | bytes 6148
  262.9 127.1 %copy-start.102 = (f32[1,512]{1,0:T(1,128)}, f32[1,512]{1,0:T(1,128)S(1)}, u32[]{:S(2)}) copy-start(f32[1,512]{1,0:T(1,128)S(1)} %get-tuple-element.207) | copy-start | bytes 6148
  262.9 127.1 %copy-start.103 = (f32[1,512]{1,0:T(1,128)}, f32[1,512]{1,0:T(1,128)S(1)}, u32[]{:S(2)}) copy-start(f32[1,512]{1,0:T(1,128)S(1)} %get-tuple-element.209) | copy-start | bytes 6148
  266.2 128.1 %copy-start.14 = (bf16[2,256,512]{2,1,0:T(8,128)(2,1)}, bf16[2,256,512]{2,1,0:T(8,128)(2,1)S(1)}, u32[]{:S(2)}) copy-start(bf16[2,256,512]{2,1,0:T(8,128)(2,1)S(1)} %get-tuple-element.178) | copy-start | bytes 1572868
  268.2 67.6 %copy-start.31 = (f32[128,24,24]{0,2,1:T(8,128)}, f32[128,24,24]{0,2,1:T(8,128)S(1)}, u32[]{:S(2)}) copy-start(f32[128,24,24]{0,2,1:T(8,128)S(1)} %get-tuple-element.220) | copy-start | bytes 884740
  268.2 67.6 %copy-start.16 = (bf16[8,576,128]{2,1,0:T(8,128)(2,1)S(1)}, bf16[8,576,128]{2,1,0:T(8,128)(2,1)}, u32[]{:S(2)}) copy-start(bf16[8,576,128]{2,1,0:T(8,128)(2,1)} %get-tuple-element.33) | copy-start | bytes 3538948
  338.9 29.1 %copy-start.19 = (f32[24,24,128]{2,1,0:T(8,128)}, f32[24,24,128]{2,1,0:T(8,128)S(1)}, u32[]{:S(2)}) copy-start(f32[24,24,128]{2,1,0:T(8,128)S(1)} %get-tuple-element.221) | copy-start | bytes 884740
  403.3 59.5 %all-gather.8.cloned.1.call-start = ((), (), s32[]{:S(2)}) async-start(), calls=%async_computation.11 | async-start | bytes 2949120 | tf_op jit(solution)/shard_map/all_gather | solution.py:834
  404.7 119.0 %reduce-scatter.16.cloned.1.call-start = ((), (), s32[]{:S(2)}) async-start(), calls=%async_computation.8 | async-start | bytes 368640 | tf_op jit(solution)/shard_map/reduce_scatter | solution.py:842
  408.9 44.7 %copy-start.116 = (f32[128]{0:T(128)S(1)}, f32[128]{0:T(128)}, u32[]{:S(2)}) copy-start(f32[128]{0:T(128)} %get-tuple-element.190) | copy-start | bytes 1540
  422.5 42.2 %copy-start.35 = (f32[1,50,128]{2,1,0:T(8,128)}, f32[1,50,128]{2,1,0:T(8,128)S(1)}, u32[]{:S(2)}) copy-start(f32[1,50,128]{2,1,0:T(8,128)S(1)} %convert_element_type.728) | copy-start | bytes 76804
  505.5 161.5 %reduce-scatter.24.cloned.1.call-start = ((), (), s32[]{:S(2)}) async-start(), calls=%async_computation.13 | async-start | bytes 163840
  634.2 69.9 %reduce-scatter.18.cloned.1.call-start = ((), (), s32[]{:S(2)}) async-start(), calls=%async_computation.9 | async-start | bytes 2949120 | tf_op jit(solution)/shard_map/reduce_scatter | solution.py:897
  661.5 37.3 %copy-start.29 = (bf16[2,256,512]{2,1,0:T(8,128)(2,1)S(1)}, bf16[2,256,512]{2,1,0:T(8,128)(2,1)}, u32[]{:S(2)}) copy-start(bf16[2,256,512]{2,1,0:T(8,128)(2,1)} %get-tuple-element.180) | copy-start | bytes 1572868
  661.5 37.3 %copy-start.141 = (f32[3,3]{1,0:T(4,128)S(1)}, f32[3,3]{1,0:T(4,128)}, u32[]{:S(2)}) copy-start(f32[3,3]{1,0:T(4,128)} %broadcast_multiply_fusion.3) | copy-start | bytes 112
  661.6 94.6 %reduce-scatter.26.cloned.1.call-start = ((), (), s32[]{:S(2)}) async-start(), calls=%async_computation.14 | async-start | bytes 819200
  666.9 32.2 %copy-start.202 = (s32[3]{0:T(128)S(1)}, s32[3]{0:T(128)}, u32[]{:S(2)}) copy-start(s32[3]{0:T(128)} %copy-done.200) | copy-start | bytes 40
  666.9 32.2 %copy-start.205 = (s32[3]{0:T(128)S(1)}, s32[3]{0:T(128)}, u32[]{:S(2)}) copy-start(s32[3]{0:T(128)} %copy-done.203) | copy-start | bytes 40
  666.9 32.5 %copy-start.164 = (s32[3]{0:T(128)S(1)}, s32[3]{0:T(128)}, u32[]{:S(2)}) copy-start(s32[3]{0:T(128)} %copy-done.162) | copy-start | bytes 40
  666.9 32.5 %copy-start.167 = (s32[3]{0:T(128)S(1)}, s32[3]{0:T(128)}, u32[]{:S(2)}) copy-start(s32[3]{0:T(128)} %copy-done.165) | copy-start | bytes 40
  737.6 78.1 %reduce-scatter.20.cloned.1.call-start = ((), (), s32[]{:S(2)}) async-start(), calls=%async_computation.10 | async-start | bytes 368640 | tf_op jit(solution)/shard_map/reduce_scatter | solution.py:848
  742.3 37.8 %copy-start.134 = (f32[128]{0:T(128)S(1)}, f32[128]{0:T(128)}, u32[]{:S(2)}) copy-start(f32[128]{0:T(128)} %get-tuple-element.148) | copy-start | bytes 1540
  794.1 31.7 %copy-start.149 = (f32[64]{0:T(128)}, f32[64]{0:T(128)S(1)}, u32[]{:S(2)}) copy-start(f32[64]{0:T(128)S(1)} %get-tuple-element.137) | copy-start | bytes 772
  794.1 31.8 %copy-start.151 = (f32[64]{0:T(128)}, f32[64]{0:T(128)S(1)}, u32[]{:S(2)}) copy-start(f32[64]{0:T(128)S(1)} %get-tuple-element.138) | copy-start | bytes 772
  795.2 42.5 %reduce-scatter.28.cloned.1.call-start = ((), (), s32[]{:S(2)}) async-start(), calls=%async_computation.15 | async-start | bytes 819200
  826.3 36.0 %copy-start.126 = (bf16[1984]{0:T(1024)(128)(2,1)S(1)}, bf16[1984]{0:T(1024)(128)(2,1)}, u32[]{:S(2)}) copy-start(bf16[1984]{0:T(1024)(128)(2,1)} %custom-call.2) | copy-start | bytes 11908
  826.5 36.2 %copy-start.179 = (bf16[128]{0:T(256)(128)(2,1)S(1)}, bf16[128]{0:T(256)(128)(2,1)}, u32[]{:S(2)}) copy-start(bf16[128]{0:T(256)(128)(2,1)} %convert.365) | copy-start | bytes 772
  827.1 36.0 %copy-start.139 = (bf16[128]{0:T(256)(128)(2,1)S(1)}, bf16[128]{0:T(256)(128)(2,1)}, u32[]{:S(2)}) copy-start(bf16[128]{0:T(256)(128)(2,1)} %get-tuple-element.133) | copy-start | bytes 772
  827.1 36.2 %copy-start.178 = (bf16[128]{0:T(256)(128)(2,1)S(1)}, bf16[128]{0:T(256)(128)(2,1)}, u32[]{:S(2)}) copy-start(bf16[128]{0:T(256)(128)(2,1)} %convert.368) | copy-start | bytes 772
  827.1 36.4 %copy-start.177 = (bf16[128]{0:T(256)(128)(2,1)S(1)}, bf16[128]{0:T(256)(128)(2,1)}, u32[]{:S(2)}) copy-start(bf16[128]{0:T(256)(128)(2,1)} %convert.369) | copy-start | bytes 772
  827.1 36.6 %copy-start.176 = (bf16[128]{0:T(256)(128)(2,1)S(1)}, bf16[128]{0:T(256)(128)(2,1)}, u32[]{:S(2)}) copy-start(bf16[128]{0:T(256)(128)(2,1)} %convert.370) | copy-start | bytes 772
  827.1 36.8 %copy-start.172 = (bf16[128]{0:T(256)(128)(2,1)S(1)}, bf16[128]{0:T(256)(128)(2,1)}, u32[]{:S(2)}) copy-start(bf16[128]{0:T(256)(128)(2,1)} %convert.371) | copy-start | bytes 772
  827.1 37.2 %copy-start.125 = (bf16[1984]{0:T(1024)(128)(2,1)S(1)}, bf16[1984]{0:T(1024)(128)(2,1)}, u32[]{:S(2)}) copy-start(bf16[1984]{0:T(1024)(128)(2,1)} %custom-call.1) | copy-start | bytes 11908
  827.1 38.0 %copy-start.138 = (bf16[128]{0:T(256)(128)(2,1)S(1)}, bf16[128]{0:T(256)(128)(2,1)}, u32[]{:S(2)}) copy-start(bf16[128]{0:T(256)(128)(2,1)} %get-tuple-element.216) | copy-start | bytes 772
  827.2 38.2 %copy-start.175 = (bf16[128]{0:T(256)(128)(2,1)S(1)}, bf16[128]{0:T(256)(128)(2,1)}, u32[]{:S(2)}) copy-start(bf16[128]{0:T(256)(128)(2,1)} %convert.377) | copy-start | bytes 772
  827.2 38.4 %copy-start.174 = (bf16[128]{0:T(256)(128)(2,1)S(1)}, bf16[128]{0:T(256)(128)(2,1)}, u32[]{:S(2)}) copy-start(bf16[128]{0:T(256)(128)(2,1)} %convert.378) | copy-start | bytes 772
  827.2 38.6 %copy-start.173 = (bf16[128]{0:T(256)(128)(2,1)S(1)}, bf16[128]{0:T(256)(128)(2,1)}, u32[]{:S(2)}) copy-start(bf16[128]{0:T(256)(128)(2,1)} %convert.379) | copy-start | bytes 772
  827.2 38.8 %copy-start.171 = (bf16[128]{0:T(256)(128)(2,1)S(1)}, bf16[128]{0:T(256)(128)(2,1)}, u32[]{:S(2)}) copy-start(bf16[128]{0:T(256)(128)(2,1)} %convert.380) | copy-start | bytes 772
  827.2 39.3 %copy-start.49 = (bf16[8,2400]{1,0:T(8,128)(2,1)S(1)}, bf16[8,2400]{1,0:T(8,128)(2,1)}, u32[]{:S(2)}) copy-start(bf16[8,2400]{1,0:T(8,128)(2,1)} %reshape.3280) | copy-start | bytes 115204
  827.2 40.1 %copy-start.150 = (f32[64]{0:T(128)S(1)}, f32[64]{0:T(128)}, u32[]{:S(2)}) copy-start(f32[64]{0:T(128)} %copy-done.149) | copy-start | bytes 772
  827.2 40.1 %copy-start.152 = (f32[64]{0:T(128)S(1)}, f32[64]{0:T(128)}, u32[]{:S(2)}) copy-start(f32[64]{0:T(128)} %copy-done.151) | copy-start | bytes 772
  839.8 29.4 %copy-start.39 = (bf16[1,24,24,128]{3,2,1,0:T(8,128)(2,1)}, bf16[1,24,24,128]{3,2,1,0:T(8,128)(2,1)S(1)}, u32[]{:S(2)}) copy-start(bf16[1,24,24,128]{3,2,1,0:T(8,128)(2,1)S(1)} %copy.177) | copy-start | bytes 442372
  (163 other events, 988.5 us)
Sparse Core Ops, SparseCore 0:
  9.6 20.2 all-gather.5
  403.5 18.1 reduce-scatter.21
  423.9 24.0 all-gather.7
  505.6 18.0 reduce-scatter.15
  634.3 15.9 reduce-scatter.23
  661.5 29.3 reduce-scatter.17
  737.7 18.3 reduce-scatter.25
  795.3 16.5 reduce-scatter.19
  815.2 22.4 reduce-scatter.27

commit v2 on v0

--- a/solution.py
+++ b/solution.py
@@ -1,6 +1,10 @@
+import functools
+
 import jax
 import jax.numpy as jnp
 from jax import lax
+from jax.experimental import pallas as pl
+from jax.experimental.pallas import tpu as pltpu
 from jax.sharding import PartitionSpec as P
 
 C_IN = 1024
@@ -453,9 +457,1573 @@
     )
 
 
+CELLS = MAP * MAP
+EDGE = 104
+BATCH = "batch"
+TENSOR = "tensor"
+GROUP_ROWS = ((0, 1), (1, 5), (5, 14), (14, 50))
+BINS = 64
+BF = jnp.bfloat16
+F32 = jnp.float32
+MESH = pl.DeviceIdType.MESH
+HALF = 4
+OWNERS = 8
+SPLITS = 4
+MERGED = 4
+SLOTS = 5
+
+
+def scratch_plan():
+    plan = dict(
+        w_r=((1024, 128), BF),
+        w_s=((1024, 512), BF),
+        w_m=((4608, 128), BF),
+        w_e=((512, 512), BF),
+        w_b=((2048, 512), BF),
+        w_u=((18432, 128), BF),
+        w_own=((4608, 128), BF),
+        w_a=((4608, 128), BF),
+        w_pair=((1024, 640), BF),
+        w_c=((128, 256), BF),
+        w_ac=((64, 256), F32),
+        gain_in=((OWNERS, 32, 128), F32),
+        whole=((SPLITS, CELLS, 256), BF),
+        ins=((CELLS, 128), F32),
+        col=((CELLS, 128), F32),
+        lab=((CELLS, 128), F32),
+        table=((BINS, CELLS), F32),
+        pool=((BINS, CELLS), BF),
+        pick=((BINS, CELLS), BF),
+        cells_in=((BINS, 128), F32),
+        pad=((9, CELLS + 2 * EDGE, 128), F32),
+        grad_pad=((CELLS + 2 * EDGE, 128), F32),
+        pre_r=((CELLS, 128), F32),
+        pre_s=((CELLS, 512), F32),
+        pre_a=((CELLS, 128), F32),
+        pre_m=((CELLS, 128), F32),
+        pre_e=((CELLS, 512), F32),
+        pre_u=((CELLS, 128), F32),
+        act_a=((CELLS, 128), BF),
+        h1=((SPLITS, CELLS, 128), BF),
+        h2=((SPLITS, CELLS, 128), BF),
+        joined=((SPLITS, CELLS, 512), BF),
+        joined_t=((SPLITS, 512, CELLS), BF),
+        pooled=((BINS, 512), BF),
+        part_b=((SPLITS, BINS, 128), BF),
+        recv_b=((SPLITS, BINS, 128), BF),
+        all_b=((OWNERS, BINS, 128), BF),
+        act_b=((SPLITS, OWNERS * BINS, 128), BF),
+        zsum=((2, OWNERS * BINS, 128), F32),
+        z_send=((OWNERS, 2, BINS, 128), BF),
+        z_recv=((OWNERS, 2, BINS, 128), BF),
+        united=((CELLS, 128), BF),
+        logit_send=((CELLS, 512), BF),
+        logit_recv=((SPLITS, 144, 512), BF),
+        slope_in=((SPLITS, 144, 512), BF),
+        d_f=((CELLS, 128), F32),
+        d_f2=((CELLS, 128), F32),
+        cat_u=((CELLS, 1152), BF),
+        cat_a=((CELLS, 640), BF),
+        dz_send=((9, BINS, 128), BF),
+        dz_recv=((OWNERS, 2, BINS, 128), BF),
+        d_act_send=((SPLITS, OWNERS * BINS, 128), BF),
+        d_act_recv=((SPLITS, OWNERS * BINS, 128), BF),
+        d_img_send=((OWNERS, BINS, 128), BF),
+        d_img_recv=((OWNERS, BINS, 128), BF),
+        d_bp=((SPLITS, BINS, 128), BF),
+        dm_near=((2, CELLS, 512), BF),
+        dm_far=((CELLS, 512), BF),
+        d_sum=((CELLS, 512), F32),
+        d_e=((CELLS, 512), BF),
+        d_s=((CELLS, 512), BF),
+        dh_send=((SPLITS, CELLS, 128), BF),
+        dh_recv=((2, SPLITS, CELLS, 128), BF),
+        d_low=((CELLS, 128), BF),
+        end_t=((SPLITS, 8, 128), F32),
+    )
+    for name, rows in SYNCS.items():
+        plan["sync_" + name] = ((OWNERS, rows, 128), F32)
+    for name, (rows, lanes, kind) in PARTS.items():
+        plan["first_" + name] = ((HALF, rows, lanes), kind)
+        plan["second_" + name] = ((HALF - 1, rows, lanes), kind)
+    plan["first_u"] = ((HALF, SLOTS, 512, 128), BF)
+    plan["second_u"] = ((HALF - 1, SLOTS, 512, 128), BF)
+    return plan
+
+
+SYNCS = dict(one=16, two=8, three=8, five=8, b1=8, b3=8, b4=16, b5=8, b6=8, end=8)
+PARTS = dict(
+    r=(128, 128, BF),
+    s=(128, 512, BF),
+    m=(576, 128, BF),
+    e=(64, 512, BF),
+    b=(256, 512, BF),
+    a=(576, 128, BF),
+    c=(16, 256, BF),
+    ac=(8, 256, F32),
+)
+SEMAPHORES = 1100
+
+
+class Refs:
+    pass
+
+
+def fold(value):
+    return value.reshape(-1, 8, value.shape[-1]).sum(0)
+
+
+def total(value):
+    return jnp.sum(value, axis=0, keepdims=True)
+
+
+def wide(value, times):
+    return jnp.concatenate([value] * times, axis=1)
+
+
+def dot(left, right):
+    return jnp.dot(left, right, preferred_element_type=F32)
+
+
+def dot_nt(left, right):
+    return lax.dot_general(left, right, (((1,), (1,)), ((), ())), preferred_element_type=F32)
+
+
+def dot_tn(left, right):
+    return lax.dot_general(left, right, (((0,), (0,)), ((), ())), preferred_element_type=F32)
+
+
+def loop(count, body):
+    def step(k, carry):
+        body(k)
+        return carry
+
+    lax.fori_loop(0, count, step, 0)
+
+
+def rows_at(k, block):
+    return pl.ds(pl.multiple_of(k * block, block), block)
+
+
+def step_kernel(names, *refs):
+    (
+        sizes, lab_in, feat, gain_own, p_r, p_s, p_m, p_e, p_b, p_u, p_a, p_c, p_ac,
+        o_r, o_s, o_m, o_e, o_b, o_u, o_a, o_c, o_ac, o_gain, o_misc,
+    ) = refs[:24]
+    v = Refs()
+    for name, ref in zip(names, refs[24:]):
+        setattr(v, name, ref)
+    sems = refs[-1]
+    me = lax.axis_index(BATCH)
+    t = lax.axis_index(TENSOR)
+    partner = me + 1 - 2 * lax.rem(me, 2)
+    t_core = t + 1 - 2 * lax.rem(t, 2)
+    t_x = lax.rem(t + 2, SPLITS)
+    t_diag = lax.rem(t_core + 2, SPLITS)
+    taken = [0]
+
+    def take(count):
+        start = taken[0]
+        taken[0] = start + count
+        assert taken[0] <= SEMAPHORES
+        return start
+
+    def far_peer(base, step):
+        return lax.rem(base + 2 * step, OWNERS)
+
+    def remote(src, dst, send, recv, device):
+        return pltpu.make_async_remote_copy(
+            src_ref=src,
+            dst_ref=dst,
+            send_sem=sems.at[send],
+            recv_sem=sems.at[recv],
+            device_id=device,
+            device_id_type=MESH,
+        )
+
+    late = []
+
+    barrier = pltpu.get_barrier_semaphore()
+    for k in range(1, OWNERS):
+        pl.semaphore_signal(
+            barrier, inc=1, device_id={BATCH: lax.rem(me + k, OWNERS)}, device_id_type=MESH
+        )
+    for k in range(1, SPLITS):
+        pl.semaphore_signal(
+            barrier, inc=1, device_id={TENSOR: lax.rem(t + k, SPLITS)}, device_id_type=MESH
+        )
+    pl.semaphore_wait(barrier, OWNERS + SPLITS - 2)
+
+    class Gather:
+        def __init__(self, piece, full, rows):
+            self.piece, self.full, self.rows = piece, full, rows
+            self.near_s, self.far_s, self.pass_s = take(1), take(HALF), take(HALF)
+            self.recv, self.keep = take(OWNERS), take(1)
+
+        def at(self, owner):
+            if self.rows is None:
+                return self.full.at[owner]
+            return self.full.at[rows_at(owner, self.rows), :]
+
+        def local(self):
+            return pltpu.make_async_copy(self.piece, self.at(me), sems.at[self.keep])
+
+        def near(self):
+            return remote(
+                self.piece, self.at(me), self.near_s, self.recv + me, {BATCH: partner}
+            )
+
+        def far(self, step):
+            return remote(
+                self.piece,
+                self.at(me),
+                self.far_s + step,
+                self.recv + me,
+                {BATCH: far_peer(me, step)},
+            )
+
+        def passed(self, step, base):
+            source = far_peer(base, step)
+            return remote(
+                self.at(source),
+                self.at(source),
+                self.pass_s + step,
+                self.recv + source,
+                {BATCH: partner},
+            )
+
+        def start(self):
+            self.local().start()
+            for step in range(1, HALF):
+                self.far(step).start()
+            self.near().start()
+
+        def forward(self):
+            for step in range(1, HALF):
+                self.passed(step, me).wait_recv()
+                self.passed(step, me).start()
+
+        def finish(self):
+            for step in range(HALF):
+                self.passed(step, partner).wait_recv()
+            self.local().wait()
+            self.near().wait_send()
+            for step in range(1, HALF):
+                self.far(step).wait_send()
+
+        def drain(self):
+            for step in range(1, HALF):
+                self.passed(step, me).wait_send()
+
+    g_gain = Gather(gain_own, v.gain_in, None)
+    g_r = Gather(p_r, v.w_r, 128)
+    g_s = Gather(p_s, v.w_s, 128)
+    g_a = Gather(p_a, v.w_a, 576)
+    g_m = Gather(p_m, v.w_m, 576)
+    g_e = Gather(p_e, v.w_e, 64)
+    g_b = Gather(p_b, v.w_b, 256)
+    g_c = Gather(p_c, v.w_c, 16)
+    g_ac = Gather(p_ac, v.w_ac, 8)
+
+    def chunk_of(owner, j):
+        return lax.rem(owner + j, 8)
+
+    def merged_rows(owner, j):
+        tap = owner + lax.div(owner + j, 8)
+        return pl.ds(pl.multiple_of((tap * MERGED + chunk_of(owner, j)) * 512, 512), 512)
+
+    def each_merged(owner, body):
+        def step(j):
+            pl.when(chunk_of(owner, j) < MERGED)(lambda: body(j))
+
+        loop(9, step)
+
+    class GatherUnite:
+        def __init__(self):
+            self.near_s, self.far_s, self.pass_s = take(9), take(9 * HALF), take(9 * HALF)
+            self.recv, self.keep, self.keep_all = take(9 * OWNERS), take(9), take(1)
+
+        def source(self, j):
+            return p_u.at[rows_at(j, 512), :]
+
+        def full(self, owner, j):
+            return v.w_u.at[merged_rows(owner, j), :]
+
+        def local(self, j):
+            return pltpu.make_async_copy(
+                self.source(j), self.full(me, j), sems.at[self.keep + j]
+            )
+
+        def whole(self):
+            return pltpu.make_async_copy(p_u, v.w_own, sems.at[self.keep_all])
+
+        def near(self, j):
+            return remote(
+                self.source(j),
+                self.full(me, j),
+                self.near_s + j,
+                self.recv + me * 9 + j,
+                {BATCH: partner},
+            )
+
+        def far(self, step, j):
+            return remote(
+                self.source(j),
+                self.full(me, j),
+                self.far_s + step * 9 + j,
+                self.recv + me * 9 + j,
+                {BATCH: far_peer(me, step)},
+            )
+
+        def passed(self, step, j, base):
+            source = far_peer(base, step)
+            return remote(
+                self.full(source, j),
+                self.full(source, j),
+                self.pass_s + step * 9 + j,
+                self.recv + source * 9 + j,
+                {BATCH: partner},
+            )
+
+        def start(self):
+            self.whole().start()
+
+            def begin(j):
+                self.local(j).start()
+                for step in range(1, HALF):
+                    self.far(step, j).start()
+                self.near(j).start()
+
+            each_merged(me, begin)
+
+        def forward(self, step):
+            def go(j):
+                self.passed(step, j, me).wait_recv()
+                self.passed(step, j, me).start()
+
+            each_merged(far_peer(me, step), go)
+
+        def finish(self):
+            for step in range(HALF):
+                each_merged(
+                    far_peer(partner, step),
+                    lambda j, step=step: self.passed(step, j, partner).wait_recv(),
+                )
+
+            def end(j):
+                self.local(j).wait()
+                self.near(j).wait_send()
+                for step in range(1, HALF):
+                    self.far(step, j).wait_send()
+
+            each_merged(me, end)
+
+        def drain(self):
+            for step in range(1, HALF):
+                each_merged(
+                    far_peer(me, step),
+                    lambda j, step=step: self.passed(step, j, me).wait_send(),
+                )
+
+    g_u = GatherUnite()
+
+    class Sync:
+        def __init__(self, buf):
+            self.buf = buf
+            self.send, self.recv = take(OWNERS), take(OWNERS)
+
+        def copy(self, k, slot):
+            return remote(
+                self.buf.at[slot],
+                self.buf.at[slot],
+                self.send + k,
+                self.recv + slot,
+                {BATCH: lax.rem(me + k, OWNERS)},
+            )
+
+        def start(self, rows):
+            for index, row in enumerate(rows):
+                self.buf[me, index : index + 1, :] = row
+            for index in range(len(rows), self.buf.shape[1]):
+                self.buf[me, index : index + 1, :] = jnp.zeros((1, 128), F32)
+            for k in range(1, OWNERS):
+                self.copy(k, me).start()
+
+        def wait(self):
+            for k in range(1, OWNERS):
+                self.copy(k, lax.rem(me + k, OWNERS)).wait_recv()
+            for k in range(1, OWNERS):
+                self.copy(k, me).wait_send()
+            value = self.buf[0]
+            for slot in range(1, OWNERS):
+                value = value + self.buf[slot]
+            return value
+
+    class Spread:
+
+        def __init__(self, buf):
+            self.buf = buf
+            self.send, self.recv = take(SPLITS), take(SPLITS)
+
+        def copy(self, k, slot):
+            return remote(
+                self.buf.at[slot],
+                self.buf.at[slot],
+                self.send + k,
+                self.recv + slot,
+                {TENSOR: lax.rem(t + k, SPLITS)},
+            )
+
+        def start(self):
+            for k in range(1, SPLITS):
+                self.copy(k, t).start()
+
+        def wait(self):
+            for k in range(1, SPLITS):
+                self.copy(k, lax.rem(t + k, SPLITS)).wait_recv()
+            for k in range(1, SPLITS):
+                self.copy(k, t).wait_send()
+
+    class Exchange:
+
+        def __init__(self, axis, count, part, into):
+            self.axis, self.count, self.part, self.into = axis, count, part, into
+            self.mine = me if axis == BATCH else t
+            self.send, self.recv = take(count), take(count)
+
+        def copy(self, k, slot):
+            other = lax.rem(self.mine + k, self.count)
+            return remote(
+                self.part(other),
+                self.into(slot),
+                self.send + k,
+                self.recv + slot,
+                {self.axis: other},
+            )
+
+        def start(self):
+            for k in range(1, self.count):
+                self.copy(k, self.mine).start()
+
+        def wait(self):
+            for k in range(1, self.count):
+                self.copy(k, lax.rem(self.mine + k, self.count)).wait_recv()
+            for k in range(1, self.count):
+                self.copy(k, self.mine).wait_send()
+
+    feat_keep = take(1)
+    feat_local = pltpu.make_async_copy(feat, v.whole.at[t], sems.at[feat_keep])
+    feat_spread = Exchange(TENSOR, SPLITS, lambda other: feat, lambda slot: v.whole.at[slot])
+    for item in (g_gain, g_r, g_s, g_a):
+        item.start()
+    feat_local.start()
+    feat_spread.start()
+
+    high, across = sizes[0, 0], sizes[0, 1]
+    place = lax.broadcasted_iota(jnp.int32, (CELLS, 128), 0).astype(F32)
+    row_of = jnp.floor((place + 0.5) / MAP)
+    col_of = place - MAP * row_of
+    within = (row_of < high.astype(F32)) & (col_of < across.astype(F32))
+    v.ins[...] = jnp.where(within, 1.0, 0.0)
+    v.col[...] = col_of
+    v.lab[...] = jnp.where(within, lab_in[...], -1.0)
+    v.table[...] = jnp.zeros((BINS, CELLS), F32)
+    lane_place = lax.broadcasted_iota(jnp.int32, (1, CELLS), 1).astype(F32)
+    lane_row = jnp.floor((lane_place + 0.5) / MAP)
+    lane_col = lane_place - MAP * lane_row
+
+    def ranges(extent, bins, where):
+        inside, chosen, counts = [], [], []
+        for k in range(bins):
+            low = lax.div(k * extent, bins)
+            top = lax.div((k + 1) * extent + (bins - 1), bins)
+            member = (where >= low.astype(F32)) & (where < top.astype(F32))
+            inside.append(jnp.where(member, 1.0, 0.0))
+            picked = where * bins >= (k * extent).astype(F32)
+            if k < bins - 1:
+                picked = picked & (where * bins < ((k + 1) * extent).astype(F32))
+            chosen.append(jnp.where(picked, 1.0, 0.0))
+            counts.append(top - low)
+        return inside, chosen, counts
+
+    picks = []
+    v.cells_in[...] = jnp.ones((BINS, 128), F32)
+    for group, bins in enumerate(BIN_COUNTS):
+        r_in, r_pick, r_count = ranges(high, bins, lane_row)
+        c_in, c_pick, c_count = ranges(across, bins, lane_col)
+        for a in range(bins):
+            for b in range(bins):
+                spot = BIN_STARTS[group] + a * bins + b
+                v.table[spot : spot + 1, :] = r_in[a] * c_in[b]
+                v.cells_in[spot : spot + 1, :] = jnp.full(
+                    (1, 128), (r_count[a] * c_count[b]).astype(F32)
+                )
+                picks.append((spot, r_pick[a] * c_pick[b]))
+    v.pool[...] = v.table[...].astype(BF)
+    for spot, value in picks:
+        v.table[spot : spot + 1, :] = value
+    v.pick[...] = v.table[...].astype(BF)
+    zeros_edge = jnp.zeros((EDGE, 128), F32)
+    for tap in range(9):
+        v.pad[tap, 0:EDGE, :] = zeros_edge
+        v.pad[tap, EDGE + CELLS :, :] = zeros_edge
+    v.grad_pad[0:EDGE, :] = zeros_edge
+    v.grad_pad[EDGE + CELLS :, :] = zeros_edge
+    lanes = lax.broadcasted_iota(jnp.int32, (1, 256), 1).astype(F32)
+    counts = jnp.zeros((8, 256), F32)
+    for k in range(0, CELLS, 96):
+        counts = counts + fold(
+            jnp.where(wide(v.lab[k : k + 96, :], 2) == lanes, 1.0, 0.0)
+        )
+    class_local = total(counts)
+    cells_local = jnp.full((1, 128), (high * across).astype(F32))
+    left_half = lax.broadcasted_iota(jnp.int32, (64, 128), 1) < 64
+
+    for item in (g_gain, g_r, g_s, g_a):
+        item.forward()
+    for item in (g_m, g_e, g_b, g_c, g_ac):
+        item.start()
+    g_u.start()
+    for item in (g_gain, g_r, g_s, g_a):
+        item.finish()
+    feat_local.wait()
+    feat_spread.wait()
+    gains = v.gain_in[0]
+    for slot in range(1, OWNERS):
+        gains = gains + v.gain_in[slot]
+
+    def gamma(row, width=1):
+        return jnp.concatenate([gains[row + k : row + k + 1] for k in range(width)], axis=1)
+
+    def beta(row, width=1):
+        return gamma(16 + row, width)
+
+    def unpack(chunk):
+        for pair in range(5):
+            even = v.w_a[rows_at(2 * pair * 8 + chunk, 64), :].astype(F32)
+            if pair < 4:
+                odd = v.w_a[rows_at((2 * pair + 1) * 8 + chunk, 64), :].astype(F32)
+            else:
+                odd = jnp.zeros((64, 128), F32)
+            low = jnp.where(left_half, even, pltpu.roll(odd, 64, 1))
+            top = jnp.where(left_half, pltpu.roll(even, 64, 1), odd)
+            v.w_pair[rows_at(2 * chunk, 64), pair * 128 : pair * 128 + 128] = low.astype(BF)
+            v.w_pair[rows_at(2 * chunk + 1, 64), pair * 128 : pair * 128 + 128] = top.astype(BF)
+
+    loop(8, unpack)
+
+    def whole_feat():
+        return jnp.concatenate([v.whole[k] for k in range(SPLITS)], axis=1)
+
+    v.pre_r[...] = dot(whole_feat(), v.w_r[...])
+    for k in range(0, 512, 256):
+        v.pre_s[:, k : k + 256] = dot(whole_feat(), v.w_s[:, k : k + 256])
+    for pair in (0, 2):
+        value = dot(whole_feat(), v.w_pair[:, pair * 128 : pair * 128 + 256])
+        v.pad[pair, EDGE : EDGE + CELLS, :] = value[:, :128]
+        v.pad[pair + 1, EDGE : EDGE + CELLS, :] = value[:, 128:]
+    v.pad[4, EDGE : EDGE + CELLS, :] = dot(whole_feat(), v.w_pair[:, 512:640])
+
+    def offset(tap, spacing):
+        return ((tap // 3 - 1) * MAP + (tap % 3 - 1)) * spacing
+
+    def col_mask(at, right):
+        where = v.col[at, :] + float(right)
+        return jnp.where((where >= 0.0) & (where < float(MAP)), 1.0, 0.0)
+
+    BLOCK = 72
+
+    def shift_sum(taps, spacing, at, slot_of):
+        out = None
+        for b in (-1, 0, 1):
+            part = None
+            for tap in taps:
+                if tap % 3 - 1 != b:
+                    continue
+                start = EDGE + at + offset(tap, spacing)
+                value = v.pad[slot_of(tap), start : start + BLOCK, :]
+                part = value if part is None else part + value
+            if part is None:
+                continue
+            if b:
+                part = part * col_mask(slice(at, at + BLOCK), b * spacing)
+            out = part if out is None else out + part
+        return out
+
+    left_wide = lax.broadcasted_iota(jnp.int32, (BLOCK, 128), 1) < 64
+    for at in range(0, CELLS, BLOCK):
+        even = shift_sum((0, 2, 4, 6, 8), 1, at, lambda tap: tap // 2)
+        odd = shift_sum((1, 3, 5, 7), 1, at, lambda tap: tap // 2)
+        v.pre_a[at : at + BLOCK, :] = jnp.where(left_wide, even + pltpu.roll(odd, 64, 1), 0.0)
+
+    def masked_sums(ref):
+        width = ref.shape[1]
+
+        def step(k, carry):
+            at = rows_at(k, 96)
+            value = ref[at, :]
+            kept = value * (v.ins[at, :] if width == 128 else wide(v.ins[at, :], width // 128))
+            return (carry[0] + fold(kept), carry[1] + fold(kept * value))
+
+        zero = jnp.zeros((8, width), F32)
+        sums = lax.fori_loop(0, 6, step, (zero, zero))
+        return total(sums[0]), total(sums[1])
+
+    def split_rows(value):
+        return [value[:, k : k + 128] for k in range(0, value.shape[1], 128)]
+
+    def join_rows(value, row, count):
+        return jnp.concatenate([value[row + k : row + k + 1] for k in range(count)], axis=1)
+
+    def moments(first, second, count):
+        mean = first / count
+        return mean, lax.rsqrt(second / count - mean * mean + 1e-05)
+
+    sync = Sync(v.sync_one)
+    r1, r2 = masked_sums(v.pre_r)
+    s1, s2 = masked_sums(v.pre_s)
+    a1, a2 = masked_sums(v.pre_a)
+    sync.start(
+        [r1, r2] + split_rows(s1) + split_rows(s2) + [a1, a2, cells_local] + split_rows(class_local)
+    )
+    g_m.forward()
+    sums = sync.wait()
+    count = sums[12:13]
+    count4 = wide(count, 4)
+    norm_r = moments(sums[0:1], sums[1:2], count)
+    norm_s = moments(join_rows(sums, 2, 4), join_rows(sums, 6, 4), count4)
+    norm_a = moments(sums[10:11], sums[11:12], count)
+    class_count = join_rows(sums, 13, 2)
+
+    def normed(ref, at, norm):
+        return (ref[at, :] - norm[0]) * norm[1]
+
+    spread_1 = Spread(v.h1)
+
+    def make_h1(k):
+        at = rows_at(k, 96)
+        v.h1[t, at, :] = jax.nn.silu(gamma(0) * normed(v.pre_r, at, norm_r) + beta(0)).astype(BF)
+
+    loop(6, make_h1)
+    spread_1.start()
+
+    def make_a(k):
+        at = rows_at(k, 96)
+        v.act_a[at, :] = jax.nn.silu(gamma(15) * normed(v.pre_a, at, norm_a) + beta(15)).astype(BF)
+
+    loop(6, make_a)
+    g_e.forward()
+    g_m.finish()
+    spread_1.wait()
+
+    def full_h(ref):
+        return jnp.concatenate([ref[k] for k in range(SPLITS)], axis=1)
+
+    def middle(tap):
+        v.pad[tap, EDGE : EDGE + CELLS, :] = dot(full_h(v.h1), v.w_m[rows_at(tap, 512), :])
+
+    loop(9, middle)
+    for at in range(0, CELLS, BLOCK):
+        v.pre_m[at : at + BLOCK, :] = shift_sum(range(9), 4, at, lambda tap: tap)
+    sync = Sync(v.sync_two)
+    sync.start(list(masked_sums(v.pre_m)))
+    g_e.finish()
+    sums = sync.wait()
+    norm_m = moments(sums[0:1], sums[1:2], count)
+    spread_2 = Spread(v.h2)
+
+    def make_h2(k):
+        at = rows_at(k, 96)
+        v.h2[t, at, :] = jax.nn.silu(gamma(5) * normed(v.pre_m, at, norm_m) + beta(5)).astype(BF)
+
+    loop(6, make_h2)
+    spread_2.start()
+    g_b.forward()
+    spread_2.wait()
+    for k in range(0, 512, 256):
+        v.pre_e[:, k : k + 256] = dot(full_h(v.h2), v.w_e[:, k : k + 256])
+    sync = Sync(v.sync_three)
+    e1, e2 = masked_sums(v.pre_e)
+    sync.start(split_rows(e1) + split_rows(e2))
+    g_c.forward()
+    g_ac.forward()
+    sums = sync.wait()
+    norm_e = moments(join_rows(sums, 0, 4), join_rows(sums, 4, 4), count4)
+
+    def summed(at):
+        return (
+            gamma(6, 4) * normed(v.pre_e, at, norm_e)
+            + beta(6, 4)
+            + gamma(1, 4) * normed(v.pre_s, at, norm_s)
+            + beta(1, 4)
+        )
+
+    def make_merged(k):
+        at = rows_at(k, 48)
+        v.joined[t, at, :] = jax.nn.silu(summed(at)).astype(BF)
+
+    loop(12, make_merged)
+
+    j_send, j_recv = take(3), take(SPLITS)
+
+    def joined_copy(k, slot, device):
+        return remote(
+            v.joined.at[slot], v.joined.at[slot], j_send + k, j_recv + slot, {TENSOR: device}
+        )
+
+    joined_copy(0, t, t_x).start()
+    joined_copy(1, t, t_core).start()
+
+    bin_row = lax.broadcasted_iota(jnp.int32, (BINS, 1), 0)
+
+    def group_mask(group, shape=None):
+        low, top = GROUP_ROWS[group]
+        kept = jnp.where((bin_row >= low) & (bin_row < top), 1.0, 0.0)
+        return kept if shape is None else jnp.broadcast_to(kept, shape)
+
+    cells_in = wide(v.cells_in[...], 4)
+    pooled = dot(v.pool[...], v.joined[t]) / cells_in
+    v.pooled[...] = pooled.astype(BF)
+    g_b.finish()
+    part = jnp.zeros((BINS, 512), F32)
+    for group in range(4):
+        rows = (v.pooled[...].astype(F32) * group_mask(group)).astype(BF)
+        part = part + dot(rows, v.w_b[group * 512 : group * 512 + 512, :])
+    for k in range(SPLITS):
+        v.part_b[k] = part[:, k * 128 : k * 128 + 128].astype(BF)
+    v.recv_b[t] = v.part_b[t]
+    ex = Exchange(TENSOR, SPLITS, lambda o: v.part_b.at[o], lambda s: v.recv_b.at[s])
+    ex.start()
+    joined_copy(0, t_x, t_x).wait_recv()
+    joined_copy(2, t_x, t_core).start()
+    ex.wait()
+    own_b = v.recv_b[0].astype(F32)
+    for k in range(1, SPLITS):
+        own_b = own_b + v.recv_b[k].astype(F32)
+    v.all_b[me] = own_b.astype(BF)
+    ex = Exchange(BATCH, OWNERS, lambda o: v.all_b.at[me], lambda s: v.all_b.at[s])
+    ex.start()
+    g_u.forward(1)
+    ex.wait()
+    all_b = [v.all_b[k].astype(F32) for k in range(OWNERS)]
+    sum_b, square_b = all_b[0], all_b[0] * all_b[0]
+    for k in range(1, OWNERS):
+        sum_b = sum_b + all_b[k]
+        square_b = square_b + all_b[k] * all_b[k]
+    mean_b = jnp.zeros((BINS, 128), F32)
+    scale_b = jnp.zeros((BINS, 128), F32)
+    gamma_b = jnp.zeros((BINS, 128), F32)
+    beta_b = jnp.zeros((BINS, 128), F32)
+    count_b = jnp.zeros((BINS, 1), F32)
+    for group, bins in enumerate(BIN_COUNTS):
+        kept = group_mask(group)
+        size = float(OWNERS * bins * bins)
+        mean, scaling = moments(total(sum_b * kept), total(square_b * kept), size)
+        mean_b = mean_b + kept * mean
+        scale_b = scale_b + kept * scaling
+        gamma_b = gamma_b + kept * gamma(10 + group)
+        beta_b = beta_b + kept * beta(10 + group)
+        count_b = count_b + kept / size
+    spread_b = Spread(v.act_b)
+    for k in range(OWNERS):
+        out = gamma_b * ((all_b[k] - mean_b) * scale_b) + beta_b
+        v.act_b[t, k * BINS : k * BINS + BINS, :] = jax.nn.silu(out).astype(BF)
+    spread_b.start()
+    g_u.forward(2)
+    spread_b.wait()
+    g_u.whole().wait()
+    row_512 = lax.broadcasted_iota(jnp.int32, (OWNERS * BINS, 1), 0) & (BINS - 1)
+    group_id = jnp.where(
+        row_512 < 1, 0, jnp.where(row_512 < 5, 1, jnp.where(row_512 < 14, 2, jnp.where(row_512 < 50, 3, 9)))
+    )
+
+    def full_act():
+        return jnp.concatenate([v.act_b[k] for k in range(SPLITS)], axis=1)
+
+    v.zsum[...] = jnp.zeros((2, OWNERS * BINS, 128), F32)
+
+    def own_branch(j, body):
+        chunk = chunk_of(me, j)
+        pl.when(chunk >= MERGED)(lambda: body(chunk - MERGED, lax.div(me + j, 8)))
+
+    def make_z(j):
+        def body(group, side):
+            kept = jnp.where(group_id == group, 1.0, 0.0)
+            rows = (full_act().astype(F32) * kept).astype(BF)
+            v.zsum[side] = v.zsum[side] + dot(rows, v.w_own[rows_at(j, 512), :])
+
+        own_branch(j, body)
+
+    loop(9, make_z)
+    for k in range(OWNERS):
+        for side in range(2):
+            v.z_send[k, side] = v.zsum[side, k * BINS : k * BINS + BINS, :].astype(BF)
+    v.z_recv[me] = v.z_send[me]
+    ex = Exchange(BATCH, OWNERS, lambda o: v.z_send.at[o], lambda s: v.z_recv.at[s])
+    ex.start()
+    g_u.forward(3)
+    joined_copy(1, t_core, t_core).wait_recv()
+    joined_copy(2, t_diag, t_core).wait_recv()
+    for k in range(SPLITS):
+        v.joined_t[k] = v.joined[k].T
+    ex.wait()
+    g_u.finish()
+
+    pick2 = jnp.concatenate([v.pick[...], v.pick[...]], axis=0)
+
+    def tap_z(tap):
+        if tap == 0:
+            return v.z_recv[0, 0].astype(F32)
+        if tap == 8:
+            return v.z_recv[7, 1].astype(F32)
+        return v.z_recv[tap, 0].astype(F32) + v.z_recv[tap - 1, 1].astype(F32)
+
+    def full_joined():
+        return jnp.concatenate([v.joined[k] for k in range(SPLITS)], axis=1)
+
+    def w_tap(tap):
+        return v.w_u[rows_at(tap, 2048), :]
+
+    def unite_pair(p):
+        value = dot(full_joined(), jnp.concatenate([w_tap(2 * p), w_tap(2 * p + 1)], axis=1))
+        v.pad[2 * p, EDGE : EDGE + CELLS, :] = value[:, :128]
+        v.pad[2 * p + 1, EDGE : EDGE + CELLS, :] = value[:, 128:]
+
+    loop(4, unite_pair)
+    v.pad[8, EDGE : EDGE + CELLS, :] = dot(full_joined(), w_tap(8))
+    for tap in range(9):
+        z = tap_z(tap)
+        high_z = z.astype(BF)
+        low_z = (z - high_z.astype(F32)).astype(BF)
+        v.pad[tap, EDGE : EDGE + CELLS, :] = v.pad[tap, EDGE : EDGE + CELLS, :] + dot_tn(
+            pick2, jnp.concatenate([high_z, low_z], axis=0)
+        )
+    for at in range(0, CELLS, BLOCK):
+        v.pre_u[at : at + BLOCK, :] = shift_sum(range(9), 1, at, lambda tap: tap)
+    sync = Sync(v.sync_five)
+    sync.start(list(masked_sums(v.pre_u)))
+    for item in (g_c, g_ac):
+        item.finish()
+    for item in (g_gain, g_r, g_s, g_a, g_m, g_e, g_b, g_c, g_ac, g_u):
+        item.drain()
+    joined_copy(0, t, t_x).wait_send()
+    joined_copy(1, t, t_core).wait_send()
+    joined_copy(2, t_x, t_core).wait_send()
+    w_ac = jnp.concatenate([v.w_ac[...], jnp.zeros((64, 256), F32)], axis=0).astype(BF)
+    sums = sync.wait()
+    norm_u = moments(sums[0:1], sums[1:2], count)
+
+    def make_u(k):
+        at = rows_at(k, 96)
+        v.united[at, :] = jax.nn.silu(gamma(14) * normed(v.pre_u, at, norm_u) + beta(14)).astype(BF)
+
+    loop(6, make_u)
+
+    v.logit_send[:, :256] = dot(v.united[...], v.w_c[...]).astype(BF)
+    v.logit_send[:, 256:] = dot(v.act_a[...], w_ac).astype(BF)
+    ex = Exchange(
+        TENSOR,
+        SPLITS,
+        lambda o: v.logit_send.at[rows_at(o, 144), :],
+        lambda s: v.logit_recv.at[s],
+    )
+    ex.start()
+    v.logit_recv[t] = v.logit_send[rows_at(t, 144), :]
+    total_valid = jnp.sum(class_count, axis=1, keepdims=True)
+    class_weight = total_valid / (NCLS * class_count + total_valid)
+    loss_weight = jnp.sum(class_count * class_weight, axis=1, keepdims=True)
+    class_weight = jnp.where(lanes < float(NCLS), class_weight, 0.0)
+    hot = jnp.where(wide(v.lab[rows_at(t, 144), :], 2) == lanes, 1.0, 0.0)
+    cell_weight = jnp.sum(hot * class_weight, axis=1, keepdims=True)
+    ex.wait()
+    logits = v.logit_recv[0].astype(F32)
+    for k in range(1, SPLITS):
+        logits = logits + v.logit_recv[k].astype(F32)
+
+    def log_softmax(value):
+        value = jnp.where(lanes < float(NCLS), value, -1e30)
+        value = value - jnp.max(value, axis=1, keepdims=True)
+        powers = jnp.exp(value)
+        mass = jnp.sum(powers, axis=1, keepdims=True)
+        return value - jnp.log(mass), powers / mass
+
+    log_main, p_main = log_softmax(logits[:, :256])
+    log_aux, p_aux = log_softmax(logits[:, 256:])
+    loss_rows = total(fold(-cell_weight * hot * (log_main + 0.4 * log_aux)))
+    loss_local = loss_rows[:, :128] + loss_rows[:, 128:]
+    o_misc[1:2, :] = loss_local
+    v.slope_in[t, :, :256] = (cell_weight * (p_main - hot) / loss_weight).astype(BF)
+    v.slope_in[t, :, 256:] = (0.4 * cell_weight * (p_aux - hot) / loss_weight).astype(BF)
+    spread_g = Spread(v.slope_in)
+    spread_g.start()
+    spread_g.wait()
+    g_main = v.slope_in[:, :, :256].reshape(CELLS, 256)
+    g_aux = v.slope_in[:, :, 256:].reshape(CELLS, 256)
+    v.d_f[...] = dot_nt(g_main, v.w_c[...])
+    v.d_f2[...] = dot_nt(g_aux, w_ac)
+
+    def slope(value):
+        gate = jax.nn.sigmoid(value)
+        return gate * (1.0 + value * (1.0 - gate))
+
+    def through_silu(ref, pre, norm, row):
+        def step(k, carry):
+            at = rows_at(k, 96)
+            unit = normed(pre, at, norm)
+            value = ref[at, :] * slope(gamma(row) * unit + beta(row))
+            ref[at, :] = value
+            return (carry[0] + fold(value), carry[1] + fold(value * unit))
+
+        zero = jnp.zeros((8, 128), F32)
+        sums = lax.fori_loop(0, 6, step, (zero, zero))
+        return [total(sums[0]), total(sums[1])]
+
+    def back_norm(value, unit, mask, norm, gain, first, second, size):
+        inner = value - mask * (first + unit * second) / size
+        return gain * norm[1] * inner
+
+    gain_grads = {}
+    sync = Sync(v.sync_b1)
+    sync.start(
+        through_silu(v.d_f, v.pre_u, norm_u, 14) + through_silu(v.d_f2, v.pre_a, norm_a, 15)
+    )
+
+    class Scatter:
+        def __init__(self, first, second, full, rows, out):
+            self.full, self.rows, self.out = full, rows, out
+            self.first, self.second = first, second
+            self.near_s, self.near_r = take(HALF), take(HALF)
+            self.far_s, self.far_r = take(HALF), take(HALF)
+            self.block = min(rows, 64)
+
+        def near(self, step):
+            dest = far_peer(partner, step)
+            return remote(
+                self.full.at[rows_at(dest, self.rows), :],
+                self.first.at[step],
+                self.near_s + step,
+                self.near_r + step,
+                {BATCH: partner},
+            )
+
+        def far(self, step):
+            return remote(
+                self.first.at[step],
+                self.second.at[step - 1],
+                self.far_s + step,
+                self.far_r + step,
+                {BATCH: far_peer(me, step)},
+            )
+
+        def start(self):
+            for step in (1, 2, 3, 0):
+                self.near(step).start()
+
+        def middle(self):
+            kind = self.first.dtype
+            for step in (1, 2, 3, 0):
+                self.near(step).wait_recv()
+                base = far_peer(me, step) * (self.rows // self.block)
+
+                def add(k, step=step, base=base):
+                    at = rows_at(k, self.block)
+                    value = self.full[rows_at(base + k, self.block), :].astype(F32)
+                    value = value + self.first[step, at, :].astype(F32)
+                    if step:
+                        self.first[step, at, :] = value.astype(kind)
+                    else:
+                        self.out[at, :] = value
+
+                loop(self.rows // self.block, add)
+                if step:
+                    self.far(step).start()
+
+        def end(self):
+            for step in range(1, HALF):
+                self.far(step).wait_recv()
+
+            def add(k, carry):
+                at = rows_at(k, self.block)
+                value = self.out[at, :]
+                for step in range(1, HALF):
+                    value = value + self.second[step - 1, at, :].astype(F32)
+                self.out[at, :] = value
+                return carry + fold(value * value)
+
+            squares = lax.fori_loop(
+                0, self.rows // self.block, add, jnp.zeros((8, self.out.shape[1]), F32)
+            )
+            for step in (1, 2, 3, 0):
+                self.near(step).wait_send()
+                if step:
+                    self.far(step).wait_send()
+            return sum(split_rows(total(squares)))
+
+    s_c = Scatter(v.first_c, v.second_c, v.w_c, 16, o_c)
+    s_ac = Scatter(v.first_ac, v.second_ac, v.w_ac, 8, o_ac)
+    s_a = Scatter(v.first_a, v.second_a, v.w_a, 576, o_a)
+    s_b = Scatter(v.first_b, v.second_b, v.w_b, 256, o_b)
+    s_s = Scatter(v.first_s, v.second_s, v.w_s, 128, o_s)
+    s_e = Scatter(v.first_e, v.second_e, v.w_e, 64, o_e)
+    s_m = Scatter(v.first_m, v.second_m, v.w_m, 576, o_m)
+    s_r = Scatter(v.first_r, v.second_r, v.w_r, 128, o_r)
+
+    class ScatterUnite:
+        def __init__(self):
+            self.near_s, self.near_r = take(9 * HALF), take(9 * HALF)
+            self.far_s, self.far_r = take(9 * HALF), take(9 * HALF)
+
+        def slot(self, owner, j):
+            return jnp.where(j == 8, SLOTS - 1, chunk_of(owner, j))
+
+        def near(self, step, j, base):
+            dest = far_peer(base, step)
+            return remote(
+                v.w_u.at[merged_rows(dest, j), :],
+                v.first_u.at[step, self.slot(dest, j)],
+                self.near_s + step * 9 + j,
+                self.near_r + step * 9 + j,
+                {BATCH: partner},
+            )
+
+        def far(self, step, j, owner):
+            at = self.slot(owner, j)
+            return remote(
+                v.first_u.at[step, at],
+                v.second_u.at[step - 1, at],
+                self.far_s + step * 9 + j,
+                self.far_r + step * 9 + j,
+                {BATCH: far_peer(me, step)},
+            )
+
+        def start(self):
+            for step in (1, 2, 3, 0):
+                each_merged(
+                    far_peer(partner, step),
+                    lambda j, step=step: self.near(step, j, partner).start(),
+                )
+
+        def middle(self, step):
+            owner = far_peer(me, step)
+
+            def go(j):
+                self.near(step, j, me).wait_recv()
+                slot = self.slot(owner, j)
+                tap = owner + lax.div(owner + j, 8)
+                base = (tap * MERGED + chunk_of(owner, j)) * 8
+
+                def add(k):
+                    at = rows_at(k, 64)
+                    value = v.w_u[rows_at(base + k, 64), :].astype(F32)
+                    value = value + v.first_u[step, slot, at, :].astype(F32)
+                    if step:
+                        v.first_u[step, slot, at, :] = value.astype(BF)
+                    else:
+                        o_u[rows_at(j * 8 + k, 64), :] = value
+
+                loop(8, add)
+                if step:
+                    self.far(step, j, owner).start()
+
+            each_merged(owner, go)
+
+        def end(self):
+            def go(j):
+                slot = self.slot(me, j)
+                for step in range(1, HALF):
+                    self.far(step, j, me).wait_recv()
+
+                def add(k):
+                    at = rows_at(k, 64)
+                    value = o_u[rows_at(j * 8 + k, 64), :]
+                    for step in range(1, HALF):
+                        value = value + v.second_u[step - 1, slot, at, :].astype(F32)
+                    o_u[rows_at(j * 8 + k, 64), :] = value
+
+                loop(8, add)
+
+            each_merged(me, go)
+            for step in (1, 2, 3, 0):
+                each_merged(
+                    far_peer(partner, step),
+                    lambda j, step=step: self.near(step, j, partner).wait_send(),
+                )
+                if step:
+                    each_merged(
+                        far_peer(me, step),
+                        lambda j, step=step: self.far(step, j, far_peer(me, step)).wait_send(),
+                    )
+
+            def square(k, carry):
+                value = o_u[rows_at(k, 64), :]
+                return carry + fold(value * value)
+
+            squares = lax.fori_loop(0, 72, square, jnp.zeros((8, 128), F32))
+            return sum(split_rows(total(squares)))
+
+    s_u = ScatterUnite()
+
+    v.w_c[...] = dot_tn(v.united[...], g_main).astype(BF)
+    v.w_ac[...] = dot_tn(v.act_a[...], g_aux)[:64]
+    s_c.start()
+    s_ac.start()
+    sums = sync.wait()
+    gain_grads[14] = (sums[1:2], sums[0:1])
+    gain_grads[15] = (sums[3:4], sums[2:3])
+
+    def spread_taps(ref, pre, norm, row, first, second):
+        def step(k):
+            at = rows_at(k, 96)
+            value = back_norm(
+                ref[at, :], normed(pre, at, norm), v.ins[at, :], norm, gamma(row), first, second, count
+            )
+            ref[at, :] = value.astype(BF).astype(F32)
+
+        loop(6, step)
+        v.grad_pad[EDGE : EDGE + CELLS, :] = ref[...]
+
+    def back_tap(tap, spacing, at):
+        start = EDGE + at - offset(tap, spacing)
+        value = v.grad_pad[start : start + 96, :]
+        right = tap % 3 - 1
+        if right:
+            value = value * col_mask(slice(at, at + 96), -right * spacing)
+        return value
+
+    def fill(cat, spacing):
+        for tap in range(9):
+            for at in range(0, CELLS, 96):
+                cat[at : at + 96, tap * 128 : tap * 128 + 128] = back_tap(tap, spacing, at).astype(
+                    BF
+                )
+
+    spread_taps(v.d_f, v.pre_u, norm_u, 14, sums[0:1], sums[1:2])
+    fill(v.cat_u, 1)
+
+    dz = dot(v.pick[...], v.cat_u[...])
+    for tap in range(9):
+        v.dz_send[tap] = dz[:, tap * 128 : tap * 128 + 128].astype(BF)
+    v.dz_recv[me] = v.dz_send[pl.ds(me, 2)]
+    ex_dz = Exchange(
+        BATCH, OWNERS, lambda o: v.dz_send.at[pl.ds(o, 2)], lambda s: v.dz_recv.at[s]
+    )
+    ex_dz.start()
+
+    def merged_back(c):
+        weight = jnp.concatenate(
+            [v.w_u[rows_at(tap * MERGED + c, 512), :] for tap in range(9)], axis=1
+        )
+        v.joined[c] = dot_nt(v.cat_u[...], weight).astype(BF)
+
+    near_s, near_r, far_s, far_r = take(2), take(2), take(1), take(1)
+
+    def dm_near(k, slot):
+        return remote(
+            v.joined.at[slot], v.dm_near.at[k], near_s + k, near_r + k, {TENSOR: t_core}
+        )
+
+    merged_back(t_diag)
+    dm_near(1, t_diag).start()
+    merged_back(t_core)
+    dm_near(0, t_core).start()
+    ex_dz.wait()
+
+    d_act = v.d_sum.at[0 : OWNERS * BINS, :]
+    d_act[...] = jnp.zeros((OWNERS * BINS, 512), F32)
+
+    def branch_back(j):
+        def body(group, side):
+            kept = jnp.where(group_id == group, 1.0, 0.0)
+            value = v.dz_recv[:, side].reshape(OWNERS * BINS, 128).astype(F32) * kept
+            value = value.astype(BF)
+            o_u[rows_at(j, 512), :] = dot_tn(full_act(), value)
+            d_act[...] = d_act[...] + dot_nt(value, v.w_own[rows_at(j, 512), :])
+
+        own_branch(j, body)
+
+    loop(9, branch_back)
+    for k in range(SPLITS):
+        v.d_act_send[k] = d_act[:, k * 128 : k * 128 + 128].astype(BF)
+    v.d_act_recv[t] = v.d_act_send[t]
+    ex = Exchange(TENSOR, SPLITS, lambda o: v.d_act_send.at[o], lambda s: v.d_act_recv.at[s])
+    ex.start()
+    merged_back(t_x)
+    merged_back(t)
+    dm_near(1, t_x).wait_recv()
+
+    def add_x(k):
+        at = rows_at(k, 48)
+        value = v.joined[t_x, at, :].astype(F32) + v.dm_near[1, at, :].astype(F32)
+        v.joined[t_x, at, :] = value.astype(BF)
+
+    loop(12, add_x)
+    dm_far = remote(v.joined.at[t_x], v.dm_far, far_s, far_r, {TENSOR: t_x})
+    dm_far.start()
+    ex.wait()
+    for k in range(OWNERS):
+        at = slice(k * BINS, k * BINS + BINS)
+        value = v.d_act_recv[0, at, :].astype(F32)
+        for slot in range(1, SPLITS):
+            value = value + v.d_act_recv[slot, at, :].astype(F32)
+        v.d_img_send[k] = value.astype(BF)
+    v.d_img_recv[me] = v.d_img_send[me]
+    ex = Exchange(BATCH, OWNERS, lambda o: v.d_img_send.at[o], lambda s: v.d_img_recv.at[s])
+    ex.start()
+
+    def unite_grad(c):
+        for p in range(5):
+            width = 256 if p < 4 else 128
+            value = dot(v.joined_t[c], v.cat_u[:, p * 256 : p * 256 + width])
+            v.w_u[rows_at(2 * p * MERGED + c, 512), :] = value[:, :128].astype(BF)
+            if p < 4:
+                v.w_u[rows_at((2 * p + 1) * MERGED + c, 512), :] = value[:, 128:].astype(BF)
+
+    loop(SPLITS, unite_grad)
+    s_u.start()
+    ex.wait()
+    d_b = v.d_img_recv[0].astype(F32)
+    for k in range(1, OWNERS):
+        d_b = d_b + v.d_img_recv[k].astype(F32)
+    unit_b = (v.all_b[me].astype(F32) - mean_b) * scale_b
+    d_b = d_b * slope(gamma_b * unit_b + beta_b)
+    sync = Sync(v.sync_b3)
+    sync.start(
+        [total(d_b * group_mask(g)) for g in range(4)]
+        + [total(d_b * unit_b * group_mask(g)) for g in range(4)]
+    )
+    spread_taps(v.d_f2, v.pre_a, norm_a, 15, sums[2:3], sums[3:4])
+    for p in range(5):
+        for at in range(0, CELLS, 96):
+            value = back_tap(2 * p, 1, at)
+            if p < 4:
+                value = value + pltpu.roll(back_tap(2 * p + 1, 1, at), 64, 1)
+            v.cat_a[at : at + 96, p * 128 : p * 128 + 128] = value.astype(BF)
+    sums = sync.wait()
+    first_b = jnp.zeros((BINS, 128), F32)
+    second_b = jnp.zeros((BINS, 128), F32)
+    for group in range(4):
+        kept = group_mask(group)
+        gain_grads[10 + group] = (sums[4 + group : 5 + group], sums[group : group + 1])
+        first_b = first_b + kept * sums[group : group + 1]
+        second_b = second_b + kept * sums[4 + group : 5 + group]
+    inner = d_b - (first_b + unit_b * second_b) * count_b
+    v.d_bp[t] = (gamma_b * scale_b * inner).astype(BF)
+    spread_d = Spread(v.d_bp)
+    spread_d.start()
+
+    def aux_grad(c2):
+        value2 = dot_tn(v.whole[c2], v.cat_a[...])
+        for half in range(2):
+            value = value2[half * 128 : half * 128 + 128]
+            c = 2 * c2 + half
+            for p in range(5):
+                low = value[:64, p * 128 : p * 128 + 128]
+                top = value[64:, p * 128 : p * 128 + 128]
+                even = jnp.where(left_half, low, pltpu.roll(top, 64, 1))
+                v.w_a[rows_at(2 * p * 8 + c, 64), :] = even.astype(BF)
+                if p < 4:
+                    odd = jnp.where(left_half, pltpu.roll(low, 64, 1), top)
+                    v.w_a[rows_at((2 * p + 1) * 8 + c, 64), :] = odd.astype(BF)
+
+    spread_d.wait()
+    d_bp = jnp.concatenate([v.d_bp[k] for k in range(SPLITS)], axis=1)
+    d_pooled = jnp.zeros((BINS, 512), F32)
+    d_groups = []
+    for group in range(4):
+        d_groups.append((d_bp.astype(F32) * group_mask(group)).astype(BF))
+        d_pooled = d_pooled + dot_nt(d_groups[group], v.w_b[group * 512 : group * 512 + 512, :])
+    for group in range(4):
+        v.w_b[group * 512 : group * 512 + 512, :] = dot_tn(v.pooled[...], d_groups[group]).astype(BF)
+    s_b.start()
+    d_pooled = (d_pooled / cells_in).astype(BF)
+    v.d_sum[...] = dot_tn(v.pool[...], d_pooled)
+    dm_near(0, t).wait_recv()
+    dm_far.wait_recv()
+
+    def through_sum(k, carry):
+        at = rows_at(k, 48)
+        value = v.d_sum[at, :] + v.joined[t, at, :].astype(F32) + v.dm_near[0, at, :].astype(F32)
+        value = (value + v.dm_far[at, :].astype(F32)) * slope(summed(at))
+        v.d_sum[at, :] = value
+        return (
+            carry[0] + fold(value),
+            carry[1] + fold(value * normed(v.pre_e, at, norm_e)),
+            carry[2] + fold(value * normed(v.pre_s, at, norm_s)),
+        )
+
+    zero = jnp.zeros((8, 512), F32)
+    three = [total(item) for item in lax.fori_loop(0, 12, through_sum, (zero, zero, zero))]
+    sync = Sync(v.sync_b4)
+    sync.start(split_rows(three[0]) + split_rows(three[1]) + split_rows(three[2]))
+    loop(SPLITS, aux_grad)
+    s_a.start()
+    sums = sync.wait()
+    first_s = join_rows(sums, 0, 4)
+    second_e, second_s = join_rows(sums, 4, 4), join_rows(sums, 8, 4)
+    for k in range(4):
+        gain_grads[6 + k] = (sums[4 + k : 5 + k], sums[k : k + 1])
+        gain_grads[1 + k] = (sums[8 + k : 9 + k], sums[k : k + 1])
+
+    def back_both(k):
+        at = rows_at(k, 48)
+        value, mask = v.d_sum[at, :], wide(v.ins[at, :], 4)
+        v.d_e[at, :] = back_norm(
+            value, normed(v.pre_e, at, norm_e), mask, norm_e, gamma(6, 4), first_s, second_e, count4
+        ).astype(BF)
+        v.d_s[at, :] = back_norm(
+            value, normed(v.pre_s, at, norm_s), mask, norm_s, gamma(1, 4), first_s, second_s, count4
+        ).astype(BF)
+
+    loop(12, back_both)
+
+    def back_hidden(grad, weight, index):
+        value = dot_nt(grad, weight)
+        for k in range(SPLITS):
+            v.dh_send[k] = value[:, k * 128 : k * 128 + 128].astype(BF)
+        v.dh_recv[index, t] = v.dh_send[t]
+        ex = Exchange(
+            TENSOR, SPLITS, lambda o: v.dh_send.at[o], lambda s: v.dh_recv.at[index, s]
+        )
+        ex.start()
+        return ex
+
+    def hidden_sum(index):
+        def step(k):
+            at = rows_at(k, 96)
+            value = v.dh_recv[index, 0, at, :].astype(F32)
+            for slot in range(1, SPLITS):
+                value = value + v.dh_recv[index, slot, at, :].astype(F32)
+            v.d_f[at, :] = value
+
+        loop(6, step)
+
+    ex = back_hidden(v.d_e[...], v.w_e[...], 0)
+    s_u.middle(1)
+    for k in range(SPLITS):
+        v.w_e[k * 128 : k * 128 + 128, :] = dot_tn(v.h2[k], v.d_e[...]).astype(BF)
+    s_e.start()
+    ex.wait()
+    hidden_sum(0)
+    sync = Sync(v.sync_b5)
+    sync.start(through_silu(v.d_f, v.pre_m, norm_m, 5))
+    s_u.middle(2)
+    sums = sync.wait()
+    gain_grads[5] = (sums[1:2], sums[0:1])
+    spread_taps(v.d_f, v.pre_m, norm_m, 5, sums[0:1], sums[1:2])
+    fill(v.cat_u, 4)
+    weight = jnp.concatenate([v.w_m[tap * 512 : tap * 512 + 512, :] for tap in range(9)], axis=1)
+    ex = back_hidden(v.cat_u[...], weight, 1)
+
+    def short_grad(c):
+        v.w_s[rows_at(c, 256), :] = dot_tn(v.whole[c], v.d_s[...]).astype(BF)
+
+    loop(SPLITS, short_grad)
+    s_s.start()
+    s_u.middle(3)
+    ex.wait()
+    hidden_sum(1)
+    sync = Sync(v.sync_b6)
+    sync.start(through_silu(v.d_f, v.pre_r, norm_r, 0))
+
+    def middle_grad(k):
+        value = dot_tn(v.h1[k], v.cat_u[...])
+        for tap in range(9):
+            v.w_m[rows_at(tap * 4 + k, 128), :] = value[:, tap * 128 : tap * 128 + 128].astype(BF)
+
+    loop(SPLITS, middle_grad)
+    s_m.start()
+    s_u.middle(0)
+    sums = sync.wait()
+    gain_grads[0] = (sums[1:2], sums[0:1])
+
+    def back_reduce(k):
+        at = rows_at(k, 96)
+        v.d_low[at, :] = back_norm(
+            v.d_f[at, :], normed(v.pre_r, at, norm_r), v.ins[at, :], norm_r, gamma(0), sums[0:1], sums[1:2], count
+        ).astype(BF)
+
+    loop(6, back_reduce)
+
+    def reduce_grad(c):
+        v.w_r[rows_at(c, 256), :] = dot_tn(v.whole[c], v.d_low[...]).astype(BF)
+
+    loop(SPLITS, reduce_grad)
+    s_r.start()
+    rest = (s_c, s_ac, s_b, s_a, s_e, s_s, s_m, s_r)
+    for item in rest:
+        item.middle()
+    squares = s_u.end()
+    for item in rest:
+        squares = squares + item.end()
+    dm_near(1, t_diag).wait_send()
+    dm_near(0, t_core).wait_send()
+    dm_far.wait_send()
+
+    for row in range(16):
+        o_gain[row : row + 1, :] = gain_grads[row][0]
+        o_gain[16 + row : 17 + row, :] = gain_grads[row][1]
+    gain_square = o_gain[...] * o_gain[...]
+    squares = squares + total(gain_square) / OWNERS
+
+    sync = Sync(v.sync_end)
+    sync.start([squares, o_misc[1:2, :]])
+    v.end_t[t] = sync.wait()
+    spread_e = Spread(v.end_t)
+    spread_e.start()
+    spread_e.wait()
+    ends = v.end_t[0]
+    for k in range(1, SPLITS):
+        ends = ends + v.end_t[k]
+    o_misc[...] = ends
+    o_misc[2:3, :] = jnp.broadcast_to(loss_weight, (1, 128))
+
+
+def whole_step(sizes, labels, feat, gains, pieces):
+    plan = scratch_plan()
+    vmem = pl.BlockSpec(memory_space=pltpu.VMEM)
+    anywhere = pl.BlockSpec(memory_space=pl.ANY)
+    outs = [(128, 128), (128, 512), (576, 128), (64, 512), (256, 512), (4608, 128), (576, 128)]
+    outs = outs + [(16, 256), (8, 256), (32, 128), (8, 128)]
+    return pl.pallas_call(
+        functools.partial(step_kernel, tuple(plan)),
+        out_shape=[jax.ShapeDtypeStruct(shape, F32) for shape in outs],
+        in_specs=[pl.BlockSpec(memory_space=pltpu.SMEM), vmem, anywhere, anywhere]
+        + [anywhere] * len(pieces),
+        out_specs=[vmem] * len(outs),
+        scratch_shapes=[pltpu.VMEM(shape, kind) for shape, kind in plan.values()]
+        + [pltpu.SemaphoreType.DMA((SEMAPHORES,))],
+        compiler_params=pltpu.CompilerParams(
+            collective_id=0, has_side_effects=True, vmem_limit_bytes=63 * 1024 * 1024
+        ),
+        name="whole_step",
+    )(sizes, labels, feat, gains, *pieces)
+
+
+def update_kernel(scale, grad, param, first, second, average, o_param, o_first, o_second, o_average):
+    clipped = grad[...] * scale[0]
+    new_first = 0.5 * first[...] + 0.5 * clipped
+    new_second = 0.5 * second[...] + 0.5 * clipped * clipped
+    keep = 1.0 - 0.5**STEP
+    old = param[...]
+    new = old - 0.01 * (new_first / keep / (jnp.sqrt(new_second / keep) + 1e-08) + 0.01 * old)
+    o_param[...] = new
+    o_first[...] = new_first
+    o_second[...] = new_second
+    o_average[...] = 0.999 * average[...] + 0.001 * new
+
+
+def update(scale, grad, param, first, second, average):
+    rows = grad.shape[0]
+    block = pl.BlockSpec((512, 128), lambda i: (i, 0))
+    return pl.pallas_call(
+        update_kernel,
+        grid=(pl.cdiv(rows, 512),),
+        out_shape=[jax.ShapeDtypeStruct((rows, 128), jnp.float32)] * 4,
+        in_specs=[pl.BlockSpec(memory_space=pltpu.SMEM)] + [block] * 5,
+        out_specs=[block] * 4,
+        name="update",
+    )(scale.reshape(1), grad, param, first, second, average)
+
+def fits(splits, owners):
+    return splits == SPLITS and owners == OWNERS
+
+
+def local_fast(features, labels, valid, sizes, params, first_moment, squared_mean, average):
+    me = lax.axis_index("batch")
+    shapes = segment_shapes(SPLITS)
+    counts = []
+    for shape in shapes:
+        count = 1
+        for extent in shape:
+            count = count * extent
+        counts.append(count // OWNERS)
+    starts = [0]
+    for count in counts:
+        starts.append(starts[-1] + count)
+    flat = params.reshape(-1, 128)
+    low = flat.astype(BF)
+    tail = flat[starts[6] // 128 :].reshape(-1)
+    cut = [tail[starts[k] - starts[6] : starts[k + 1] - starts[6]] for k in range(6, 10)]
+    rows = [low[starts[k] // 128 : starts[k + 1] // 128] for k in range(6)]
+    aux = cut[1].astype(BF).reshape(9, 2, 64, 64)
+    pieces = [
+        rows[0],
+        rows[1].reshape(128, 512),
+        rows[2],
+        rows[3].reshape(64, 512),
+        rows[4].reshape(256, 512),
+        rows[5],
+        jnp.concatenate([aux[:, 0], aux[:, 1]], axis=-1).reshape(576, 128),
+        jnp.pad(cut[0].astype(BF).reshape(16, NCLS), ((0, 0), (0, 256 - NCLS))),
+        jnp.pad(
+            cut[2].astype(BF).astype(F32).reshape(8, NCLS), ((0, 0), (0, 256 - NCLS))
+        ),
+    ]
+    width = shapes[9][1]
+    share = counts[9]
+    per_row = width // share
+    spot = jnp.zeros((2, 2048), F32)
+    spot = lax.dynamic_update_slice(
+        spot,
+        cut[3].astype(BF).astype(F32).reshape(1, share),
+        (me // per_row, (me % per_row) * share),
+    )
+    marked = jnp.where(valid > 0, labels, -1).astype(F32).reshape(CELLS, 1)
+    outs = whole_step(
+        sizes,
+        jnp.broadcast_to(marked, (CELLS, 128)),
+        features.reshape(CELLS, -1),
+        spot.reshape(32, 128),
+        pieces,
+    )
+    gain_grad = lax.dynamic_slice(
+        outs[9].reshape(2, 2048)[:, :width].reshape(-1), (me * share,), (share,)
+    )
+    aux_grad = outs[6].reshape(9, 64, 2, 64).transpose(0, 2, 1, 3)
+    grad_share = jnp.concatenate(
+        [outs[k].reshape(-1, 128) for k in range(6)]
+        + [
+            jnp.concatenate(
+                [
+                    outs[7][:, :NCLS].reshape(-1),
+                    aux_grad.reshape(-1),
+                    outs[8][:, :NCLS].reshape(-1),
+                    gain_grad,
+                ]
+            ).reshape(-1, 128)
+        ]
+    )
+    misc = outs[10]
+    grad_norm = jnp.sqrt(jnp.sum(misc[0]))
+    scale = jnp.minimum(1.0, 0.05 / (grad_norm + 1e-06))
+    new_params, new_first, new_second, new_average = [
+        item.reshape(params.shape)
+        for item in update(
+            scale,
+            grad_share,
+            flat,
+            first_moment.reshape(-1, 128),
+            squared_mean.reshape(-1, 128),
+            average.reshape(-1, 128),
+        )
+    ]
+    return (
+        new_params,
+        new_first,
+        new_second,
+        new_average,
+        new_params.astype(BF),
+        grad_norm,
+        jnp.sum(misc[1]),
+        misc[2, 0],
+        outs[9][30],
+    )
+
+
 def solution(mesh):
+    chosen = local_fast if fits(mesh.shape["tensor"], mesh.shape["batch"]) else local
     return jax.shard_map(
-        local,
+        chosen,
         mesh=mesh,
         in_specs=(
             P("batch", None, None, "tensor"),

time: 2360 us -> 619 us (0.26)
  waiting for transfers between devices: 1520 us -> 0 us
  Pallas kernels: 0 us -> 557 us
  blocking collectives: 284 us -> 0 us
  matrix products: 207 us -> 0 us
  local copies, waits for them, and re-layouts: 183 us -> 37.9 us
  other arithmetic: 128 us -> 19.3 us
    unnamed x16 -> x0, waiting for transfers between devices: 934 us -> none
    all_gather x3 -> x0, waiting for transfers between devices: 575 us -> none  [the longest x1 575 us: local(): lax.all_gather(params.astype(jnp.bfloat16), 'batch', axis=0, tiled=True)]
    pallas_call x0 -> x2, Pallas kernels: none -> 557 us  [the longest x1 538 us: whole_step(): pl.pallas_call(functools.partial(step_kernel, tuple(plan)), out_shape=[ja...]
    psum x11 -> x0, blocking collectives: 238 us -> none  [the longest x5 101 us: norm_backward(): totals = lax.psum(tuple(sends), 'batch')]
    dot_general x122 -> x0, matrix products: 207 us -> none  [the longest x18 81.5 us: conv_input_back(): product = jnp.dot(grad, kernel[tap].T, preferred_element_type=jnp.float32)]
    unnamed x525 -> x10, local copies, waits for them, and re-layouts: 85.6 us -> 11.8 us
    all_gather x6 -> x0, blocking collectives: 45.9 us -> none  [the longest x2 14.9 us: gather_channels(): return lax.all_gather(field, 'tensor', axis=3, tiled=True)]
    reshape x18 -> x14, local copies, waits for them, and re-layouts: 53.2 us -> 12.7 us  [the longest x3 5.26 us: local_fast(): outs[k].reshape(-1, 128)]
  transfers between devices with their start and end apart: 11 -> 0, of which waited for: 5 -> 0; matrix products, arithmetic and copies ran while one was open for 8% -> 0% of each run, Pallas kernels for 0% -> 0%
where the time goes in v2:
time: 619 us; the launch traced here: 617 us
  Pallas kernels  557 us (90%)
  local copies, waits for them, and re-layouts  37.9 us (6%)
  other arithmetic  19.3 us (3%)
    pallas_call x1, Pallas kernels, whole_step(): pl.pallas_call(functools.partial(step_kernel, tuple(plan)), out_shape=[ja...  538 us
    pallas_call x1, Pallas kernels, update(): pl.pallas_call(update_kernel, grid=(pl.cdiv(rows, 512),), out_shape=[jax....  18.8 us

profile of v2, /device:TPU:0, one launch (start us, length us, event | category | flops | bytes accessed | tf_op | source)
XLA Modules:
  0.0 617.1 jit_solution(1772259094570203095)
XLA Ops:
  0.7 0.7 select_convert_fusion
  1.4 0.1 broadcast_in_dim.15
  1.5 0.9 broadcast_in_dim.16.refs_1_
  2.3 2.3 convert_element_type.47
  4.7 0.6 slice.91.refs_4_
  5.3 0.7 reshape.132.refs_7_
  6.0 0.7 reshape.131.refs_5_
  6.7 0.7 slice.93.refs_6_
  7.4 1.1 slice.96.refs_9_
  8.5 0.9 reshape.133.refs_8_
  9.3 6.0 convert.9
  15.3 0.0 copy-start
  15.3 1.9 copy-done
  17.2 0.1 slice_convert_fusion
  17.3 0.2 dynamic_update_slice.3
  17.6 0.6 reshape.129.refs_3_
  18.2 0.8 slice_reduce_fusion.2
  19.0 0.1 convert_element_type.50
  19.1 0.6 pad_convert_fusion.refs_12_
  19.7 0.7 slice_reduce_fusion.1
  20.4 1.8 slice_reduce_fusion
  22.2 0.1 convert_element_type.49
  22.3 0.6 pad.10.refs_11_
  22.9 0.1 convert_element_type.48
  23.1 0.8 pad_maximum_fusion.refs_10_
  23.9 538.4 %whole_step.1 = (f32[128,128]{1,0:T(8,128)}, f32[128,512]{1,0:T(8,128)}, f32[576,128]{1,0:T(8,128)}, f32[64,512]{1,0:T(8,128)}, f32[256,512]{1,0:T(8,128)}, /*in...) custom-call(s32[1,2]{1,0:T(1,128)} %refs_0_.1, ...), custom_call_target="tpu_custom_call" | custom-call | tf_op jit(solution)/shard_map/whole_step/pallas_call | solution.py:1887
  562.3 1.2 slice.88
  563.5 1.2 slice_bitcast_fusion
  564.7 0.7 reshape.142
  565.4 0.1 reshape.143
  565.5 0.1 dynamic_slice.3
  565.6 1.4 slice_reduce_fusion.3
  567.7 1.4 reshape.141
  569.0 0.8 reshape.138
  569.9 0.0 copy-start.1
  569.9 1.7 reshape.136
  571.6 1.7 reshape.135
  573.3 1.9 reshape.137
  575.1 1.3 reshape.139
  576.5 0.1 copy.25
  576.5 0.1 reshape.140
  576.7 2.4 concatenate.17
  579.1 1.5 constant_dynamic-update-slice_fusion.5
  580.6 1.7 constant_dynamic-update-slice_fusion.4
  582.2 1.7 constant_dynamic-update-slice_fusion.3
  583.9 1.6 constant_dynamic-update-slice_fusion.2
  585.5 1.9 constant_dynamic-update-slice_fusion.1
  587.4 0.0 copy-done.1
  587.4 1.6 constant_dynamic-update-slice_fusion
  588.9 0.7 bitcast_dynamic-update-slice_fusion.grad
  589.7 18.8 %update.1 = (f32[7712,128]{1,0:T(8,128)}, f32[7712,128]{1,0:T(8,128)}, f32[7712,128]{1,0:T(8,128)}, f32[7712,128]{1,0:T(8,128)}) custom-call(f32[1]{0:T(128)} %bitcast.4.scale, f32[7712,128]{1,0:T(8,128)} %bitcast_dynamic-update-slice_fusion.grad, f32[7712,128]{1,0:T(8,128)} %bitcast.30, f32[7712,128]{1,0:T(8,128)} %bitcast.31, f32[7712,128]{1,0:T(8,128)} %bitcast.32, ...), custom_call_target="tpu_custom_call" | custom-call | tf_op jit(solution)/shard_map/update/pallas_call | solution.py:1918
  608.5 7.5 %convert_element_type.51 = bf16[1,987136]{1,0:T(2,128)(2,1)} convert(f32[1,987136]{1,0:T(1,128)} %bitcast.34) | non-fusion elementwise | flops 987136 | bytes 5922816 | tf_op jit(solution)/shard_map/convert_element_type | solution.py:2015
  (5 shorter events, 0.1 us)
Async XLA Ops:
  15.3 1.9 copy-start
  569.9 17.5 %copy-start.1 = (f32[4608,128]{1,0:T(8,128)S(1)}, f32[4608,128]{1,0:T(8,128)}, u32[]{:S(2)}) copy-start(f32[4608,128]{1,0:T(8,128)} %get-tuple-element.30) | copy-start | bytes 7077892

commit v3 on v2

--- a/solution.py
+++ b/solution.py
@@ -692,10 +692,12 @@
                 {BATCH: partner},
             )
 
-        def start(self):
+        def start_far(self):
             self.local().start()
             for step in range(1, HALF):
                 self.far(step).start()
+
+        def start_near(self):
             self.near().start()
 
         def forward(self):
@@ -785,23 +787,31 @@
                 {BATCH: partner},
             )
 
-        def start(self):
+        def start_far(self):
             self.whole().start()
 
             def begin(j):
                 self.local(j).start()
                 for step in range(1, HALF):
                     self.far(step, j).start()
-                self.near(j).start()
 
             each_merged(me, begin)
 
-        def forward(self, step):
-            def go(j):
-                self.passed(step, j, me).wait_recv()
-                self.passed(step, j, me).start()
-
-            each_merged(far_peer(me, step), go)
+        def start_near(self):
+            each_merged(me, lambda j: self.near(j).start())
+
+        def forward(self, low, top):
+            def step_j(k):
+                j = low + k
+                for step in range(1, HALF):
+
+                    def go(step=step):
+                        self.passed(step, j, me).wait_recv()
+                        self.passed(step, j, me).start()
+
+                    pl.when(chunk_of(far_peer(me, step), j) < MERGED)(go)
+
+            loop(top - low, step_j)
 
         def finish(self):
             for step in range(HALF):
@@ -915,7 +925,8 @@
     feat_local = pltpu.make_async_copy(feat, v.whole.at[t], sems.at[feat_keep])
     feat_spread = Exchange(TENSOR, SPLITS, lambda other: feat, lambda slot: v.whole.at[slot])
     for item in (g_gain, g_r, g_s, g_a):
-        item.start()
+        item.start_far()
+        item.start_near()
     feat_local.start()
     feat_spread.start()
 
@@ -979,13 +990,17 @@
     cells_local = jnp.full((1, 128), (high * across).astype(F32))
     left_half = lax.broadcasted_iota(jnp.int32, (64, 128), 1) < 64
 
-    for item in (g_gain, g_r, g_s, g_a):
+    for item in (g_gain, g_r, g_s):
         item.forward()
-    for item in (g_m, g_e, g_b, g_c, g_ac):
-        item.start()
-    g_u.start()
+    for item in (g_m, g_e):
+        item.start_far()
+    g_a.forward()
+    for item in (g_b, g_c, g_ac, g_u):
+        item.start_far()
     for item in (g_gain, g_r, g_s, g_a):
         item.finish()
+    for item in (g_m, g_e, g_b, g_c, g_ac):
+        item.start_near()
     feat_local.wait()
     feat_spread.wait()
     gains = v.gain_in[0]
@@ -1023,6 +1038,7 @@
         v.pad[pair, EDGE : EDGE + CELLS, :] = value[:, :128]
         v.pad[pair + 1, EDGE : EDGE + CELLS, :] = value[:, 128:]
     v.pad[4, EDGE : EDGE + CELLS, :] = dot(whole_feat(), v.w_pair[:, 512:640])
+    g_m.forward()
 
     def offset(tap, spacing):
         return ((tap // 3 - 1) * MAP + (tap % 3 - 1)) * spacing
@@ -1086,8 +1102,8 @@
     sync.start(
         [r1, r2] + split_rows(s1) + split_rows(s2) + [a1, a2, cells_local] + split_rows(class_local)
     )
-    g_m.forward()
     sums = sync.wait()
+    g_u.start_near()
     count = sums[12:13]
     count4 = wide(count, 4)
     norm_r = moments(sums[0:1], sums[1:2], count)
@@ -1129,6 +1145,7 @@
     sync.start(list(masked_sums(v.pre_m)))
     g_e.finish()
     sums = sync.wait()
+    g_b.forward()
     norm_m = moments(sums[0:1], sums[1:2], count)
     spread_2 = Spread(v.h2)
 
@@ -1138,7 +1155,6 @@
 
     loop(6, make_h2)
     spread_2.start()
-    g_b.forward()
     spread_2.wait()
     for k in range(0, 512, 256):
         v.pre_e[:, k : k + 256] = dot(full_h(v.h2), v.w_e[:, k : k + 256])
@@ -1194,6 +1210,7 @@
     v.recv_b[t] = v.part_b[t]
     ex = Exchange(TENSOR, SPLITS, lambda o: v.part_b.at[o], lambda s: v.recv_b.at[s])
     ex.start()
+    g_u.forward(0, 2)
     joined_copy(0, t_x, t_x).wait_recv()
     joined_copy(2, t_x, t_core).start()
     ex.wait()
@@ -1203,7 +1220,7 @@
     v.all_b[me] = own_b.astype(BF)
     ex = Exchange(BATCH, OWNERS, lambda o: v.all_b.at[me], lambda s: v.all_b.at[s])
     ex.start()
-    g_u.forward(1)
+    g_u.forward(2, 4)
     ex.wait()
     all_b = [v.all_b[k].astype(F32) for k in range(OWNERS)]
     sum_b, square_b = all_b[0], all_b[0] * all_b[0]
@@ -1229,7 +1246,7 @@
         out = gamma_b * ((all_b[k] - mean_b) * scale_b) + beta_b
         v.act_b[t, k * BINS : k * BINS + BINS, :] = jax.nn.silu(out).astype(BF)
     spread_b.start()
-    g_u.forward(2)
+    g_u.forward(4, 6)
     spread_b.wait()
     g_u.whole().wait()
     row_512 = lax.broadcasted_iota(jnp.int32, (OWNERS * BINS, 1), 0) & (BINS - 1)
@@ -1261,7 +1278,7 @@
     v.z_recv[me] = v.z_send[me]
     ex = Exchange(BATCH, OWNERS, lambda o: v.z_send.at[o], lambda s: v.z_recv.at[s])
     ex.start()
-    g_u.forward(3)
+    g_u.forward(6, 9)
     joined_copy(1, t_core, t_core).wait_recv()
     joined_copy(2, t_diag, t_core).wait_recv()
     for k in range(SPLITS):
@@ -1757,6 +1774,7 @@
     sync.start(split_rows(three[0]) + split_rows(three[1]) + split_rows(three[2]))
     loop(SPLITS, aux_grad)
     s_a.start()
+    s_u.middle(1)
     sums = sync.wait()
     first_s = join_rows(sums, 0, 4)
     second_e, second_s = join_rows(sums, 4, 4), join_rows(sums, 8, 4)
@@ -1798,7 +1816,9 @@
         loop(6, step)
 
     ex = back_hidden(v.d_e[...], v.w_e[...], 0)
-    s_u.middle(1)
+    s_c.middle()
+    s_ac.middle()
+    s_u.middle(2)
     for k in range(SPLITS):
         v.w_e[k * 128 : k * 128 + 128, :] = dot_tn(v.h2[k], v.d_e[...]).astype(BF)
     s_e.start()
@@ -1806,7 +1826,7 @@
     hidden_sum(0)
     sync = Sync(v.sync_b5)
     sync.start(through_silu(v.d_f, v.pre_m, norm_m, 5))
-    s_u.middle(2)
+    s_u.middle(3)
     sums = sync.wait()
     gain_grads[5] = (sums[1:2], sums[0:1])
     spread_taps(v.d_f, v.pre_m, norm_m, 5, sums[0:1], sums[1:2])
@@ -1819,7 +1839,8 @@
 
     loop(SPLITS, short_grad)
     s_s.start()
-    s_u.middle(3)
+    s_u.middle(0)
+    s_b.middle()
     ex.wait()
     hidden_sum(1)
     sync = Sync(v.sync_b6)
@@ -1832,7 +1853,8 @@
 
     loop(SPLITS, middle_grad)
     s_m.start()
-    s_u.middle(0)
+    s_a.middle()
+    s_e.middle()
     sums = sync.wait()
     gain_grads[0] = (sums[1:2], sums[0:1])
 
@@ -1849,9 +1871,9 @@
 
     loop(SPLITS, reduce_grad)
     s_r.start()
+    for item in (s_s, s_m, s_r):
+        item.middle()
     rest = (s_c, s_ac, s_b, s_a, s_e, s_s, s_m, s_r)
-    for item in rest:
-        item.middle()
     squares = s_u.end()
     for item in rest:
         squares = squares + item.end()

time: 619 us -> 567 us (0.916)
  Pallas kernels: 557 us -> 505 us
    pallas_call x1, Pallas kernels: 538 us -> 487 us  [whole_step(): pl.pallas_call(functools.partial(step_kernel, tuple(plan)), out_shape=[ja...]
where the time goes in v3:
time: 567 us; the launch traced here: 565 us
  Pallas kernels  505 us (89%)
  local copies, waits for them, and re-layouts  37.9 us (7%)
  other arithmetic  19.3 us (3%)
    pallas_call x1, Pallas kernels, whole_step(): pl.pallas_call(functools.partial(step_kernel, tuple(plan)), out_shape=[ja...  487 us
    pallas_call x1, Pallas kernels, update(): pl.pallas_call(update_kernel, grid=(pl.cdiv(rows, 512),), out_shape=[jax....  18.8 us
    unnamed x10, local copies, waits for them, and re-layouts  11.8 us

profile of v3, /device:TPU:0, one launch (start us, length us, event | category | flops | bytes accessed | tf_op | source)
XLA Modules:
  0.0 565.3 jit_solution(14918822516423362886)
XLA Ops:
  0.7 0.7 select_convert_fusion
  1.4 0.1 broadcast_in_dim.15
  1.5 0.9 broadcast_in_dim.16.refs_1_
  2.3 2.3 convert_element_type.47
  4.7 0.6 slice.91.refs_4_
  5.3 0.7 reshape.132.refs_7_
  6.0 0.7 reshape.131.refs_5_
  6.7 0.7 slice.93.refs_6_
  7.4 1.1 slice.96.refs_9_
  8.5 0.9 reshape.133.refs_8_
  9.3 6.0 %convert.9 = bf16[1,987136]{1,0:T(2,128)(2,1)S(1)} convert(f32[1,987136]{1,0:T(1,128)} %param.12) | non-fusion elementwise | flops 987136 | bytes 5922816 | tf_op jit(solution)/shard_map/convert.6
  15.3 0.0 copy-start
  15.3 1.9 copy-done
  17.2 0.1 slice_convert_fusion
  17.3 0.2 dynamic_update_slice.3
  17.6 0.6 reshape.129.refs_3_
  18.2 0.8 slice_reduce_fusion.2
  19.0 0.1 convert_element_type.50
  19.1 0.6 pad_convert_fusion.refs_12_
  19.7 0.7 slice_reduce_fusion.1
  20.4 1.8 slice_reduce_fusion
  22.2 0.1 convert_element_type.49
  22.3 0.6 pad.10.refs_11_
  22.9 0.1 convert_element_type.48
  23.1 0.8 pad_maximum_fusion.refs_10_
  23.9 486.6 %whole_step.1 = (f32[128,128]{1,0:T(8,128)}, f32[128,512]{1,0:T(8,128)}, f32[576,128]{1,0:T(8,128)}, f32[64,512]{1,0:T(8,128)}, f32[256,512]{1,0:T(8,128)}, /*in...) custom-call(s32[1,2]{1,0:T(1,128)} %refs_0_.1, ...), custom_call_target="tpu_custom_call" | custom-call | tf_op jit(solution)/shard_map/whole_step/pallas_call | solution.py:1909
  510.5 1.2 slice.88
  511.7 1.2 slice_bitcast_fusion
  512.9 0.7 reshape.142
  513.6 0.1 reshape.143
  513.7 0.1 dynamic_slice.3
  513.7 1.4 slice_reduce_fusion.3
  515.8 1.4 reshape.141
  517.2 0.8 reshape.138
  518.0 0.0 copy-start.1
  518.0 1.7 reshape.136
  519.8 1.7 reshape.135
  521.4 1.9 reshape.137
  523.3 1.3 reshape.139
  524.6 0.1 copy.25
  524.7 0.1 reshape.140
  524.8 2.4 concatenate.17
  527.3 1.5 constant_dynamic-update-slice_fusion.5
  528.7 1.7 constant_dynamic-update-slice_fusion.4
  530.4 1.7 constant_dynamic-update-slice_fusion.3
  532.1 1.6 constant_dynamic-update-slice_fusion.2
  533.7 1.9 constant_dynamic-update-slice_fusion.1
  535.5 0.0 copy-done.1
  535.5 1.6 constant_dynamic-update-slice_fusion
  537.1 0.7 bitcast_dynamic-update-slice_fusion.grad
  537.8 18.8 %update.1 = (f32[7712,128]{1,0:T(8,128)}, f32[7712,128]{1,0:T(8,128)}, f32[7712,128]{1,0:T(8,128)}, f32[7712,128]{1,0:T(8,128)}) custom-call(f32[1]{0:T(128)} %bitcast.4.scale, f32[7712,128]{1,0:T(8,128)} %bitcast_dynamic-update-slice_fusion.grad, f32[7712,128]{1,0:T(8,128)} %bitcast.30, f32[7712,128]{1,0:T(8,128)} %bitcast.31, f32[7712,128]{1,0:T(8,128)} %bitcast.32, ...), custom_call_target="tpu_custom_call" | custom-call | tf_op jit(solution)/shard_map/update/pallas_call | solution.py:1940
  556.6 7.5 %convert_element_type.51 = bf16[1,987136]{1,0:T(2,128)(2,1)} convert(f32[1,987136]{1,0:T(1,128)} %bitcast.34) | non-fusion elementwise | flops 987136 | bytes 5922816 | tf_op jit(solution)/shard_map/convert_element_type | solution.py:2037
  (5 shorter events, 0.1 us)
Async XLA Ops:
  15.3 1.9 copy-start
  518.0 17.5 %copy-start.1 = (f32[4608,128]{1,0:T(8,128)S(1)}, f32[4608,128]{1,0:T(8,128)}, u32[]{:S(2)}) copy-start(f32[4608,128]{1,0:T(8,128)} %get-tuple-element.30) | copy-start | bytes 7077892

commit v4 on v3

--- a/solution.py
+++ b/solution.py
@@ -1164,6 +1164,7 @@
     g_c.forward()
     g_ac.forward()
     sums = sync.wait()
+    g_u.forward(0, 1)
     norm_e = moments(join_rows(sums, 0, 4), join_rows(sums, 4, 4), count4)
 
     def summed(at):
@@ -1210,7 +1211,7 @@
     v.recv_b[t] = v.part_b[t]
     ex = Exchange(TENSOR, SPLITS, lambda o: v.part_b.at[o], lambda s: v.recv_b.at[s])
     ex.start()
-    g_u.forward(0, 2)
+    g_u.forward(1, 3)
     joined_copy(0, t_x, t_x).wait_recv()
     joined_copy(2, t_x, t_core).start()
     ex.wait()
@@ -1220,7 +1221,7 @@
     v.all_b[me] = own_b.astype(BF)
     ex = Exchange(BATCH, OWNERS, lambda o: v.all_b.at[me], lambda s: v.all_b.at[s])
     ex.start()
-    g_u.forward(2, 4)
+    g_u.forward(3, 5)
     ex.wait()
     all_b = [v.all_b[k].astype(F32) for k in range(OWNERS)]
     sum_b, square_b = all_b[0], all_b[0] * all_b[0]
@@ -1246,7 +1247,7 @@
         out = gamma_b * ((all_b[k] - mean_b) * scale_b) + beta_b
         v.act_b[t, k * BINS : k * BINS + BINS, :] = jax.nn.silu(out).astype(BF)
     spread_b.start()
-    g_u.forward(4, 6)
+    g_u.forward(5, 7)
     spread_b.wait()
     g_u.whole().wait()
     row_512 = lax.broadcasted_iota(jnp.int32, (OWNERS * BINS, 1), 0) & (BINS - 1)
@@ -1278,7 +1279,7 @@
     v.z_recv[me] = v.z_send[me]
     ex = Exchange(BATCH, OWNERS, lambda o: v.z_send.at[o], lambda s: v.z_recv.at[s])
     ex.start()
-    g_u.forward(6, 9)
+    g_u.forward(7, 9)
     joined_copy(1, t_core, t_core).wait_recv()
     joined_copy(2, t_diag, t_core).wait_recv()
     for k in range(SPLITS):
@@ -1438,7 +1439,7 @@
 
         def middle(self):
             kind = self.first.dtype
-            for step in (1, 2, 3, 0):
+            for step in range(1, HALF):
                 self.near(step).wait_recv()
                 base = far_peer(me, step) * (self.rows // self.block)
 
@@ -1446,22 +1447,21 @@
                     at = rows_at(k, self.block)
                     value = self.full[rows_at(base + k, self.block), :].astype(F32)
                     value = value + self.first[step, at, :].astype(F32)
-                    if step:
-                        self.first[step, at, :] = value.astype(kind)
-                    else:
-                        self.out[at, :] = value
+                    self.first[step, at, :] = value.astype(kind)
 
                 loop(self.rows // self.block, add)
-                if step:
-                    self.far(step).start()
+                self.far(step).start()
 
         def end(self):
+            self.near(0).wait_recv()
             for step in range(1, HALF):
                 self.far(step).wait_recv()
+            base = me * (self.rows // self.block)
 
             def add(k, carry):
                 at = rows_at(k, self.block)
-                value = self.out[at, :]
+                value = self.full[rows_at(base + k, self.block), :].astype(F32)
+                value = value + self.first[0, at, :].astype(F32)
                 for step in range(1, HALF):
                     value = value + self.second[step - 1, at, :].astype(F32)
                 self.out[at, :] = value
@@ -1533,26 +1533,26 @@
                     at = rows_at(k, 64)
                     value = v.w_u[rows_at(base + k, 64), :].astype(F32)
                     value = value + v.first_u[step, slot, at, :].astype(F32)
-                    if step:
-                        v.first_u[step, slot, at, :] = value.astype(BF)
-                    else:
-                        o_u[rows_at(j * 8 + k, 64), :] = value
+                    v.first_u[step, slot, at, :] = value.astype(BF)
 
                 loop(8, add)
-                if step:
-                    self.far(step, j, owner).start()
+                self.far(step, j, owner).start()
 
             each_merged(owner, go)
 
         def end(self):
             def go(j):
                 slot = self.slot(me, j)
+                self.near(0, j, me).wait_recv()
                 for step in range(1, HALF):
                     self.far(step, j, me).wait_recv()
+                tap = me + lax.div(me + j, 8)
+                base = (tap * MERGED + chunk_of(me, j)) * 8
 
                 def add(k):
                     at = rows_at(k, 64)
-                    value = o_u[rows_at(j * 8 + k, 64), :]
+                    value = v.w_u[rows_at(base + k, 64), :].astype(F32)
+                    value = value + v.first_u[0, slot, at, :].astype(F32)
                     for step in range(1, HALF):
                         value = value + v.second_u[step - 1, slot, at, :].astype(F32)
                     o_u[rows_at(j * 8 + k, 64), :] = value
@@ -1643,6 +1643,29 @@
     dm_near(1, t_diag).start()
     merged_back(t_core)
     dm_near(0, t_core).start()
+    merged_back(t_x)
+    merged_back(t)
+
+    def unite_grad(c):
+        for p in range(5):
+            width = 256 if p < 4 else 128
+            value = dot(v.joined_t[c], v.cat_u[:, p * 256 : p * 256 + width])
+            v.w_u[rows_at(2 * p * MERGED + c, 512), :] = value[:, :128].astype(BF)
+            if p < 4:
+                v.w_u[rows_at((2 * p + 1) * MERGED + c, 512), :] = value[:, 128:].astype(BF)
+
+    loop(SPLITS, unite_grad)
+    s_u.start()
+    dm_near(1, t_x).wait_recv()
+
+    def add_x(k):
+        at = rows_at(k, 48)
+        value = v.joined[t_x, at, :].astype(F32) + v.dm_near[1, at, :].astype(F32)
+        v.joined[t_x, at, :] = value.astype(BF)
+
+    loop(12, add_x)
+    dm_far = remote(v.joined.at[t_x], v.dm_far, far_s, far_r, {TENSOR: t_x})
+    dm_far.start()
     ex_dz.wait()
 
     d_act = v.d_sum.at[0 : OWNERS * BINS, :]
@@ -1664,50 +1687,6 @@
     v.d_act_recv[t] = v.d_act_send[t]
     ex = Exchange(TENSOR, SPLITS, lambda o: v.d_act_send.at[o], lambda s: v.d_act_recv.at[s])
     ex.start()
-    merged_back(t_x)
-    merged_back(t)
-    dm_near(1, t_x).wait_recv()
-
-    def add_x(k):
-        at = rows_at(k, 48)
-        value = v.joined[t_x, at, :].astype(F32) + v.dm_near[1, at, :].astype(F32)
-        v.joined[t_x, at, :] = value.astype(BF)
-
-    loop(12, add_x)
-    dm_far = remote(v.joined.at[t_x], v.dm_far, far_s, far_r, {TENSOR: t_x})
-    dm_far.start()
-    ex.wait()
-    for k in range(OWNERS):
-        at = slice(k * BINS, k * BINS + BINS)
-        value = v.d_act_recv[0, at, :].astype(F32)
-        for slot in range(1, SPLITS):
-            value = value + v.d_act_recv[slot, at, :].astype(F32)
-        v.d_img_send[k] = value.astype(BF)
-    v.d_img_recv[me] = v.d_img_send[me]
-    ex = Exchange(BATCH, OWNERS, lambda o: v.d_img_send.at[o], lambda s: v.d_img_recv.at[s])
-    ex.start()
-
-    def unite_grad(c):
-        for p in range(5):
-            width = 256 if p < 4 else 128
-            value = dot(v.joined_t[c], v.cat_u[:, p * 256 : p * 256 + width])
-            v.w_u[rows_at(2 * p * MERGED + c, 512), :] = value[:, :128].astype(BF)
-            if p < 4:
-                v.w_u[rows_at((2 * p + 1) * MERGED + c, 512), :] = value[:, 128:].astype(BF)
-
-    loop(SPLITS, unite_grad)
-    s_u.start()
-    ex.wait()
-    d_b = v.d_img_recv[0].astype(F32)
-    for k in range(1, OWNERS):
-        d_b = d_b + v.d_img_recv[k].astype(F32)
-    unit_b = (v.all_b[me].astype(F32) - mean_b) * scale_b
-    d_b = d_b * slope(gamma_b * unit_b + beta_b)
-    sync = Sync(v.sync_b3)
-    sync.start(
-        [total(d_b * group_mask(g)) for g in range(4)]
-        + [total(d_b * unit_b * group_mask(g)) for g in range(4)]
-    )
     spread_taps(v.d_f2, v.pre_a, norm_a, 15, sums[2:3], sums[3:4])
     for p in range(5):
         for at in range(0, CELLS, 96):
@@ -1715,18 +1694,6 @@
             if p < 4:
                 value = value + pltpu.roll(back_tap(2 * p + 1, 1, at), 64, 1)
             v.cat_a[at : at + 96, p * 128 : p * 128 + 128] = value.astype(BF)
-    sums = sync.wait()
-    first_b = jnp.zeros((BINS, 128), F32)
-    second_b = jnp.zeros((BINS, 128), F32)
-    for group in range(4):
-        kept = group_mask(group)
-        gain_grads[10 + group] = (sums[4 + group : 5 + group], sums[group : group + 1])
-        first_b = first_b + kept * sums[group : group + 1]
-        second_b = second_b + kept * sums[4 + group : 5 + group]
-    inner = d_b - (first_b + unit_b * second_b) * count_b
-    v.d_bp[t] = (gamma_b * scale_b * inner).astype(BF)
-    spread_d = Spread(v.d_bp)
-    spread_d.start()
 
     def aux_grad(c2):
         value2 = dot_tn(v.whole[c2], v.cat_a[...])
@@ -1741,6 +1708,45 @@
                 if p < 4:
                     odd = jnp.where(left_half, pltpu.roll(low, 64, 1), top)
                     v.w_a[rows_at((2 * p + 1) * 8 + c, 64), :] = odd.astype(BF)
+
+    loop(SPLITS, aux_grad)
+    s_a.start()
+    ex.wait()
+    for k in range(OWNERS):
+        at = slice(k * BINS, k * BINS + BINS)
+        value = v.d_act_recv[0, at, :].astype(F32)
+        for slot in range(1, SPLITS):
+            value = value + v.d_act_recv[slot, at, :].astype(F32)
+        v.d_img_send[k] = value.astype(BF)
+    v.d_img_recv[me] = v.d_img_send[me]
+    ex = Exchange(BATCH, OWNERS, lambda o: v.d_img_send.at[o], lambda s: v.d_img_recv.at[s])
+    ex.start()
+
+    s_u.middle(1)
+    ex.wait()
+    d_b = v.d_img_recv[0].astype(F32)
+    for k in range(1, OWNERS):
+        d_b = d_b + v.d_img_recv[k].astype(F32)
+    unit_b = (v.all_b[me].astype(F32) - mean_b) * scale_b
+    d_b = d_b * slope(gamma_b * unit_b + beta_b)
+    sync = Sync(v.sync_b3)
+    sync.start(
+        [total(d_b * group_mask(g)) for g in range(4)]
+        + [total(d_b * unit_b * group_mask(g)) for g in range(4)]
+    )
+    s_u.middle(2)
+    sums = sync.wait()
+    first_b = jnp.zeros((BINS, 128), F32)
+    second_b = jnp.zeros((BINS, 128), F32)
+    for group in range(4):
+        kept = group_mask(group)
+        gain_grads[10 + group] = (sums[4 + group : 5 + group], sums[group : group + 1])
+        first_b = first_b + kept * sums[group : group + 1]
+        second_b = second_b + kept * sums[4 + group : 5 + group]
+    inner = d_b - (first_b + unit_b * second_b) * count_b
+    v.d_bp[t] = (gamma_b * scale_b * inner).astype(BF)
+    spread_d = Spread(v.d_bp)
+    spread_d.start()
 
     spread_d.wait()
     d_bp = jnp.concatenate([v.d_bp[k] for k in range(SPLITS)], axis=1)
@@ -1772,9 +1778,7 @@
     three = [total(item) for item in lax.fori_loop(0, 12, through_sum, (zero, zero, zero))]
     sync = Sync(v.sync_b4)
     sync.start(split_rows(three[0]) + split_rows(three[1]) + split_rows(three[2]))
-    loop(SPLITS, aux_grad)
-    s_a.start()
-    s_u.middle(1)
+    s_u.middle(3)
     sums = sync.wait()
     first_s = join_rows(sums, 0, 4)
     second_e, second_s = join_rows(sums, 4, 4), join_rows(sums, 8, 4)
@@ -1818,7 +1822,7 @@
     ex = back_hidden(v.d_e[...], v.w_e[...], 0)
     s_c.middle()
     s_ac.middle()
-    s_u.middle(2)
+    s_a.middle()
     for k in range(SPLITS):
         v.w_e[k * 128 : k * 128 + 128, :] = dot_tn(v.h2[k], v.d_e[...]).astype(BF)
     s_e.start()
@@ -1826,7 +1830,7 @@
     hidden_sum(0)
     sync = Sync(v.sync_b5)
     sync.start(through_silu(v.d_f, v.pre_m, norm_m, 5))
-    s_u.middle(3)
+    s_b.middle()
     sums = sync.wait()
     gain_grads[5] = (sums[1:2], sums[0:1])
     spread_taps(v.d_f, v.pre_m, norm_m, 5, sums[0:1], sums[1:2])
@@ -1839,8 +1843,7 @@
 
     loop(SPLITS, short_grad)
     s_s.start()
-    s_u.middle(0)
-    s_b.middle()
+    s_e.middle()
     ex.wait()
     hidden_sum(1)
     sync = Sync(v.sync_b6)
@@ -1853,8 +1856,7 @@
 
     loop(SPLITS, middle_grad)
     s_m.start()
-    s_a.middle()
-    s_e.middle()
+    s_s.middle()
     sums = sync.wait()
     gain_grads[0] = (sums[1:2], sums[0:1])
 
@@ -1871,7 +1873,7 @@
 
     loop(SPLITS, reduce_grad)
     s_r.start()
-    for item in (s_s, s_m, s_r):
+    for item in (s_m, s_r):
         item.middle()
     rest = (s_c, s_ac, s_b, s_a, s_e, s_s, s_m, s_r)
     squares = s_u.end()
@@ -1964,7 +1966,7 @@
         starts.append(starts[-1] + count)
     flat = params.reshape(-1, 128)
     low = flat.astype(BF)
-    tail = flat[starts[6] // 128 :].reshape(-1)
+    tail = lax.optimization_barrier(flat[starts[6] // 128 :]).reshape(-1)
     cut = [tail[starts[k] - starts[6] : starts[k + 1] - starts[6]] for k in range(6, 10)]
     rows = [low[starts[k] // 128 : starts[k + 1] // 128] for k in range(6)]
     aux = cut[1].astype(BF).reshape(9, 2, 64, 64)

time: 567 us -> 532 us (0.938)
  Pallas kernels: 505 us -> 480 us
  other arithmetic: 19.3 us -> 13.4 us
    pallas_call x1, Pallas kernels: 487 us -> 461 us  [whole_step(): pl.pallas_call(functools.partial(step_kernel, tuple(plan)), out_shape=[ja...]
    another operation x1, other arithmetic: 5.97 us -> 0.02 us
    unnamed x10 -> x8, local copies, waits for them, and re-layouts: 11.8 us -> 9.83 us
where the time goes in v4:
time: 532 us; the launch traced here: 530 us
  Pallas kernels  480 us (90%)
  local copies, waits for them, and re-layouts  33.8 us (6%)
  other arithmetic  13.4 us (3%)
    pallas_call x1, Pallas kernels, whole_step(): pl.pallas_call(functools.partial(step_kernel, tuple(plan)), out_shape=[ja...  461 us
    pallas_call x1, Pallas kernels, update(): pl.pallas_call(update_kernel, grid=(pl.cdiv(rows, 512),), out_shape=[jax....  18.8 us

profile of v4, /device:TPU:0, one launch (start us, length us, event | category | flops | bytes accessed | tf_op | source)
XLA Modules:
  0.0 530.2 jit_solution(8549237960624183421)
XLA Ops:
  0.7 0.7 select_convert_fusion
  1.4 0.1 broadcast_in_dim.15
  1.5 0.9 broadcast_in_dim.16.refs_1_
  2.3 1.0 slice.67
  3.4 0.1 slice_convert_fusion
  3.4 0.2 dynamic_update_slice.3
  3.7 0.6 reshape.134.refs_3_
  4.3 0.1 slice.99
  4.4 0.1 convert_element_type.45
  4.5 0.6 pad_convert_fusion.refs_12_
  5.1 0.1 slice.95
  5.2 0.1 convert_element_type.44
  5.3 0.6 pad.10.refs_11_
  5.9 0.1 convert_element_type.43
  6.1 0.8 pad_maximum_fusion.refs_10_
  6.9 2.3 convert_element_type.42
  9.2 0.6 slice.89.refs_4_
  9.8 0.7 reshape.137.refs_7_
  10.5 0.7 reshape.136.refs_5_
  11.2 0.7 slice.91.refs_6_
  11.9 1.1 slice.94.refs_9_
  13.0 0.9 reshape.138.refs_8_
  13.9 461.5 %whole_step.1 = (f32[128,128]{1,0:T(8,128)}, f32[128,512]{1,0:T(8,128)}, f32[576,128]{1,0:T(8,128)}, f32[64,512]{1,0:T(8,128)}, f32[256,512]{1,0:T(8,128)}, /*in...) custom-call(s32[1,2]{1,0:T(1,128)} %refs_0_.1, ...), custom_call_target="tpu_custom_call" | custom-call | tf_op jit(solution)/shard_map/whole_step/pallas_call | solution.py:1911
  475.3 1.2 slice.86
  476.5 1.2 slice_bitcast_fusion
  477.7 0.7 reshape.147
  478.4 0.1 reshape.148
  478.5 0.1 dynamic_slice.3
  478.6 1.4 slice_reduce_fusion
  480.7 1.4 reshape.146
  482.1 0.8 reshape.143
  482.9 0.0 copy-start
  482.9 1.7 reshape.141
  484.6 1.7 reshape.140
  486.3 1.9 reshape.142
  488.1 1.3 reshape.144
  489.5 0.1 copy.19
  489.5 0.1 reshape.145
  489.7 2.4 concatenate.17
  492.1 1.5 constant_dynamic-update-slice_fusion.5
  493.6 1.7 constant_dynamic-update-slice_fusion.4
  495.3 1.7 constant_dynamic-update-slice_fusion.3
  496.9 1.6 constant_dynamic-update-slice_fusion.2
  498.5 1.9 constant_dynamic-update-slice_fusion.1
  500.4 0.0 copy-done
  500.4 1.6 constant_dynamic-update-slice_fusion
  501.9 0.7 bitcast_dynamic-update-slice_fusion.grad
  502.7 18.8 %update.1 = (f32[7712,128]{1,0:T(8,128)}, f32[7712,128]{1,0:T(8,128)}, f32[7712,128]{1,0:T(8,128)}, f32[7712,128]{1,0:T(8,128)}) custom-call(f32[1]{0:T(128)} %bitcast.7.scale, f32[7712,128]{1,0:T(8,128)} %bitcast_dynamic-update-slice_fusion.grad, f32[7712,128]{1,0:T(8,128)} %bitcast.30, f32[7712,128]{1,0:T(8,128)} %bitcast.31, f32[7712,128]{1,0:T(8,128)} %bitcast.32, ...), custom_call_target="tpu_custom_call" | custom-call | tf_op jit(solution)/shard_map/update/pallas_call | solution.py:1942
  521.5 7.5 %convert_element_type.46 = bf16[1,987136]{1,0:T(2,128)(2,1)} convert(f32[1,987136]{1,0:T(1,128)} %bitcast.34) | non-fusion elementwise | flops 987136 | bytes 5922816 | tf_op jit(solution)/shard_map/convert_element_type | solution.py:2039
  (7 shorter events, 0.1 us)
Async XLA Ops:
  482.9 17.5 %copy-start = (f32[4608,128]{1,0:T(8,128)S(1)}, f32[4608,128]{1,0:T(8,128)}, u32[]{:S(2)}) copy-start(f32[4608,128]{1,0:T(8,128)} %get-tuple-element.30) | copy-start | bytes 7077892

commit v5 on v4

--- a/solution.py
+++ b/solution.py
@@ -608,12 +608,13 @@
 def step_kernel(names, *refs):
     (
         sizes, lab_in, feat, gain_own, p_r, p_s, p_m, p_e, p_b, p_u, p_a, p_c, p_ac,
-        o_r, o_s, o_m, o_e, o_b, o_u, o_a, o_c, o_ac, o_gain, o_misc,
-    ) = refs[:24]
+        o_flat, o_a, o_c, o_ac, o_gain, o_misc,
+    ) = refs[:19]
     v = Refs()
-    for name, ref in zip(names, refs[24:]):
+    for name, ref in zip(names, refs[19:]):
         setattr(v, name, ref)
     sems = refs[-1]
+    o_u = o_flat.at[2496:7104, :]
     me = lax.axis_index(BATCH)
     t = lax.axis_index(TENSOR)
     partner = me + 1 - 2 * lax.rem(me, 2)
@@ -655,15 +656,19 @@
     pl.semaphore_wait(barrier, OWNERS + SPLITS - 2)
 
     class Gather:
-        def __init__(self, piece, full, rows):
+        def __init__(self, piece, full, rows, skip=0, step=None):
             self.piece, self.full, self.rows = piece, full, rows
+            self.skip, self.part = skip, step or rows
+            if step:
+                self.piece = piece.at[skip : skip + step, :]
             self.near_s, self.far_s, self.pass_s = take(1), take(HALF), take(HALF)
             self.recv, self.keep = take(OWNERS), take(1)
 
         def at(self, owner):
             if self.rows is None:
                 return self.full.at[owner]
-            return self.full.at[rows_at(owner, self.rows), :]
+            start = pl.multiple_of(owner * self.rows + self.skip, self.part)
+            return self.full.at[pl.ds(start, self.part), :]
 
         def local(self):
             return pltpu.make_async_copy(self.piece, self.at(me), sems.at[self.keep])
@@ -723,117 +728,121 @@
     g_a = Gather(p_a, v.w_a, 576)
     g_m = Gather(p_m, v.w_m, 576)
     g_e = Gather(p_e, v.w_e, 64)
-    g_b = Gather(p_b, v.w_b, 256)
+    g_b0 = Gather(p_b, v.w_b, 256, 0, 128)
+    g_b1 = Gather(p_b, v.w_b, 256, 128, 128)
     g_c = Gather(p_c, v.w_c, 16)
     g_ac = Gather(p_ac, v.w_ac, 8)
 
-    def chunk_of(owner, j):
-        return lax.rem(owner + j, 8)
-
-    def merged_rows(owner, j):
-        tap = owner + lax.div(owner + j, 8)
-        return pl.ds(pl.multiple_of((tap * MERGED + chunk_of(owner, j)) * 512, 512), 512)
-
-    def each_merged(owner, body):
-        def step(j):
-            pl.when(chunk_of(owner, j) < MERGED)(lambda: body(j))
-
-        loop(9, step)
+    def block_of(owner, slot):
+        return 8 if slot == SLOTS - 1 else lax.rem(slot - owner + 8, 8)
+
+    def merged_rows(owner, slot):
+        block = owner * 9 + block_of(owner, slot)
+        index = lax.div(block, 8) * MERGED + lax.rem(block, 8)
+        return pl.ds(pl.multiple_of(index * 512, 512), 512)
+
+    def has(owner, slot, body):
+        if slot == SLOTS - 1:
+            pl.when(owner < MERGED)(body)
+        else:
+            body()
 
     class GatherUnite:
         def __init__(self):
-            self.near_s, self.far_s, self.pass_s = take(9), take(9 * HALF), take(9 * HALF)
-            self.recv, self.keep, self.keep_all = take(9 * OWNERS), take(9), take(1)
-
-        def source(self, j):
-            return p_u.at[rows_at(j, 512), :]
-
-        def full(self, owner, j):
-            return v.w_u.at[merged_rows(owner, j), :]
-
-        def local(self, j):
+            self.near_s, self.far_s, self.pass_s = (
+                take(SLOTS),
+                take(SLOTS * HALF),
+                take(SLOTS * HALF),
+            )
+            self.recv, self.keep, self.keep_all = take(SLOTS * OWNERS), take(SLOTS), take(1)
+
+        def source(self, slot):
+            return p_u.at[rows_at(block_of(me, slot), 512), :]
+
+        def full(self, owner, slot):
+            return v.w_u.at[merged_rows(owner, slot), :]
+
+        def local(self, slot):
             return pltpu.make_async_copy(
-                self.source(j), self.full(me, j), sems.at[self.keep + j]
+                self.source(slot), self.full(me, slot), sems.at[self.keep + slot]
             )
 
         def whole(self):
             return pltpu.make_async_copy(p_u, v.w_own, sems.at[self.keep_all])
 
-        def near(self, j):
+        def near(self, slot):
             return remote(
-                self.source(j),
-                self.full(me, j),
-                self.near_s + j,
-                self.recv + me * 9 + j,
+                self.source(slot),
+                self.full(me, slot),
+                self.near_s + slot,
+                self.recv + me * SLOTS + slot,
                 {BATCH: partner},
             )
 
-        def far(self, step, j):
+        def far(self, step, slot):
             return remote(
-                self.source(j),
-                self.full(me, j),
-                self.far_s + step * 9 + j,
-                self.recv + me * 9 + j,
+                self.source(slot),
+                self.full(me, slot),
+                self.far_s + step * SLOTS + slot,
+                self.recv + me * SLOTS + slot,
                 {BATCH: far_peer(me, step)},
             )
 
-        def passed(self, step, j, base):
+        def passed(self, step, slot, base):
             source = far_peer(base, step)
             return remote(
-                self.full(source, j),
-                self.full(source, j),
-                self.pass_s + step * 9 + j,
-                self.recv + source * 9 + j,
+                self.full(source, slot),
+                self.full(source, slot),
+                self.pass_s + step * SLOTS + slot,
+                self.recv + source * SLOTS + slot,
                 {BATCH: partner},
             )
 
-        def start_far(self):
-            self.whole().start()
-
-            def begin(j):
-                self.local(j).start()
+        def start_far(self, slot):
+            def go():
+                self.local(slot).start()
                 for step in range(1, HALF):
-                    self.far(step, j).start()
-
-            each_merged(me, begin)
-
-        def start_near(self):
-            each_merged(me, lambda j: self.near(j).start())
-
-        def forward(self, low, top):
-            def step_j(k):
-                j = low + k
+                    self.far(step, slot).start()
+
+            has(me, slot, go)
+
+        def start_near(self, slot):
+            has(me, slot, lambda: self.near(slot).start())
+
+        def forward(self, slot):
+            for step in range(1, HALF):
+
+                def go(step=step):
+                    self.passed(step, slot, me).wait_recv()
+                    self.passed(step, slot, me).start()
+
+                has(far_peer(me, step), slot, go)
+
+        def finish(self):
+            for slot in range(SLOTS):
+                for step in range(HALF):
+                    has(
+                        far_peer(partner, step),
+                        slot,
+                        lambda step=step, slot=slot: self.passed(step, slot, partner).wait_recv(),
+                    )
+
+                def end(slot=slot):
+                    self.local(slot).wait()
+                    self.near(slot).wait_send()
+                    for step in range(1, HALF):
+                        self.far(step, slot).wait_send()
+
+                has(me, slot, end)
+
+        def drain(self):
+            for slot in range(SLOTS):
                 for step in range(1, HALF):
-
-                    def go(step=step):
-                        self.passed(step, j, me).wait_recv()
-                        self.passed(step, j, me).start()
-
-                    pl.when(chunk_of(far_peer(me, step), j) < MERGED)(go)
-
-            loop(top - low, step_j)
-
-        def finish(self):
-            for step in range(HALF):
-                each_merged(
-                    far_peer(partner, step),
-                    lambda j, step=step: self.passed(step, j, partner).wait_recv(),
-                )
-
-            def end(j):
-                self.local(j).wait()
-                self.near(j).wait_send()
-                for step in range(1, HALF):
-                    self.far(step, j).wait_send()
-
-            each_merged(me, end)
-
-        def drain(self):
-            for step in range(1, HALF):
-                each_merged(
-                    far_peer(me, step),
-                    lambda j, step=step: self.passed(step, j, me).wait_send(),
-                )
+                    has(
+                        far_peer(me, step),
+                        slot,
+                        lambda step=step, slot=slot: self.passed(step, slot, me).wait_send(),
+                    )
 
     g_u = GatherUnite()
 
@@ -992,15 +1001,12 @@
 
     for item in (g_gain, g_r, g_s):
         item.forward()
+    g_a.forward()
     for item in (g_m, g_e):
         item.start_far()
-    g_a.forward()
-    for item in (g_b, g_c, g_ac, g_u):
-        item.start_far()
+    g_u.whole().start()
     for item in (g_gain, g_r, g_s, g_a):
         item.finish()
-    for item in (g_m, g_e, g_b, g_c, g_ac):
-        item.start_near()
     feat_local.wait()
     feat_spread.wait()
     gains = v.gain_in[0]
@@ -1038,7 +1044,6 @@
         v.pad[pair, EDGE : EDGE + CELLS, :] = value[:, :128]
         v.pad[pair + 1, EDGE : EDGE + CELLS, :] = value[:, 128:]
     v.pad[4, EDGE : EDGE + CELLS, :] = dot(whole_feat(), v.w_pair[:, 512:640])
-    g_m.forward()
 
     def offset(tap, spacing):
         return ((tap // 3 - 1) * MAP + (tap % 3 - 1)) * spacing
@@ -1102,8 +1107,10 @@
     sync.start(
         [r1, r2] + split_rows(s1) + split_rows(s2) + [a1, a2, cells_local] + split_rows(class_local)
     )
+    for item in (g_m, g_e):
+        item.start_near()
+    g_b0.start_far()
     sums = sync.wait()
-    g_u.start_near()
     count = sums[12:13]
     count4 = wide(count, 4)
     norm_r = moments(sums[0:1], sums[1:2], count)
@@ -1122,6 +1129,7 @@
 
     loop(6, make_h1)
     spread_1.start()
+    g_m.forward()
 
     def make_a(k):
         at = rows_at(k, 96)
@@ -1143,9 +1151,10 @@
         v.pre_m[at : at + BLOCK, :] = shift_sum(range(9), 4, at, lambda tap: tap)
     sync = Sync(v.sync_two)
     sync.start(list(masked_sums(v.pre_m)))
+    g_b1.start_far()
+    g_b0.start_near()
     g_e.finish()
     sums = sync.wait()
-    g_b.forward()
     norm_m = moments(sums[0:1], sums[1:2], count)
     spread_2 = Spread(v.h2)
 
@@ -1155,16 +1164,19 @@
 
     loop(6, make_h2)
     spread_2.start()
+    g_u.start_far(0)
+    g_b0.forward()
+    g_b1.start_near()
     spread_2.wait()
     for k in range(0, 512, 256):
         v.pre_e[:, k : k + 256] = dot(full_h(v.h2), v.w_e[:, k : k + 256])
     sync = Sync(v.sync_three)
     e1, e2 = masked_sums(v.pre_e)
     sync.start(split_rows(e1) + split_rows(e2))
-    g_c.forward()
-    g_ac.forward()
+    g_u.start_far(1)
+    g_b1.forward()
+    g_u.start_near(0)
     sums = sync.wait()
-    g_u.forward(0, 1)
     norm_e = moments(join_rows(sums, 0, 4), join_rows(sums, 4, 4), count4)
 
     def summed(at):
@@ -1201,7 +1213,8 @@
     cells_in = wide(v.cells_in[...], 4)
     pooled = dot(v.pool[...], v.joined[t]) / cells_in
     v.pooled[...] = pooled.astype(BF)
-    g_b.finish()
+    g_b0.finish()
+    g_b1.finish()
     part = jnp.zeros((BINS, 512), F32)
     for group in range(4):
         rows = (v.pooled[...].astype(F32) * group_mask(group)).astype(BF)
@@ -1211,7 +1224,9 @@
     v.recv_b[t] = v.part_b[t]
     ex = Exchange(TENSOR, SPLITS, lambda o: v.part_b.at[o], lambda s: v.recv_b.at[s])
     ex.start()
-    g_u.forward(1, 3)
+    g_u.start_far(2)
+    g_u.forward(0)
+    g_u.start_near(1)
     joined_copy(0, t_x, t_x).wait_recv()
     joined_copy(2, t_x, t_core).start()
     ex.wait()
@@ -1221,7 +1236,9 @@
     v.all_b[me] = own_b.astype(BF)
     ex = Exchange(BATCH, OWNERS, lambda o: v.all_b.at[me], lambda s: v.all_b.at[s])
     ex.start()
-    g_u.forward(3, 5)
+    g_u.start_far(3)
+    g_u.forward(1)
+    g_u.start_near(2)
     ex.wait()
     all_b = [v.all_b[k].astype(F32) for k in range(OWNERS)]
     sum_b, square_b = all_b[0], all_b[0] * all_b[0]
@@ -1247,7 +1264,12 @@
         out = gamma_b * ((all_b[k] - mean_b) * scale_b) + beta_b
         v.act_b[t, k * BINS : k * BINS + BINS, :] = jax.nn.silu(out).astype(BF)
     spread_b.start()
-    g_u.forward(5, 7)
+    g_u.start_far(4)
+    for item in (g_c, g_ac):
+        item.start_far()
+        item.start_near()
+    g_u.forward(2)
+    g_u.start_near(3)
     spread_b.wait()
     g_u.whole().wait()
     row_512 = lax.broadcasted_iota(jnp.int32, (OWNERS * BINS, 1), 0) & (BINS - 1)
@@ -1261,7 +1283,7 @@
     v.zsum[...] = jnp.zeros((2, OWNERS * BINS, 128), F32)
 
     def own_branch(j, body):
-        chunk = chunk_of(me, j)
+        chunk = lax.rem(me + j, 8)
         pl.when(chunk >= MERGED)(lambda: body(chunk - MERGED, lax.div(me + j, 8)))
 
     def make_z(j):
@@ -1279,7 +1301,11 @@
     v.z_recv[me] = v.z_send[me]
     ex = Exchange(BATCH, OWNERS, lambda o: v.z_send.at[o], lambda s: v.z_recv.at[s])
     ex.start()
-    g_u.forward(7, 9)
+    g_u.start_near(4)
+    g_u.forward(3)
+    g_u.forward(4)
+    g_c.forward()
+    g_ac.forward()
     joined_copy(1, t_core, t_core).wait_recv()
     joined_copy(2, t_diag, t_core).wait_recv()
     for k in range(SPLITS):
@@ -1322,7 +1348,7 @@
     sync.start(list(masked_sums(v.pre_u)))
     for item in (g_c, g_ac):
         item.finish()
-    for item in (g_gain, g_r, g_s, g_a, g_m, g_e, g_b, g_c, g_ac, g_u):
+    for item in (g_gain, g_r, g_s, g_a, g_m, g_e, g_b0, g_b1, g_c, g_ac, g_u):
         item.drain()
     joined_copy(0, t, t_x).wait_send()
     joined_copy(1, t, t_core).wait_send()
@@ -1407,8 +1433,8 @@
     )
 
     class Scatter:
-        def __init__(self, first, second, full, rows, out):
-            self.full, self.rows, self.out = full, rows, out
+        def __init__(self, first, second, full, rows, out, base=0):
+            self.full, self.rows, self.out, self.base = full, rows, out, base
             self.first, self.second = first, second
             self.near_s, self.near_r = take(HALF), take(HALF)
             self.far_s, self.far_r = take(HALF), take(HALF)
@@ -1464,11 +1490,18 @@
                 value = value + self.first[0, at, :].astype(F32)
                 for step in range(1, HALF):
                     value = value + self.second[step - 1, at, :].astype(F32)
-                self.out[at, :] = value
+                if self.out is o_flat:
+                    times = value.shape[1] // 128
+                    start = self.base + k * self.block * times
+                    for q in range(times):
+                        where = pl.ds(start + q, self.block, stride=times if times > 1 else None)
+                        self.out[where, :] = value[:, q * 128 : q * 128 + 128]
+                else:
+                    self.out[at, :] = value
                 return carry + fold(value * value)
 
             squares = lax.fori_loop(
-                0, self.rows // self.block, add, jnp.zeros((8, self.out.shape[1]), F32)
+                0, self.rows // self.block, add, jnp.zeros((8, self.full.shape[1]), F32)
             )
             for step in (1, 2, 3, 0):
                 self.near(step).wait_send()
@@ -1479,97 +1512,99 @@
     s_c = Scatter(v.first_c, v.second_c, v.w_c, 16, o_c)
     s_ac = Scatter(v.first_ac, v.second_ac, v.w_ac, 8, o_ac)
     s_a = Scatter(v.first_a, v.second_a, v.w_a, 576, o_a)
-    s_b = Scatter(v.first_b, v.second_b, v.w_b, 256, o_b)
-    s_s = Scatter(v.first_s, v.second_s, v.w_s, 128, o_s)
-    s_e = Scatter(v.first_e, v.second_e, v.w_e, 64, o_e)
-    s_m = Scatter(v.first_m, v.second_m, v.w_m, 576, o_m)
-    s_r = Scatter(v.first_r, v.second_r, v.w_r, 128, o_r)
+    s_b = Scatter(v.first_b, v.second_b, v.w_b, 256, o_flat, 1472)
+    s_s = Scatter(v.first_s, v.second_s, v.w_s, 128, o_flat, 128)
+    s_e = Scatter(v.first_e, v.second_e, v.w_e, 64, o_flat, 1216)
+    s_m = Scatter(v.first_m, v.second_m, v.w_m, 576, o_flat, 640)
+    s_r = Scatter(v.first_r, v.second_r, v.w_r, 128, o_flat, 0)
 
     class ScatterUnite:
         def __init__(self):
-            self.near_s, self.near_r = take(9 * HALF), take(9 * HALF)
-            self.far_s, self.far_r = take(9 * HALF), take(9 * HALF)
-
-        def slot(self, owner, j):
-            return jnp.where(j == 8, SLOTS - 1, chunk_of(owner, j))
-
-        def near(self, step, j, base):
+            self.near_s, self.near_r = take(SLOTS * HALF), take(SLOTS * HALF)
+            self.far_s, self.far_r = take(SLOTS * HALF), take(SLOTS * HALF)
+
+        def near(self, step, slot, base):
             dest = far_peer(base, step)
             return remote(
-                v.w_u.at[merged_rows(dest, j), :],
-                v.first_u.at[step, self.slot(dest, j)],
-                self.near_s + step * 9 + j,
-                self.near_r + step * 9 + j,
+                v.w_u.at[merged_rows(dest, slot), :],
+                v.first_u.at[step, slot],
+                self.near_s + step * SLOTS + slot,
+                self.near_r + step * SLOTS + slot,
                 {BATCH: partner},
             )
 
-        def far(self, step, j, owner):
-            at = self.slot(owner, j)
+        def far(self, step, slot):
             return remote(
-                v.first_u.at[step, at],
-                v.second_u.at[step - 1, at],
-                self.far_s + step * 9 + j,
-                self.far_r + step * 9 + j,
+                v.first_u.at[step, slot],
+                v.second_u.at[step - 1, slot],
+                self.far_s + step * SLOTS + slot,
+                self.far_r + step * SLOTS + slot,
                 {BATCH: far_peer(me, step)},
             )
 
-        def start(self):
+        def own_rows(self, owner, slot, k):
+            block = owner * 9 + block_of(owner, slot)
+            index = lax.div(block, 8) * MERGED + lax.rem(block, 8)
+            return rows_at(index * 8 + k, 64)
+
+        def start(self, slot):
             for step in (1, 2, 3, 0):
-                each_merged(
+                has(
                     far_peer(partner, step),
-                    lambda j, step=step: self.near(step, j, partner).start(),
+                    slot,
+                    lambda step=step: self.near(step, slot, partner).start(),
                 )
 
-        def middle(self, step):
-            owner = far_peer(me, step)
-
-            def go(j):
-                self.near(step, j, me).wait_recv()
-                slot = self.slot(owner, j)
-                tap = owner + lax.div(owner + j, 8)
-                base = (tap * MERGED + chunk_of(owner, j)) * 8
-
-                def add(k):
-                    at = rows_at(k, 64)
-                    value = v.w_u[rows_at(base + k, 64), :].astype(F32)
-                    value = value + v.first_u[step, slot, at, :].astype(F32)
-                    v.first_u[step, slot, at, :] = value.astype(BF)
-
-                loop(8, add)
-                self.far(step, j, owner).start()
-
-            each_merged(owner, go)
+        def middle(self, slot):
+            for step in range(1, HALF):
+                owner = far_peer(me, step)
+
+                def go(step=step, owner=owner):
+                    self.near(step, slot, me).wait_recv()
+
+                    def add(k):
+                        at = rows_at(k, 64)
+                        value = v.w_u[self.own_rows(owner, slot, k), :].astype(F32)
+                        value = value + v.first_u[step, slot, at, :].astype(F32)
+                        v.first_u[step, slot, at, :] = value.astype(BF)
+
+                    loop(8, add)
+                    self.far(step, slot).start()
+
+                has(owner, slot, go)
 
         def end(self):
-            def go(j):
-                slot = self.slot(me, j)
-                self.near(0, j, me).wait_recv()
-                for step in range(1, HALF):
-                    self.far(step, j, me).wait_recv()
-                tap = me + lax.div(me + j, 8)
-                base = (tap * MERGED + chunk_of(me, j)) * 8
-
-                def add(k):
-                    at = rows_at(k, 64)
-                    value = v.w_u[rows_at(base + k, 64), :].astype(F32)
-                    value = value + v.first_u[0, slot, at, :].astype(F32)
+            for slot in range(SLOTS):
+
+                def go(slot=slot):
+                    self.near(0, slot, me).wait_recv()
                     for step in range(1, HALF):
-                        value = value + v.second_u[step - 1, slot, at, :].astype(F32)
-                    o_u[rows_at(j * 8 + k, 64), :] = value
-
-                loop(8, add)
-
-            each_merged(me, go)
-            for step in (1, 2, 3, 0):
-                each_merged(
-                    far_peer(partner, step),
-                    lambda j, step=step: self.near(step, j, partner).wait_send(),
-                )
-                if step:
-                    each_merged(
-                        far_peer(me, step),
-                        lambda j, step=step: self.far(step, j, far_peer(me, step)).wait_send(),
+                        self.far(step, slot).wait_recv()
+                    j = block_of(me, slot)
+
+                    def add(k):
+                        at = rows_at(k, 64)
+                        value = v.w_u[self.own_rows(me, slot, k), :].astype(F32)
+                        value = value + v.first_u[0, slot, at, :].astype(F32)
+                        for step in range(1, HALF):
+                            value = value + v.second_u[step - 1, slot, at, :].astype(F32)
+                        o_u[rows_at(j * 8 + k, 64), :] = value
+
+                    loop(8, add)
+
+                has(me, slot, go)
+                for step in (1, 2, 3, 0):
+                    has(
+                        far_peer(partner, step),
+                        slot,
+                        lambda step=step, slot=slot: self.near(step, slot, partner).wait_send(),
                     )
+                    if step:
+                        has(
+                            far_peer(me, step),
+                            slot,
+                            lambda step=step, slot=slot: self.far(step, slot).wait_send(),
+                        )
 
             def square(k, carry):
                 value = o_u[rows_at(k, 64), :]
@@ -1643,6 +1678,27 @@
     dm_near(1, t_diag).start()
     merged_back(t_core)
     dm_near(0, t_core).start()
+    ex_dz.wait()
+
+    d_act = v.d_sum.at[0 : OWNERS * BINS, :]
+    d_act[...] = jnp.zeros((OWNERS * BINS, 512), F32)
+
+    def branch_back(j):
+        def body(group, side):
+            kept = jnp.where(group_id == group, 1.0, 0.0)
+            value = v.dz_recv[:, side].reshape(OWNERS * BINS, 128).astype(F32) * kept
+            value = value.astype(BF)
+            o_u[rows_at(j, 512), :] = dot_tn(full_act(), value)
+            d_act[...] = d_act[...] + dot_nt(value, v.w_own[rows_at(j, 512), :])
+
+        own_branch(j, body)
+
+    loop(9, branch_back)
+    for k in range(SPLITS):
+        v.d_act_send[k] = d_act[:, k * 128 : k * 128 + 128].astype(BF)
+    v.d_act_recv[t] = v.d_act_send[t]
+    ex = Exchange(TENSOR, SPLITS, lambda o: v.d_act_send.at[o], lambda s: v.d_act_recv.at[s])
+    ex.start()
     merged_back(t_x)
     merged_back(t)
 
@@ -1655,7 +1711,7 @@
                 v.w_u[rows_at((2 * p + 1) * MERGED + c, 512), :] = value[:, 128:].astype(BF)
 
     loop(SPLITS, unite_grad)
-    s_u.start()
+    s_u.start(0)
     dm_near(1, t_x).wait_recv()
 
     def add_x(k):
@@ -1665,28 +1721,19 @@
 
     loop(12, add_x)
     dm_far = remote(v.joined.at[t_x], v.dm_far, far_s, far_r, {TENSOR: t_x})
+    ex.wait()
+    for k in range(OWNERS):
+        at = slice(k * BINS, k * BINS + BINS)
+        value = v.d_act_recv[0, at, :].astype(F32)
+        for slot in range(1, SPLITS):
+            value = value + v.d_act_recv[slot, at, :].astype(F32)
+        v.d_img_send[k] = value.astype(BF)
+    v.d_img_recv[me] = v.d_img_send[me]
+    ex = Exchange(BATCH, OWNERS, lambda o: v.d_img_send.at[o], lambda s: v.d_img_recv.at[s])
+    ex.start()
     dm_far.start()
-    ex_dz.wait()
-
-    d_act = v.d_sum.at[0 : OWNERS * BINS, :]
-    d_act[...] = jnp.zeros((OWNERS * BINS, 512), F32)
-
-    def branch_back(j):
-        def body(group, side):
-            kept = jnp.where(group_id == group, 1.0, 0.0)
-            value = v.dz_recv[:, side].reshape(OWNERS * BINS, 128).astype(F32) * kept
-            value = value.astype(BF)
-            o_u[rows_at(j, 512), :] = dot_tn(full_act(), value)
-            d_act[...] = d_act[...] + dot_nt(value, v.w_own[rows_at(j, 512), :])
-
-        own_branch(j, body)
-
-    loop(9, branch_back)
-    for k in range(SPLITS):
-        v.d_act_send[k] = d_act[:, k * 128 : k * 128 + 128].astype(BF)
-    v.d_act_recv[t] = v.d_act_send[t]
-    ex = Exchange(TENSOR, SPLITS, lambda o: v.d_act_send.at[o], lambda s: v.d_act_recv.at[s])
-    ex.start()
+    s_u.start(1)
+
     spread_taps(v.d_f2, v.pre_a, norm_a, 15, sums[2:3], sums[3:4])
     for p in range(5):
         for at in range(0, CELLS, 96):
@@ -1710,19 +1757,7 @@
                     v.w_a[rows_at((2 * p + 1) * 8 + c, 64), :] = odd.astype(BF)
 
     loop(SPLITS, aux_grad)
-    s_a.start()
-    ex.wait()
-    for k in range(OWNERS):
-        at = slice(k * BINS, k * BINS + BINS)
-        value = v.d_act_recv[0, at, :].astype(F32)
-        for slot in range(1, SPLITS):
-            value = value + v.d_act_recv[slot, at, :].astype(F32)
-        v.d_img_send[k] = value.astype(BF)
-    v.d_img_recv[me] = v.d_img_send[me]
-    ex = Exchange(BATCH, OWNERS, lambda o: v.d_img_send.at[o], lambda s: v.d_img_recv.at[s])
-    ex.start()
-
-    s_u.middle(1)
+    s_u.middle(0)
     ex.wait()
     d_b = v.d_img_recv[0].astype(F32)
     for k in range(1, OWNERS):
@@ -1734,7 +1769,8 @@
         [total(d_b * group_mask(g)) for g in range(4)]
         + [total(d_b * unit_b * group_mask(g)) for g in range(4)]
     )
-    s_u.middle(2)
+    s_u.start(2)
+    s_a.start()
     sums = sync.wait()
     first_b = jnp.zeros((BINS, 128), F32)
     second_b = jnp.zeros((BINS, 128), F32)
@@ -1747,7 +1783,8 @@
     v.d_bp[t] = (gamma_b * scale_b * inner).astype(BF)
     spread_d = Spread(v.d_bp)
     spread_d.start()
-
+    s_u.start(3)
+    s_u.middle(1)
     spread_d.wait()
     d_bp = jnp.concatenate([v.d_bp[k] for k in range(SPLITS)], axis=1)
     d_pooled = jnp.zeros((BINS, 512), F32)
@@ -1757,7 +1794,6 @@
         d_pooled = d_pooled + dot_nt(d_groups[group], v.w_b[group * 512 : group * 512 + 512, :])
     for group in range(4):
         v.w_b[group * 512 : group * 512 + 512, :] = dot_tn(v.pooled[...], d_groups[group]).astype(BF)
-    s_b.start()
     d_pooled = (d_pooled / cells_in).astype(BF)
     v.d_sum[...] = dot_tn(v.pool[...], d_pooled)
     dm_near(0, t).wait_recv()
@@ -1778,7 +1814,8 @@
     three = [total(item) for item in lax.fori_loop(0, 12, through_sum, (zero, zero, zero))]
     sync = Sync(v.sync_b4)
     sync.start(split_rows(three[0]) + split_rows(three[1]) + split_rows(three[2]))
-    s_u.middle(3)
+    s_u.start(4)
+    s_u.middle(2)
     sums = sync.wait()
     first_s = join_rows(sums, 0, 4)
     second_e, second_s = join_rows(sums, 4, 4), join_rows(sums, 8, 4)
@@ -1820,17 +1857,19 @@
         loop(6, step)
 
     ex = back_hidden(v.d_e[...], v.w_e[...], 0)
-    s_c.middle()
-    s_ac.middle()
-    s_a.middle()
+    s_b.start()
+    s_u.middle(3)
     for k in range(SPLITS):
         v.w_e[k * 128 : k * 128 + 128, :] = dot_tn(v.h2[k], v.d_e[...]).astype(BF)
-    s_e.start()
     ex.wait()
     hidden_sum(0)
     sync = Sync(v.sync_b5)
     sync.start(through_silu(v.d_f, v.pre_m, norm_m, 5))
-    s_b.middle()
+    s_e.start()
+    s_c.middle()
+    s_ac.middle()
+    s_a.middle()
+    s_u.middle(4)
     sums = sync.wait()
     gain_grads[5] = (sums[1:2], sums[0:1])
     spread_taps(v.d_f, v.pre_m, norm_m, 5, sums[0:1], sums[1:2])
@@ -1843,7 +1882,7 @@
 
     loop(SPLITS, short_grad)
     s_s.start()
-    s_e.middle()
+    s_b.middle()
     ex.wait()
     hidden_sum(1)
     sync = Sync(v.sync_b6)
@@ -1856,6 +1895,7 @@
 
     loop(SPLITS, middle_grad)
     s_m.start()
+    s_e.middle()
     s_s.middle()
     sums = sync.wait()
     gain_grads[0] = (sums[1:2], sums[0:1])
@@ -1906,8 +1946,7 @@
     plan = scratch_plan()
     vmem = pl.BlockSpec(memory_space=pltpu.VMEM)
     anywhere = pl.BlockSpec(memory_space=pl.ANY)
-    outs = [(128, 128), (128, 512), (576, 128), (64, 512), (256, 512), (4608, 128), (576, 128)]
-    outs = outs + [(16, 256), (8, 256), (32, 128), (8, 128)]
+    outs = [(7712, 128), (576, 128), (16, 256), (8, 256), (32, 128), (8, 128)]
     return pl.pallas_call(
         functools.partial(step_kernel, tuple(plan)),
         out_shape=[jax.ShapeDtypeStruct(shape, F32) for shape in outs],
@@ -2001,23 +2040,19 @@
         pieces,
     )
     gain_grad = lax.dynamic_slice(
-        outs[9].reshape(2, 2048)[:, :width].reshape(-1), (me * share,), (share,)
-    )
-    aux_grad = outs[6].reshape(9, 64, 2, 64).transpose(0, 2, 1, 3)
-    grad_share = jnp.concatenate(
-        [outs[k].reshape(-1, 128) for k in range(6)]
-        + [
-            jnp.concatenate(
-                [
-                    outs[7][:, :NCLS].reshape(-1),
-                    aux_grad.reshape(-1),
-                    outs[8][:, :NCLS].reshape(-1),
-                    gain_grad,
-                ]
-            ).reshape(-1, 128)
+        outs[4].reshape(2, 2048)[:, :width].reshape(-1), (me * share,), (share,)
+    )
+    aux_grad = outs[1].reshape(9, 64, 2, 64).transpose(0, 2, 1, 3)
+    tail_grad = jnp.concatenate(
+        [
+            outs[2][:, :NCLS].reshape(-1),
+            aux_grad.reshape(-1),
+            outs[3][:, :NCLS].reshape(-1),
+            gain_grad,
         ]
-    )
-    misc = outs[10]
+    ).reshape(-1, 128)
+    grad_share = lax.dynamic_update_slice(outs[0], tail_grad, (starts[6] // 128, 0))
+    misc = outs[5]
     grad_norm = jnp.sqrt(jnp.sum(misc[0]))
     scale = jnp.minimum(1.0, 0.05 / (grad_norm + 1e-06))
     new_params, new_first, new_second, new_average = [
@@ -2040,7 +2075,7 @@
         grad_norm,
         jnp.sum(misc[1]),
         misc[2, 0],
-        outs[9][30],
+        outs[4][30],
     )
 
 

time: 532 us -> 440 us (0.83)
  Pallas kernels: 480 us -> 405 us
  local copies, waits for them, and re-layouts: 33.8 us -> 17.4 us
    pallas_call x1, Pallas kernels: 461 us -> 386 us  [whole_step(): pl.pallas_call(functools.partial(step_kernel, tuple(plan)), out_shape=[ja...]
    unnamed x8 -> x0, local copies, waits for them, and re-layouts: 9.83 us -> none
    reshape x9 -> x6, local copies, waits for them, and re-layouts: 9.62 us -> 3.77 us  [the longest x2 1.37 us: local_fast(): aux_grad = outs[1].reshape(9, 64, 2, 64).transpose(0, 2, 1, 3)]
where the time goes in v5:
time: 440 us; the launch traced here: 439 us
  Pallas kernels  405 us (92%)
  local copies, waits for them, and re-layouts  17.4 us (4%)
  other arithmetic  13.4 us (3%)
    pallas_call x1, Pallas kernels, whole_step(): pl.pallas_call(functools.partial(step_kernel, tuple(plan)), out_shape=[ja...  386 us
    pallas_call x1, Pallas kernels, update(): pl.pallas_call(update_kernel, grid=(pl.cdiv(rows, 512),), out_shape=[jax....  18.8 us

profile of v5, /device:TPU:0, one launch (start us, length us, event | category | flops | bytes accessed | tf_op | source)
XLA Modules:
  0.0 438.7 jit_solution(9799325189443092864)
XLA Ops:
  0.7 0.7 select_convert_fusion
  1.4 0.1 broadcast_in_dim.15
  1.5 0.9 broadcast_in_dim.16.refs_1_
  2.3 1.0 slice.67
  3.4 0.1 slice_convert_fusion
  3.4 0.2 dynamic_update_slice.6
  3.7 0.6 reshape.125.refs_3_
  4.3 0.1 slice.99
  4.4 0.1 convert_element_type.45
  4.4 0.6 pad_convert_fusion.refs_12_
  5.1 0.1 slice.95
  5.2 0.1 convert_element_type.44
  5.3 0.6 pad.10.refs_11_
  5.9 0.1 convert_element_type.43
  6.1 0.8 pad_maximum_fusion.refs_10_
  6.9 2.3 convert_element_type.42
  9.2 0.6 slice.89.refs_4_
  9.8 0.7 reshape.128.refs_7_
  10.5 0.7 reshape.127.refs_5_
  11.2 0.7 slice.91.refs_6_
  11.9 1.1 slice.94.refs_9_
  13.0 0.9 reshape.129.refs_8_
  13.8 386.4 %whole_step.1 = (f32[7712,128]{1,0:T(8,128)}, f32[576,128]{1,0:T(8,128)}, f32[16,256]{1,0:T(8,128)}, f32[8,256]{1,0:T(8,128)}, f32[32,128]{1,0:T(8,128)}, /*index=5*/f32[8,128]{1,0:T(8,128)}) custom-call(s32[1,2]{1,0:T(1,128)} %refs_0_.1, f32[576,128]{1,0:T(8,128)} %broadcast_in_dim.16.refs_1_, bf16[576,256]{1,0:T(8,128)(2,1)} %bitcast.40, ...), custom_call_target="tpu_custom_call" | custom-call | tf_op jit(solution)/shard_map/whole_step/pallas_call | solution.py:1950
  400.2 1.2 slice.86
  401.4 0.8 reshape.131
  402.2 1.2 slice_bitcast_fusion
  403.4 0.7 reshape.135
  404.2 0.1 reshape.136
  404.2 0.1 dynamic_slice.3
  404.3 1.4 slice_reduce_fusion
  406.4 0.8 reshape.134
  407.2 1.3 reshape.132
  408.5 0.1 copy.19
  408.6 0.1 reshape.133
  408.7 1.7 concatenate.14
  410.5 0.7 bitcast_dynamic-update-slice_fusion.grad
  411.2 18.8 %update.1 = (f32[7712,128]{1,0:T(8,128)}, f32[7712,128]{1,0:T(8,128)}, f32[7712,128]{1,0:T(8,128)}, f32[7712,128]{1,0:T(8,128)}) custom-call(f32[1]{0:T(128)} %bitcast.7.scale, f32[7712,128]{1,0:T(8,128)} %bitcast_dynamic-update-slice_fusion.grad, f32[7712,128]{1,0:T(8,128)} %bitcast.30, f32[7712,128]{1,0:T(8,128)} %bitcast.31, f32[7712,128]{1,0:T(8,128)} %bitcast.32, ...), custom_call_target="tpu_custom_call" | custom-call | tf_op jit(solution)/shard_map/update/pallas_call | solution.py:1981
  430.0 7.5 %convert_element_type.46 = bf16[1,987136]{1,0:T(2,128)(2,1)} convert(f32[1,987136]{1,0:T(1,128)} %bitcast.34) | non-fusion elementwise | flops 987136 | bytes 5922816 | tf_op jit(solution)/shard_map/convert_element_type | solution.py:2074
  (7 shorter events, 0.1 us)

commit v6 on v5

--- a/solution.py
+++ b/solution.py
@@ -509,6 +509,9 @@
         joined=((SPLITS, CELLS, 512), BF),
         joined_t=((SPLITS, 512, CELLS), BF),
         pooled=((BINS, 512), BF),
+        pool_half=((2, BINS, 256), BF),
+        pool_all=((OWNERS, BINS, 256), BF),
+        d_bp_all=((OWNERS, SPLITS, BINS, 128), BF),
         part_b=((SPLITS, BINS, 128), BF),
         recv_b=((SPLITS, BINS, 128), BF),
         all_b=((OWNERS, BINS, 128), BF),
@@ -551,13 +554,12 @@
     return plan
 
 
-SYNCS = dict(one=16, two=8, three=8, five=8, b1=8, b3=8, b4=16, b5=8, b6=8, end=8)
+SYNCS = dict(one=8, two=8, three=16, five=8, aux=8, b1=8, b3=8, b4=16, b5=8, b6=8, end=8)
 PARTS = dict(
     r=(128, 128, BF),
     s=(128, 512, BF),
     m=(576, 128, BF),
     e=(64, 512, BF),
-    b=(256, 512, BF),
     a=(576, 128, BF),
     c=(16, 256, BF),
     ac=(8, 256, F32),
@@ -644,6 +646,8 @@
 
     late = []
 
+    v.pool_all[...] = jnp.zeros((OWNERS, BINS, 256), BF)
+    v.d_bp_all[...] = jnp.zeros((OWNERS, SPLITS, BINS, 128), BF)
     barrier = pltpu.get_barrier_semaphore()
     for k in range(1, OWNERS):
         pl.semaphore_signal(
@@ -878,6 +882,37 @@
                 value = value + self.buf[slot]
             return value
 
+    class ToGroup:
+        def __init__(self, part, into):
+            self.part, self.into = part, into
+            self.send, self.recv = take(OWNERS), take(OWNERS)
+
+        def each(self, k, owner, slot, act):
+            for rows, fits_ in ((16, owner < 6), (BINS, owner >= 6)):
+
+                def go(rows=rows):
+                    act(
+                        remote(
+                            self.part(owner, rows),
+                            self.into(slot, rows),
+                            self.send + k,
+                            self.recv + slot,
+                            {BATCH: lax.rem(me + k, OWNERS)},
+                        )
+                    )
+
+                pl.when(fits_)(go)
+
+        def start(self):
+            for k in range(1, OWNERS):
+                self.each(k, lax.rem(me + k, OWNERS), me, lambda c: c.start())
+
+        def wait(self):
+            for k in range(1, OWNERS):
+                self.each(k, me, lax.rem(me + k, OWNERS), lambda c: c.wait_recv())
+            for k in range(1, OWNERS):
+                self.each(k, lax.rem(me + k, OWNERS), me, lambda c: c.wait_send())
+
     class Spread:
 
         def __init__(self, buf):
@@ -933,11 +968,14 @@
     feat_keep = take(1)
     feat_local = pltpu.make_async_copy(feat, v.whole.at[t], sems.at[feat_keep])
     feat_spread = Exchange(TENSOR, SPLITS, lambda other: feat, lambda slot: v.whole.at[slot])
-    for item in (g_gain, g_r, g_s, g_a):
+    for item in (g_gain, g_r):
         item.start_far()
         item.start_near()
     feat_local.start()
     feat_spread.start()
+    for item in (g_m, g_e):
+        item.start_far()
+        item.start_near()
 
     high, across = sizes[0, 0], sizes[0, 1]
     place = lax.broadcasted_iota(jnp.int32, (CELLS, 128), 0).astype(F32)
@@ -999,13 +1037,9 @@
     cells_local = jnp.full((1, 128), (high * across).astype(F32))
     left_half = lax.broadcasted_iota(jnp.int32, (64, 128), 1) < 64
 
-    for item in (g_gain, g_r, g_s):
+    for item in (g_gain, g_r):
         item.forward()
-    g_a.forward()
-    for item in (g_m, g_e):
-        item.start_far()
-    g_u.whole().start()
-    for item in (g_gain, g_r, g_s, g_a):
+    for item in (g_gain, g_r):
         item.finish()
     feat_local.wait()
     feat_spread.wait()
@@ -1019,32 +1053,10 @@
     def beta(row, width=1):
         return gamma(16 + row, width)
 
-    def unpack(chunk):
-        for pair in range(5):
-            even = v.w_a[rows_at(2 * pair * 8 + chunk, 64), :].astype(F32)
-            if pair < 4:
-                odd = v.w_a[rows_at((2 * pair + 1) * 8 + chunk, 64), :].astype(F32)
-            else:
-                odd = jnp.zeros((64, 128), F32)
-            low = jnp.where(left_half, even, pltpu.roll(odd, 64, 1))
-            top = jnp.where(left_half, pltpu.roll(even, 64, 1), odd)
-            v.w_pair[rows_at(2 * chunk, 64), pair * 128 : pair * 128 + 128] = low.astype(BF)
-            v.w_pair[rows_at(2 * chunk + 1, 64), pair * 128 : pair * 128 + 128] = top.astype(BF)
-
-    loop(8, unpack)
-
     def whole_feat():
         return jnp.concatenate([v.whole[k] for k in range(SPLITS)], axis=1)
 
     v.pre_r[...] = dot(whole_feat(), v.w_r[...])
-    for k in range(0, 512, 256):
-        v.pre_s[:, k : k + 256] = dot(whole_feat(), v.w_s[:, k : k + 256])
-    for pair in (0, 2):
-        value = dot(whole_feat(), v.w_pair[:, pair * 128 : pair * 128 + 256])
-        v.pad[pair, EDGE : EDGE + CELLS, :] = value[:, :128]
-        v.pad[pair + 1, EDGE : EDGE + CELLS, :] = value[:, 128:]
-    v.pad[4, EDGE : EDGE + CELLS, :] = dot(whole_feat(), v.w_pair[:, 512:640])
-
     def offset(tap, spacing):
         return ((tap // 3 - 1) * MAP + (tap % 3 - 1)) * spacing
 
@@ -1071,12 +1083,6 @@
             out = part if out is None else out + part
         return out
 
-    left_wide = lax.broadcasted_iota(jnp.int32, (BLOCK, 128), 1) < 64
-    for at in range(0, CELLS, BLOCK):
-        even = shift_sum((0, 2, 4, 6, 8), 1, at, lambda tap: tap // 2)
-        odd = shift_sum((1, 3, 5, 7), 1, at, lambda tap: tap // 2)
-        v.pre_a[at : at + BLOCK, :] = jnp.where(left_wide, even + pltpu.roll(odd, 64, 1), 0.0)
-
     def masked_sums(ref):
         width = ref.shape[1]
 
@@ -1102,21 +1108,16 @@
 
     sync = Sync(v.sync_one)
     r1, r2 = masked_sums(v.pre_r)
-    s1, s2 = masked_sums(v.pre_s)
-    a1, a2 = masked_sums(v.pre_a)
-    sync.start(
-        [r1, r2] + split_rows(s1) + split_rows(s2) + [a1, a2, cells_local] + split_rows(class_local)
-    )
-    for item in (g_m, g_e):
-        item.start_near()
-    g_b0.start_far()
+    sync.start([r1, r2, cells_local] + split_rows(class_local))
+    g_m.forward()
+    g_e.forward()
+    g_s.start_far()
+    g_u.whole().start()
     sums = sync.wait()
-    count = sums[12:13]
+    count = sums[2:3]
     count4 = wide(count, 4)
     norm_r = moments(sums[0:1], sums[1:2], count)
-    norm_s = moments(join_rows(sums, 2, 4), join_rows(sums, 6, 4), count4)
-    norm_a = moments(sums[10:11], sums[11:12], count)
-    class_count = join_rows(sums, 13, 2)
+    class_count = join_rows(sums, 3, 2)
 
     def normed(ref, at, norm):
         return (ref[at, :] - norm[0]) * norm[1]
@@ -1129,14 +1130,8 @@
 
     loop(6, make_h1)
     spread_1.start()
-    g_m.forward()
-
-    def make_a(k):
-        at = rows_at(k, 96)
-        v.act_a[at, :] = jax.nn.silu(gamma(15) * normed(v.pre_a, at, norm_a) + beta(15)).astype(BF)
-
-    loop(6, make_a)
-    g_e.forward()
+    g_s.start_near()
+    g_b0.start_far()
     g_m.finish()
     spread_1.wait()
 
@@ -1151,9 +1146,9 @@
         v.pre_m[at : at + BLOCK, :] = shift_sum(range(9), 4, at, lambda tap: tap)
     sync = Sync(v.sync_two)
     sync.start(list(masked_sums(v.pre_m)))
+    g_s.forward()
+    g_b0.start_near()
     g_b1.start_far()
-    g_b0.start_near()
-    g_e.finish()
     sums = sync.wait()
     norm_m = moments(sums[0:1], sums[1:2], count)
     spread_2 = Spread(v.h2)
@@ -1164,20 +1159,29 @@
 
     loop(6, make_h2)
     spread_2.start()
-    g_u.start_far(0)
     g_b0.forward()
     g_b1.start_near()
+    g_u.start_far(0)
+    g_e.finish()
+    g_s.finish()
+    for k in range(0, 512, 256):
+        v.pre_s[:, k : k + 256] = dot(whole_feat(), v.w_s[:, k : k + 256])
+    s1, s2 = masked_sums(v.pre_s)
     spread_2.wait()
     for k in range(0, 512, 256):
         v.pre_e[:, k : k + 256] = dot(full_h(v.h2), v.w_e[:, k : k + 256])
     sync = Sync(v.sync_three)
     e1, e2 = masked_sums(v.pre_e)
-    sync.start(split_rows(e1) + split_rows(e2))
-    g_u.start_far(1)
+    sync.start(split_rows(e1) + split_rows(e2) + split_rows(s1) + split_rows(s2))
     g_b1.forward()
     g_u.start_near(0)
+    g_u.start_far(1)
+    for item in (g_c, g_ac):
+        item.start_far()
+        item.start_near()
     sums = sync.wait()
     norm_e = moments(join_rows(sums, 0, 4), join_rows(sums, 4, 4), count4)
+    norm_s = moments(join_rows(sums, 8, 4), join_rows(sums, 12, 4), count4)
 
     def summed(at):
         return (
@@ -1203,6 +1207,10 @@
     joined_copy(0, t, t_x).start()
     joined_copy(1, t, t_core).start()
 
+    pool_move = ToGroup(
+        lambda owner, rows: v.pool_half.at[lax.rem(owner, 2), 0:rows, :],
+        lambda slot, rows: v.pool_all.at[slot, 0:rows, :],
+    )
     bin_row = lax.broadcasted_iota(jnp.int32, (BINS, 1), 0)
 
     def group_mask(group, shape=None):
@@ -1213,6 +1221,9 @@
     cells_in = wide(v.cells_in[...], 4)
     pooled = dot(v.pool[...], v.joined[t]) / cells_in
     v.pooled[...] = pooled.astype(BF)
+    for k in range(2):
+        v.pool_half[k] = v.pooled[:, k * 256 : k * 256 + 256]
+    v.pool_all[me] = v.pool_half[lax.rem(me, 2)]
     g_b0.finish()
     g_b1.finish()
     part = jnp.zeros((BINS, 512), F32)
@@ -1224,9 +1235,9 @@
     v.recv_b[t] = v.part_b[t]
     ex = Exchange(TENSOR, SPLITS, lambda o: v.part_b.at[o], lambda s: v.recv_b.at[s])
     ex.start()
-    g_u.start_far(2)
     g_u.forward(0)
     g_u.start_near(1)
+    g_u.start_far(2)
     joined_copy(0, t_x, t_x).wait_recv()
     joined_copy(2, t_x, t_core).start()
     ex.wait()
@@ -1236,9 +1247,9 @@
     v.all_b[me] = own_b.astype(BF)
     ex = Exchange(BATCH, OWNERS, lambda o: v.all_b.at[me], lambda s: v.all_b.at[s])
     ex.start()
-    g_u.start_far(3)
     g_u.forward(1)
     g_u.start_near(2)
+    g_u.start_far(3)
     ex.wait()
     all_b = [v.all_b[k].astype(F32) for k in range(OWNERS)]
     sum_b, square_b = all_b[0], all_b[0] * all_b[0]
@@ -1264,12 +1275,9 @@
         out = gamma_b * ((all_b[k] - mean_b) * scale_b) + beta_b
         v.act_b[t, k * BINS : k * BINS + BINS, :] = jax.nn.silu(out).astype(BF)
     spread_b.start()
-    g_u.start_far(4)
-    for item in (g_c, g_ac):
-        item.start_far()
-        item.start_near()
     g_u.forward(2)
     g_u.start_near(3)
+    g_u.start_far(4)
     spread_b.wait()
     g_u.whole().wait()
     row_512 = lax.broadcasted_iota(jnp.int32, (OWNERS * BINS, 1), 0) & (BINS - 1)
@@ -1301,17 +1309,20 @@
     v.z_recv[me] = v.z_send[me]
     ex = Exchange(BATCH, OWNERS, lambda o: v.z_send.at[o], lambda s: v.z_recv.at[s])
     ex.start()
+    g_u.forward(3)
     g_u.start_near(4)
-    g_u.forward(3)
-    g_u.forward(4)
-    g_c.forward()
-    g_ac.forward()
+    g_a.start_far()
     joined_copy(1, t_core, t_core).wait_recv()
     joined_copy(2, t_diag, t_core).wait_recv()
     for k in range(SPLITS):
         v.joined_t[k] = v.joined[k].T
+    g_u.forward(4)
+    g_a.start_near()
+    g_c.forward()
+    g_ac.forward()
     ex.wait()
     g_u.finish()
+    g_a.forward()
 
     pick2 = jnp.concatenate([v.pick[...], v.pick[...]], axis=0)
 
@@ -1346,8 +1357,38 @@
         v.pre_u[at : at + BLOCK, :] = shift_sum(range(9), 1, at, lambda tap: tap)
     sync = Sync(v.sync_five)
     sync.start(list(masked_sums(v.pre_u)))
-    for item in (g_c, g_ac):
+    pool_move.start()
+    for item in (g_a, g_c, g_ac):
         item.finish()
+
+    def unpack(chunk):
+        for pair in range(5):
+            even = v.w_a[rows_at(2 * pair * 8 + chunk, 64), :].astype(F32)
+            if pair < 4:
+                odd = v.w_a[rows_at((2 * pair + 1) * 8 + chunk, 64), :].astype(F32)
+            else:
+                odd = jnp.zeros((64, 128), F32)
+            low = jnp.where(left_half, even, pltpu.roll(odd, 64, 1))
+            top = jnp.where(left_half, pltpu.roll(even, 64, 1), odd)
+            v.w_pair[rows_at(2 * chunk, 64), pair * 128 : pair * 128 + 128] = low.astype(BF)
+            v.w_pair[rows_at(2 * chunk + 1, 64), pair * 128 : pair * 128 + 128] = top.astype(BF)
+
+    loop(8, unpack)
+
+    for pair in (0, 2):
+        value = dot(whole_feat(), v.w_pair[:, pair * 128 : pair * 128 + 256])
+        v.pad[pair, EDGE : EDGE + CELLS, :] = value[:, :128]
+        v.pad[pair + 1, EDGE : EDGE + CELLS, :] = value[:, 128:]
+    v.pad[4, EDGE : EDGE + CELLS, :] = dot(whole_feat(), v.w_pair[:, 512:640])
+
+    left_wide = lax.broadcasted_iota(jnp.int32, (BLOCK, 128), 1) < 64
+    for at in range(0, CELLS, BLOCK):
+        even = shift_sum((0, 2, 4, 6, 8), 1, at, lambda tap: tap // 2)
+        odd = shift_sum((1, 3, 5, 7), 1, at, lambda tap: tap // 2)
+        v.pre_a[at : at + BLOCK, :] = jnp.where(left_wide, even + pltpu.roll(odd, 64, 1), 0.0)
+
+    sync_a = Sync(v.sync_aux)
+    sync_a.start(list(masked_sums(v.pre_a)))
     for item in (g_gain, g_r, g_s, g_a, g_m, g_e, g_b0, g_b1, g_c, g_ac, g_u):
         item.drain()
     joined_copy(0, t, t_x).wait_send()
@@ -1362,8 +1403,16 @@
         v.united[at, :] = jax.nn.silu(gamma(14) * normed(v.pre_u, at, norm_u) + beta(14)).astype(BF)
 
     loop(6, make_u)
-
     v.logit_send[:, :256] = dot(v.united[...], v.w_c[...]).astype(BF)
+    sums = sync_a.wait()
+    norm_a = moments(sums[0:1], sums[1:2], count)
+
+    def make_a(k):
+        at = rows_at(k, 96)
+        v.act_a[at, :] = jax.nn.silu(gamma(15) * normed(v.pre_a, at, norm_a) + beta(15)).astype(BF)
+
+    loop(6, make_a)
+
     v.logit_send[:, 256:] = dot(v.act_a[...], w_ac).astype(BF)
     ex = Exchange(
         TENSOR,
@@ -1512,7 +1561,6 @@
     s_c = Scatter(v.first_c, v.second_c, v.w_c, 16, o_c)
     s_ac = Scatter(v.first_ac, v.second_ac, v.w_ac, 8, o_ac)
     s_a = Scatter(v.first_a, v.second_a, v.w_a, 576, o_a)
-    s_b = Scatter(v.first_b, v.second_b, v.w_b, 256, o_flat, 1472)
     s_s = Scatter(v.first_s, v.second_s, v.w_s, 128, o_flat, 128)
     s_e = Scatter(v.first_e, v.second_e, v.w_e, 64, o_flat, 1216)
     s_m = Scatter(v.first_m, v.second_m, v.w_m, 576, o_flat, 640)
@@ -1770,7 +1818,6 @@
         + [total(d_b * unit_b * group_mask(g)) for g in range(4)]
     )
     s_u.start(2)
-    s_a.start()
     sums = sync.wait()
     first_b = jnp.zeros((BINS, 128), F32)
     second_b = jnp.zeros((BINS, 128), F32)
@@ -1786,14 +1833,17 @@
     s_u.start(3)
     s_u.middle(1)
     spread_d.wait()
+    d_bp_move = ToGroup(
+        lambda owner, rows: v.d_bp.at[:, 0:rows, :],
+        lambda slot, rows: v.d_bp_all.at[slot, :, 0:rows, :],
+    )
+    d_bp_move.start()
+    v.d_bp_all[me] = v.d_bp[...]
     d_bp = jnp.concatenate([v.d_bp[k] for k in range(SPLITS)], axis=1)
     d_pooled = jnp.zeros((BINS, 512), F32)
-    d_groups = []
     for group in range(4):
-        d_groups.append((d_bp.astype(F32) * group_mask(group)).astype(BF))
-        d_pooled = d_pooled + dot_nt(d_groups[group], v.w_b[group * 512 : group * 512 + 512, :])
-    for group in range(4):
-        v.w_b[group * 512 : group * 512 + 512, :] = dot_tn(v.pooled[...], d_groups[group]).astype(BF)
+        rows = (d_bp.astype(F32) * group_mask(group)).astype(BF)
+        d_pooled = d_pooled + dot_nt(rows, v.w_b[group * 512 : group * 512 + 512, :])
     d_pooled = (d_pooled / cells_in).astype(BF)
     v.d_sum[...] = dot_tn(v.pool[...], d_pooled)
     dm_near(0, t).wait_recv()
@@ -1857,7 +1907,7 @@
         loop(6, step)
 
     ex = back_hidden(v.d_e[...], v.w_e[...], 0)
-    s_b.start()
+    s_a.start()
     s_u.middle(3)
     for k in range(SPLITS):
         v.w_e[k * 128 : k * 128 + 128, :] = dot_tn(v.h2[k], v.d_e[...]).astype(BF)
@@ -1868,7 +1918,6 @@
     s_e.start()
     s_c.middle()
     s_ac.middle()
-    s_a.middle()
     s_u.middle(4)
     sums = sync.wait()
     gain_grads[5] = (sums[1:2], sums[0:1])
@@ -1882,7 +1931,7 @@
 
     loop(SPLITS, short_grad)
     s_s.start()
-    s_b.middle()
+    s_a.middle()
     ex.wait()
     hidden_sum(1)
     sync = Sync(v.sync_b6)
@@ -1915,8 +1964,18 @@
     s_r.start()
     for item in (s_m, s_r):
         item.middle()
-    rest = (s_c, s_ac, s_b, s_a, s_e, s_s, s_m, s_r)
-    squares = s_u.end()
+    pool_move.wait()
+    d_bp_move.wait()
+    own_group = jnp.where(group_id == lax.div(me, 2), 1.0, 0.0)
+    d_rows = jnp.concatenate(
+        [v.d_bp_all[:, k].reshape(OWNERS * BINS, 128) for k in range(SPLITS)], axis=1
+    )
+    d_rows = (d_rows.astype(F32) * own_group).astype(BF)
+    branch_grad = dot_tn(v.pool_all[...].reshape(OWNERS * BINS, 256), d_rows)
+    for k in range(4):
+        o_flat[pl.ds(1472 + k, 256, stride=4), :] = branch_grad[:, k * 128 : k * 128 + 128]
+    rest = (s_c, s_ac, s_a, s_e, s_s, s_m, s_r)
+    squares = s_u.end() + sum(split_rows(total(branch_grad * branch_grad)))
     for item in rest:
         squares = squares + item.end()
     dm_near(1, t_diag).wait_send()

time: 440 us -> 401 us (0.911)
  Pallas kernels: 405 us -> 366 us
    pallas_call x1, Pallas kernels: 386 us -> 347 us  [whole_step(): pl.pallas_call(functools.partial(step_kernel, tuple(plan)), out_shape=[ja...]
where the time goes in v6:
time: 401 us; the launch traced here: 400 us
  Pallas kernels  366 us (91%)
  local copies, waits for them, and re-layouts  17.4 us (4%)
  other arithmetic  13.4 us (3%)
    pallas_call x1, Pallas kernels, whole_step(): pl.pallas_call(functools.partial(step_kernel, tuple(plan)), out_shape=[ja...  347 us
    pallas_call x1, Pallas kernels, update(): pl.pallas_call(update_kernel, grid=(pl.cdiv(rows, 512),), out_shape=[jax....  18.8 us

profile of v6, /device:TPU:0, one launch (start us, length us, event | category | flops | bytes accessed | tf_op | source)
XLA Modules:
  0.0 399.7 jit_solution(14750043539676569092)
XLA Ops:
  0.7 0.7 select_convert_fusion
  1.4 0.1 broadcast_in_dim.15
  1.5 0.9 broadcast_in_dim.16.refs_1_
  2.3 1.0 slice.67
  3.4 0.1 slice_convert_fusion
  3.4 0.2 dynamic_update_slice.6
  3.7 0.6 reshape.125.refs_3_
  4.3 0.1 slice.99
  4.4 0.1 convert_element_type.45
  4.4 0.6 pad_convert_fusion.refs_12_
  5.1 0.1 slice.95
  5.2 0.1 convert_element_type.44
  5.3 0.6 pad.10.refs_11_
  5.9 0.1 convert_element_type.43
  6.1 0.8 pad_maximum_fusion.refs_10_
  6.9 2.3 convert_element_type.42
  9.2 0.6 slice.89.refs_4_
  9.8 0.7 reshape.128.refs_7_
  10.5 0.7 reshape.127.refs_5_
  11.2 0.7 slice.91.refs_6_
  11.9 1.1 slice.94.refs_9_
  13.0 0.9 reshape.129.refs_8_
  13.8 347.4 %whole_step.1 = (f32[7712,128]{1,0:T(8,128)}, f32[576,128]{1,0:T(8,128)}, f32[16,256]{1,0:T(8,128)}, f32[8,256]{1,0:T(8,128)}, f32[32,128]{1,0:T(8,128)}, /*index=5*/f32[8,128]{1,0:T(8,128)}) custom-call(s32[1,2]{1,0:T(1,128)} %refs_0_.1, f32[576,128]{1,0:T(8,128)} %broadcast_in_dim.16.refs_1_, bf16[576,256]{1,0:T(8,128)(2,1)} %bitcast.40, ...), custom_call_target="tpu_custom_call" | custom-call | tf_op jit(solution)/shard_map/whole_step/pallas_call | solution.py:2009
  361.3 1.2 slice.86
  362.5 0.8 reshape.131
  363.3 1.2 slice_bitcast_fusion
  364.5 0.7 reshape.135
  365.2 0.1 reshape.136
  365.3 0.1 dynamic_slice.3
  365.4 1.4 slice_reduce_fusion
  367.5 0.8 reshape.134
  368.3 1.3 reshape.132
  369.6 0.1 copy.19
  369.6 0.1 reshape.133
  369.8 1.7 concatenate.14
  371.5 0.7 bitcast_dynamic-update-slice_fusion.grad
  372.3 18.8 %update.1 = (f32[7712,128]{1,0:T(8,128)}, f32[7712,128]{1,0:T(8,128)}, f32[7712,128]{1,0:T(8,128)}, f32[7712,128]{1,0:T(8,128)}) custom-call(f32[1]{0:T(128)} %bitcast.7.scale, f32[7712,128]{1,0:T(8,128)} %bitcast_dynamic-update-slice_fusion.grad, f32[7712,128]{1,0:T(8,128)} %bitcast.30, f32[7712,128]{1,0:T(8,128)} %bitcast.31, f32[7712,128]{1,0:T(8,128)} %bitcast.32, ...), custom_call_target="tpu_custom_call" | custom-call | tf_op jit(solution)/shard_map/update/pallas_call | solution.py:2040
  391.1 7.5 %convert_element_type.46 = bf16[1,987136]{1,0:T(2,128)(2,1)} convert(f32[1,987136]{1,0:T(1,128)} %bitcast.34) | non-fusion elementwise | flops 987136 | bytes 5922816 | tf_op jit(solution)/shard_map/convert_element_type | solution.py:2133
  (7 shorter events, 0.1 us)

commit v7 on v6

--- a/solution.py
+++ b/solution.py
@@ -486,7 +486,11 @@
         w_pair=((1024, 640), BF),
         w_c=((128, 256), BF),
         w_ac=((64, 256), F32),
-        gain_in=((OWNERS, 32, 128), F32),
+        gain_in=((OWNERS, 8, 128), F32),
+        gain_rows=((40, 128), F32),
+        out_a=((576, 128), F32),
+        out_c=((16, 256), F32),
+        out_ac=((8, 256), F32),
         whole=((SPLITS, CELLS, 256), BF),
         ins=((CELLS, 128), F32),
         col=((CELLS, 128), F32),
@@ -565,6 +569,8 @@
     ac=(8, 256, F32),
 )
 SEMAPHORES = 1100
+LOADS = (0, 128, 640, 1216, 1472, 2496, 7104, 7712)
+LOAD_ORDER = (0, 2, 3, 1, 4, 6, 5)
 
 
 class Refs:
@@ -609,11 +615,10 @@
 
 def step_kernel(names, *refs):
     (
-        sizes, lab_in, feat, gain_own, p_r, p_s, p_m, p_e, p_b, p_u, p_a, p_c, p_ac,
-        o_flat, o_a, o_c, o_ac, o_gain, o_misc,
-    ) = refs[:19]
+        sizes, lab_in, feat, flat, o_flat, o_shift, o_misc,
+    ) = refs[:7]
     v = Refs()
-    for name, ref in zip(names, refs[19:]):
+    for name, ref in zip(names, refs[7:]):
         setattr(v, name, ref)
     sems = refs[-1]
     o_u = o_flat.at[2496:7104, :]
@@ -646,6 +651,14 @@
 
     late = []
 
+    load_at = take(len(LOADS))
+
+    def load(index):
+        at = pl.ds(LOADS[index], LOADS[index + 1] - LOADS[index])
+        return pltpu.make_async_copy(flat.at[at, :], o_flat.at[at, :], sems.at[load_at + index])
+
+    for index in LOAD_ORDER:
+        load(index).start()
     v.pool_all[...] = jnp.zeros((OWNERS, BINS, 256), BF)
     v.d_bp_all[...] = jnp.zeros((OWNERS, SPLITS, BINS, 128), BF)
     barrier = pltpu.get_barrier_semaphore()
@@ -660,11 +673,9 @@
     pl.semaphore_wait(barrier, OWNERS + SPLITS - 2)
 
     class Gather:
-        def __init__(self, piece, full, rows, skip=0, step=None):
-            self.piece, self.full, self.rows = piece, full, rows
+        def __init__(self, full, rows, skip=0, step=None, piece=None):
+            self.full, self.rows, self.piece = full, rows, piece
             self.skip, self.part = skip, step or rows
-            if step:
-                self.piece = piece.at[skip : skip + step, :]
             self.near_s, self.far_s, self.pass_s = take(1), take(HALF), take(HALF)
             self.recv, self.keep = take(OWNERS), take(1)
 
@@ -674,17 +685,20 @@
             start = pl.multiple_of(owner * self.rows + self.skip, self.part)
             return self.full.at[pl.ds(start, self.part), :]
 
+        def source(self):
+            return self.at(me) if self.piece is None else self.piece
+
         def local(self):
             return pltpu.make_async_copy(self.piece, self.at(me), sems.at[self.keep])
 
         def near(self):
             return remote(
-                self.piece, self.at(me), self.near_s, self.recv + me, {BATCH: partner}
+                self.source(), self.at(me), self.near_s, self.recv + me, {BATCH: partner}
             )
 
         def far(self, step):
             return remote(
-                self.piece,
+                self.source(),
                 self.at(me),
                 self.far_s + step,
                 self.recv + me,
@@ -702,7 +716,8 @@
             )
 
         def start_far(self):
-            self.local().start()
+            if self.piece is not None:
+                self.local().start()
             for step in range(1, HALF):
                 self.far(step).start()
 
@@ -717,7 +732,8 @@
         def finish(self):
             for step in range(HALF):
                 self.passed(step, partner).wait_recv()
-            self.local().wait()
+            if self.piece is not None:
+                self.local().wait()
             self.near().wait_send()
             for step in range(1, HALF):
                 self.far(step).wait_send()
@@ -726,16 +742,16 @@
             for step in range(1, HALF):
                 self.passed(step, me).wait_send()
 
-    g_gain = Gather(gain_own, v.gain_in, None)
-    g_r = Gather(p_r, v.w_r, 128)
-    g_s = Gather(p_s, v.w_s, 128)
-    g_a = Gather(p_a, v.w_a, 576)
-    g_m = Gather(p_m, v.w_m, 576)
-    g_e = Gather(p_e, v.w_e, 64)
-    g_b0 = Gather(p_b, v.w_b, 256, 0, 128)
-    g_b1 = Gather(p_b, v.w_b, 256, 128, 128)
-    g_c = Gather(p_c, v.w_c, 16)
-    g_ac = Gather(p_ac, v.w_ac, 8)
+    g_gain = Gather(v.gain_in, None, piece=flat.at[7704:7712, :])
+    g_r = Gather(v.w_r, 128)
+    g_s = Gather(v.w_s, 128)
+    g_a = Gather(v.w_a, 576)
+    g_m = Gather(v.w_m, 576)
+    g_e = Gather(v.w_e, 64)
+    g_b0 = Gather(v.w_b, 256, 0, 128)
+    g_b1 = Gather(v.w_b, 256, 128, 128)
+    g_c = Gather(v.w_c, 16)
+    g_ac = Gather(v.w_ac, 8)
 
     def block_of(owner, slot):
         return 8 if slot == SLOTS - 1 else lax.rem(slot - owner + 8, 8)
@@ -758,10 +774,10 @@
                 take(SLOTS * HALF),
                 take(SLOTS * HALF),
             )
-            self.recv, self.keep, self.keep_all = take(SLOTS * OWNERS), take(SLOTS), take(1)
+            self.recv, self.keep = take(SLOTS * OWNERS), take(SLOTS)
 
         def source(self, slot):
-            return p_u.at[rows_at(block_of(me, slot), 512), :]
+            return v.w_own.at[rows_at(block_of(me, slot), 512), :]
 
         def full(self, owner, slot):
             return v.w_u.at[merged_rows(owner, slot), :]
@@ -770,9 +786,6 @@
             return pltpu.make_async_copy(
                 self.source(slot), self.full(me, slot), sems.at[self.keep + slot]
             )
-
-        def whole(self):
-            return pltpu.make_async_copy(p_u, v.w_own, sems.at[self.keep_all])
 
         def near(self, slot):
             return remote(
@@ -968,14 +981,29 @@
     feat_keep = take(1)
     feat_local = pltpu.make_async_copy(feat, v.whole.at[t], sems.at[feat_keep])
     feat_spread = Exchange(TENSOR, SPLITS, lambda other: feat, lambda slot: v.whole.at[slot])
+    def wide_rows(into, rows, low):
+        for k in range(4):
+            value = o_flat[pl.ds(low + k, rows, stride=4), :]
+            into[rows_at(me, rows), k * 128 : k * 128 + 128] = value.astype(BF)
+
+    load(0).wait()
+    v.w_r[rows_at(me, 128), :] = o_flat[0:128, :].astype(BF)
     for item in (g_gain, g_r):
         item.start_far()
         item.start_near()
     feat_local.start()
     feat_spread.start()
+    load(2).wait()
+    v.w_m[rows_at(me, 576), :] = o_flat[640:1216, :].astype(BF)
+    load(3).wait()
+    wide_rows(v.w_e, 64, 1216)
     for item in (g_m, g_e):
         item.start_far()
         item.start_near()
+    lane = lax.broadcasted_iota(jnp.int32, (1, 128), 1)
+
+    def roll(value, shift):
+        return pltpu.roll(value, shift % 128, 1) if shift % 128 else value
 
     high, across = sizes[0, 0], sizes[0, 1]
     place = lax.broadcasted_iota(jnp.int32, (CELLS, 128), 0).astype(F32)
@@ -1039,16 +1067,58 @@
 
     for item in (g_gain, g_r):
         item.forward()
+    load(1).wait()
+    wide_rows(v.w_s, 128, 128)
+    load(4).wait()
+    wide_rows(v.w_b, 256, 1472)
+    load(6).wait()
+    before = pltpu.roll(o_flat[7122:7698, :], 32, 1)
+    after = pltpu.roll(o_flat[7123:7699, :], 32, 1)
+    v.w_a[rows_at(me, 576), :] = jnp.where(lane < 32, before, after).astype(BF)
+
+    def class_rows(count, base, into):
+        for row in range(count):
+            first, shift = divmod(base + NCLS * row, 128)
+            three = [
+                roll(o_flat[7104 + first + k : 7105 + first + k, :], 128 - shift) for k in range(3)
+            ]
+            into[row : row + 1, :128] = jnp.where(lane < 128 - shift, three[0], three[1])
+            high_half = jnp.where(lane < 128 - shift, three[1], three[2])
+            into[row : row + 1, 128:] = jnp.where(lane < NCLS - 128, high_half, 0.0)
+
+    class_rows(16, 0, v.out_c)
+    class_rows(8, 76128, v.out_ac)
+    v.w_c[rows_at(me, 16), :] = v.out_c[...].astype(BF)
+    v.w_ac[rows_at(me, 8), :] = v.out_ac[...].astype(BF).astype(F32)
+    load(5).wait()
+
+    def own_rows(j):
+        at = pl.ds(pl.multiple_of(2496 + 512 * j, 64), 512)
+        v.w_own[rows_at(j, 512), :] = o_flat[at, :].astype(BF)
+
+    loop(9, own_rows)
     for item in (g_gain, g_r):
         item.finish()
     feat_local.wait()
     feat_spread.wait()
-    gains = v.gain_in[0]
-    for slot in range(1, OWNERS):
-        gains = gains + v.gain_in[slot]
+    gain_of = [None] * 33
+    for owner in range(OWNERS):
+        start = 496 * (owner % 4) - 16
+        first, shift = start // 128, start % 128
+        for k in range(4):
+            value = v.gain_in[owner, 4 + k : 5 + k, :].astype(BF).astype(F32)
+            if k == 0:
+                value = jnp.where(lane < 16, 0.0, value)
+            value = roll(value, shift)
+            spot = 16 * (owner // 4) + first + k
+            for where, part in (
+                (spot, jnp.where(lane >= shift, value, 0.0)),
+                (spot + 1, jnp.where(lane < shift, value, 0.0)),
+            ):
+                gain_of[where] = part if gain_of[where] is None else gain_of[where] + part
 
     def gamma(row, width=1):
-        return jnp.concatenate([gains[row + k : row + k + 1] for k in range(width)], axis=1)
+        return jnp.concatenate([gain_of[row + k] for k in range(width)], axis=1)
 
     def beta(row, width=1):
         return gamma(16 + row, width)
@@ -1112,7 +1182,6 @@
     g_m.forward()
     g_e.forward()
     g_s.start_far()
-    g_u.whole().start()
     sums = sync.wait()
     count = sums[2:3]
     count4 = wide(count, 4)
@@ -1279,7 +1348,6 @@
     g_u.start_near(3)
     g_u.start_far(4)
     spread_b.wait()
-    g_u.whole().wait()
     row_512 = lax.broadcasted_iota(jnp.int32, (OWNERS * BINS, 1), 0) & (BINS - 1)
     group_id = jnp.where(
         row_512 < 1, 0, jnp.where(row_512 < 5, 1, jnp.where(row_512 < 14, 2, jnp.where(row_512 < 50, 3, 9)))
@@ -1370,8 +1438,10 @@
                 odd = jnp.zeros((64, 128), F32)
             low = jnp.where(left_half, even, pltpu.roll(odd, 64, 1))
             top = jnp.where(left_half, pltpu.roll(even, 64, 1), odd)
-            v.w_pair[rows_at(2 * chunk, 64), pair * 128 : pair * 128 + 128] = low.astype(BF)
-            v.w_pair[rows_at(2 * chunk + 1, 64), pair * 128 : pair * 128 + 128] = top.astype(BF)
+            v.pad[pair, pl.ds(EDGE, 64, stride=2), :] = low
+            v.pad[pair, pl.ds(EDGE + 1, 64, stride=2), :] = top
+            both = v.pad[pair, EDGE : EDGE + 128, :]
+            v.w_pair[rows_at(chunk, 128), pair * 128 : pair * 128 + 128] = both.astype(BF)
 
     loop(8, unpack)
 
@@ -1558,9 +1628,9 @@
                     self.far(step).wait_send()
             return sum(split_rows(total(squares)))
 
-    s_c = Scatter(v.first_c, v.second_c, v.w_c, 16, o_c)
-    s_ac = Scatter(v.first_ac, v.second_ac, v.w_ac, 8, o_ac)
-    s_a = Scatter(v.first_a, v.second_a, v.w_a, 576, o_a)
+    s_c = Scatter(v.first_c, v.second_c, v.w_c, 16, v.out_c)
+    s_ac = Scatter(v.first_ac, v.second_ac, v.w_ac, 8, v.out_ac)
+    s_a = Scatter(v.first_a, v.second_a, v.w_a, 576, v.out_a)
     s_s = Scatter(v.first_s, v.second_s, v.w_s, 128, o_flat, 128)
     s_e = Scatter(v.first_e, v.second_e, v.w_e, 64, o_flat, 1216)
     s_m = Scatter(v.first_m, v.second_m, v.w_m, 576, o_flat, 640)
@@ -1796,8 +1866,9 @@
             value = value2[half * 128 : half * 128 + 128]
             c = 2 * c2 + half
             for p in range(5):
-                low = value[:64, p * 128 : p * 128 + 128]
-                top = value[64:, p * 128 : p * 128 + 128]
+                v.pad[p, EDGE : EDGE + 128, :] = value[:, p * 128 : p * 128 + 128]
+                low = v.pad[p, pl.ds(EDGE, 64, stride=2), :]
+                top = v.pad[p, pl.ds(EDGE + 1, 64, stride=2), :]
                 even = jnp.where(left_half, low, pltpu.roll(top, 64, 1))
                 v.w_a[rows_at(2 * p * 8 + c, 64), :] = even.astype(BF)
                 if p < 4:
@@ -1982,14 +2053,57 @@
     dm_near(0, t_core).wait_send()
     dm_far.wait_send()
 
-    for row in range(16):
-        o_gain[row : row + 1, :] = gain_grads[row][0]
-        o_gain[16 + row : 17 + row, :] = gain_grads[row][1]
-    gain_square = o_gain[...] * o_gain[...]
-    squares = squares + total(gain_square) / OWNERS
+    v.gain_rows[...] = jnp.zeros((40, 128), F32)
+    gammas = [gain_grads[row][0] for row in range(16)]
+    betas = [pltpu.roll(gain_grads[row][1], 64, 1) for row in range(16)]
+    o_shift[...] = gain_grads[14][1]
+    for row in range(31):
+        if row < 15:
+            value = gammas[row]
+        else:
+            left = gammas[15] if row == 15 else betas[row - 16]
+            value = jnp.where(lane < 64, left, betas[row - 15])
+        v.gain_rows[row + 1 : row + 2, :] = value
+    squares = squares + total(fold(v.gain_rows[...] * v.gain_rows[...])) / OWNERS
 
     sync = Sync(v.sync_end)
     sync.start([squares, o_misc[1:2, :]])
+
+    tail = {}
+
+    def put(where, value):
+        tail[where] = value if where not in tail else tail[where] + value
+
+    def class_tail(ref, count, base):
+        for row in range(count):
+            first, shift = divmod(base + NCLS * row, 128)
+            for k in range(2):
+                value = roll(ref[row : row + 1, k * 128 : k * 128 + 128], shift)
+                put(first + k, jnp.where(lane >= shift, value, 0.0))
+                if shift:
+                    put(first + k + 1, jnp.where(lane < shift, value, 0.0))
+
+    class_tail(v.out_c, 16, 0)
+    class_tail(v.out_ac, 8, 76128)
+    start = lax.rem(496 * me, 128)
+    first = lax.div(496 * me, 128)
+    own = [
+        pltpu.roll(v.gain_rows[pl.ds(first + k, 1), :], lax.rem(16 - start + 128, 128), 1)
+        for k in range(6)
+    ]
+    spot = lane - 16 + start
+    for k in range(4):
+        value = jnp.where(spot < 0, own[k], jnp.where(spot >= 128, own[k + 2], own[k + 1]))
+        put(604 + k, jnp.where(lane >= 16, value, 0.0) if k == 0 else value)
+    v.grad_pad[EDGE : EDGE + 576, :] = pltpu.roll(v.out_a[...], 96, 1)
+    o_flat[7122:7706, :] = jnp.where(
+        lane >= 96, v.grad_pad[EDGE : EDGE + 584, :], v.grad_pad[EDGE - 1 : EDGE + 583, :]
+    )
+    for row in range(608):
+        if row in (18, 594):
+            o_flat[7104 + row : 7105 + row, :] = o_flat[7104 + row : 7105 + row, :] + tail[row]
+        elif row < 18 or row > 594:
+            o_flat[7104 + row : 7105 + row, :] = tail[row]
     v.end_t[t] = sync.wait()
     spread_e = Spread(v.end_t)
     spread_e.start()
@@ -2001,16 +2115,15 @@
     o_misc[2:3, :] = jnp.broadcast_to(loss_weight, (1, 128))
 
 
-def whole_step(sizes, labels, feat, gains, pieces):
+def whole_step(sizes, labels, feat, flat):
     plan = scratch_plan()
     vmem = pl.BlockSpec(memory_space=pltpu.VMEM)
     anywhere = pl.BlockSpec(memory_space=pl.ANY)
-    outs = [(7712, 128), (576, 128), (16, 256), (8, 256), (32, 128), (8, 128)]
+    outs = [flat.shape, (1, 128), (8, 128)]
     return pl.pallas_call(
         functools.partial(step_kernel, tuple(plan)),
         out_shape=[jax.ShapeDtypeStruct(shape, F32) for shape in outs],
-        in_specs=[pl.BlockSpec(memory_space=pltpu.SMEM), vmem, anywhere, anywhere]
-        + [anywhere] * len(pieces),
+        in_specs=[pl.BlockSpec(memory_space=pltpu.SMEM), vmem, anywhere, anywhere],
         out_specs=[vmem] * len(outs),
         scratch_shapes=[pltpu.VMEM(shape, kind) for shape, kind in plan.values()]
         + [pltpu.SemaphoreType.DMA((SEMAPHORES,))],
@@ -2018,112 +2131,67 @@
             collective_id=0, has_side_effects=True, vmem_limit_bytes=63 * 1024 * 1024
         ),
         name="whole_step",
-    )(sizes, labels, feat, gains, *pieces)
-
-
-def update_kernel(scale, grad, param, first, second, average, o_param, o_first, o_second, o_average):
-    clipped = grad[...] * scale[0]
+    )(sizes, labels, feat, flat)
+
+
+def update_kernel(
+    misc, grad, param, first, second, average,
+    o_param, o_first, o_second, o_average, o_norm, o_loss, o_weight,
+):
+    norm = jnp.sqrt(jnp.sum(misc[0:1, :], axis=1, keepdims=True))
+    o_norm[...] = norm
+    o_loss[...] = jnp.sum(misc[1:2, :], axis=1, keepdims=True)
+    o_weight[...] = misc[2:3, 0:1]
+    clipped = grad[...] * jnp.minimum(1.0, 0.05 / (norm + 1e-06))
     new_first = 0.5 * first[...] + 0.5 * clipped
     new_second = 0.5 * second[...] + 0.5 * clipped * clipped
-    keep = 1.0 - 0.5**STEP
+    lift = 1.0 / (1.0 - 0.5**STEP)
     old = param[...]
-    new = old - 0.01 * (new_first / keep / (jnp.sqrt(new_second / keep) + 1e-08) + 0.01 * old)
+    ratio = (new_first * lift) / (jnp.sqrt(new_second * lift) + 1e-08)
+    new = old - 0.01 * (ratio + 0.01 * old)
     o_param[...] = new
     o_first[...] = new_first
     o_second[...] = new_second
     o_average[...] = 0.999 * average[...] + 0.001 * new
 
 
-def update(scale, grad, param, first, second, average):
+def update(misc, grad, param, first, second, average):
     rows = grad.shape[0]
-    block = pl.BlockSpec((512, 128), lambda i: (i, 0))
+    block = pl.BlockSpec((1024, 128), lambda i: (i, 0))
+    whole = pl.BlockSpec((8, 128), lambda i: (0, 0))
+    one = pl.BlockSpec((1, 1), lambda i: (0, 0))
+    big = jax.ShapeDtypeStruct((rows, 128), F32)
     return pl.pallas_call(
         update_kernel,
-        grid=(pl.cdiv(rows, 512),),
-        out_shape=[jax.ShapeDtypeStruct((rows, 128), jnp.float32)] * 4,
-        in_specs=[pl.BlockSpec(memory_space=pltpu.SMEM)] + [block] * 5,
-        out_specs=[block] * 4,
+        grid=(pl.cdiv(rows, 1024),),
+        out_shape=[big] * 4 + [jax.ShapeDtypeStruct((1, 1), F32)] * 3,
+        in_specs=[whole] + [block] * 5,
+        out_specs=[block] * 4 + [one] * 3,
+        compiler_params=pltpu.CompilerParams(vmem_limit_bytes=32 * 1024 * 1024),
         name="update",
-    )(scale.reshape(1), grad, param, first, second, average)
+    )(misc, grad, param, first, second, average)
+
 
 def fits(splits, owners):
     return splits == SPLITS and owners == OWNERS
 
 
 def local_fast(features, labels, valid, sizes, params, first_moment, squared_mean, average):
-    me = lax.axis_index("batch")
-    shapes = segment_shapes(SPLITS)
-    counts = []
-    for shape in shapes:
-        count = 1
-        for extent in shape:
-            count = count * extent
-        counts.append(count // OWNERS)
-    starts = [0]
-    for count in counts:
-        starts.append(starts[-1] + count)
     flat = params.reshape(-1, 128)
-    low = flat.astype(BF)
-    tail = lax.optimization_barrier(flat[starts[6] // 128 :]).reshape(-1)
-    cut = [tail[starts[k] - starts[6] : starts[k + 1] - starts[6]] for k in range(6, 10)]
-    rows = [low[starts[k] // 128 : starts[k + 1] // 128] for k in range(6)]
-    aux = cut[1].astype(BF).reshape(9, 2, 64, 64)
-    pieces = [
-        rows[0],
-        rows[1].reshape(128, 512),
-        rows[2],
-        rows[3].reshape(64, 512),
-        rows[4].reshape(256, 512),
-        rows[5],
-        jnp.concatenate([aux[:, 0], aux[:, 1]], axis=-1).reshape(576, 128),
-        jnp.pad(cut[0].astype(BF).reshape(16, NCLS), ((0, 0), (0, 256 - NCLS))),
-        jnp.pad(
-            cut[2].astype(BF).astype(F32).reshape(8, NCLS), ((0, 0), (0, 256 - NCLS))
-        ),
-    ]
-    width = shapes[9][1]
-    share = counts[9]
-    per_row = width // share
-    spot = jnp.zeros((2, 2048), F32)
-    spot = lax.dynamic_update_slice(
-        spot,
-        cut[3].astype(BF).astype(F32).reshape(1, share),
-        (me // per_row, (me % per_row) * share),
-    )
     marked = jnp.where(valid > 0, labels, -1).astype(F32).reshape(CELLS, 1)
-    outs = whole_step(
-        sizes,
-        jnp.broadcast_to(marked, (CELLS, 128)),
-        features.reshape(CELLS, -1),
-        spot.reshape(32, 128),
-        pieces,
-    )
-    gain_grad = lax.dynamic_slice(
-        outs[4].reshape(2, 2048)[:, :width].reshape(-1), (me * share,), (share,)
-    )
-    aux_grad = outs[1].reshape(9, 64, 2, 64).transpose(0, 2, 1, 3)
-    tail_grad = jnp.concatenate(
-        [
-            outs[2][:, :NCLS].reshape(-1),
-            aux_grad.reshape(-1),
-            outs[3][:, :NCLS].reshape(-1),
-            gain_grad,
-        ]
-    ).reshape(-1, 128)
-    grad_share = lax.dynamic_update_slice(outs[0], tail_grad, (starts[6] // 128, 0))
-    misc = outs[5]
-    grad_norm = jnp.sqrt(jnp.sum(misc[0]))
-    scale = jnp.minimum(1.0, 0.05 / (grad_norm + 1e-06))
+    grad, shift_grad, misc = whole_step(
+        sizes, jnp.broadcast_to(marked, (CELLS, 128)), features.reshape(CELLS, -1), flat
+    )
+    news = update(
+        misc,
+        grad,
+        flat,
+        first_moment.reshape(-1, 128),
+        squared_mean.reshape(-1, 128),
+        average.reshape(-1, 128),
+    )
     new_params, new_first, new_second, new_average = [
-        item.reshape(params.shape)
-        for item in update(
-            scale,
-            grad_share,
-            flat,
-            first_moment.reshape(-1, 128),
-            squared_mean.reshape(-1, 128),
-            average.reshape(-1, 128),
-        )
+        item.reshape(params.shape) for item in news[:4]
     ]
     return (
         new_params,
@@ -2131,10 +2199,10 @@
         new_second,
         new_average,
         new_params.astype(BF),
-        grad_norm,
-        jnp.sum(misc[1]),
-        misc[2, 0],
-        outs[4][30],
+        news[4].reshape(()),
+        news[5].reshape(()),
+        news[6].reshape(()),
+        shift_grad.reshape(128),
     )
 
 

time: 401 us -> 376 us (0.938)
  Pallas kernels: 366 us -> 354 us
  other arithmetic: 13.4 us -> 8.25 us
  local copies, waits for them, and re-layouts: 17.4 us -> 12.7 us
    unnamed x0 -> x15, local copies, waits for them, and re-layouts: none -> 11.8 us
    pallas_call x1, Pallas kernels: 18.8 us -> 9.72 us  [update(): pl.pallas_call(update_kernel, grid=(pl.cdiv(rows, 1024),), out_shape=[big...]
    reshape x11 -> x0, local copies, waits for them, and re-layouts: 6.79 us -> none  [the longest x2 1.37 us: local_fast(): aux_grad = outs[1].reshape(9, 64, 2, 64).transpose(0, 2, 1, 3)]
    slice x12 -> x0, local copies, waits for them, and re-layouts: 4.83 us -> none  [the longest x6 2.41 us: local_fast(): rows = [low[starts[k] // 128:starts[k + 1] // 128] for k in range(6)]]
where the time goes in v7:
time: 376 us
  Pallas kernels  354 us (94%)
  local copies, waits for them, and re-layouts  12.7 us (3%)
  other arithmetic  8.25 us (2%)
    pallas_call x1, Pallas kernels, whole_step(): pl.pallas_call(functools.partial(step_kernel, tuple(plan)), out_shape=[ja...  344 us
    unnamed x15, local copies, waits for them, and re-layouts  11.8 us
    pallas_call x1, Pallas kernels, update(): pl.pallas_call(update_kernel, grid=(pl.cdiv(rows, 1024),), out_shape=[big...  9.72 us
    convert_element_type x1, other arithmetic, local_fast(): new_params.astype(BF)  7.52 us

profile of v7, /device:TPU:0, one launch (start us, length us, event | category | flops | bytes accessed | tf_op | source)
XLA Modules:
  0.0 375.8 jit_solution(13368115105015770194)
XLA Ops:
  0.6 0.7 select_convert_fusion
  1.4 0.1 broadcast_in_dim.12
  1.5 0.9 broadcast_in_dim.13.refs_1_
  2.3 344.4 %whole_step.1 = (f32[7712,128]{1,0:T(8,128)}, f32[1,128]{1,0:T(1,128)}, f32[8,128]{1,0:T(8,128)}) custom-call(s32[1,2]{1,0:T(1,128)} %refs_0_.1, f32[576,128]{1,0:T(8,128)} %broadcast_in_dim.13.refs_1_, bf16[576,256]{1,0:T(8,128)(2,1)} %bitcast.20, f32[7712,128]{1,0:T(8,128)} %bitcast.13), custom_call_target="tpu_custom_call" | custom-call | tf_op jit(solution)/shard_map/whole_step/pallas_call | solution.py:2123
  346.8 0.0 copy-start
  346.8 2.1 copy-done
  348.9 0.0 copy-start.1
  348.9 2.1 copy-done.1
  351.0 0.0 copy-start.2
  351.0 2.1 copy-done.2
  353.1 0.0 copy-start.3
  353.1 2.1 copy-done.3
  355.2 0.0 copy-start.4
  355.2 2.1 copy-done.4
  357.3 0.0 copy-start.5
  357.3 0.7 copy-done.5
  358.0 9.7 %update.1 = (f32[7712,128]{1,0:T(8,128)}, f32[7712,128]{1,0:T(8,128)}, f32[7712,128]{1,0:T(8,128)}, f32[7712,128]{1,0:T(8,128)}, f32[1,1]{1,0:T(1,128)}, /*index=5*/f32[1,1]{1,0:T(1,128)}, f32[1,1]{1,0:T(1,128)}) custom-call(f32[8,128]{1,0:T(8,128)S(1)} %copy-done.5, f32[7712,128]{1,0:T(8,128)S(1)} %copy-done.4, f32[7712,128]{1,0:T(8,128)S(1)} %bitcast.14, ...), custom_call_target="tpu_custom_call" | custom-call | tf_op jit(solution)/shard_map/update/pallas_call | solution.py:2164
  367.7 0.0 copy-start.6
  367.7 7.5 %convert_element_type.15 = bf16[1,987136]{1,0:T(2,128)(2,1)} convert(f32[1,987136]{1,0:T(1,128)} %bitcast.18) | non-fusion elementwise | flops 987136 | bytes 5922816 | tf_op jit(solution)/shard_map/convert_element_type | solution.py:2201
  375.3 0.0 copy-done.6
  375.3 0.5 copy.18
Async XLA Ops:
  346.8 2.1 copy-start
  348.9 2.1 copy-start.1
  351.0 2.1 copy-start.2
  353.1 2.1 copy-start.3
  355.2 2.1 copy-start.4
  357.3 0.7 copy-start.5
  367.7 7.5 %copy-start.6 = (f32[1,128]{1,0:T(1,128)S(1)}, f32[1,128]{1,0:T(1,128)}, u32[]{:S(2)}) copy-start(f32[1,128]{1,0:T(1,128)} %get-tuple-element.28) | copy-start | bytes 1540

commit v8 on v7

--- a/solution.py
+++ b/solution.py
@@ -520,6 +520,8 @@
         recv_b=((SPLITS, BINS, 128), BF),
         all_b=((OWNERS, BINS, 128), BF),
         act_b=((SPLITS, OWNERS * BINS, 128), BF),
+        pick_t=((CELLS, 128), BF),
+        z_cat=((9, 128, 128), BF),
         zsum=((2, OWNERS * BINS, 128), F32),
         z_send=((OWNERS, 2, BINS, 128), BF),
         z_recv=((OWNERS, 2, BINS, 128), BF),
@@ -558,7 +560,7 @@
     return plan
 
 
-SYNCS = dict(one=8, two=8, three=16, five=8, aux=8, b1=8, b3=8, b4=16, b5=8, b6=8, end=8)
+SYNCS = dict(one=8, two=8, three=16, five=8, aux=8, b1=8, b2=8, b3=8, b4=16, b5=8, b6=8, end=8)
 PARTS = dict(
     r=(128, 128, BF),
     s=(128, 512, BF),
@@ -928,14 +930,17 @@
 
     class Spread:
 
-        def __init__(self, buf):
-            self.buf = buf
+        def __init__(self, buf, lanes_=None):
+            self.buf, self.lanes = buf, lanes_
             self.send, self.recv = take(SPLITS), take(SPLITS)
+
+        def view(self, slot):
+            return self.buf.at[slot] if self.lanes is None else self.buf.at[slot, :, self.lanes]
 
         def copy(self, k, slot):
             return remote(
-                self.buf.at[slot],
-                self.buf.at[slot],
+                self.view(slot),
+                self.view(slot),
                 self.send + k,
                 self.recv + slot,
                 {TENSOR: lax.rem(t + k, SPLITS)},
@@ -1049,6 +1054,7 @@
     for spot, value in picks:
         v.table[spot : spot + 1, :] = value
     v.pick[...] = v.table[...].astype(BF)
+    v.pick_t[...] = jnp.concatenate([v.pick[...], v.pick[...]], axis=0).T
     zeros_edge = jnp.zeros((EDGE, 128), F32)
     for tap in range(9):
         v.pad[tap, 0:EDGE, :] = zeros_edge
@@ -1379,20 +1385,15 @@
     ex.start()
     g_u.forward(3)
     g_u.start_near(4)
-    g_a.start_far()
     joined_copy(1, t_core, t_core).wait_recv()
     joined_copy(2, t_diag, t_core).wait_recv()
     for k in range(SPLITS):
         v.joined_t[k] = v.joined[k].T
     g_u.forward(4)
-    g_a.start_near()
     g_c.forward()
     g_ac.forward()
     ex.wait()
     g_u.finish()
-    g_a.forward()
-
-    pick2 = jnp.concatenate([v.pick[...], v.pick[...]], axis=0)
 
     def tap_z(tap):
         if tap == 0:
@@ -1401,11 +1402,17 @@
             return v.z_recv[7, 1].astype(F32)
         return v.z_recv[tap, 0].astype(F32) + v.z_recv[tap - 1, 1].astype(F32)
 
+    for tap in range(9):
+        z = tap_z(tap)
+        high_z = z.astype(BF)
+        v.z_cat[tap, :BINS, :] = high_z
+        v.z_cat[tap, BINS:, :] = (z - high_z.astype(F32)).astype(BF)
+
     def full_joined():
-        return jnp.concatenate([v.joined[k] for k in range(SPLITS)], axis=1)
+        return jnp.concatenate([v.joined[k] for k in range(SPLITS)] + [v.pick_t[...]], axis=1)
 
     def w_tap(tap):
-        return v.w_u[rows_at(tap, 2048), :]
+        return jnp.concatenate([v.w_u[rows_at(tap, 2048), :], v.z_cat[tap]], axis=0)
 
     def unite_pair(p):
         value = dot(full_joined(), jnp.concatenate([w_tap(2 * p), w_tap(2 * p + 1)], axis=1))
@@ -1414,20 +1421,80 @@
 
     loop(4, unite_pair)
     v.pad[8, EDGE : EDGE + CELLS, :] = dot(full_joined(), w_tap(8))
-    for tap in range(9):
-        z = tap_z(tap)
-        high_z = z.astype(BF)
-        low_z = (z - high_z.astype(F32)).astype(BF)
-        v.pad[tap, EDGE : EDGE + CELLS, :] = v.pad[tap, EDGE : EDGE + CELLS, :] + dot_tn(
-            pick2, jnp.concatenate([high_z, low_z], axis=0)
-        )
     for at in range(0, CELLS, BLOCK):
         v.pre_u[at : at + BLOCK, :] = shift_sum(range(9), 1, at, lambda tap: tap)
     sync = Sync(v.sync_five)
     sync.start(list(masked_sums(v.pre_u)))
     pool_move.start()
-    for item in (g_a, g_c, g_ac):
+    g_a.start_far()
+    g_a.start_near()
+    for item in (g_c, g_ac):
         item.finish()
+    for item in (g_gain, g_r, g_s, g_m, g_e, g_b0, g_b1, g_c, g_ac, g_u):
+        item.drain()
+    joined_copy(0, t, t_x).wait_send()
+    joined_copy(1, t, t_core).wait_send()
+    joined_copy(2, t_x, t_core).wait_send()
+    w_ac = jnp.concatenate([v.w_ac[...], jnp.zeros((64, 256), F32)], axis=0).astype(BF)
+    sums = sync.wait()
+    norm_u = moments(sums[0:1], sums[1:2], count)
+
+    def make_u(k):
+        at = rows_at(k, 96)
+        v.united[at, :] = jax.nn.silu(gamma(14) * normed(v.pre_u, at, norm_u) + beta(14)).astype(BF)
+
+    loop(6, make_u)
+    class Band:
+        def __init__(self, at):
+            self.at = at
+            self.ex = Exchange(
+                TENSOR,
+                SPLITS,
+                lambda o: v.logit_send.at[rows_at(o, 144), at],
+                lambda s: v.logit_recv.at[s, :, at],
+            )
+            self.back = Spread(v.slope_in, at)
+
+        def start(self, value):
+            v.logit_send[:, self.at] = value.astype(BF)
+            self.ex.start()
+            v.logit_recv[t, :, self.at] = v.logit_send[rows_at(t, 144), self.at]
+
+        def finish(self, factor):
+            self.ex.wait()
+            logits = v.logit_recv[0, :, self.at].astype(F32)
+            for k in range(1, SPLITS):
+                logits = logits + v.logit_recv[k, :, self.at].astype(F32)
+            class_weight, loss_weight = class_weights()
+            hot = jnp.where(wide(v.lab[rows_at(t, 144), :], 2) == lanes, 1.0, 0.0)
+            cell_weight = factor * jnp.sum(hot * class_weight, axis=1, keepdims=True)
+            value = jnp.where(lanes < float(NCLS), logits, -1e30)
+            value = value - jnp.max(value, axis=1, keepdims=True)
+            powers = jnp.exp(value)
+            mass = jnp.sum(powers, axis=1, keepdims=True)
+            loss_rows = total(fold(-cell_weight * hot * (value - jnp.log(mass))))
+            grad = cell_weight * (powers / mass - hot) / loss_weight
+            v.slope_in[t, :, self.at] = grad.astype(BF)
+            self.back.start()
+            return loss_rows[:, :128] + loss_rows[:, 128:]
+
+        def grad(self):
+            self.back.wait()
+            return v.slope_in[:, :, self.at].reshape(CELLS, 256)
+
+    def class_weights():
+        total_valid = jnp.sum(class_count, axis=1, keepdims=True)
+        weight = total_valid / (NCLS * class_count + total_valid)
+        whole = jnp.sum(class_count * weight, axis=1, keepdims=True)
+        return jnp.where(lanes < float(NCLS), weight, 0.0), whole
+
+    main_head, aux_head = Band(slice(0, 256)), Band(slice(256, 512))
+    main_head.start(dot(v.united[...], v.w_c[...]))
+    g_a.forward()
+    o_misc[1:2, :] = main_head.finish(1.0)
+
+    g_a.finish()
+    g_a.drain()
 
     def unpack(chunk):
         for pair in range(5):
@@ -1459,71 +1526,8 @@
 
     sync_a = Sync(v.sync_aux)
     sync_a.start(list(masked_sums(v.pre_a)))
-    for item in (g_gain, g_r, g_s, g_a, g_m, g_e, g_b0, g_b1, g_c, g_ac, g_u):
-        item.drain()
-    joined_copy(0, t, t_x).wait_send()
-    joined_copy(1, t, t_core).wait_send()
-    joined_copy(2, t_x, t_core).wait_send()
-    w_ac = jnp.concatenate([v.w_ac[...], jnp.zeros((64, 256), F32)], axis=0).astype(BF)
-    sums = sync.wait()
-    norm_u = moments(sums[0:1], sums[1:2], count)
-
-    def make_u(k):
-        at = rows_at(k, 96)
-        v.united[at, :] = jax.nn.silu(gamma(14) * normed(v.pre_u, at, norm_u) + beta(14)).astype(BF)
-
-    loop(6, make_u)
-    v.logit_send[:, :256] = dot(v.united[...], v.w_c[...]).astype(BF)
-    sums = sync_a.wait()
-    norm_a = moments(sums[0:1], sums[1:2], count)
-
-    def make_a(k):
-        at = rows_at(k, 96)
-        v.act_a[at, :] = jax.nn.silu(gamma(15) * normed(v.pre_a, at, norm_a) + beta(15)).astype(BF)
-
-    loop(6, make_a)
-
-    v.logit_send[:, 256:] = dot(v.act_a[...], w_ac).astype(BF)
-    ex = Exchange(
-        TENSOR,
-        SPLITS,
-        lambda o: v.logit_send.at[rows_at(o, 144), :],
-        lambda s: v.logit_recv.at[s],
-    )
-    ex.start()
-    v.logit_recv[t] = v.logit_send[rows_at(t, 144), :]
-    total_valid = jnp.sum(class_count, axis=1, keepdims=True)
-    class_weight = total_valid / (NCLS * class_count + total_valid)
-    loss_weight = jnp.sum(class_count * class_weight, axis=1, keepdims=True)
-    class_weight = jnp.where(lanes < float(NCLS), class_weight, 0.0)
-    hot = jnp.where(wide(v.lab[rows_at(t, 144), :], 2) == lanes, 1.0, 0.0)
-    cell_weight = jnp.sum(hot * class_weight, axis=1, keepdims=True)
-    ex.wait()
-    logits = v.logit_recv[0].astype(F32)
-    for k in range(1, SPLITS):
-        logits = logits + v.logit_recv[k].astype(F32)
-
-    def log_softmax(value):
-        value = jnp.where(lanes < float(NCLS), value, -1e30)
-        value = value - jnp.max(value, axis=1, keepdims=True)
-        powers = jnp.exp(value)
-        mass = jnp.sum(powers, axis=1, keepdims=True)
-        return value - jnp.log(mass), powers / mass
-
-    log_main, p_main = log_softmax(logits[:, :256])
-    log_aux, p_aux = log_softmax(logits[:, 256:])
-    loss_rows = total(fold(-cell_weight * hot * (log_main + 0.4 * log_aux)))
-    loss_local = loss_rows[:, :128] + loss_rows[:, 128:]
-    o_misc[1:2, :] = loss_local
-    v.slope_in[t, :, :256] = (cell_weight * (p_main - hot) / loss_weight).astype(BF)
-    v.slope_in[t, :, 256:] = (0.4 * cell_weight * (p_aux - hot) / loss_weight).astype(BF)
-    spread_g = Spread(v.slope_in)
-    spread_g.start()
-    spread_g.wait()
-    g_main = v.slope_in[:, :, :256].reshape(CELLS, 256)
-    g_aux = v.slope_in[:, :, 256:].reshape(CELLS, 256)
+    g_main = main_head.grad()
     v.d_f[...] = dot_nt(g_main, v.w_c[...])
-    v.d_f2[...] = dot_nt(g_aux, w_ac)
 
     def slope(value):
         gate = jax.nn.sigmoid(value)
@@ -1547,9 +1551,16 @@
 
     gain_grads = {}
     sync = Sync(v.sync_b1)
-    sync.start(
-        through_silu(v.d_f, v.pre_u, norm_u, 14) + through_silu(v.d_f2, v.pre_a, norm_a, 15)
-    )
+    sync.start(through_silu(v.d_f, v.pre_u, norm_u, 14))
+    sums = sync_a.wait()
+    norm_a = moments(sums[0:1], sums[1:2], count)
+
+    def make_a(k):
+        at = rows_at(k, 96)
+        v.act_a[at, :] = jax.nn.silu(gamma(15) * normed(v.pre_a, at, norm_a) + beta(15)).astype(BF)
+
+    loop(6, make_a)
+    aux_head.start(dot(v.act_a[...], w_ac))
 
     class Scatter:
         def __init__(self, first, second, full, rows, out, base=0):
@@ -1734,12 +1745,9 @@
     s_u = ScatterUnite()
 
     v.w_c[...] = dot_tn(v.united[...], g_main).astype(BF)
-    v.w_ac[...] = dot_tn(v.act_a[...], g_aux)[:64]
     s_c.start()
-    s_ac.start()
     sums = sync.wait()
     gain_grads[14] = (sums[1:2], sums[0:1])
-    gain_grads[15] = (sums[3:4], sums[2:3])
 
     def spread_taps(ref, pre, norm, row, first, second):
         def step(k):
@@ -1796,6 +1804,7 @@
     dm_near(1, t_diag).start()
     merged_back(t_core)
     dm_near(0, t_core).start()
+    o_misc[1:2, :] = o_misc[1:2, :] + aux_head.finish(0.4)
     ex_dz.wait()
 
     d_act = v.d_sum.at[0 : OWNERS * BINS, :]
@@ -1819,6 +1828,12 @@
     ex.start()
     merged_back(t_x)
     merged_back(t)
+    g_aux = aux_head.grad()
+    v.d_f2[...] = dot_nt(g_aux, w_ac)
+    sync_a = Sync(v.sync_b2)
+    sync_a.start(through_silu(v.d_f2, v.pre_a, norm_a, 15))
+    v.w_ac[...] = dot_tn(v.act_a[...], g_aux)[:64]
+    s_ac.start()
 
     def unite_grad(c):
         for p in range(5):
@@ -1852,7 +1867,9 @@
     dm_far.start()
     s_u.start(1)
 
-    spread_taps(v.d_f2, v.pre_a, norm_a, 15, sums[2:3], sums[3:4])
+    sums = sync_a.wait()
+    gain_grads[15] = (sums[1:2], sums[0:1])
+    spread_taps(v.d_f2, v.pre_a, norm_a, 15, sums[0:1], sums[1:2])
     for p in range(5):
         for at in range(0, CELLS, 96):
             value = back_tap(2 * p, 1, at)
@@ -2112,7 +2129,7 @@
     for k in range(1, SPLITS):
         ends = ends + v.end_t[k]
     o_misc[...] = ends
-    o_misc[2:3, :] = jnp.broadcast_to(loss_weight, (1, 128))
+    o_misc[2:3, :] = jnp.broadcast_to(class_weights()[1], (1, 128))
 
 
 def whole_step(sizes, labels, feat, flat):
@@ -2167,7 +2184,7 @@
         out_shape=[big] * 4 + [jax.ShapeDtypeStruct((1, 1), F32)] * 3,
         in_specs=[whole] + [block] * 5,
         out_specs=[block] * 4 + [one] * 3,
-        compiler_params=pltpu.CompilerParams(vmem_limit_bytes=32 * 1024 * 1024),
+        compiler_params=pltpu.CompilerParams(vmem_limit_bytes=60 * 1024 * 1024),
         name="update",
     )(misc, grad, param, first, second, average)
 

time: 376 us -> 365 us (0.971)
  local copies, waits for them, and re-layouts: 12.7 us -> 1.45 us
    unnamed x15 -> x3, local copies, waits for them, and re-layouts: 11.8 us -> 0.52 us
    pallas_call x1, Pallas kernels: 9.72 us -> 17.2 us  [update(): pl.pallas_call(update_kernel, grid=(pl.cdiv(rows, 1024),), out_shape=[big...]
    pallas_call x1, Pallas kernels: 344 us -> 337 us  [whole_step(): pl.pallas_call(functools.partial(step_kernel, tuple(plan)), out_shape=[ja...]
where the time goes in v8:
time: 365 us
  Pallas kernels  354 us (97%)
  other arithmetic  8.26 us (2%)
    pallas_call x1, Pallas kernels, whole_step(): pl.pallas_call(functools.partial(step_kernel, tuple(plan)), out_shape=[ja...  337 us
    pallas_call x1, Pallas kernels, update(): pl.pallas_call(update_kernel, grid=(pl.cdiv(rows, 1024),), out_shape=[big...  17.2 us
    convert_element_type x1, other arithmetic, local_fast(): new_params.astype(BF)  7.53 us

profile of v8, /device:TPU:0, one launch (start us, length us, event | category | flops | bytes accessed | tf_op | source)
XLA Modules:
  0.0 364.6 jit_solution(6404438615928636483)
XLA Ops:
  0.6 0.7 select_convert_fusion
  1.4 0.1 broadcast_in_dim.12
  1.5 0.9 broadcast_in_dim.13.refs_1_
  2.3 337.1 %whole_step.1 = (f32[7712,128]{1,0:T(8,128)}, f32[1,128]{1,0:T(1,128)}, f32[8,128]{1,0:T(8,128)}) custom-call(s32[1,2]{1,0:T(1,128)} %refs_0_.1, f32[576,128]{1,0:T(8,128)} %broadcast_in_dim.13.refs_1_, bf16[576,256]{1,0:T(8,128)(2,1)} %bitcast.20, f32[7712,128]{1,0:T(8,128)} %bitcast.13), custom_call_target="tpu_custom_call" | custom-call | tf_op jit(solution)/shard_map/whole_step/pallas_call | solution.py:2140
  339.4 17.2 %update.1 = (f32[7712,128]{1,0:T(8,128)}, f32[7712,128]{1,0:T(8,128)}, f32[7712,128]{1,0:T(8,128)}, f32[7712,128]{1,0:T(8,128)}, f32[1,1]{1,0:T(1,128)}, /*index=5*/f32[1,1]{1,0:T(1,128)}, f32[1,1]{1,0:T(1,128)}) custom-call(f32[8,128]{1,0:T(8,128)} %get-tuple-element.19.misc, f32[7712,128]{1,0:T(8,128)} %get-tuple-element.20.grad, f32[7712,128]{1,0:T(8,128)} %bitcast.14, ...), custom_call_target="tpu_custom_call" | custom-call | tf_op jit(solution)/shard_map/update/pallas_call | solution.py:2181
  356.6 0.0 copy-start
  356.6 7.5 %convert_element_type.15 = bf16[1,987136]{1,0:T(2,128)(2,1)} convert(f32[1,987136]{1,0:T(1,128)} %bitcast.18) | non-fusion elementwise | flops 987136 | bytes 5922816 | tf_op jit(solution)/shard_map/convert_element_type | solution.py:2218
  364.1 0.0 copy-done
  364.1 0.5 copy.18
Async XLA Ops:
  356.6 7.5 %copy-start = (f32[1,128]{1,0:T(1,128)S(1)}, f32[1,128]{1,0:T(1,128)}, u32[]{:S(2)}) copy-start(f32[1,128]{1,0:T(1,128)} %get-tuple-element.28) | copy-start | bytes 1540

commit v9 on v8

--- a/solution.py
+++ b/solution.py
@@ -522,6 +522,7 @@
         act_b=((SPLITS, OWNERS * BINS, 128), BF),
         pick_t=((CELLS, 128), BF),
         z_cat=((9, 128, 128), BF),
+        act_t=((512, OWNERS * BINS), BF),
         zsum=((2, OWNERS * BINS, 128), F32),
         z_send=((OWNERS, 2, BINS, 128), BF),
         z_recv=((OWNERS, 2, BINS, 128), BF),
@@ -985,7 +986,12 @@
 
     feat_keep = take(1)
     feat_local = pltpu.make_async_copy(feat, v.whole.at[t], sems.at[feat_keep])
-    feat_spread = Exchange(TENSOR, SPLITS, lambda other: feat, lambda slot: v.whole.at[slot])
+    feat_s, feat_r = take(3), take(SPLITS)
+
+    def feat_copy(k, slot, device):
+        source = feat if k < 2 else v.whole.at[slot]
+        return remote(source, v.whole.at[slot], feat_s + k, feat_r + slot, {TENSOR: device})
+
     def wide_rows(into, rows, low):
         for k in range(4):
             value = o_flat[pl.ds(low + k, rows, stride=4), :]
@@ -997,7 +1003,8 @@
         item.start_far()
         item.start_near()
     feat_local.start()
-    feat_spread.start()
+    feat_copy(0, t, t_x).start()
+    feat_copy(1, t, t_core).start()
     load(2).wait()
     v.w_m[rows_at(me, 576), :] = o_flat[640:1216, :].astype(BF)
     load(3).wait()
@@ -1073,6 +1080,8 @@
 
     for item in (g_gain, g_r):
         item.forward()
+    feat_copy(0, t_x, t_x).wait_recv()
+    feat_copy(2, t_x, t_core).start()
     load(1).wait()
     wide_rows(v.w_s, 128, 128)
     load(4).wait()
@@ -1106,7 +1115,11 @@
     for item in (g_gain, g_r):
         item.finish()
     feat_local.wait()
-    feat_spread.wait()
+    feat_copy(1, t_core, t_core).wait_recv()
+    feat_copy(2, t_diag, t_core).wait_recv()
+    feat_copy(0, t, t_x).wait_send()
+    feat_copy(1, t, t_core).wait_send()
+    feat_copy(2, t_x, t_core).wait_send()
     gain_of = [None] * 33
     for owner in range(OWNERS):
         start = 496 * (owner % 4) - 16
@@ -1371,8 +1384,7 @@
     def make_z(j):
         def body(group, side):
             kept = jnp.where(group_id == group, 1.0, 0.0)
-            rows = (full_act().astype(F32) * kept).astype(BF)
-            v.zsum[side] = v.zsum[side] + dot(rows, v.w_own[rows_at(j, 512), :])
+            v.zsum[side] = v.zsum[side] + kept * dot(full_act(), v.w_own[rows_at(j, 512), :])
 
         own_branch(j, body)
 
@@ -1385,6 +1397,7 @@
     ex.start()
     g_u.forward(3)
     g_u.start_near(4)
+    v.act_t[...] = full_act().T
     joined_copy(1, t_core, t_core).wait_recv()
     joined_copy(2, t_diag, t_core).wait_recv()
     for k in range(SPLITS):
@@ -1804,36 +1817,8 @@
     dm_near(1, t_diag).start()
     merged_back(t_core)
     dm_near(0, t_core).start()
-    o_misc[1:2, :] = o_misc[1:2, :] + aux_head.finish(0.4)
-    ex_dz.wait()
-
-    d_act = v.d_sum.at[0 : OWNERS * BINS, :]
-    d_act[...] = jnp.zeros((OWNERS * BINS, 512), F32)
-
-    def branch_back(j):
-        def body(group, side):
-            kept = jnp.where(group_id == group, 1.0, 0.0)
-            value = v.dz_recv[:, side].reshape(OWNERS * BINS, 128).astype(F32) * kept
-            value = value.astype(BF)
-            o_u[rows_at(j, 512), :] = dot_tn(full_act(), value)
-            d_act[...] = d_act[...] + dot_nt(value, v.w_own[rows_at(j, 512), :])
-
-        own_branch(j, body)
-
-    loop(9, branch_back)
-    for k in range(SPLITS):
-        v.d_act_send[k] = d_act[:, k * 128 : k * 128 + 128].astype(BF)
-    v.d_act_recv[t] = v.d_act_send[t]
-    ex = Exchange(TENSOR, SPLITS, lambda o: v.d_act_send.at[o], lambda s: v.d_act_recv.at[s])
-    ex.start()
     merged_back(t_x)
     merged_back(t)
-    g_aux = aux_head.grad()
-    v.d_f2[...] = dot_nt(g_aux, w_ac)
-    sync_a = Sync(v.sync_b2)
-    sync_a.start(through_silu(v.d_f2, v.pre_a, norm_a, 15))
-    v.w_ac[...] = dot_tn(v.act_a[...], g_aux)[:64]
-    s_ac.start()
 
     def unite_grad(c):
         for p in range(5):
@@ -1843,8 +1828,32 @@
             if p < 4:
                 v.w_u[rows_at((2 * p + 1) * MERGED + c, 512), :] = value[:, 128:].astype(BF)
 
-    loop(SPLITS, unite_grad)
+    unite_grad(0)
     s_u.start(0)
+    o_misc[1:2, :] = o_misc[1:2, :] + aux_head.finish(0.4)
+    ex_dz.wait()
+
+    d_act = v.d_sum.at[0 : OWNERS * BINS, :]
+    d_act[...] = jnp.zeros((OWNERS * BINS, 512), F32)
+
+    def branch_back(j):
+        def body(group, side):
+            kept = jnp.where(group_id == group, 1.0, 0.0)
+            value = v.dz_recv[:, side].reshape(OWNERS * BINS, 128).astype(F32) * kept
+            value = value.astype(BF)
+            o_u[rows_at(j, 512), :] = dot(v.act_t[...], value)
+            d_act[...] = d_act[...] + dot_nt(value, v.w_own[rows_at(j, 512), :])
+
+        own_branch(j, body)
+
+    loop(9, branch_back)
+    for k in range(SPLITS):
+        v.d_act_send[k] = d_act[:, k * 128 : k * 128 + 128].astype(BF)
+    v.d_act_recv[t] = v.d_act_send[t]
+    ex = Exchange(TENSOR, SPLITS, lambda o: v.d_act_send.at[o], lambda s: v.d_act_recv.at[s])
+    ex.start()
+    unite_grad(1)
+    s_u.start(1)
     dm_near(1, t_x).wait_recv()
 
     def add_x(k):
@@ -1854,6 +1863,16 @@
 
     loop(12, add_x)
     dm_far = remote(v.joined.at[t_x], v.dm_far, far_s, far_r, {TENSOR: t_x})
+    dm_far.start()
+    g_aux = aux_head.grad()
+    v.d_f2[...] = dot_nt(g_aux, w_ac)
+    sync_a = Sync(v.sync_b2)
+    sync_a.start(through_silu(v.d_f2, v.pre_a, norm_a, 15))
+    v.w_ac[...] = dot_tn(v.act_a[...], g_aux)[:64]
+    s_ac.start()
+
+    unite_grad(2)
+    unite_grad(3)
     ex.wait()
     for k in range(OWNERS):
         at = slice(k * BINS, k * BINS + BINS)
@@ -1864,8 +1883,8 @@
     v.d_img_recv[me] = v.d_img_send[me]
     ex = Exchange(BATCH, OWNERS, lambda o: v.d_img_send.at[o], lambda s: v.d_img_recv.at[s])
     ex.start()
-    dm_far.start()
-    s_u.start(1)
+    s_u.start(2)
+    s_u.middle(0)
 
     sums = sync_a.wait()
     gain_grads[15] = (sums[1:2], sums[0:1])
@@ -1893,7 +1912,6 @@
                     v.w_a[rows_at((2 * p + 1) * 8 + c, 64), :] = odd.astype(BF)
 
     loop(SPLITS, aux_grad)
-    s_u.middle(0)
     ex.wait()
     d_b = v.d_img_recv[0].astype(F32)
     for k in range(1, OWNERS):
@@ -1905,7 +1923,8 @@
         [total(d_b * group_mask(g)) for g in range(4)]
         + [total(d_b * unit_b * group_mask(g)) for g in range(4)]
     )
-    s_u.start(2)
+    s_u.start(3)
+    s_u.middle(1)
     sums = sync.wait()
     first_b = jnp.zeros((BINS, 128), F32)
     second_b = jnp.zeros((BINS, 128), F32)
@@ -1918,8 +1937,8 @@
     v.d_bp[t] = (gamma_b * scale_b * inner).astype(BF)
     spread_d = Spread(v.d_bp)
     spread_d.start()
-    s_u.start(3)
-    s_u.middle(1)
+    s_u.start(4)
+    s_u.middle(2)
     spread_d.wait()
     d_bp_move = ToGroup(
         lambda owner, rows: v.d_bp.at[:, 0:rows, :],
@@ -1952,8 +1971,8 @@
     three = [total(item) for item in lax.fori_loop(0, 12, through_sum, (zero, zero, zero))]
     sync = Sync(v.sync_b4)
     sync.start(split_rows(three[0]) + split_rows(three[1]) + split_rows(three[2]))
-    s_u.start(4)
-    s_u.middle(2)
+    s_a.start()
+    s_u.middle(3)
     sums = sync.wait()
     first_s = join_rows(sums, 0, 4)
     second_e, second_s = join_rows(sums, 4, 4), join_rows(sums, 8, 4)
@@ -1995,8 +2014,12 @@
         loop(6, step)
 
     ex = back_hidden(v.d_e[...], v.w_e[...], 0)
-    s_a.start()
-    s_u.middle(3)
+    def short_grad(c):
+        v.w_s[rows_at(c, 256), :] = dot_tn(v.whole[c], v.d_s[...]).astype(BF)
+
+    loop(SPLITS, short_grad)
+    s_s.start()
+    s_u.middle(4)
     for k in range(SPLITS):
         v.w_e[k * 128 : k * 128 + 128, :] = dot_tn(v.h2[k], v.d_e[...]).astype(BF)
     ex.wait()
@@ -2006,7 +2029,7 @@
     s_e.start()
     s_c.middle()
     s_ac.middle()
-    s_u.middle(4)
+    s_a.middle()
     sums = sync.wait()
     gain_grads[5] = (sums[1:2], sums[0:1])
     spread_taps(v.d_f, v.pre_m, norm_m, 5, sums[0:1], sums[1:2])
@@ -2014,26 +2037,20 @@
     weight = jnp.concatenate([v.w_m[tap * 512 : tap * 512 + 512, :] for tap in range(9)], axis=1)
     ex = back_hidden(v.cat_u[...], weight, 1)
 
-    def short_grad(c):
-        v.w_s[rows_at(c, 256), :] = dot_tn(v.whole[c], v.d_s[...]).astype(BF)
-
-    loop(SPLITS, short_grad)
-    s_s.start()
-    s_a.middle()
+    def middle_grad(k):
+        value = dot_tn(v.h1[k], v.cat_u[...])
+        for tap in range(9):
+            v.w_m[rows_at(tap * 4 + k, 128), :] = value[:, tap * 128 : tap * 128 + 128].astype(BF)
+
+    loop(SPLITS, middle_grad)
+    s_m.start()
+    s_s.middle()
     ex.wait()
     hidden_sum(1)
     sync = Sync(v.sync_b6)
     sync.start(through_silu(v.d_f, v.pre_r, norm_r, 0))
 
-    def middle_grad(k):
-        value = dot_tn(v.h1[k], v.cat_u[...])
-        for tap in range(9):
-            v.w_m[rows_at(tap * 4 + k, 128), :] = value[:, tap * 128 : tap * 128 + 128].astype(BF)
-
-    loop(SPLITS, middle_grad)
-    s_m.start()
     s_e.middle()
-    s_s.middle()
     sums = sync.wait()
     gain_grads[0] = (sums[1:2], sums[0:1])
 

time: 365 us -> 363 us (level)
  no operation moved by 1% of the time
where the time goes in v9:
time: 363 us; the launch traced here: 362 us
  Pallas kernels  352 us (97%)
  other arithmetic  8.26 us (2%)
    pallas_call x1, Pallas kernels, whole_step(): pl.pallas_call(functools.partial(step_kernel, tuple(plan)), out_shape=[ja...  335 us
    pallas_call x1, Pallas kernels, update(): pl.pallas_call(update_kernel, grid=(pl.cdiv(rows, 1024),), out_shape=[big...  17.2 us
    convert_element_type x1, other arithmetic, local_fast(): new_params.astype(BF)  7.53 us

profile of v9, /device:TPU:0, one launch (start us, length us, event | category | flops | bytes accessed | tf_op | source)
XLA Modules:
  0.0 362.3 jit_solution(6104691029618495988)
XLA Ops:
  0.6 0.7 select_convert_fusion
  1.4 0.1 broadcast_in_dim.12
  1.5 0.9 broadcast_in_dim.13.refs_1_
  2.3 334.7 %whole_step.1 = (f32[7712,128]{1,0:T(8,128)}, f32[1,128]{1,0:T(1,128)}, f32[8,128]{1,0:T(8,128)}) custom-call(s32[1,2]{1,0:T(1,128)} %refs_0_.1, f32[576,128]{1,0:T(8,128)} %broadcast_in_dim.13.refs_1_, bf16[576,256]{1,0:T(8,128)(2,1)} %bitcast.20, f32[7712,128]{1,0:T(8,128)} %bitcast.13), custom_call_target="tpu_custom_call" | custom-call | tf_op jit(solution)/shard_map/whole_step/pallas_call | solution.py:2157
  337.1 17.2 %update.1 = (f32[7712,128]{1,0:T(8,128)}, f32[7712,128]{1,0:T(8,128)}, f32[7712,128]{1,0:T(8,128)}, f32[7712,128]{1,0:T(8,128)}, f32[1,1]{1,0:T(1,128)}, /*index=5*/f32[1,1]{1,0:T(1,128)}, f32[1,1]{1,0:T(1,128)}) custom-call(f32[8,128]{1,0:T(8,128)} %get-tuple-element.19.misc, f32[7712,128]{1,0:T(8,128)} %get-tuple-element.20.grad, f32[7712,128]{1,0:T(8,128)} %bitcast.14, ...), custom_call_target="tpu_custom_call" | custom-call | tf_op jit(solution)/shard_map/update/pallas_call | solution.py:2198
  354.3 0.0 copy-start
  354.3 7.5 %convert_element_type.15 = bf16[1,987136]{1,0:T(2,128)(2,1)} convert(f32[1,987136]{1,0:T(1,128)} %bitcast.18) | non-fusion elementwise | flops 987136 | bytes 5922816 | tf_op jit(solution)/shard_map/convert_element_type | solution.py:2235
  361.8 0.0 copy-done
  361.8 0.5 copy.18
Async XLA Ops:
  354.3 7.5 %copy-start = (f32[1,128]{1,0:T(1,128)S(1)}, f32[1,128]{1,0:T(1,128)}, u32[]{:S(2)}) copy-start(f32[1,128]{1,0:T(1,128)} %get-tuple-element.28) | copy-start | bytes 1540

commit v10 on v9

--- a/solution.py
+++ b/solution.py
@@ -652,7 +652,11 @@
             device_id_type=MESH,
         )
 
-    late = []
+    def mix(*lists):
+        for turn in range(max(len(items) for items in lists)):
+            for items in lists:
+                if turn < len(items):
+                    items[turn]()
 
     load_at = take(len(LOADS))
 
@@ -718,19 +722,23 @@
                 {BATCH: partner},
             )
 
-        def start_far(self):
-            if self.piece is not None:
-                self.local().start()
-            for step in range(1, HALF):
+        def fars(self):
+            def go(step):
+                if step == 1 and self.piece is not None:
+                    self.local().start()
                 self.far(step).start()
 
-        def start_near(self):
-            self.near().start()
-
-        def forward(self):
-            for step in range(1, HALF):
+            return [functools.partial(go, step) for step in range(1, HALF)]
+
+        def nears(self):
+            return [lambda: self.near().start()]
+
+        def passes(self):
+            def go(step):
                 self.passed(step, me).wait_recv()
                 self.passed(step, me).start()
+
+            return [functools.partial(go, step) for step in range(1, HALF)]
 
         def finish(self):
             for step in range(HALF):
@@ -818,25 +826,29 @@
                 {BATCH: partner},
             )
 
-        def start_far(self, slot):
-            def go():
-                self.local(slot).start()
-                for step in range(1, HALF):
-                    self.far(step, slot).start()
-
-            has(me, slot, go)
-
-        def start_near(self, slot):
-            has(me, slot, lambda: self.near(slot).start())
-
-        def forward(self, slot):
-            for step in range(1, HALF):
-
-                def go(step=step):
-                    self.passed(step, slot, me).wait_recv()
-                    self.passed(step, slot, me).start()
-
-                has(far_peer(me, step), slot, go)
+        def fars(self, slot):
+            def go(step):
+                if step == 1:
+                    self.local(slot).start()
+                self.far(step, slot).start()
+
+            return [
+                functools.partial(has, me, slot, functools.partial(go, step))
+                for step in range(1, HALF)
+            ]
+
+        def nears(self, slot):
+            return [lambda: has(me, slot, lambda: self.near(slot).start())]
+
+        def passes(self, slot):
+            def go(step):
+                self.passed(step, slot, me).wait_recv()
+                self.passed(step, slot, me).start()
+
+            return [
+                functools.partial(has, far_peer(me, step), slot, functools.partial(go, step))
+                for step in range(1, HALF)
+            ]
 
         def finish(self):
             for slot in range(SLOTS):
@@ -999,9 +1011,7 @@
 
     load(0).wait()
     v.w_r[rows_at(me, 128), :] = o_flat[0:128, :].astype(BF)
-    for item in (g_gain, g_r):
-        item.start_far()
-        item.start_near()
+    mix(g_r.nears() + g_gain.nears(), g_r.fars() + g_gain.fars())
     feat_local.start()
     feat_copy(0, t, t_x).start()
     feat_copy(1, t, t_core).start()
@@ -1009,9 +1019,7 @@
     v.w_m[rows_at(me, 576), :] = o_flat[640:1216, :].astype(BF)
     load(3).wait()
     wide_rows(v.w_e, 64, 1216)
-    for item in (g_m, g_e):
-        item.start_far()
-        item.start_near()
+    mix(g_m.nears() + g_e.nears(), g_m.fars() + g_e.fars())
     lane = lax.broadcasted_iota(jnp.int32, (1, 128), 1)
 
     def roll(value, shift):
@@ -1078,8 +1086,7 @@
     cells_local = jnp.full((1, 128), (high * across).astype(F32))
     left_half = lax.broadcasted_iota(jnp.int32, (64, 128), 1) < 64
 
-    for item in (g_gain, g_r):
-        item.forward()
+    mix(g_r.passes() + g_gain.passes())
     feat_copy(0, t_x, t_x).wait_recv()
     feat_copy(2, t_x, t_core).start()
     load(1).wait()
@@ -1198,9 +1205,7 @@
     sync = Sync(v.sync_one)
     r1, r2 = masked_sums(v.pre_r)
     sync.start([r1, r2, cells_local] + split_rows(class_local))
-    g_m.forward()
-    g_e.forward()
-    g_s.start_far()
+    mix(g_m.passes() + g_e.passes(), g_s.fars())
     sums = sync.wait()
     count = sums[2:3]
     count4 = wide(count, 4)
@@ -1218,25 +1223,29 @@
 
     loop(6, make_h1)
     spread_1.start()
-    g_s.start_near()
-    g_b0.start_far()
+    mix(g_s.nears(), g_b0.fars())
     g_m.finish()
     spread_1.wait()
 
     def full_h(ref):
         return jnp.concatenate([ref[k] for k in range(SPLITS)], axis=1)
 
-    def middle(tap):
-        v.pad[tap, EDGE : EDGE + CELLS, :] = dot(full_h(v.h1), v.w_m[rows_at(tap, 512), :])
-
-    loop(9, middle)
+    def w_middle(tap):
+        return v.w_m[rows_at(tap, 512), :]
+
+    def middle_pair(p):
+        both = jnp.concatenate([w_middle(2 * p), w_middle(2 * p + 1)], axis=1)
+        value = dot(full_h(v.h1), both)
+        v.pad[2 * p, EDGE : EDGE + CELLS, :] = value[:, :128]
+        v.pad[2 * p + 1, EDGE : EDGE + CELLS, :] = value[:, 128:]
+
+    loop(4, middle_pair)
+    v.pad[8, EDGE : EDGE + CELLS, :] = dot(full_h(v.h1), w_middle(8))
     for at in range(0, CELLS, BLOCK):
         v.pre_m[at : at + BLOCK, :] = shift_sum(range(9), 4, at, lambda tap: tap)
     sync = Sync(v.sync_two)
     sync.start(list(masked_sums(v.pre_m)))
-    g_s.forward()
-    g_b0.start_near()
-    g_b1.start_far()
+    mix(g_s.passes() + g_b0.nears(), g_b1.fars())
     sums = sync.wait()
     norm_m = moments(sums[0:1], sums[1:2], count)
     spread_2 = Spread(v.h2)
@@ -1247,9 +1256,7 @@
 
     loop(6, make_h2)
     spread_2.start()
-    g_b0.forward()
-    g_b1.start_near()
-    g_u.start_far(0)
+    mix(g_b0.passes() + g_b1.nears(), g_u.fars(0))
     g_e.finish()
     g_s.finish()
     for k in range(0, 512, 256):
@@ -1261,12 +1268,8 @@
     sync = Sync(v.sync_three)
     e1, e2 = masked_sums(v.pre_e)
     sync.start(split_rows(e1) + split_rows(e2) + split_rows(s1) + split_rows(s2))
-    g_b1.forward()
-    g_u.start_near(0)
-    g_u.start_far(1)
-    for item in (g_c, g_ac):
-        item.start_far()
-        item.start_near()
+    mix(g_b1.passes() + g_u.nears(0), g_u.fars(1))
+    mix(g_c.nears() + g_ac.nears(), g_c.fars() + g_ac.fars())
     sums = sync.wait()
     norm_e = moments(join_rows(sums, 0, 4), join_rows(sums, 4, 4), count4)
     norm_s = moments(join_rows(sums, 8, 4), join_rows(sums, 12, 4), count4)
@@ -1323,9 +1326,7 @@
     v.recv_b[t] = v.part_b[t]
     ex = Exchange(TENSOR, SPLITS, lambda o: v.part_b.at[o], lambda s: v.recv_b.at[s])
     ex.start()
-    g_u.forward(0)
-    g_u.start_near(1)
-    g_u.start_far(2)
+    mix(g_u.passes(0) + g_u.nears(1), g_u.fars(2))
     joined_copy(0, t_x, t_x).wait_recv()
     joined_copy(2, t_x, t_core).start()
     ex.wait()
@@ -1335,9 +1336,7 @@
     v.all_b[me] = own_b.astype(BF)
     ex = Exchange(BATCH, OWNERS, lambda o: v.all_b.at[me], lambda s: v.all_b.at[s])
     ex.start()
-    g_u.forward(1)
-    g_u.start_near(2)
-    g_u.start_far(3)
+    mix(g_u.passes(1) + g_u.nears(2), g_u.fars(3))
     ex.wait()
     all_b = [v.all_b[k].astype(F32) for k in range(OWNERS)]
     sum_b, square_b = all_b[0], all_b[0] * all_b[0]
@@ -1363,9 +1362,7 @@
         out = gamma_b * ((all_b[k] - mean_b) * scale_b) + beta_b
         v.act_b[t, k * BINS : k * BINS + BINS, :] = jax.nn.silu(out).astype(BF)
     spread_b.start()
-    g_u.forward(2)
-    g_u.start_near(3)
-    g_u.start_far(4)
+    mix(g_u.passes(2) + g_u.nears(3), g_u.fars(4))
     spread_b.wait()
     row_512 = lax.broadcasted_iota(jnp.int32, (OWNERS * BINS, 1), 0) & (BINS - 1)
     group_id = jnp.where(
@@ -1395,16 +1392,13 @@
     v.z_recv[me] = v.z_send[me]
     ex = Exchange(BATCH, OWNERS, lambda o: v.z_send.at[o], lambda s: v.z_recv.at[s])
     ex.start()
-    g_u.forward(3)
-    g_u.start_near(4)
+    mix(g_u.passes(3) + g_u.nears(4))
     v.act_t[...] = full_act().T
     joined_copy(1, t_core, t_core).wait_recv()
     joined_copy(2, t_diag, t_core).wait_recv()
     for k in range(SPLITS):
         v.joined_t[k] = v.joined[k].T
-    g_u.forward(4)
-    g_c.forward()
-    g_ac.forward()
+    mix(g_u.passes(4) + g_c.passes() + g_ac.passes())
     ex.wait()
     g_u.finish()
 
@@ -1439,8 +1433,7 @@
     sync = Sync(v.sync_five)
     sync.start(list(masked_sums(v.pre_u)))
     pool_move.start()
-    g_a.start_far()
-    g_a.start_near()
+    mix(g_a.nears(), g_a.fars())
     for item in (g_c, g_ac):
         item.finish()
     for item in (g_gain, g_r, g_s, g_m, g_e, g_b0, g_b1, g_c, g_ac, g_u):
@@ -1503,7 +1496,7 @@
 
     main_head, aux_head = Band(slice(0, 256)), Band(slice(256, 512))
     main_head.start(dot(v.united[...], v.w_c[...]))
-    g_a.forward()
+    mix(g_a.passes())
     o_misc[1:2, :] = main_head.finish(1.0)
 
     g_a.finish()
@@ -1602,24 +1595,24 @@
                 {BATCH: far_peer(me, step)},
             )
 
-        def start(self):
-            for step in (1, 2, 3, 0):
-                self.near(step).start()
-
-        def middle(self):
-            kind = self.first.dtype
-            for step in range(1, HALF):
+        def starts(self):
+            return [lambda step=step: self.near(step).start() for step in (1, 2, 3, 0)]
+
+        def middles(self):
+            def go(step):
                 self.near(step).wait_recv()
                 base = far_peer(me, step) * (self.rows // self.block)
 
-                def add(k, step=step, base=base):
+                def add(k):
                     at = rows_at(k, self.block)
                     value = self.full[rows_at(base + k, self.block), :].astype(F32)
                     value = value + self.first[step, at, :].astype(F32)
-                    self.first[step, at, :] = value.astype(kind)
+                    self.first[step, at, :] = value.astype(self.first.dtype)
 
                 loop(self.rows // self.block, add)
                 self.far(step).start()
+
+            return [functools.partial(go, step) for step in range(1, HALF)]
 
         def end(self):
             self.near(0).wait_recv()
@@ -1689,31 +1682,33 @@
             index = lax.div(block, 8) * MERGED + lax.rem(block, 8)
             return rows_at(index * 8 + k, 64)
 
-        def start(self, slot):
-            for step in (1, 2, 3, 0):
-                has(
-                    far_peer(partner, step),
-                    slot,
-                    lambda step=step: self.near(step, slot, partner).start(),
-                )
-
-        def middle(self, slot):
-            for step in range(1, HALF):
+        def starts(self, slot):
+            def go(step):
+                self.near(step, slot, partner).start()
+
+            return [
+                functools.partial(has, far_peer(partner, step), slot, functools.partial(go, step))
+                for step in (1, 2, 3, 0)
+            ]
+
+        def middles(self, slot):
+            def go(step):
+                self.near(step, slot, me).wait_recv()
                 owner = far_peer(me, step)
 
-                def go(step=step, owner=owner):
-                    self.near(step, slot, me).wait_recv()
-
-                    def add(k):
-                        at = rows_at(k, 64)
-                        value = v.w_u[self.own_rows(owner, slot, k), :].astype(F32)
-                        value = value + v.first_u[step, slot, at, :].astype(F32)
-                        v.first_u[step, slot, at, :] = value.astype(BF)
-
-                    loop(8, add)
-                    self.far(step, slot).start()
-
-                has(owner, slot, go)
+                def add(k):
+                    at = rows_at(k, 64)
+                    value = v.w_u[self.own_rows(owner, slot, k), :].astype(F32)
+                    value = value + v.first_u[step, slot, at, :].astype(F32)
+                    v.first_u[step, slot, at, :] = value.astype(BF)
+
+                loop(8, add)
+                self.far(step, slot).start()
+
+            return [
+                functools.partial(has, far_peer(me, step), slot, functools.partial(go, step))
+                for step in range(1, HALF)
+            ]
 
         def end(self):
             for slot in range(SLOTS):
@@ -1758,7 +1753,7 @@
     s_u = ScatterUnite()
 
     v.w_c[...] = dot_tn(v.united[...], g_main).astype(BF)
-    s_c.start()
+    mix(s_c.starts())
     sums = sync.wait()
     gain_grads[14] = (sums[1:2], sums[0:1])
 
@@ -1829,7 +1824,7 @@
                 v.w_u[rows_at((2 * p + 1) * MERGED + c, 512), :] = value[:, 128:].astype(BF)
 
     unite_grad(0)
-    s_u.start(0)
+    mix(s_u.starts(0))
     o_misc[1:2, :] = o_misc[1:2, :] + aux_head.finish(0.4)
     ex_dz.wait()
 
@@ -1853,7 +1848,7 @@
     ex = Exchange(TENSOR, SPLITS, lambda o: v.d_act_send.at[o], lambda s: v.d_act_recv.at[s])
     ex.start()
     unite_grad(1)
-    s_u.start(1)
+    mix(s_u.starts(1))
     dm_near(1, t_x).wait_recv()
 
     def add_x(k):
@@ -1869,7 +1864,7 @@
     sync_a = Sync(v.sync_b2)
     sync_a.start(through_silu(v.d_f2, v.pre_a, norm_a, 15))
     v.w_ac[...] = dot_tn(v.act_a[...], g_aux)[:64]
-    s_ac.start()
+    mix(s_ac.starts())
 
     unite_grad(2)
     unite_grad(3)
@@ -1883,8 +1878,7 @@
     v.d_img_recv[me] = v.d_img_send[me]
     ex = Exchange(BATCH, OWNERS, lambda o: v.d_img_send.at[o], lambda s: v.d_img_recv.at[s])
     ex.start()
-    s_u.start(2)
-    s_u.middle(0)
+    mix(s_u.starts(2), s_u.middles(0))
 
     sums = sync_a.wait()
     gain_grads[15] = (sums[1:2], sums[0:1])
@@ -1923,8 +1917,7 @@
         [total(d_b * group_mask(g)) for g in range(4)]
         + [total(d_b * unit_b * group_mask(g)) for g in range(4)]
     )
-    s_u.start(3)
-    s_u.middle(1)
+    mix(s_u.starts(3), s_u.middles(1))
     sums = sync.wait()
     first_b = jnp.zeros((BINS, 128), F32)
     second_b = jnp.zeros((BINS, 128), F32)
@@ -1937,8 +1930,7 @@
     v.d_bp[t] = (gamma_b * scale_b * inner).astype(BF)
     spread_d = Spread(v.d_bp)
     spread_d.start()
-    s_u.start(4)
-    s_u.middle(2)
+    mix(s_u.starts(4), s_u.middles(2))
     spread_d.wait()
     d_bp_move = ToGroup(
         lambda owner, rows: v.d_bp.at[:, 0:rows, :],
@@ -1971,8 +1963,7 @@
     three = [total(item) for item in lax.fori_loop(0, 12, through_sum, (zero, zero, zero))]
     sync = Sync(v.sync_b4)
     sync.start(split_rows(three[0]) + split_rows(three[1]) + split_rows(three[2]))
-    s_a.start()
-    s_u.middle(3)
+    mix(s_a.starts(), s_u.middles(3))
     sums = sync.wait()
     first_s = join_rows(sums, 0, 4)
     second_e, second_s = join_rows(sums, 4, 4), join_rows(sums, 8, 4)
@@ -2018,18 +2009,17 @@
         v.w_s[rows_at(c, 256), :] = dot_tn(v.whole[c], v.d_s[...]).astype(BF)
 
     loop(SPLITS, short_grad)
-    s_s.start()
-    s_u.middle(4)
+    mix(s_s.starts(), s_u.middles(4))
     for k in range(SPLITS):
         v.w_e[k * 128 : k * 128 + 128, :] = dot_tn(v.h2[k], v.d_e[...]).astype(BF)
     ex.wait()
     hidden_sum(0)
     sync = Sync(v.sync_b5)
     sync.start(through_silu(v.d_f, v.pre_m, norm_m, 5))
-    s_e.start()
-    s_c.middle()
-    s_ac.middle()
-    s_a.middle()
+    mix(s_e.starts())
+    mix(s_c.middles())
+    mix(s_ac.middles())
+    mix(s_a.middles())
     sums = sync.wait()
     gain_grads[5] = (sums[1:2], sums[0:1])
     spread_taps(v.d_f, v.pre_m, norm_m, 5, sums[0:1], sums[1:2])
@@ -2043,14 +2033,14 @@
             v.w_m[rows_at(tap * 4 + k, 128), :] = value[:, tap * 128 : tap * 128 + 128].astype(BF)
 
     loop(SPLITS, middle_grad)
-    s_m.start()
-    s_s.middle()
+    mix(s_m.starts())
+    mix(s_s.middles())
     ex.wait()
     hidden_sum(1)
     sync = Sync(v.sync_b6)
     sync.start(through_silu(v.d_f, v.pre_r, norm_r, 0))
 
-    s_e.middle()
+    mix(s_e.middles())
     sums = sync.wait()
     gain_grads[0] = (sums[1:2], sums[0:1])
 
@@ -2066,9 +2056,8 @@
         v.w_r[rows_at(c, 256), :] = dot_tn(v.whole[c], v.d_low[...]).astype(BF)
 
     loop(SPLITS, reduce_grad)
-    s_r.start()
-    for item in (s_m, s_r):
-        item.middle()
+    mix(s_r.starts())
+    mix(s_m.middles() + s_r.middles())
     pool_move.wait()
     d_bp_move.wait()
     own_group = jnp.where(group_id == lax.div(me, 2), 1.0, 0.0)

time: 363 us -> 363 us (level)
  no operation moved by 1% of the time
where the time goes in v10:
time: 363 us; the launch traced here: 362 us
  Pallas kernels  352 us (97%)
  other arithmetic  8.26 us (2%)
    pallas_call x1, Pallas kernels, whole_step(): pl.pallas_call(functools.partial(step_kernel, tuple(plan)), out_shape=[ja...  335 us
    pallas_call x1, Pallas kernels, update(): pl.pallas_call(update_kernel, grid=(pl.cdiv(rows, 1024),), out_shape=[big...  17.2 us
    convert_element_type x1, other arithmetic, local_fast(): new_params.astype(BF)  7.53 us

profile of v10, /device:TPU:0, one launch (start us, length us, event | category | flops | bytes accessed | tf_op | source)
XLA Modules:
  0.0 362.3 jit_solution(15910063244059474113)
XLA Ops:
  0.6 0.7 select_convert_fusion
  1.4 0.1 broadcast_in_dim.12
  1.5 0.9 broadcast_in_dim.13.refs_1_
  2.3 334.8 %whole_step.1 = (f32[7712,128]{1,0:T(8,128)}, f32[1,128]{1,0:T(1,128)}, f32[8,128]{1,0:T(8,128)}) custom-call(s32[1,2]{1,0:T(1,128)} %refs_0_.1, f32[576,128]{1,0:T(8,128)} %broadcast_in_dim.13.refs_1_, bf16[576,256]{1,0:T(8,128)(2,1)} %bitcast.20, f32[7712,128]{1,0:T(8,128)} %bitcast.13), custom_call_target="tpu_custom_call" | custom-call | tf_op jit(solution)/shard_map/whole_step/pallas_call | solution.py:2146
  337.1 17.2 %update.1 = (f32[7712,128]{1,0:T(8,128)}, f32[7712,128]{1,0:T(8,128)}, f32[7712,128]{1,0:T(8,128)}, f32[7712,128]{1,0:T(8,128)}, f32[1,1]{1,0:T(1,128)}, /*index=5*/f32[1,1]{1,0:T(1,128)}, f32[1,1]{1,0:T(1,128)}) custom-call(f32[8,128]{1,0:T(8,128)} %get-tuple-element.19.misc, f32[7712,128]{1,0:T(8,128)} %get-tuple-element.20.grad, f32[7712,128]{1,0:T(8,128)} %bitcast.14, ...), custom_call_target="tpu_custom_call" | custom-call | tf_op jit(solution)/shard_map/update/pallas_call | solution.py:2187
  354.3 0.0 copy-start
  354.3 7.5 %convert_element_type.15 = bf16[1,987136]{1,0:T(2,128)(2,1)} convert(f32[1,987136]{1,0:T(1,128)} %bitcast.18) | non-fusion elementwise | flops 987136 | bytes 5922816 | tf_op jit(solution)/shard_map/convert_element_type | solution.py:2224
  361.8 0.0 copy-done
  361.8 0.5 copy.18
Async XLA Ops:
  354.3 7.5 %copy-start = (f32[1,128]{1,0:T(1,128)S(1)}, f32[1,128]{1,0:T(1,128)}, u32[]{:S(2)}) copy-start(f32[1,128]{1,0:T(1,128)} %get-tuple-element.28) | copy-start | bytes 1540

commit v11 on v10

--- a/solution.py
+++ b/solution.py
@@ -492,6 +492,9 @@
         out_c=((16, 256), F32),
         out_ac=((8, 256), F32),
         whole=((SPLITS, CELLS, 256), BF),
+        whole_t=((SPLITS, 256, CELLS), BF),
+        w_c_all=((SPLITS, 128, 256), BF),
+        slope_main=((CELLS, 256), BF),
         ins=((CELLS, 128), F32),
         col=((CELLS, 128), F32),
         lab=((CELLS, 128), F32),
@@ -526,7 +529,7 @@
         zsum=((2, OWNERS * BINS, 128), F32),
         z_send=((OWNERS, 2, BINS, 128), BF),
         z_recv=((OWNERS, 2, BINS, 128), BF),
-        united=((CELLS, 128), BF),
+        united=((SPLITS, CELLS, 128), BF),
         logit_send=((CELLS, 512), BF),
         logit_recv=((SPLITS, 144, 512), BF),
         slope_in=((SPLITS, 144, 512), BF),
@@ -850,8 +853,8 @@
                 for step in range(1, HALF)
             ]
 
-        def finish(self):
-            for slot in range(SLOTS):
+        def finish(self, slots):
+            for slot in slots:
                 for step in range(HALF):
                     has(
                         far_peer(partner, step),
@@ -1336,7 +1339,7 @@
     v.all_b[me] = own_b.astype(BF)
     ex = Exchange(BATCH, OWNERS, lambda o: v.all_b.at[me], lambda s: v.all_b.at[s])
     ex.start()
-    mix(g_u.passes(1) + g_u.nears(2), g_u.fars(3))
+    mix(g_u.passes(1) + g_u.nears(2), g_u.fars(4))
     ex.wait()
     all_b = [v.all_b[k].astype(F32) for k in range(OWNERS)]
     sum_b, square_b = all_b[0], all_b[0] * all_b[0]
@@ -1362,7 +1365,7 @@
         out = gamma_b * ((all_b[k] - mean_b) * scale_b) + beta_b
         v.act_b[t, k * BINS : k * BINS + BINS, :] = jax.nn.silu(out).astype(BF)
     spread_b.start()
-    mix(g_u.passes(2) + g_u.nears(3), g_u.fars(4))
+    mix(g_u.passes(2) + g_u.nears(4), g_u.fars(3))
     spread_b.wait()
     row_512 = lax.broadcasted_iota(jnp.int32, (OWNERS * BINS, 1), 0) & (BINS - 1)
     group_id = jnp.where(
@@ -1392,15 +1395,15 @@
     v.z_recv[me] = v.z_send[me]
     ex = Exchange(BATCH, OWNERS, lambda o: v.z_send.at[o], lambda s: v.z_recv.at[s])
     ex.start()
-    mix(g_u.passes(3) + g_u.nears(4))
+    mix(g_u.passes(4) + g_u.nears(3))
     v.act_t[...] = full_act().T
     joined_copy(1, t_core, t_core).wait_recv()
     joined_copy(2, t_diag, t_core).wait_recv()
     for k in range(SPLITS):
         v.joined_t[k] = v.joined[k].T
-    mix(g_u.passes(4) + g_c.passes() + g_ac.passes())
+    mix(g_u.passes(3) + g_c.passes() + g_ac.passes())
     ex.wait()
-    g_u.finish()
+    g_u.finish((0, 1, 2, 4))
 
     def tap_z(tap):
         if tap == 0:
@@ -1415,19 +1418,38 @@
         v.z_cat[tap, :BINS, :] = high_z
         v.z_cat[tap, BINS:, :] = (z - high_z.astype(F32)).astype(BF)
 
-    def full_joined():
-        return jnp.concatenate([v.joined[k] for k in range(SPLITS)] + [v.pick_t[...]], axis=1)
-
-    def w_tap(tap):
-        return jnp.concatenate([v.w_u[rows_at(tap, 2048), :], v.z_cat[tap]], axis=0)
-
-    def unite_pair(p):
-        value = dot(full_joined(), jnp.concatenate([w_tap(2 * p), w_tap(2 * p + 1)], axis=1))
-        v.pad[2 * p, EDGE : EDGE + CELLS, :] = value[:, :128]
-        v.pad[2 * p + 1, EDGE : EDGE + CELLS, :] = value[:, 128:]
-
-    loop(4, unite_pair)
-    v.pad[8, EDGE : EDGE + CELLS, :] = dot(full_joined(), w_tap(8))
+    def most_joined():
+        return jnp.concatenate([v.joined[k] for k in range(3)], axis=1)
+
+    def rest_joined():
+        return jnp.concatenate([v.joined[3], v.pick_t[...]], axis=1)
+
+    def most_weight(tap):
+        return v.w_u[pl.ds(pl.multiple_of(tap * 2048, 512), 1536), :]
+
+    def rest_weight(tap):
+        last = v.w_u[pl.ds(pl.multiple_of(tap * 2048 + 1536, 512), 512), :]
+        return jnp.concatenate([last, v.z_cat[tap]], axis=0)
+
+    inner = slice(EDGE, EDGE + CELLS)
+
+    def most_pair(p):
+        both = jnp.concatenate([most_weight(2 * p), most_weight(2 * p + 1)], axis=1)
+        value = dot(most_joined(), both)
+        v.pad[2 * p, inner, :] = value[:, :128]
+        v.pad[2 * p + 1, inner, :] = value[:, 128:]
+
+    def rest_pair(p):
+        both = jnp.concatenate([rest_weight(2 * p), rest_weight(2 * p + 1)], axis=1)
+        value = dot(rest_joined(), both)
+        v.pad[2 * p, inner, :] = v.pad[2 * p, inner, :] + value[:, :128]
+        v.pad[2 * p + 1, inner, :] = v.pad[2 * p + 1, inner, :] + value[:, 128:]
+
+    loop(4, most_pair)
+    v.pad[8, inner, :] = dot(most_joined(), most_weight(8))
+    g_u.finish((3,))
+    loop(4, rest_pair)
+    v.pad[8, inner, :] = v.pad[8, inner, :] + dot(rest_joined(), rest_weight(8))
     for at in range(0, CELLS, BLOCK):
         v.pre_u[at : at + BLOCK, :] = shift_sum(range(9), 1, at, lambda tap: tap)
     sync = Sync(v.sync_five)
@@ -1436,6 +1458,11 @@
     mix(g_a.nears(), g_a.fars())
     for item in (g_c, g_ac):
         item.finish()
+    v.w_c_all[t] = v.w_c[...]
+    spread_c = Spread(v.w_c_all)
+    spread_c.start()
+    for k in range(SPLITS):
+        v.whole_t[k] = v.whole[k].T
     for item in (g_gain, g_r, g_s, g_m, g_e, g_b0, g_b1, g_c, g_ac, g_u):
         item.drain()
     joined_copy(0, t, t_x).wait_send()
@@ -1447,9 +1474,11 @@
 
     def make_u(k):
         at = rows_at(k, 96)
-        v.united[at, :] = jax.nn.silu(gamma(14) * normed(v.pre_u, at, norm_u) + beta(14)).astype(BF)
+        v.united[t, at, :] = jax.nn.silu(gamma(14) * normed(v.pre_u, at, norm_u) + beta(14)).astype(BF)
 
     loop(6, make_u)
+    spread_u = Spread(v.united)
+    spread_u.start()
     class Band:
         def __init__(self, at):
             self.at = at
@@ -1471,17 +1500,10 @@
             logits = v.logit_recv[0, :, self.at].astype(F32)
             for k in range(1, SPLITS):
                 logits = logits + v.logit_recv[k, :, self.at].astype(F32)
-            class_weight, loss_weight = class_weights()
-            hot = jnp.where(wide(v.lab[rows_at(t, 144), :], 2) == lanes, 1.0, 0.0)
-            cell_weight = factor * jnp.sum(hot * class_weight, axis=1, keepdims=True)
-            value = jnp.where(lanes < float(NCLS), logits, -1e30)
-            value = value - jnp.max(value, axis=1, keepdims=True)
-            powers = jnp.exp(value)
-            mass = jnp.sum(powers, axis=1, keepdims=True)
-            loss_rows = total(fold(-cell_weight * hot * (value - jnp.log(mass))))
-            grad = cell_weight * (powers / mass - hot) / loss_weight
-            v.slope_in[t, :, self.at] = grad.astype(BF)
+            loss_rows, grad = soft_loss(logits, rows_at(t, 144), factor)
+            v.slope_in[t, :, self.at] = grad
             self.back.start()
+            loss_rows = total(loss_rows)
             return loss_rows[:, :128] + loss_rows[:, 128:]
 
         def grad(self):
@@ -1494,10 +1516,20 @@
         whole = jnp.sum(class_count * weight, axis=1, keepdims=True)
         return jnp.where(lanes < float(NCLS), weight, 0.0), whole
 
-    main_head, aux_head = Band(slice(0, 256)), Band(slice(256, 512))
-    main_head.start(dot(v.united[...], v.w_c[...]))
+    def soft_loss(logits, at, factor):
+        class_weight, loss_weight = class_weights()
+        hot = jnp.where(wide(v.lab[at, :], 2) == lanes, 1.0, 0.0)
+        cell_weight = factor * jnp.sum(hot * class_weight, axis=1, keepdims=True)
+        value = jnp.where(lanes < float(NCLS), logits, -1e30)
+        value = value - jnp.max(value, axis=1, keepdims=True)
+        powers = jnp.exp(value)
+        mass = jnp.sum(powers, axis=1, keepdims=True)
+        grad = cell_weight * (powers / mass - hot) / loss_weight
+        return fold(-cell_weight * hot * (value - jnp.log(mass))), grad.astype(BF)
+
+    aux_head = Band(slice(256, 512))
     mix(g_a.passes())
-    o_misc[1:2, :] = main_head.finish(1.0)
+    spread_c.wait()
 
     g_a.finish()
     g_a.drain()
@@ -1532,7 +1564,19 @@
 
     sync_a = Sync(v.sync_aux)
     sync_a.start(list(masked_sums(v.pre_a)))
-    g_main = main_head.grad()
+    spread_u.wait()
+    weight_c = v.w_c_all[...].reshape(512, 256)
+
+    def main_loss(k, carry):
+        at = rows_at(k, 144)
+        rows = jnp.concatenate([v.united[slot, at, :] for slot in range(SPLITS)], axis=1)
+        loss_rows, grad = soft_loss(dot(rows, weight_c), at, 1.0)
+        v.slope_main[at, :] = grad
+        return carry + loss_rows
+
+    loss_rows = total(lax.fori_loop(0, 4, main_loss, jnp.zeros((8, 256), F32)))
+    o_misc[1:2, :] = (loss_rows[:, :128] + loss_rows[:, 128:]) / SPLITS
+    g_main = v.slope_main[...]
     v.d_f[...] = dot_nt(g_main, v.w_c[...])
 
     def slope(value):
@@ -1752,7 +1796,7 @@
 
     s_u = ScatterUnite()
 
-    v.w_c[...] = dot_tn(v.united[...], g_main).astype(BF)
+    v.w_c[...] = dot_tn(v.united[t], g_main).astype(BF)
     mix(s_c.starts())
     sums = sync.wait()
     gain_grads[14] = (sums[1:2], sums[0:1])
@@ -1812,20 +1856,6 @@
     dm_near(1, t_diag).start()
     merged_back(t_core)
     dm_near(0, t_core).start()
-    merged_back(t_x)
-    merged_back(t)
-
-    def unite_grad(c):
-        for p in range(5):
-            width = 256 if p < 4 else 128
-            value = dot(v.joined_t[c], v.cat_u[:, p * 256 : p * 256 + width])
-            v.w_u[rows_at(2 * p * MERGED + c, 512), :] = value[:, :128].astype(BF)
-            if p < 4:
-                v.w_u[rows_at((2 * p + 1) * MERGED + c, 512), :] = value[:, 128:].astype(BF)
-
-    unite_grad(0)
-    mix(s_u.starts(0))
-    o_misc[1:2, :] = o_misc[1:2, :] + aux_head.finish(0.4)
     ex_dz.wait()
 
     d_act = v.d_sum.at[0 : OWNERS * BINS, :]
@@ -1847,27 +1877,8 @@
     v.d_act_recv[t] = v.d_act_send[t]
     ex = Exchange(TENSOR, SPLITS, lambda o: v.d_act_send.at[o], lambda s: v.d_act_recv.at[s])
     ex.start()
-    unite_grad(1)
-    mix(s_u.starts(1))
-    dm_near(1, t_x).wait_recv()
-
-    def add_x(k):
-        at = rows_at(k, 48)
-        value = v.joined[t_x, at, :].astype(F32) + v.dm_near[1, at, :].astype(F32)
-        v.joined[t_x, at, :] = value.astype(BF)
-
-    loop(12, add_x)
-    dm_far = remote(v.joined.at[t_x], v.dm_far, far_s, far_r, {TENSOR: t_x})
-    dm_far.start()
-    g_aux = aux_head.grad()
-    v.d_f2[...] = dot_nt(g_aux, w_ac)
-    sync_a = Sync(v.sync_b2)
-    sync_a.start(through_silu(v.d_f2, v.pre_a, norm_a, 15))
-    v.w_ac[...] = dot_tn(v.act_a[...], g_aux)[:64]
-    mix(s_ac.starts())
-
-    unite_grad(2)
-    unite_grad(3)
+    merged_back(t_x)
+    merged_back(t)
     ex.wait()
     for k in range(OWNERS):
         at = slice(k * BINS, k * BINS + BINS)
@@ -1878,8 +1889,140 @@
     v.d_img_recv[me] = v.d_img_send[me]
     ex = Exchange(BATCH, OWNERS, lambda o: v.d_img_send.at[o], lambda s: v.d_img_recv.at[s])
     ex.start()
+
+    def unite_grad(c):
+        for p in range(5):
+            width = 256 if p < 4 else 128
+            value = dot(v.joined_t[c], v.cat_u[:, p * 256 : p * 256 + width])
+            v.w_u[rows_at(2 * p * MERGED + c, 512), :] = value[:, :128].astype(BF)
+            if p < 4:
+                v.w_u[rows_at((2 * p + 1) * MERGED + c, 512), :] = value[:, 128:].astype(BF)
+
+    unite_grad(0)
+    mix(s_u.starts(0))
+    dm_near(1, t_x).wait_recv()
+
+    def add_x(k):
+        at = rows_at(k, 48)
+        value = v.joined[t_x, at, :].astype(F32) + v.dm_near[1, at, :].astype(F32)
+        v.joined[t_x, at, :] = value.astype(BF)
+
+    loop(12, add_x)
+    dm_far = remote(v.joined.at[t_x], v.dm_far, far_s, far_r, {TENSOR: t_x})
+    dm_far.start()
+    ex.wait()
+    d_b = v.d_img_recv[0].astype(F32)
+    for k in range(1, OWNERS):
+        d_b = d_b + v.d_img_recv[k].astype(F32)
+    unit_b = (v.all_b[me].astype(F32) - mean_b) * scale_b
+    d_b = d_b * slope(gamma_b * unit_b + beta_b)
+    sync = Sync(v.sync_b3)
+    sync.start(
+        [total(d_b * group_mask(g)) for g in range(4)]
+        + [total(d_b * unit_b * group_mask(g)) for g in range(4)]
+    )
+    unite_grad(1)
+    mix(s_u.starts(1))
+    o_misc[1:2, :] = o_misc[1:2, :] + aux_head.finish(0.4)
+    sums = sync.wait()
+    first_b = jnp.zeros((BINS, 128), F32)
+    second_b = jnp.zeros((BINS, 128), F32)
+    for group in range(4):
+        kept = group_mask(group)
+        gain_grads[10 + group] = (sums[4 + group : 5 + group], sums[group : group + 1])
+        first_b = first_b + kept * sums[group : group + 1]
+        second_b = second_b + kept * sums[4 + group : 5 + group]
+    inner = d_b - (first_b + unit_b * second_b) * count_b
+    v.d_bp[t] = (gamma_b * scale_b * inner).astype(BF)
+    spread_d = Spread(v.d_bp)
+    spread_d.start()
+    unite_grad(2)
     mix(s_u.starts(2), s_u.middles(0))
-
+    spread_d.wait()
+    d_bp_move = ToGroup(
+        lambda owner, rows: v.d_bp.at[:, 0:rows, :],
+        lambda slot, rows: v.d_bp_all.at[slot, :, 0:rows, :],
+    )
+    d_bp_move.start()
+    v.d_bp_all[me] = v.d_bp[...]
+    d_bp = jnp.concatenate([v.d_bp[k] for k in range(SPLITS)], axis=1)
+    d_pooled = jnp.zeros((BINS, 512), F32)
+    for group in range(4):
+        rows = (d_bp.astype(F32) * group_mask(group)).astype(BF)
+        d_pooled = d_pooled + dot_nt(rows, v.w_b[group * 512 : group * 512 + 512, :])
+    d_pooled = (d_pooled / cells_in).astype(BF)
+    v.d_sum[...] = dot_tn(v.pool[...], d_pooled)
+    dm_near(0, t).wait_recv()
+    dm_far.wait_recv()
+
+    def through_sum(k, carry):
+        at = rows_at(k, 48)
+        value = v.d_sum[at, :] + v.joined[t, at, :].astype(F32) + v.dm_near[0, at, :].astype(F32)
+        value = (value + v.dm_far[at, :].astype(F32)) * slope(summed(at))
+        v.d_sum[at, :] = value
+        return (
+            carry[0] + fold(value),
+            carry[1] + fold(value * normed(v.pre_e, at, norm_e)),
+            carry[2] + fold(value * normed(v.pre_s, at, norm_s)),
+        )
+
+    zero = jnp.zeros((8, 512), F32)
+    three = [total(item) for item in lax.fori_loop(0, 12, through_sum, (zero, zero, zero))]
+    sync = Sync(v.sync_b4)
+    sync.start(split_rows(three[0]) + split_rows(three[1]) + split_rows(three[2]))
+    unite_grad(3)
+    mix(s_u.starts(3), s_u.middles(1))
+    g_aux = aux_head.grad()
+    v.d_f2[...] = dot_nt(g_aux, w_ac)
+    sync_a = Sync(v.sync_b2)
+    sync_a.start(through_silu(v.d_f2, v.pre_a, norm_a, 15))
+    v.w_ac[...] = dot_tn(v.act_a[...], g_aux)[:64]
+    mix(s_ac.starts())
+    sums = sync.wait()
+    first_s = join_rows(sums, 0, 4)
+    second_e, second_s = join_rows(sums, 4, 4), join_rows(sums, 8, 4)
+    for k in range(4):
+        gain_grads[6 + k] = (sums[4 + k : 5 + k], sums[k : k + 1])
+        gain_grads[1 + k] = (sums[8 + k : 9 + k], sums[k : k + 1])
+
+    def back_both(k):
+        at = rows_at(k, 48)
+        value, mask = v.d_sum[at, :], wide(v.ins[at, :], 4)
+        v.d_e[at, :] = back_norm(
+            value, normed(v.pre_e, at, norm_e), mask, norm_e, gamma(6, 4), first_s, second_e, count4
+        ).astype(BF)
+        v.d_s[at, :] = back_norm(
+            value, normed(v.pre_s, at, norm_s), mask, norm_s, gamma(1, 4), first_s, second_s, count4
+        ).astype(BF)
+
+    loop(12, back_both)
+
+    def back_hidden(grad, weight, index):
+        value = dot_nt(grad, weight)
+        for k in range(SPLITS):
+            v.dh_send[k] = value[:, k * 128 : k * 128 + 128].astype(BF)
+        v.dh_recv[index, t] = v.dh_send[t]
+        ex = Exchange(
+            TENSOR, SPLITS, lambda o: v.dh_send.at[o], lambda s: v.dh_recv.at[index, s]
+        )
+        ex.start()
+        return ex
+
+    def hidden_sum(index):
+        def step(k):
+            at = rows_at(k, 96)
+            value = v.dh_recv[index, 0, at, :].astype(F32)
+            for slot in range(1, SPLITS):
+                value = value + v.dh_recv[index, slot, at, :].astype(F32)
+            v.d_f[at, :] = value
+
+        loop(6, step)
+
+    ex = back_hidden(v.d_e[...], v.w_e[...], 0)
+    mix(s_u.starts(4), s_u.middles(2))
+    for k in range(SPLITS):
+        v.w_e[k * 128 : k * 128 + 128, :] = dot_tn(v.h2[k], v.d_e[...]).astype(BF)
+    mix(s_e.starts())
     sums = sync_a.wait()
     gain_grads[15] = (sums[1:2], sums[0:1])
     spread_taps(v.d_f2, v.pre_a, norm_a, 15, sums[0:1], sums[1:2])
@@ -1890,8 +2033,12 @@
                 value = value + pltpu.roll(back_tap(2 * p + 1, 1, at), 64, 1)
             v.cat_a[at : at + 96, p * 128 : p * 128 + 128] = value.astype(BF)
 
+    ex.wait()
+    hidden_sum(0)
+    sync = Sync(v.sync_b5)
+    sync.start(through_silu(v.d_f, v.pre_m, norm_m, 5))
     def aux_grad(c2):
-        value2 = dot_tn(v.whole[c2], v.cat_a[...])
+        value2 = dot(v.whole_t[c2], v.cat_a[...])
         for half in range(2):
             value = value2[half * 128 : half * 128 + 128]
             c = 2 * c2 + half
@@ -1906,120 +2053,8 @@
                     v.w_a[rows_at((2 * p + 1) * 8 + c, 64), :] = odd.astype(BF)
 
     loop(SPLITS, aux_grad)
-    ex.wait()
-    d_b = v.d_img_recv[0].astype(F32)
-    for k in range(1, OWNERS):
-        d_b = d_b + v.d_img_recv[k].astype(F32)
-    unit_b = (v.all_b[me].astype(F32) - mean_b) * scale_b
-    d_b = d_b * slope(gamma_b * unit_b + beta_b)
-    sync = Sync(v.sync_b3)
-    sync.start(
-        [total(d_b * group_mask(g)) for g in range(4)]
-        + [total(d_b * unit_b * group_mask(g)) for g in range(4)]
-    )
-    mix(s_u.starts(3), s_u.middles(1))
-    sums = sync.wait()
-    first_b = jnp.zeros((BINS, 128), F32)
-    second_b = jnp.zeros((BINS, 128), F32)
-    for group in range(4):
-        kept = group_mask(group)
-        gain_grads[10 + group] = (sums[4 + group : 5 + group], sums[group : group + 1])
-        first_b = first_b + kept * sums[group : group + 1]
-        second_b = second_b + kept * sums[4 + group : 5 + group]
-    inner = d_b - (first_b + unit_b * second_b) * count_b
-    v.d_bp[t] = (gamma_b * scale_b * inner).astype(BF)
-    spread_d = Spread(v.d_bp)
-    spread_d.start()
-    mix(s_u.starts(4), s_u.middles(2))
-    spread_d.wait()
-    d_bp_move = ToGroup(
-        lambda owner, rows: v.d_bp.at[:, 0:rows, :],
-        lambda slot, rows: v.d_bp_all.at[slot, :, 0:rows, :],
-    )
-    d_bp_move.start()
-    v.d_bp_all[me] = v.d_bp[...]
-    d_bp = jnp.concatenate([v.d_bp[k] for k in range(SPLITS)], axis=1)
-    d_pooled = jnp.zeros((BINS, 512), F32)
-    for group in range(4):
-        rows = (d_bp.astype(F32) * group_mask(group)).astype(BF)
-        d_pooled = d_pooled + dot_nt(rows, v.w_b[group * 512 : group * 512 + 512, :])
-    d_pooled = (d_pooled / cells_in).astype(BF)
-    v.d_sum[...] = dot_tn(v.pool[...], d_pooled)
-    dm_near(0, t).wait_recv()
-    dm_far.wait_recv()
-
-    def through_sum(k, carry):
-        at = rows_at(k, 48)
-        value = v.d_sum[at, :] + v.joined[t, at, :].astype(F32) + v.dm_near[0, at, :].astype(F32)
-        value = (value + v.dm_far[at, :].astype(F32)) * slope(summed(at))
-        v.d_sum[at, :] = value
-        return (
-            carry[0] + fold(value),
-            carry[1] + fold(value * normed(v.pre_e, at, norm_e)),
-            carry[2] + fold(value * normed(v.pre_s, at, norm_s)),
-        )
-
-    zero = jnp.zeros((8, 512), F32)
-    three = [total(item) for item in lax.fori_loop(0, 12, through_sum, (zero, zero, zero))]
-    sync = Sync(v.sync_b4)
-    sync.start(split_rows(three[0]) + split_rows(three[1]) + split_rows(three[2]))
     mix(s_a.starts(), s_u.middles(3))
-    sums = sync.wait()
-    first_s = join_rows(sums, 0, 4)
-    second_e, second_s = join_rows(sums, 4, 4), join_rows(sums, 8, 4)
-    for k in range(4):
-        gain_grads[6 + k] = (sums[4 + k : 5 + k], sums[k : k + 1])
-        gain_grads[1 + k] = (sums[8 + k : 9 + k], sums[k : k + 1])
-
-    def back_both(k):
-        at = rows_at(k, 48)
-        value, mask = v.d_sum[at, :], wide(v.ins[at, :], 4)
-        v.d_e[at, :] = back_norm(
-            value, normed(v.pre_e, at, norm_e), mask, norm_e, gamma(6, 4), first_s, second_e, count4
-        ).astype(BF)
-        v.d_s[at, :] = back_norm(
-            value, normed(v.pre_s, at, norm_s), mask, norm_s, gamma(1, 4), first_s, second_s, count4
-        ).astype(BF)
-
-    loop(12, back_both)
-
-    def back_hidden(grad, weight, index):
-        value = dot_nt(grad, weight)
-        for k in range(SPLITS):
-            v.dh_send[k] = value[:, k * 128 : k * 128 + 128].astype(BF)
-        v.dh_recv[index, t] = v.dh_send[t]
-        ex = Exchange(
-            TENSOR, SPLITS, lambda o: v.dh_send.at[o], lambda s: v.dh_recv.at[index, s]
-        )
-        ex.start()
-        return ex
-
-    def hidden_sum(index):
-        def step(k):
-            at = rows_at(k, 96)
-            value = v.dh_recv[index, 0, at, :].astype(F32)
-            for slot in range(1, SPLITS):
-                value = value + v.dh_recv[index, slot, at, :].astype(F32)
-            v.d_f[at, :] = value
-
-        loop(6, step)
-
-    ex = back_hidden(v.d_e[...], v.w_e[...], 0)
-    def short_grad(c):
-        v.w_s[rows_at(c, 256), :] = dot_tn(v.whole[c], v.d_s[...]).astype(BF)
-
-    loop(SPLITS, short_grad)
-    mix(s_s.starts(), s_u.middles(4))
-    for k in range(SPLITS):
-        v.w_e[k * 128 : k * 128 + 128, :] = dot_tn(v.h2[k], v.d_e[...]).astype(BF)
-    ex.wait()
-    hidden_sum(0)
-    sync = Sync(v.sync_b5)
-    sync.start(through_silu(v.d_f, v.pre_m, norm_m, 5))
-    mix(s_e.starts())
-    mix(s_c.middles())
-    mix(s_ac.middles())
-    mix(s_a.middles())
+    mix(s_c.middles() + s_ac.middles())
     sums = sync.wait()
     gain_grads[5] = (sums[1:2], sums[0:1])
     spread_taps(v.d_f, v.pre_m, norm_m, 5, sums[0:1], sums[1:2])
@@ -2033,14 +2068,17 @@
             v.w_m[rows_at(tap * 4 + k, 128), :] = value[:, tap * 128 : tap * 128 + 128].astype(BF)
 
     loop(SPLITS, middle_grad)
-    mix(s_m.starts())
-    mix(s_s.middles())
+    mix(s_m.starts(), s_u.middles(4))
     ex.wait()
     hidden_sum(1)
     sync = Sync(v.sync_b6)
     sync.start(through_silu(v.d_f, v.pre_r, norm_r, 0))
 
-    mix(s_e.middles())
+    def short_grad(c):
+        v.w_s[rows_at(c, 256), :] = dot(v.whole_t[c], v.d_s[...]).astype(BF)
+
+    loop(SPLITS, short_grad)
+    mix(s_s.starts(), s_e.middles() + s_a.middles())
     sums = sync.wait()
     gain_grads[0] = (sums[1:2], sums[0:1])
 
@@ -2053,11 +2091,11 @@
     loop(6, back_reduce)
 
     def reduce_grad(c):
-        v.w_r[rows_at(c, 256), :] = dot_tn(v.whole[c], v.d_low[...]).astype(BF)
+        v.w_r[rows_at(c, 256), :] = dot(v.whole_t[c], v.d_low[...]).astype(BF)
 
     loop(SPLITS, reduce_grad)
     mix(s_r.starts())
-    mix(s_m.middles() + s_r.middles())
+    mix(s_m.middles() + s_s.middles() + s_r.middles())
     pool_move.wait()
     d_bp_move.wait()
     own_group = jnp.where(group_id == lax.div(me, 2), 1.0, 0.0)

time: 363 us -> 371 us (1.022)
  Pallas kernels: 352 us -> 360 us
    pallas_call x1, Pallas kernels: 335 us -> 343 us  [whole_step(): pl.pallas_call(functools.partial(step_kernel, tuple(plan)), out_shape=[ja...]
where the time goes in v11:
time: 371 us
  Pallas kernels  360 us (97%)
  other arithmetic  8.26 us (2%)
    pallas_call x1, Pallas kernels, whole_step(): pl.pallas_call(functools.partial(step_kernel, tuple(plan)), out_shape=[ja...  343 us
    pallas_call x1, Pallas kernels, update(): pl.pallas_call(update_kernel, grid=(pl.cdiv(rows, 1024),), out_shape=[big...  17.2 us
    convert_element_type x1, other arithmetic, local_fast(): new_params.astype(BF)  7.53 us

profile of v11, /device:TPU:0, one launch (start us, length us, event | category | flops | bytes accessed | tf_op | source)
XLA Modules:
  0.0 370.6 jit_solution(1713586563424652984)
XLA Ops:
  0.6 0.7 select_convert_fusion
  1.4 0.1 broadcast_in_dim.12
  1.5 0.9 broadcast_in_dim.13.refs_1_
  2.3 343.1 %whole_step.1 = (f32[7712,128]{1,0:T(8,128)}, f32[1,128]{1,0:T(1,128)}, f32[8,128]{1,0:T(8,128)}) custom-call(s32[1,2]{1,0:T(1,128)} %refs_0_.1, f32[576,128]{1,0:T(8,128)} %broadcast_in_dim.13.refs_1_, bf16[576,256]{1,0:T(8,128)(2,1)} %bitcast.20, f32[7712,128]{1,0:T(8,128)} %bitcast.13), custom_call_target="tpu_custom_call" | custom-call | tf_op jit(solution)/shard_map/whole_step/pallas_call | solution.py:2184
  345.4 17.2 %update.1 = (f32[7712,128]{1,0:T(8,128)}, f32[7712,128]{1,0:T(8,128)}, f32[7712,128]{1,0:T(8,128)}, f32[7712,128]{1,0:T(8,128)}, f32[1,1]{1,0:T(1,128)}, /*index=5*/f32[1,1]{1,0:T(1,128)}, f32[1,1]{1,0:T(1,128)}) custom-call(f32[8,128]{1,0:T(8,128)} %get-tuple-element.19.misc, f32[7712,128]{1,0:T(8,128)} %get-tuple-element.20.grad, f32[7712,128]{1,0:T(8,128)} %bitcast.14, ...), custom_call_target="tpu_custom_call" | custom-call | tf_op jit(solution)/shard_map/update/pallas_call | solution.py:2225
  362.6 0.0 copy-start
  362.6 7.5 %convert_element_type.15 = bf16[1,987136]{1,0:T(2,128)(2,1)} convert(f32[1,987136]{1,0:T(1,128)} %bitcast.18) | non-fusion elementwise | flops 987136 | bytes 5922816 | tf_op jit(solution)/shard_map/convert_element_type | solution.py:2262
  370.1 0.0 copy-done
  370.1 0.5 copy.18
Async XLA Ops:
  362.6 7.5 %copy-start = (f32[1,128]{1,0:T(1,128)S(1)}, f32[1,128]{1,0:T(1,128)}, u32[]{:S(2)}) copy-start(f32[1,128]{1,0:T(1,128)} %get-tuple-element.28) | copy-start | bytes 1540

commit v12 on v10

--- a/solution.py
+++ b/solution.py
@@ -492,6 +492,9 @@
         out_c=((16, 256), F32),
         out_ac=((8, 256), F32),
         whole=((SPLITS, CELLS, 256), BF),
+        whole_t=((SPLITS, 256, CELLS), BF),
+        w_c_all=((SPLITS, 128, 256), BF),
+        slope_main=((CELLS, 256), BF),
         ins=((CELLS, 128), F32),
         col=((CELLS, 128), F32),
         lab=((CELLS, 128), F32),
@@ -526,7 +529,7 @@
         zsum=((2, OWNERS * BINS, 128), F32),
         z_send=((OWNERS, 2, BINS, 128), BF),
         z_recv=((OWNERS, 2, BINS, 128), BF),
-        united=((CELLS, 128), BF),
+        united=((SPLITS, CELLS, 128), BF),
         logit_send=((CELLS, 512), BF),
         logit_recv=((SPLITS, 144, 512), BF),
         slope_in=((SPLITS, 144, 512), BF),
@@ -850,8 +853,8 @@
                 for step in range(1, HALF)
             ]
 
-        def finish(self):
-            for slot in range(SLOTS):
+        def finish(self, slots):
+            for slot in slots:
                 for step in range(HALF):
                     has(
                         far_peer(partner, step),
@@ -1336,7 +1339,7 @@
     v.all_b[me] = own_b.astype(BF)
     ex = Exchange(BATCH, OWNERS, lambda o: v.all_b.at[me], lambda s: v.all_b.at[s])
     ex.start()
-    mix(g_u.passes(1) + g_u.nears(2), g_u.fars(3))
+    mix(g_u.passes(1) + g_u.nears(2), g_u.fars(4))
     ex.wait()
     all_b = [v.all_b[k].astype(F32) for k in range(OWNERS)]
     sum_b, square_b = all_b[0], all_b[0] * all_b[0]
@@ -1362,7 +1365,7 @@
         out = gamma_b * ((all_b[k] - mean_b) * scale_b) + beta_b
         v.act_b[t, k * BINS : k * BINS + BINS, :] = jax.nn.silu(out).astype(BF)
     spread_b.start()
-    mix(g_u.passes(2) + g_u.nears(3), g_u.fars(4))
+    mix(g_u.passes(2) + g_u.nears(4), g_u.fars(3))
     spread_b.wait()
     row_512 = lax.broadcasted_iota(jnp.int32, (OWNERS * BINS, 1), 0) & (BINS - 1)
     group_id = jnp.where(
@@ -1392,15 +1395,15 @@
     v.z_recv[me] = v.z_send[me]
     ex = Exchange(BATCH, OWNERS, lambda o: v.z_send.at[o], lambda s: v.z_recv.at[s])
     ex.start()
-    mix(g_u.passes(3) + g_u.nears(4))
+    mix(g_u.passes(4) + g_u.nears(3))
     v.act_t[...] = full_act().T
     joined_copy(1, t_core, t_core).wait_recv()
     joined_copy(2, t_diag, t_core).wait_recv()
     for k in range(SPLITS):
         v.joined_t[k] = v.joined[k].T
-    mix(g_u.passes(4) + g_c.passes() + g_ac.passes())
+    mix(g_u.passes(3) + g_c.passes() + g_ac.passes())
     ex.wait()
-    g_u.finish()
+    g_u.finish((0, 1, 2, 4))
 
     def tap_z(tap):
         if tap == 0:
@@ -1415,19 +1418,38 @@
         v.z_cat[tap, :BINS, :] = high_z
         v.z_cat[tap, BINS:, :] = (z - high_z.astype(F32)).astype(BF)
 
-    def full_joined():
-        return jnp.concatenate([v.joined[k] for k in range(SPLITS)] + [v.pick_t[...]], axis=1)
-
-    def w_tap(tap):
-        return jnp.concatenate([v.w_u[rows_at(tap, 2048), :], v.z_cat[tap]], axis=0)
-
-    def unite_pair(p):
-        value = dot(full_joined(), jnp.concatenate([w_tap(2 * p), w_tap(2 * p + 1)], axis=1))
-        v.pad[2 * p, EDGE : EDGE + CELLS, :] = value[:, :128]
-        v.pad[2 * p + 1, EDGE : EDGE + CELLS, :] = value[:, 128:]
-
-    loop(4, unite_pair)
-    v.pad[8, EDGE : EDGE + CELLS, :] = dot(full_joined(), w_tap(8))
+    def most_joined():
+        return jnp.concatenate([v.joined[k] for k in range(3)], axis=1)
+
+    def rest_joined():
+        return jnp.concatenate([v.joined[3], v.pick_t[...]], axis=1)
+
+    def most_weight(tap):
+        return v.w_u[pl.ds(pl.multiple_of(tap * 2048, 512), 1536), :]
+
+    def rest_weight(tap):
+        last = v.w_u[pl.ds(pl.multiple_of(tap * 2048 + 1536, 512), 512), :]
+        return jnp.concatenate([last, v.z_cat[tap]], axis=0)
+
+    inner = slice(EDGE, EDGE + CELLS)
+
+    def most_pair(p):
+        both = jnp.concatenate([most_weight(2 * p), most_weight(2 * p + 1)], axis=1)
+        value = dot(most_joined(), both)
+        v.pad[2 * p, inner, :] = value[:, :128]
+        v.pad[2 * p + 1, inner, :] = value[:, 128:]
+
+    def rest_pair(p):
+        both = jnp.concatenate([rest_weight(2 * p), rest_weight(2 * p + 1)], axis=1)
+        value = dot(rest_joined(), both)
+        v.pad[2 * p, inner, :] = v.pad[2 * p, inner, :] + value[:, :128]
+        v.pad[2 * p + 1, inner, :] = v.pad[2 * p + 1, inner, :] + value[:, 128:]
+
+    loop(4, most_pair)
+    v.pad[8, inner, :] = dot(most_joined(), most_weight(8))
+    g_u.finish((3,))
+    loop(4, rest_pair)
+    v.pad[8, inner, :] = v.pad[8, inner, :] + dot(rest_joined(), rest_weight(8))
     for at in range(0, CELLS, BLOCK):
         v.pre_u[at : at + BLOCK, :] = shift_sum(range(9), 1, at, lambda tap: tap)
     sync = Sync(v.sync_five)
@@ -1436,6 +1458,11 @@
     mix(g_a.nears(), g_a.fars())
     for item in (g_c, g_ac):
         item.finish()
+    v.w_c_all[t] = v.w_c[...]
+    spread_c = Spread(v.w_c_all)
+    spread_c.start()
+    for k in range(SPLITS):
+        v.whole_t[k] = v.whole[k].T
     for item in (g_gain, g_r, g_s, g_m, g_e, g_b0, g_b1, g_c, g_ac, g_u):
         item.drain()
     joined_copy(0, t, t_x).wait_send()
@@ -1447,9 +1474,11 @@
 
     def make_u(k):
         at = rows_at(k, 96)
-        v.united[at, :] = jax.nn.silu(gamma(14) * normed(v.pre_u, at, norm_u) + beta(14)).astype(BF)
+        v.united[t, at, :] = jax.nn.silu(gamma(14) * normed(v.pre_u, at, norm_u) + beta(14)).astype(BF)
 
     loop(6, make_u)
+    spread_u = Spread(v.united)
+    spread_u.start()
     class Band:
         def __init__(self, at):
             self.at = at
@@ -1471,17 +1500,10 @@
             logits = v.logit_recv[0, :, self.at].astype(F32)
             for k in range(1, SPLITS):
                 logits = logits + v.logit_recv[k, :, self.at].astype(F32)
-            class_weight, loss_weight = class_weights()
-            hot = jnp.where(wide(v.lab[rows_at(t, 144), :], 2) == lanes, 1.0, 0.0)
-            cell_weight = factor * jnp.sum(hot * class_weight, axis=1, keepdims=True)
-            value = jnp.where(lanes < float(NCLS), logits, -1e30)
-            value = value - jnp.max(value, axis=1, keepdims=True)
-            powers = jnp.exp(value)
-            mass = jnp.sum(powers, axis=1, keepdims=True)
-            loss_rows = total(fold(-cell_weight * hot * (value - jnp.log(mass))))
-            grad = cell_weight * (powers / mass - hot) / loss_weight
-            v.slope_in[t, :, self.at] = grad.astype(BF)
+            loss_rows, grad = soft_loss(logits, rows_at(t, 144), factor)
+            v.slope_in[t, :, self.at] = grad
             self.back.start()
+            loss_rows = total(loss_rows)
             return loss_rows[:, :128] + loss_rows[:, 128:]
 
         def grad(self):
@@ -1494,10 +1516,20 @@
         whole = jnp.sum(class_count * weight, axis=1, keepdims=True)
         return jnp.where(lanes < float(NCLS), weight, 0.0), whole
 
-    main_head, aux_head = Band(slice(0, 256)), Band(slice(256, 512))
-    main_head.start(dot(v.united[...], v.w_c[...]))
+    def soft_loss(logits, at, factor):
+        class_weight, loss_weight = class_weights()
+        hot = jnp.where(wide(v.lab[at, :], 2) == lanes, 1.0, 0.0)
+        cell_weight = factor * jnp.sum(hot * class_weight, axis=1, keepdims=True)
+        value = jnp.where(lanes < float(NCLS), logits, -1e30)
+        value = value - jnp.max(value, axis=1, keepdims=True)
+        powers = jnp.exp(value)
+        mass = jnp.sum(powers, axis=1, keepdims=True)
+        grad = cell_weight * (powers / mass - hot) / loss_weight
+        return fold(-cell_weight * hot * (value - jnp.log(mass))), grad.astype(BF)
+
+    aux_head = Band(slice(256, 512))
     mix(g_a.passes())
-    o_misc[1:2, :] = main_head.finish(1.0)
+    spread_c.wait()
 
     g_a.finish()
     g_a.drain()
@@ -1532,7 +1564,19 @@
 
     sync_a = Sync(v.sync_aux)
     sync_a.start(list(masked_sums(v.pre_a)))
-    g_main = main_head.grad()
+    spread_u.wait()
+    weight_c = v.w_c_all[...].reshape(512, 256)
+
+    def main_loss(k, carry):
+        at = rows_at(k, 144)
+        rows = jnp.concatenate([v.united[slot, at, :] for slot in range(SPLITS)], axis=1)
+        loss_rows, grad = soft_loss(dot(rows, weight_c), at, 1.0)
+        v.slope_main[at, :] = grad
+        return carry + loss_rows
+
+    loss_rows = total(lax.fori_loop(0, 4, main_loss, jnp.zeros((8, 256), F32)))
+    o_misc[1:2, :] = (loss_rows[:, :128] + loss_rows[:, 128:]) / SPLITS
+    g_main = v.slope_main[...]
     v.d_f[...] = dot_nt(g_main, v.w_c[...])
 
     def slope(value):
@@ -1752,7 +1796,7 @@
 
     s_u = ScatterUnite()
 
-    v.w_c[...] = dot_tn(v.united[...], g_main).astype(BF)
+    v.w_c[...] = dot_tn(v.united[t], g_main).astype(BF)
     mix(s_c.starts())
     sums = sync.wait()
     gain_grads[14] = (sums[1:2], sums[0:1])
@@ -1891,7 +1935,7 @@
             v.cat_a[at : at + 96, p * 128 : p * 128 + 128] = value.astype(BF)
 
     def aux_grad(c2):
-        value2 = dot_tn(v.whole[c2], v.cat_a[...])
+        value2 = dot(v.whole_t[c2], v.cat_a[...])
         for half in range(2):
             value = value2[half * 128 : half * 128 + 128]
             c = 2 * c2 + half
@@ -2006,7 +2050,7 @@
 
     ex = back_hidden(v.d_e[...], v.w_e[...], 0)
     def short_grad(c):
-        v.w_s[rows_at(c, 256), :] = dot_tn(v.whole[c], v.d_s[...]).astype(BF)
+        v.w_s[rows_at(c, 256), :] = dot(v.whole_t[c], v.d_s[...]).astype(BF)
 
     loop(SPLITS, short_grad)
     mix(s_s.starts(), s_u.middles(4))
@@ -2053,7 +2097,7 @@
     loop(6, back_reduce)
 
     def reduce_grad(c):
-        v.w_r[rows_at(c, 256), :] = dot_tn(v.whole[c], v.d_low[...]).astype(BF)
+        v.w_r[rows_at(c, 256), :] = dot(v.whole_t[c], v.d_low[...]).astype(BF)
 
     loop(SPLITS, reduce_grad)
     mix(s_r.starts())

time: 363 us -> 361 us (level)
  no operation moved by 1% of the time
where the time goes in v12:
time: 361 us
  Pallas kernels  350 us (97%)
  other arithmetic  8.26 us (2%)
    pallas_call x1, Pallas kernels, whole_step(): pl.pallas_call(functools.partial(step_kernel, tuple(plan)), out_shape=[ja...  333 us
    pallas_call x1, Pallas kernels, update(): pl.pallas_call(update_kernel, grid=(pl.cdiv(rows, 1024),), out_shape=[big...  17.2 us
    convert_element_type x1, other arithmetic, local_fast(): new_params.astype(BF)  7.53 us

profile of v12, /device:TPU:0, one launch (start us, length us, event | category | flops | bytes accessed | tf_op | source)
XLA Modules:
  0.0 360.8 jit_solution(12354751636168361095)
XLA Ops:
  0.6 0.7 select_convert_fusion
  1.4 0.1 broadcast_in_dim.12
  1.5 0.9 broadcast_in_dim.13.refs_1_
  2.3 333.2 %whole_step.1 = (f32[7712,128]{1,0:T(8,128)}, f32[1,128]{1,0:T(1,128)}, f32[8,128]{1,0:T(8,128)}) custom-call(s32[1,2]{1,0:T(1,128)} %refs_0_.1, f32[576,128]{1,0:T(8,128)} %broadcast_in_dim.13.refs_1_, bf16[576,256]{1,0:T(8,128)(2,1)} %bitcast.20, f32[7712,128]{1,0:T(8,128)} %bitcast.13), custom_call_target="tpu_custom_call" | custom-call | tf_op jit(solution)/shard_map/whole_step/pallas_call | solution.py:2190
  335.5 17.2 %update.1 = (f32[7712,128]{1,0:T(8,128)}, f32[7712,128]{1,0:T(8,128)}, f32[7712,128]{1,0:T(8,128)}, f32[7712,128]{1,0:T(8,128)}, f32[1,1]{1,0:T(1,128)}, /*index=5*/f32[1,1]{1,0:T(1,128)}, f32[1,1]{1,0:T(1,128)}) custom-call(f32[8,128]{1,0:T(8,128)} %get-tuple-element.19.misc, f32[7712,128]{1,0:T(8,128)} %get-tuple-element.20.grad, f32[7712,128]{1,0:T(8,128)} %bitcast.14, ...), custom_call_target="tpu_custom_call" | custom-call | tf_op jit(solution)/shard_map/update/pallas_call | solution.py:2231
  352.7 0.0 copy-start
  352.7 7.5 %convert_element_type.15 = bf16[1,987136]{1,0:T(2,128)(2,1)} convert(f32[1,987136]{1,0:T(1,128)} %bitcast.18) | non-fusion elementwise | flops 987136 | bytes 5922816 | tf_op jit(solution)/shard_map/convert_element_type | solution.py:2268
  360.3 0.0 copy-done
  360.3 0.5 copy.18
Async XLA Ops:
  352.7 7.5 %copy-start = (f32[1,128]{1,0:T(1,128)S(1)}, f32[1,128]{1,0:T(1,128)}, u32[]{:S(2)}) copy-start(f32[1,128]{1,0:T(1,128)} %get-tuple-element.28) | copy-start | bytes 1540

commit v13 on v12

--- a/solution.py
+++ b/solution.py
@@ -1226,7 +1226,7 @@
 
     loop(6, make_h1)
     spread_1.start()
-    mix(g_s.nears(), g_b0.fars())
+    mix(g_s.nears(), g_b0.fars() + g_u.fars(0))
     g_m.finish()
     spread_1.wait()
 
@@ -1259,7 +1259,7 @@
 
     loop(6, make_h2)
     spread_2.start()
-    mix(g_b0.passes() + g_b1.nears(), g_u.fars(0))
+    mix(g_b0.passes() + g_b1.nears(), g_u.fars(1))
     g_e.finish()
     g_s.finish()
     for k in range(0, 512, 256):
@@ -1271,7 +1271,7 @@
     sync = Sync(v.sync_three)
     e1, e2 = masked_sums(v.pre_e)
     sync.start(split_rows(e1) + split_rows(e2) + split_rows(s1) + split_rows(s2))
-    mix(g_b1.passes() + g_u.nears(0), g_u.fars(1))
+    mix(g_b1.passes() + g_u.nears(0), g_u.fars(2))
     mix(g_c.nears() + g_ac.nears(), g_c.fars() + g_ac.fars())
     sums = sync.wait()
     norm_e = moments(join_rows(sums, 0, 4), join_rows(sums, 4, 4), count4)
@@ -1329,7 +1329,7 @@
     v.recv_b[t] = v.part_b[t]
     ex = Exchange(TENSOR, SPLITS, lambda o: v.part_b.at[o], lambda s: v.recv_b.at[s])
     ex.start()
-    mix(g_u.passes(0) + g_u.nears(1), g_u.fars(2))
+    mix(g_u.passes(0) + g_u.nears(1), g_u.fars(4))
     joined_copy(0, t_x, t_x).wait_recv()
     joined_copy(2, t_x, t_core).start()
     ex.wait()
@@ -1339,7 +1339,7 @@
     v.all_b[me] = own_b.astype(BF)
     ex = Exchange(BATCH, OWNERS, lambda o: v.all_b.at[me], lambda s: v.all_b.at[s])
     ex.start()
-    mix(g_u.passes(1) + g_u.nears(2), g_u.fars(4))
+    mix(g_u.passes(1) + g_u.nears(2), g_u.fars(3))
     ex.wait()
     all_b = [v.all_b[k].astype(F32) for k in range(OWNERS)]
     sum_b, square_b = all_b[0], all_b[0] * all_b[0]
@@ -1365,7 +1365,7 @@
         out = gamma_b * ((all_b[k] - mean_b) * scale_b) + beta_b
         v.act_b[t, k * BINS : k * BINS + BINS, :] = jax.nn.silu(out).astype(BF)
     spread_b.start()
-    mix(g_u.passes(2) + g_u.nears(4), g_u.fars(3))
+    mix(g_u.passes(2) + g_u.nears(4) + g_u.nears(3))
     spread_b.wait()
     row_512 = lax.broadcasted_iota(jnp.int32, (OWNERS * BINS, 1), 0) & (BINS - 1)
     group_id = jnp.where(
@@ -1395,13 +1395,13 @@
     v.z_recv[me] = v.z_send[me]
     ex = Exchange(BATCH, OWNERS, lambda o: v.z_send.at[o], lambda s: v.z_recv.at[s])
     ex.start()
-    mix(g_u.passes(4) + g_u.nears(3))
+    mix(g_u.passes(4) + g_u.passes(3))
     v.act_t[...] = full_act().T
     joined_copy(1, t_core, t_core).wait_recv()
     joined_copy(2, t_diag, t_core).wait_recv()
     for k in range(SPLITS):
         v.joined_t[k] = v.joined[k].T
-    mix(g_u.passes(3) + g_c.passes() + g_ac.passes())
+    mix(g_c.passes() + g_ac.passes())
     ex.wait()
     g_u.finish((0, 1, 2, 4))
 
@@ -2085,7 +2085,20 @@
     sync.start(through_silu(v.d_f, v.pre_r, norm_r, 0))
 
     mix(s_e.middles())
+    squares = s_u.end()
+    pool_move.wait()
+    d_bp_move.wait()
+    own_group = jnp.where(group_id == lax.div(me, 2), 1.0, 0.0)
+    d_rows = jnp.concatenate(
+        [v.d_bp_all[:, k].reshape(OWNERS * BINS, 128) for k in range(SPLITS)], axis=1
+    )
+    d_rows = (d_rows.astype(F32) * own_group).astype(BF)
+    branch_grad = dot_tn(v.pool_all[...].reshape(OWNERS * BINS, 256), d_rows)
+    for k in range(4):
+        o_flat[pl.ds(1472 + k, 256, stride=4), :] = branch_grad[:, k * 128 : k * 128 + 128]
+    squares = squares + sum(split_rows(total(branch_grad * branch_grad)))
     sums = sync.wait()
+    mix(s_m.middles())
     gain_grads[0] = (sums[1:2], sums[0:1])
 
     def back_reduce(k):
@@ -2101,20 +2114,10 @@
 
     loop(SPLITS, reduce_grad)
     mix(s_r.starts())
-    mix(s_m.middles() + s_r.middles())
-    pool_move.wait()
-    d_bp_move.wait()
-    own_group = jnp.where(group_id == lax.div(me, 2), 1.0, 0.0)
-    d_rows = jnp.concatenate(
-        [v.d_bp_all[:, k].reshape(OWNERS * BINS, 128) for k in range(SPLITS)], axis=1
-    )
-    d_rows = (d_rows.astype(F32) * own_group).astype(BF)
-    branch_grad = dot_tn(v.pool_all[...].reshape(OWNERS * BINS, 256), d_rows)
-    for k in range(4):
-        o_flat[pl.ds(1472 + k, 256, stride=4), :] = branch_grad[:, k * 128 : k * 128 + 128]
-    rest = (s_c, s_ac, s_a, s_e, s_s, s_m, s_r)
-    squares = s_u.end() + sum(split_rows(total(branch_grad * branch_grad)))
-    for item in rest:
+    for item in (s_c, s_ac, s_a, s_s, s_e):
+        squares = squares + item.end()
+    mix(s_r.middles())
+    for item in (s_m, s_r):
         squares = squares + item.end()
     dm_near(1, t_diag).wait_send()
     dm_near(0, t_core).wait_send()

time: 361 us -> 374 us (1.036)
  Pallas kernels: 350 us -> 363 us
    pallas_call x1, Pallas kernels: 333 us -> 346 us  [whole_step(): pl.pallas_call(functools.partial(step_kernel, tuple(plan)), out_shape=[ja...]
where the time goes in v13:
time: 374 us; the launch traced here: 373 us
  Pallas kernels  363 us (97%)
  other arithmetic  8.26 us (2%)
    pallas_call x1, Pallas kernels, whole_step(): pl.pallas_call(functools.partial(step_kernel, tuple(plan)), out_shape=[ja...  346 us
    pallas_call x1, Pallas kernels, update(): pl.pallas_call(update_kernel, grid=(pl.cdiv(rows, 1024),), out_shape=[big...  17.2 us
    convert_element_type x1, other arithmetic, local_fast(): new_params.astype(BF)  7.53 us

profile of v13, /device:TPU:0, one launch (start us, length us, event | category | flops | bytes accessed | tf_op | source)
XLA Modules:
  0.0 373.1 jit_solution(9570584901251785510)
XLA Ops:
  0.6 0.7 select_convert_fusion
  1.4 0.1 broadcast_in_dim.12
  1.5 0.9 broadcast_in_dim.13.refs_1_
  2.3 345.6 %whole_step.1 = (f32[7712,128]{1,0:T(8,128)}, f32[1,128]{1,0:T(1,128)}, f32[8,128]{1,0:T(8,128)}) custom-call(s32[1,2]{1,0:T(1,128)} %refs_0_.1, f32[576,128]{1,0:T(8,128)} %broadcast_in_dim.13.refs_1_, bf16[576,256]{1,0:T(8,128)(2,1)} %bitcast.20, f32[7712,128]{1,0:T(8,128)} %bitcast.13), custom_call_target="tpu_custom_call" | custom-call | tf_op jit(solution)/shard_map/whole_step/pallas_call | solution.py:2193
  347.9 17.2 %update.1 = (f32[7712,128]{1,0:T(8,128)}, f32[7712,128]{1,0:T(8,128)}, f32[7712,128]{1,0:T(8,128)}, f32[7712,128]{1,0:T(8,128)}, f32[1,1]{1,0:T(1,128)}, /*index=5*/f32[1,1]{1,0:T(1,128)}, f32[1,1]{1,0:T(1,128)}) custom-call(f32[8,128]{1,0:T(8,128)} %get-tuple-element.19.misc, f32[7712,128]{1,0:T(8,128)} %get-tuple-element.20.grad, f32[7712,128]{1,0:T(8,128)} %bitcast.14, ...), custom_call_target="tpu_custom_call" | custom-call | tf_op jit(solution)/shard_map/update/pallas_call | solution.py:2234
  365.1 0.0 copy-start
  365.1 7.5 %convert_element_type.15 = bf16[1,987136]{1,0:T(2,128)(2,1)} convert(f32[1,987136]{1,0:T(1,128)} %bitcast.18) | non-fusion elementwise | flops 987136 | bytes 5922816 | tf_op jit(solution)/shard_map/convert_element_type | solution.py:2271
  372.6 0.0 copy-done
  372.6 0.5 copy.18
Async XLA Ops:
  365.1 7.5 %copy-start = (f32[1,128]{1,0:T(1,128)S(1)}, f32[1,128]{1,0:T(1,128)}, u32[]{:S(2)}) copy-start(f32[1,128]{1,0:T(1,128)} %get-tuple-element.28) | copy-start | bytes 1540
